TPU v7x, 32 devices: a whole 2x2x4 slice. The times are simulated.
32 devices in a mesh: grp: 2 (over x), tp: 8 (over z, y), pd: 2 (over core).
Axes of the slice: x: 2, y: 2, z: 4, core: 2. Of those that a mesh axis runs over, the one named last changes fastest.
Arguments:
- kv_pages: bfloat16 [9984, 2, 16, 128], P(('grp', 'tp', 'pd')), parts along dimension 0, may hold values from -8 to 8
- page_list: int32 [4992], P('grp'), parts along dimension 0, may hold values from -1 to 2047, as said below
- block_tables: int32 [256, 128], P(('grp', 'tp')), parts along dimension 0, may hold values from 0 to 311, as said below
- lengths: int32 [32], P('grp'), parts along dimension 0, may hold values from 1 to 2048
- queries: bfloat16 [256, 2, 1024], P(('grp', 'tp')), parts along dimension 0, may hold values from -8 to 8
- fresh_kv: bfloat16 [256, 2, 2, 128], P(('grp', 'tp')), parts along dimension 0, may hold values from -8 to 8
- stream: bfloat16 [64, 8192], P('grp', ('tp', 'pd')), parts along dimension 0, may hold values from -6 to 6
- out_proj: bfloat16 [8192, 8192], P(('tp', 'pd')), may hold values from -0.0625 to 0.0625
- norm_gain: float32 [8192], replicated, may hold values from 0.5 to 1.5
- gate_weight: bfloat16 [8192, 16384], P(None, ('tp', 'pd')), may hold values from -0.0625 to 0.0625
- up_weight: bfloat16 [8192, 16384], P(None, ('tp', 'pd')), may hold values from -0.0625 to 0.0625
- down_weight: bfloat16 [16384, 8192], P(('tp', 'pd')), may hold values from -0.046875 to 0.046875
Outputs:
- kv_after: bfloat16 [9984, 2, 16, 128], P(('grp', 'tp', 'pd')), parts along dimension 0
- layer_out: bfloat16 [64, 8192], P('grp', ('tp', 'pd')), parts along dimension 0
There are 2 independent parts, one for each index of `grp`. A program takes and returns all parts, laid end to end along the dimension named above; an argument that names none is the same for every part. Nothing has to cross between parts.
Inputs may be any that keep to these rules, and one draw needn't show every extreme that they name: `page_list`: entry t * 312 + i belongs to slot i of prefill member t: -1 if the page stays, else d * 256 + s, sending it to slot 56 + s of decode member d. Every arrival slot of every decode member receives exactly one page, and every prefill member sends exactly 32 pages to every decode member. `block_tables`: entry h * 16 + r lists in token order the slots of row r's pages for KV head h in the pool of decode member h + r // 16; entries past the row's pages are valid slots.
All inputs are finite; a program needn't handle non-finite values.
Results may differ from a plain program's by a relative error of at most 0.006.
Values may be sent and summed in bfloat16 or wider, within the bound.
No kernel may reach another device: no remote copies, remote signals or barrier semaphores. Data moves between devices by JAX's collectives and lax.ppermute only.
A program may use at most 192 MiB of HBM per device.

v0:
```python
import math

import jax
import jax.numpy as jnp
from jax import lax
from jax.sharding import PartitionSpec as P

HD = 128
KVH = 8
PAGE = 16
REQ_DEV = 2
NEWP = 128
POOL = 312


def shifted(block, axis, distance):
    devices = range(lax.axis_size(axis))
    route = [(i - distance, i) for i in devices if i - distance in devices]
    return lax.ppermute(block, axis, route)


def attend(page_pool, tables, row_lengths, query_rows, fresh_rows):
    row_count = tables.shape[0]
    step_count = query_rows.shape[1]
    head_size = fresh_rows.shape[-1]
    picked = page_pool[tables]
    cache_keys = picked[:, :, 0].reshape(row_count, -1, head_size)
    cache_values = picked[:, :, 1].reshape(row_count, -1, head_size)
    queries_split = query_rows.reshape(row_count, step_count, -1, head_size)
    score_scale = 1.0 / math.sqrt(head_size)
    cached = (
        jnp.einsum("isjd,ind->isjn", queries_split, cache_keys, preferred_element_type=jnp.float32)
        * score_scale
    )
    latest = (
        jnp.einsum(
            "isjd,itd->isjt", queries_split, fresh_rows[:, :, 0], preferred_element_type=jnp.float32
        )
        * score_scale
    )
    positions = jnp.arange(cache_keys.shape[1])
    cache_ok = (positions[None, :] < row_lengths[:, None])[:, None, None, :]
    step_ids = jnp.arange(step_count)
    fresh_ok = (step_ids[None, :] <= step_ids[:, None])[None, :, None, :]
    cached = jnp.where(cache_ok, cached, -jnp.inf)
    latest = jnp.where(fresh_ok, latest, -jnp.inf)
    row_max = jnp.maximum(jnp.max(cached, axis=-1), jnp.max(latest, axis=-1))[..., None]
    prob_cache = jnp.exp(cached - row_max)
    prob_fresh = jnp.exp(latest - row_max)
    denominator = jnp.sum(prob_cache, axis=-1) + jnp.sum(prob_fresh, axis=-1)
    numerator = jnp.einsum(
        "isjn,ind->isjd",
        prob_cache.astype(jnp.bfloat16),
        cache_values,
        preferred_element_type=jnp.float32,
    )
    numerator = numerator + jnp.einsum(
        "isjt,itd->isjd",
        prob_fresh.astype(jnp.bfloat16),
        fresh_rows[:, :, 1],
        preferred_element_type=jnp.float32,
    )
    result = (numerator / denominator[..., None]).astype(jnp.bfloat16)
    return result.reshape(row_count, step_count, -1)


def local(
    kv_pages,
    page_list,
    block_tables,
    lengths,
    queries,
    fresh_kv,
    stream,
    out_proj,
    norm_gain,
    gate_weight,
    up_weight,
    down_weight,
):
    members = lax.axis_size("tp")
    member = lax.axis_index("tp")
    half_index = lax.axis_index("pd")
    arrive = REQ_DEV * NEWP
    per_peer = arrive // members
    slots_all = page_list.reshape(members, POOL)
    own_list = lax.dynamic_index_in_dim(slots_all, member, 0, keepdims=False)
    target_member = jnp.where(own_list >= 0, own_list // arrive, members)
    send_order = jnp.argsort(target_member, stable=True)[: members * per_peer]
    outgoing = kv_pages[send_order].reshape(members, per_peer, 2, PAGE, HD)
    wanted = (slots_all >= 0) & (slots_all // arrive == member)
    picked = jnp.argsort(jnp.where(wanted, 0, 1), axis=1, stable=True)[:, :per_peer]
    landing = jnp.take_along_axis(slots_all, picked, axis=1) % arrive
    arrived = lax.all_to_all(outgoing, "tp", split_axis=0, concat_axis=0, tiled=True)
    arrived = shifted(arrived, "pd", 1)
    updated = kv_pages.at[POOL - arrive + landing.reshape(-1)].set(
        arrived.reshape(arrive, 2, PAGE, HD)
    )
    kv_after = jnp.where(half_index == 1, updated, kv_pages)
    groups = members // KVH
    rows_here = block_tables.shape[0]
    step_count = queries.shape[1]
    row_group = member % groups
    row_lengths = lax.dynamic_slice_in_dim(lengths, row_group * rows_here, rows_here)
    attended = attend(kv_after, block_tables, row_lengths, queries, fresh_kv)
    gathered = lax.all_gather(attended, ("tp", "pd"), axis=0, tiled=True).reshape(
        members, 2, rows_here, step_count, -1
    )[:, 1]
    columns = out_proj.shape[0]
    weight = out_proj.reshape(columns, KVH, -1)
    blocks = gathered.reshape(KVH, groups, rows_here, step_count, -1)
    projected = jnp.einsum(
        "hgisf,chf->sgic", blocks, weight, preferred_element_type=jnp.float32
    ).reshape(-1, columns)
    residual = (stream.astype(jnp.float32) + projected).astype(jnp.bfloat16)
    whole_rows = lax.all_gather(residual, ("tp", "pd"), axis=1, tiled=True)
    wide_rows = whole_rows.astype(jnp.float32)
    normed = (
        wide_rows
        * lax.rsqrt(jnp.mean(wide_rows * wide_rows, axis=1, keepdims=True) + 1e-05)
        * norm_gain
    ).astype(jnp.bfloat16)
    gate_act = jnp.dot(normed, gate_weight, preferred_element_type=jnp.float32)
    up_act = jnp.dot(normed, up_weight, preferred_element_type=jnp.float32)
    hidden = (jax.nn.silu(gate_act) * up_act).astype(jnp.bfloat16)
    summed = lax.psum_scatter(
        lax.dot_general(
            down_weight, hidden, (((0,), (1,)), ((), ())), preferred_element_type=jnp.float32
        ),
        ("tp", "pd"),
        scatter_dimension=0,
        tiled=True,
    )
    layer_out = (residual.astype(jnp.float32) + summed.T).astype(jnp.bfloat16)
    return (kv_after, layer_out)


def solution(mesh):
    return jax.shard_map(
        local,
        mesh=mesh,
        in_specs=(
            P(("grp", "tp", "pd"), None, None, None),
            P("grp"),
            P(("grp", "tp"), None),
            P("grp"),
            P(("grp", "tp"), None, None),
            P(("grp", "tp"), None, None, None),
            P("grp", ("tp", "pd")),
            P(("tp", "pd"), None),
            P(),
            P(None, ("tp", "pd")),
            P(None, ("tp", "pd")),
            P(("tp", "pd"), None),
        ),
        out_specs=(P(("grp", "tp", "pd"), None, None, None), P("grp", ("tp", "pd"))),
        check_vma=False,
    )
```

profile of v0, /device:TPU:0, one launch (start us, length us, event | category | flops | bytes accessed | tf_op | source)
XLA Modules:
  0.0 291.9 jit_solution(14618484216717348916)
XLA Ops:
  7.2 0.8 reshape.156
  8.0 3.8 %sort.35 = (s32[312]{0:T(512)}, s32[312]{0:T(512)S(1)}) sort(s32[312]{0:T(512)S(1)} %fusion.38, s32[312]{0:T(512)S(1)} %iota.33), dimensions={0}, to_apply=%region_1.2 | sort | flops 2808 | bytes 4992 | tf_op jit(solution)/shard_map/jit(argsort)/sort | solution.py:89
  11.8 3.9 %gather_fusion = bf16[256,2,16,128]{3,2,1,0:T(8,128)(2,1)} fusion(bf16[312,2,16,128]{3,2,1,0:T(8,128)(2,1)} %param.12, s32[1024]{0:T(1024)S(1)} %pad_clamp_fusion), kind=kCustom, calls=%fused_computation | custom fusion | bytes 4195328 | tf_op jit(solution)/shard_map/gather | solution.py:90
  15.7 7.4 %all-to-all-start = ((bf16[8,32,2,16,128]{4,3,2,1,0:T(8,128)(2,1)}), bf16[8,32,2,16,128]{4,3,2,1,0:T(8,128)(2,1)}, u32[]{:S(2)}, u32[]{:S(2)}) async-start(bf16[8,32,2,16,128]{4,3,2,1,0:T(8,128)(2,1)} %bitcast.86), calls=%async_computation | async-start | bytes 4194304 | tf_op jit(solution)/shard_map/all_to_all | solution.py:94
  23.2 1.5 copy.47
  24.6 46.8 %all-to-all-done = bf16[8,32,2,16,128]{4,3,2,1,0:T(8,128)(2,1)} async-done(((bf16[8,32,2,16,128]{4,3,2,1,0:T(8,128)(2,1)}), bf16[8,32,2,16,128]{4,3,2,1,0:T(8,128)(2,1)}, u32[]{:S(2)}, u32[]{:S(2)}) %all-to-all-start) | async-done | bytes 2097184 | tf_op jit(solution)/shard_map/all_to_all | solution.py:94
  71.4 1.4 collective-permute-start
  72.9 3.9 %sort.34 = (s32[8,312]{1,0:T(8,128)}, s32[8,312]{1,0:T(8,128)S(1)}) sort(s32[8,312]{1,0:T(8,128)S(1)} %and_select_fusion, s32[8,312]{1,0:T(8,128)S(1)} %iota.32), dimensions={1}, to_apply=%region_0.1 | sort | flops 29952 | bytes 39936 | tf_op jit(solution)/shard_map/jit(argsort)/sort | solution.py:92
  76.8 0.1 reshape.182
  76.9 1.9 gather_fusion.2
  78.8 0.1 reshape.185
  78.9 0.1 select_n.101
  79.1 0.4 fusion.45
  79.6 0.1 iota_compare_fusion
  79.7 26.5 %scatter_fusion = bf16[312,2,16,128]{3,2,1,0:T(8,128)(2,1)} fusion(bf16[312,2,16,128]{3,2,1,0:T(8,128)(2,1)} %copy.47, s32[256]{0:T(256)S(1)} %bitcast.88, bf16[256,2,16,128]{3,2,1,0:T(8,128)(2,1)S(1)} %bitcast.87), kind=kCustom, calls=%fused_computation.3 | custom fusion | bytes 6292480 | tf_op jit(solution)/shard_map/scatter | solution.py:96
  106.2 2.0 broadcast_select_fusion
  108.2 19.4 %gather_fusion.1 = bf16[2048,2,16,128]{3,2,1,0:T(8,128)(2,1)} fusion(bf16[312,2,16,128]{3,2,1,0:T(8,128)(2,1)S(1)} %broadcast_select_fusion, s32[2048]{0:T(1024)S(1)} %fusion.36), kind=kCustom, calls=%fused_computation.1 | custom fusion | bytes 33562624 | tf_op jit(solution)/shard_map/gather | solution.py:26
  127.6 7.4 %fusion.42 = (bf16[16,128,1,16,128]{4,3,2,1,0:T(8,128)(2,1)S(1)}, bf16[16,128,1,16,128]{4,3,2,1,0:T(8,128)(2,1)S(1)}) fusion(bf16[16,128,2,16,128]{4,3,2,1,0:T(8,128)(2,1)} %bitcast.83), kind=kLoop, calls=%fused_computation.82 | loop fusion | bytes 33554432 | tf_op jit(solution)/shard_map/slice | solution.py:28
  135.0 2.4 fusion.44
  137.4 0.4 fusion.4
  137.8 0.1 fusion.27
  137.9 0.2 fusion.29
  138.1 1.3 fusion.7
  139.5 0.6 copy.23
  140.2 37.8 %all-gather.2.cloned.1.call-done = bf16[256,2,1024]{2,0,1:T(8,128)(2,1)} async-done(((bf16[16,2,1024]{2,0,1:T(8,128)(2,1)}), bf16[256,2,1024]{2,0,1:T(8,128)(2,1)}) %all-gather.2.cloned.1.call-update) | async-done | bytes 1048592 | tf_op jit(solution)/shard_map/all_gather | solution.py:106
  178.0 6.2 %fusion = f32[16,2,512,1]{2,0,3,1:T(8,128)S(1)} fusion(bf16[64,8,8,1024]{3,2,1,0:T(8,128)(2,1)} %bitcast.89, bf16[8,2,16,2,1024]{4,2,1,0,3:T(8,128)(2,1)} %bitcast.90), kind=kOutput, calls=%fused_computation.6 | convolution fusion | flops 268435456 | bytes 8978432 | tf_op jit(solution)/shard_map/hgisf,chf->sgic/dot_general | solution.py:112
  184.2 20.9 %all_gather.7 = bf16[32,8192]{1,0:T(8,128)(2,1)S(1)} all-gather(bf16[32,512]{1,0:T(8,128)(2,1)S(1)} %fusion.24), channel_id=1, replica_groups=mesh['grp'=2,'tp'=8,'pd'=2] {'tp','pd'}, dimensions={1}, use_global_device_ids=true | all-gather | bytes 557056 | tf_op jit(solution)/shard_map/all_gather | solution.py:116
  205.1 0.2 fusion.10
  205.4 8.8 %fusion.17 = f32[32,1024]{1,0:T(8,128)S(1)} fusion(bf16[8192,1024]{1,0:T(8,128)(2,1)} %param.21, bf16[32,8192]{1,0:T(8,128)(2,1)S(1)} %all_gather.7, f32[8192]{0:T(1024)S(1)} %copy-done.2, f32[32]{0:T(128)S(1)} %add_rsqrt_fusion), kind=kOutput, calls=%fused_computation.29 | convolution fusion | flops 537919488 | bytes 17465472 | tf_op jit(solution)/shard_map/dot_general | solution.py:123
  214.2 14.7 %convolution_bitcast_fusion = f32[8192,32]{0,1:T(8,128)} fusion(bf16[1024,8192]{1,0:T(8,128)(2,1)} %param.23, bf16[8192,1024]{1,0:T(8,128)(2,1)} %param.22, bf16[32,8192]{1,0:T(8,128)(2,1)S(1)} %all_gather.7, f32[8192]{0:T(1024)S(1)} %copy-done.2, f32[32]{0:T(128)S(1)} %add_rsqrt_fusion, f32[32,1024]{1,0:T(8,128)S(1)} %fusion.17), kind=kOutput, calls=%fused_computation.4 | convolution fusion | flops 1074987008 | bytes 35291264 | tf_op jit(solution)/shard_map/dot_general | solution.py:127
  228.9 54.7 %reduce-scatter.2.cloned.1.call-done = f32[512,32]{0,1:T(8,128)} async-done(((f32[8192,32]{0,1:T(8,128)}), f32[512,32]{0,1:T(8,128)}) %reduce-scatter.2.cloned.1.call-update) | async-done | bytes 65552 | tf_op jit(solution)/shard_map/reduce_scatter | solution.py:126
  283.6 1.5 fusion.25
  (40 shorter events, 0.4 us)
Async XLA Ops:
  15.7 7.5 %copy-start.1 = (bf16[312,2,16,128]{3,2,1,0:T(8,128)(2,1)S(1)}, bf16[312,2,16,128]{3,2,1,0:T(8,128)(2,1)}, u32[]{:S(2)}) copy-start(bf16[312,2,16,128]{3,2,1,0:T(8,128)(2,1)} %param.12) | copy-start | bytes 7667716
  15.7 55.8 %all-to-all-start = ((bf16[8,32,2,16,128]{4,3,2,1,0:T(8,128)(2,1)}), bf16[8,32,2,16,128]{4,3,2,1,0:T(8,128)(2,1)}, u32[]{:S(2)}, u32[]{:S(2)}) async-start(bf16[8,32,2,16,128]{4,3,2,1,0:T(8,128)(2,1)} %bitcast.86), calls=%async_computation | async-start | bytes 4194304 | tf_op jit(solution)/shard_map/all_to_all | solution.py:94
  23.1 154.9 %all-gather.2.cloned.1.call-start = ((), (), s32[]{:S(2)}) async-start(), calls=%async_computation.2 | async-start | bytes 1114112 | tf_op jit(solution)/shard_map/all_gather | solution.py:106
  24.6 54.3 %copy-start.3 = (bf16[16,2,1024]{2,1,0:T(2,128)(2,1)S(1)}, bf16[16,2,1024]{2,1,0:T(2,128)(2,1)}, u32[]{:S(2)}) copy-start(bf16[16,2,1024]{2,1,0:T(2,128)(2,1)} %param.16) | copy-start | bytes 196612
  24.6 54.4 %copy-start.6 = (s32[16,128]{1,0:T(8,128)S(1)}, s32[16,128]{1,0:T(8,128)}, u32[]{:S(2)}) copy-start(s32[16,128]{1,0:T(8,128)} %param.14) | copy-start | bytes 24580
  24.6 54.5 %copy-start.4 = (bf16[16,2,2,128]{3,2,1,0:T(2,128)(2,1)S(1)}, bf16[16,2,2,128]{3,2,1,0:T(2,128)(2,1)}, u32[]{:S(2)}) copy-start(bf16[16,2,2,128]{3,2,1,0:T(2,128)(2,1)} %param.17) | copy-start | bytes 49156
  24.6 54.9 %copy-start.7 = (s32[16]{0:T(128)S(1)}, s32[16]{0:T(128)}, u32[]{:S(2)}) copy-start(s32[16]{0:T(128)} %param.15) | copy-start | bytes 196
  71.4 8.2 %collective-permute-start = (bf16[8,32,2,16,128]{4,3,2,1,0:T(8,128)(2,1)}, bf16[8,32,2,16,128]{4,3,2,1,0:T(8,128)(2,1)S(1)}, u32[]{:S(2)}, u32[]{:S(2)}) collective-permute-start(bf16[8,32,2,16,128]{4,3,2,1,0:T(8,128)(2,1)} %all-to-all-done), channel_id=1, source_target_pairs={{0,1},{2,3},{4,5},{6,7},{8,9},{10,11},{12,13},{14,15},{16,17},{18,... | collective-permute-start | bytes 6291464 | tf_op jit(solution)/shard_map/ppermute | solution.py:19
  108.2 19.4 %copy-start = (bf16[312,2,16,128]{3,2,1,0:T(8,128)(2,1)}, bf16[312,2,16,128]{3,2,1,0:T(8,128)(2,1)S(1)}, u32[]{:S(2)}) copy-start(bf16[312,2,16,128]{3,2,1,0:T(8,128)(2,1)S(1)} %broadcast_select_fusion) | copy-start | bytes 7667716
  140.1 143.5 %reduce-scatter.2.cloned.1.call-start = ((), (), s32[]{:S(2)}) async-start(), calls=%async_computation.3 | async-start | bytes 1114112 | tf_op jit(solution)/shard_map/reduce_scatter | solution.py:126
  178.0 6.2 %copy-start.5 = (bf16[32,512]{1,0:T(8,128)(2,1)S(1)}, bf16[32,512]{1,0:T(8,128)(2,1)}, u32[]{:S(2)}) copy-start(bf16[32,512]{1,0:T(8,128)(2,1)} %param.18) | copy-start | bytes 98308
  178.0 27.4 %copy-start.2 = (f32[8192]{0:T(1024)S(1)}, f32[8192]{0:T(1024)}, u32[]{:S(2)}) copy-start(f32[8192]{0:T(1024)} %param.20) | copy-start | bytes 98308
Sparse Core Ops, SparseCore 0:
  140.3 37.6 all-gather.1
  229.0 54.5 reduce-scatter.1
where the time goes:
time: 293 us; the launch traced here: 292 us
  waiting for transfers between devices  139 us (47%)
  local copies, waits for them, and re-layouts  62.3 us (21%)
  matrix products  34 us (12%)
  blocking collectives  20.9 us (7%)
  between operations  14.3 us (5%)
  other arithmetic  12.1 us (4%)
  starting transfers between devices  8.9 us (3%)
    reduce_scatter x1, waiting for transfers between devices, local(): lax.psum_scatter(lax.dot_general(down_weight, hidden, (((0,), (1,)), ((),...  54.7 us
    all_to_all x1, waiting for transfers between devices, local(): lax.all_to_all(outgoing, 'tp', split_axis=0, concat_axis=0, tiled=True)  46.8 us
    all_gather x1, waiting for transfers between devices, local(): lax.all_gather(attended, ('tp', 'pd'), axis=0, tiled=True)  37.8 us
    scatter x1, local copies, waits for them, and re-layouts, local(): kv_pages.at[POOL - arrive + landing.reshape(-1)]  26.5 us
    all_gather x1, blocking collectives, local(): whole_rows = lax.all_gather(residual, ('tp', 'pd'), axis=1, tiled=True)  20.9 us
    gather x1, local copies, waits for them, and re-layouts, attend(): picked = page_pool[tables]  19.4 us
    dot_general x1, matrix products, local(): lax.dot_general(down_weight, hidden, (((0,), (1,)), ((), ())), preferred_...  14.7 us
    dot_general x1, matrix products, local(): gate_act = jnp.dot(normed, gate_weight, preferred_element_type=jnp.float32)  8.82 us
  transfers between devices with their start and end apart: 4, of which 3 were waited for; matrix products, arithmetic and copies ran while one was open for 3% of the time, Pallas kernels for 0%

commit v1 on v0

v1 whole, which is shorter than its diff:
```python
import functools
import math

import jax
import jax.numpy as jnp
from jax import lax
from jax.experimental import pallas as pl
from jax.experimental.pallas import tpu as pltpu
from jax.sharding import PartitionSpec as P

HD = 128
KVH = 8
GQ = 8
PAGE = 16
REQ_DEV = 2
NEWP = 128
ARRIVE = REQ_DEV * NEWP
MIB = 1024 * 1024
BOTH = ("tp", "pd")

VM = pl.BlockSpec(memory_space=pltpu.VMEM)
SM = pl.BlockSpec(memory_space=pltpu.SMEM)
ANY = pl.BlockSpec(memory_space=pl.ANY)


def pack_kernel(members, place, pages, pool, *refs):
    outs = refs[:members]
    packed, counts, sems = refs[members:]
    member, half = place[0], place[1]
    slots = pool.shape[0]
    per_peer = ARRIVE // members

    @pl.when(half == 0)
    def _():
        @pl.loop(0, members + 1)
        def _(i):
            counts[i] = 0

        @pl.loop(0, slots, unroll=8)
        def _(i):
            entry = pages[member * slots + i]
            target = entry // ARRIVE
            ahead = lax.rem(target - member + members, members)
            row = jnp.where(entry >= 0, ahead, members)
            count = counts[row]
            counts[row] = count + 1
            spot = jnp.where(entry >= 0, row * per_peer + count, ARRIVE)
            packed[spot] = pool[i]

        copies = [
            pltpu.make_async_copy(packed.at[pl.ds(k * per_peer, per_peer)], outs[k], sems.at[k])
            for k in range(members)
        ]
        for copy in copies:
            copy.start()
        for copy in copies:
            copy.wait()


def pack(place, pages, pool):
    members = lax.axis_size("tp")
    per_peer = ARRIVE // members
    shape = jax.ShapeDtypeStruct((per_peer, *pool.shape[1:]), pool.dtype)
    return pl.pallas_call(
        functools.partial(pack_kernel, members),
        out_shape=[shape] * members,
        in_specs=[SM, SM, VM],
        out_specs=[ANY] * members,
        scratch_shapes=[
            pltpu.VMEM((ARRIVE + 1, *pool.shape[1:]), pool.dtype),
            pltpu.SMEM((members + 1,), jnp.int32),
            pltpu.SemaphoreType.DMA((members,)),
        ],
        compiler_params=pltpu.CompilerParams(vmem_limit_bytes=16 * MIB),
        name="pack_pages",
    )(place, pages, pool)


def attend_kernel(members, place, landing, old_pool, bias, query, new_k, new_v, *refs):
    arrived = refs[:members]
    kv_out, att_out = refs[members : members + 2]
    pool, scores, sems = refs[members + 2 :]
    half = place[1]
    slots = pool.shape[0]
    resident = slots - ARRIVE
    per_peer = ARRIVE // members
    rows = bias.shape[0]
    count = query.shape[0]
    steps = count // (rows * GQ)

    @pl.when(half == 0)
    def _():
        copy = pltpu.make_async_copy(old_pool, kv_out, sems.at[0])
        copy.start()
        att_out[...] = jnp.zeros_like(att_out)
        copy.wait()

    @pl.when(half == 1)
    def _():
        copy = pltpu.make_async_copy(
            old_pool.at[pl.ds(0, resident)], pool.at[pl.ds(0, resident)], sems.at[0]
        )
        copy.start()
        for k in range(members):

            @pl.loop(0, per_peer, unroll=math.gcd(per_peer, 8))
            def _(c):
                pool[resident + landing[k * per_peer + c]] = arrived[k][c]

        copy.wait()
        copy_out = pltpu.make_async_copy(pool, kv_out, sems.at[1])
        copy_out.start()

        scale = 1.0 / math.sqrt(HD)
        q = query[...]
        nt = (((1,), (1,)), ((), ()))
        group = 24
        width = group * PAGE
        lanes = 128
        fresh = lax.dot_general(q, new_k[...], nt, preferred_element_type=jnp.float32) * scale
        q_id = lax.broadcasted_iota(jnp.int32, fresh.shape, 0)
        t_id = lax.broadcasted_iota(jnp.int32, fresh.shape, 1)
        allowed = (q_id % rows == t_id // steps) & (t_id % steps <= (q_id // rows) % steps)
        fresh = jnp.where(allowed, fresh, -jnp.inf)
        peak = fresh
        for c in range(slots // group):
            keys = pool[c * group : (c + 1) * group, 0].reshape(width, HD)
            s = lax.dot_general(q, keys, nt, preferred_element_type=jnp.float32) * scale
            b = bias[:, c * width : (c + 1) * width]
            s = (s.reshape(count // rows, rows, width) + b[None]).reshape(count, width)
            scores[:, c * width : (c + 1) * width] = s
            for i in range(width // lanes):
                peak = jnp.maximum(peak, s[:, i * lanes : (i + 1) * lanes])
        top = jnp.max(peak, axis=1, keepdims=True)
        p = jnp.exp(fresh - top)
        total = p
        acc = jnp.dot(p.astype(jnp.bfloat16), new_v[...], preferred_element_type=jnp.float32)
        for c in range(slots // group):
            p = jnp.exp(scores[:, c * width : (c + 1) * width] - top)
            for i in range(width // lanes):
                total = total + p[:, i * lanes : (i + 1) * lanes]
            values = pool[c * group : (c + 1) * group, 1].reshape(width, HD)
            acc = acc + jnp.dot(p.astype(jnp.bfloat16), values, preferred_element_type=jnp.float32)
        out = (acc / jnp.sum(total, axis=1, keepdims=True)).astype(jnp.bfloat16)
        tokens = rows * steps
        for j in range(GQ):
            att_out[:, j * HD : (j + 1) * HD] = out[j * tokens : (j + 1) * tokens]
        copy_out.wait()


def place_and_attend(place, landing, old_pool, bias, query, new_k, new_v, arrived):
    members = len(arrived)
    slots = old_pool.shape[0]
    rows = bias.shape[0]
    count = query.shape[0]
    tokens = count // GQ
    return pl.pallas_call(
        functools.partial(attend_kernel, members),
        out_shape=[
            jax.ShapeDtypeStruct(old_pool.shape, old_pool.dtype),
            jax.ShapeDtypeStruct((tokens, GQ * HD), jnp.bfloat16),
        ],
        in_specs=[SM, SM, ANY, VM, VM, VM, VM] + [VM] * members,
        out_specs=[ANY, VM],
        scratch_shapes=[
            pltpu.VMEM(old_pool.shape, old_pool.dtype),
            pltpu.VMEM((count, slots * PAGE), jnp.float32),
            pltpu.SemaphoreType.DMA((2,)),
        ],
        compiler_params=pltpu.CompilerParams(vmem_limit_bytes=28 * MIB),
        name="place_attend",
    )(place, landing, old_pool, bias, query, new_k, new_v, *arrived)


def table_bias(tables, row_lengths, slots):
    pages = jnp.arange(tables.shape[1])
    whole_pages = row_lengths // PAGE
    hit = tables[:, :, None] == jnp.arange(slots)[None, None, :]
    whole = jnp.sum(
        (hit & (pages[None, :, None] < whole_pages[:, None, None])).astype(jnp.float32), axis=1
    )
    part = jnp.sum(
        (hit & (pages[None, :, None] == whole_pages[:, None, None])).astype(jnp.float32), axis=1
    )
    inside = (jnp.arange(PAGE)[None, :] < (row_lengths % PAGE)[:, None]).astype(jnp.float32)
    times = whole[:, :, None] + part[:, :, None] * inside[:, None, :]
    return jnp.log(times).reshape(tables.shape[0], slots * PAGE)


def landing_slots(slots_from, member, per_peer):
    wanted = (slots_from >= 0) & (slots_from // ARRIVE == member)
    ahead = jnp.cumsum(wanted.astype(jnp.int32), axis=1) - 1
    pick = wanted[:, None, :] & (ahead[:, None, :] == jnp.arange(per_peer)[None, :, None])
    return jnp.sum(jnp.where(pick, (slots_from % ARRIVE)[:, None, :], 0), axis=2)


def project_kernel(members, groups, place, weight, stream, here, there, res_out):
    member, half = place[0], place[1]
    width = GQ * HD
    tokens = here.shape[1]

    def run(source):
        sums = [stream[g * tokens : (g + 1) * tokens].astype(jnp.float32) for g in range(groups)]
        if groups > 1:
            res_f32 = jnp.stack(sums)
        else:
            res_f32 = sums[0]
        for k in range(members):
            owner = lax.rem(member - k + members, members)
            head = pl.multiple_of(owner // groups * width, width)
            part = lax.dot_general(
                source[k],
                weight[:, pl.ds(head, width)],
                (((1,), (1,)), ((), ())),
                preferred_element_type=jnp.float32,
            )
            if groups > 1:
                mine = lax.broadcasted_iota(jnp.int32, res_f32.shape, 0) == lax.rem(owner, groups)
                res_f32 = res_f32 + jnp.where(mine, part[None], 0.0)
            else:
                res_f32 = res_f32 + part
        res_out[...] = res_f32.reshape(res_out.shape).astype(res_out.dtype)

    @pl.when(half == 1)
    def _():
        run(here)

    @pl.when(half == 0)
    def _():
        run(there)


def project(place, weight, stream, here, there, groups):
    members = here.shape[0]
    return pl.pallas_call(
        functools.partial(project_kernel, members, groups),
        out_shape=jax.ShapeDtypeStruct(stream.shape, jnp.bfloat16),
        in_specs=[SM, VM, VM, VM, VM],
        out_specs=VM,
        compiler_params=pltpu.CompilerParams(vmem_limit_bytes=24 * MIB),
        name="out_projection",
    )(place, weight, stream, here, there)


def ffn_kernel(place, mine, sibling, gain, gate, up, down, own_out, other_out, *scratch):
    gate_buf, up_buf, down_buf, normed, gate_sem, up_sem, down_sem = scratch
    half = place[1]
    members, tokens, width = mine.shape
    features = gate.shape[0]
    hidden_count = gate.shape[1]
    blocks = 2 * members
    order = [(t, p) for p in range(2) for t in range(members)]

    def rows_of(t, p):
        which = half if p == 0 else 1 - half
        return pl.ds(pl.multiple_of((t * 2 + which) * width, width), width)

    up_copies, gate_copies, down_copies = [], [], []
    for i, (t, p) in enumerate(order):
        rows = rows_of(t, p)
        gate_copies.append(pltpu.make_async_copy(gate.at[rows], gate_buf.at[rows], gate_sem.at[i]))
        up_copies.append(pltpu.make_async_copy(up.at[rows], up_buf.at[rows], up_sem.at[i]))
        gate_copies[-1].start()
        up_copies[-1].start()
    for t in range(members):
        cols = pl.ds(t * 2 * width, 2 * width)
        down_copies.append(
            pltpu.make_async_copy(down.at[:, cols], down_buf.at[:, cols], down_sem.at[t])
        )
        down_copies[-1].start()

    square = jnp.zeros((tokens, width), jnp.float32)
    for block in (mine, sibling):
        for t in range(members):
            x = block[t].astype(jnp.float32)
            square = square + x * x
    factor = lax.rsqrt(jnp.sum(square, axis=1, keepdims=True) / features + 1e-05)
    gate_act = jnp.zeros((tokens, hidden_count), jnp.float32)
    up_act = jnp.zeros((tokens, hidden_count), jnp.float32)
    for i, (t, p) in enumerate(order):
        rows = rows_of(t, p)
        x = (mine if p == 0 else sibling)[t].astype(jnp.float32)
        which = half if p == 0 else 1 - half
        g = gain[pl.ds(t * 2 + which, 1), :]
        n = (x * factor * g).astype(jnp.bfloat16)
        gate_copies[i].wait()
        gate_act = gate_act + jnp.dot(n, gate_buf[rows, :], preferred_element_type=jnp.float32)
        up_copies[i].wait()
        up_act = up_act + jnp.dot(n, up_buf[rows, :], preferred_element_type=jnp.float32)
    hidden = (gate_act / (1.0 + jnp.exp(-gate_act)) * up_act).astype(jnp.bfloat16)
    for t in range(members):
        down_copies[t].wait()
        part = jnp.dot(
            hidden,
            down_buf[:, 2 * t * width : 2 * (t + 1) * width],
            preferred_element_type=jnp.float32,
        )
        first, second = part[:, :width], part[:, width:]
        own_out[t] = jnp.where(half == 0, first, second)
        other_out[t] = jnp.where(half == 0, second, first).astype(jnp.bfloat16)


def feed_forward(place, mine, sibling, gain, gate, up, down):
    members, tokens, width = mine.shape
    blocks = 2 * members
    return pl.pallas_call(
        ffn_kernel,
        out_shape=[
            jax.ShapeDtypeStruct(mine.shape, jnp.float32),
            jax.ShapeDtypeStruct(mine.shape, jnp.bfloat16),
        ],
        in_specs=[SM, VM, VM, VM, ANY, ANY, ANY],
        out_specs=[VM, VM],
        scratch_shapes=[
            pltpu.VMEM(gate.shape, gate.dtype),
            pltpu.VMEM(up.shape, up.dtype),
            pltpu.VMEM(down.shape, down.dtype),
            pltpu.VMEM((8, 128), jnp.float32),
            pltpu.SemaphoreType.DMA((blocks,)),
            pltpu.SemaphoreType.DMA((blocks,)),
            pltpu.SemaphoreType.DMA((members,)),
        ],
        compiler_params=pltpu.CompilerParams(vmem_limit_bytes=56 * MIB),
        name="feed_forward",
    )(place, mine, sibling, gain.reshape(blocks, width), gate, up, down)


def local(
    kv_pages,
    page_list,
    block_tables,
    lengths,
    queries,
    fresh_kv,
    stream,
    out_proj,
    norm_gain,
    gate_weight,
    up_weight,
    down_weight,
):
    members = lax.axis_size("tp")
    member = lax.axis_index("tp")
    half = lax.axis_index("pd")
    place = jnp.stack([member, half]).astype(jnp.int32)
    slots = kv_pages.shape[0]
    per_peer = ARRIVE // members
    groups = members // KVH
    rows = block_tables.shape[0]
    steps = queries.shape[1]
    tokens = rows * steps

    def ahead(x, k, from_half, to_half):
        route = [
            (2 * t + from_half, 2 * ((t + k) % members) + to_half) for t in range(members)
        ]
        return lax.ppermute(x, BOTH, route)

    def swap(x):
        return lax.ppermute(x, "pd", [(0, 1), (1, 0)])

    outgoing = pack(place, page_list, kv_pages)
    arrived = [ahead(outgoing[k], k, 0, 1) for k in range(members)]

    behind = (member - jnp.arange(members)) % members
    landing = landing_slots(page_list.reshape(members, slots)[behind], member, per_peer)
    row_lengths = lax.dynamic_slice_in_dim(lengths, member % groups * rows, rows)
    bias = table_bias(block_tables, row_lengths, slots)
    query = queries.reshape(rows, steps, GQ, HD).transpose(2, 1, 0, 3).reshape(GQ * tokens, HD)
    padding = ((0, -tokens % 128), (0, 0))
    new_k = jnp.pad(fresh_kv[:, :, 0].reshape(tokens, HD), padding)
    new_v = jnp.pad(fresh_kv[:, :, 1].reshape(tokens, HD), padding)

    kv_after, attended = place_and_attend(
        place, landing.reshape(-1), kv_pages, bias, query, new_k, new_v, arrived
    )

    pieces = [attended] + [ahead(attended, k, 1, 1) for k in range(1, members)]
    here = jnp.stack(pieces)
    there = lax.ppermute(here, "pd", [(1, 0)])

    inner = stream.reshape(steps, groups, rows, -1).transpose(1, 0, 2, 3).reshape(stream.shape)
    residual = project(place, out_proj, inner, here, there, groups)

    spread = jnp.broadcast_to(residual[None], (members, *residual.shape))
    mine = lax.all_to_all(spread, "tp", split_axis=0, concat_axis=0)
    sibling = swap(mine)
    own, other = feed_forward(
        place, mine, sibling, norm_gain, gate_weight, up_weight, down_weight
    )
    summed = (own + swap(other).astype(jnp.float32)).astype(jnp.bfloat16)
    shares = lax.all_to_all(summed, "tp", split_axis=0, concat_axis=0)
    layer = residual.astype(jnp.float32) + jnp.sum(shares.astype(jnp.float32), axis=0)
    layer_out = (
        layer.astype(jnp.bfloat16)
        .reshape(groups, steps, rows, -1)
        .transpose(1, 0, 2, 3)
        .reshape(stream.shape)
    )
    return (kv_after, layer_out)


def solution(mesh):
    return jax.shard_map(
        local,
        mesh=mesh,
        in_specs=(
            P(("grp", "tp", "pd"), None, None, None),
            P("grp"),
            P(("grp", "tp"), None),
            P("grp"),
            P(("grp", "tp"), None, None),
            P(("grp", "tp"), None, None, None),
            P("grp", ("tp", "pd")),
            P(("tp", "pd"), None),
            P(),
            P(None, ("tp", "pd")),
            P(None, ("tp", "pd")),
            P(("tp", "pd"), None),
        ),
        out_specs=(P(("grp", "tp", "pd"), None, None, None), P("grp", ("tp", "pd"))),
        check_vma=False,
    )
```

time: 293 us -> 135 us (0.46)
  waiting for transfers between devices: 139 us -> 32.1 us
  local copies, waits for them, and re-layouts: 62.3 us -> 13.3 us
  matrix products: 34 us -> 0 us
  Pallas kernels: 0 us -> 32.5 us
  between operations: 14.3 us -> 1.1 us
  starting transfers between devices: 8.9 us -> 20 us
  blocking collectives: 20.9 us -> 27.1 us
  other arithmetic: 12.1 us -> 7.9 us
    reduce_scatter x1 -> x0, waiting for transfers between devices: 54.7 us -> none  [local(): lax.psum_scatter(lax.dot_general(down_weight, hidden, (((0,), (1,)), ((),...]
    all_to_all x1 -> x0, waiting for transfers between devices: 46.8 us -> none  [local(): lax.all_to_all(outgoing, 'tp', split_axis=0, concat_axis=0, tiled=True)]
    all_gather x1 -> x0, waiting for transfers between devices: 37.8 us -> none  [local(): lax.all_gather(attended, ('tp', 'pd'), axis=0, tiled=True)]
    dot_general x7 -> x0, matrix products: 34 us -> none  [the longest x1 14.7 us: local(): lax.dot_general(down_weight, hidden, (((0,), (1,)), ((), ())), preferred_...]
    pallas_call x0 -> x4, Pallas kernels: none -> 32.5 us  [the longest x1 21.2 us: feed_forward(): pl.pallas_call(ffn_kernel, out_shape=[jax.ShapeDtypeStruct(mine.shape, jn...]
    ppermute x1 -> x18, waiting for transfers between devices: 0.01 us -> 32.1 us  [the longest x1 29 us: local(): there = lax.ppermute(here, 'pd', [(1, 0)])]
    all_to_all x0 -> x2, blocking collectives: none -> 27.1 us  [the longest x1 14.4 us: local(): mine = lax.all_to_all(spread, 'tp', split_axis=0, concat_axis=0)]
    scatter x1 -> x0, local copies, waits for them, and re-layouts: 26.5 us -> none  [local(): kv_pages.at[POOL - arrive + landing.reshape(-1)]]
  transfers between devices with their start and end apart: 4 -> 18, of which waited for: 3 -> 4; matrix products, arithmetic and copies ran while one was open for 3% -> 8% of each run, Pallas kernels for 0% -> 0%
where the time goes in v1:
time: 135 us; the launch traced here: 134 us
  Pallas kernels  32.5 us (24%)
  waiting for transfers between devices  32.1 us (24%)
  blocking collectives  27.1 us (20%)
  starting transfers between devices  20 us (15%)
  local copies, waits for them, and re-layouts  13.3 us (10%)
  other arithmetic  7.9 us (6%)
    ppermute x1, waiting for transfers between devices, local(): there = lax.ppermute(here, 'pd', [(1, 0)])  29 us
    pallas_call x1, Pallas kernels, feed_forward(): pl.pallas_call(ffn_kernel, out_shape=[jax.ShapeDtypeStruct(mine.shape, jn...  21.2 us
    ppermute x15, starting transfers between devices, ahead(): return lax.ppermute(x, BOTH, route)  18.5 us
    all_to_all x1, blocking collectives, local(): mine = lax.all_to_all(spread, 'tp', split_axis=0, concat_axis=0)  14.4 us
    all_to_all x1, blocking collectives, local(): shares = lax.all_to_all(summed, 'tp', split_axis=0, concat_axis=0)  12.6 us
    unnamed x39, local copies, waits for them, and re-layouts  8.29 us
    pallas_call x1, Pallas kernels, pack(): pl.pallas_call(functools.partial(pack_kernel, members), out_shape=[shape]...  5.39 us
    pallas_call x1, Pallas kernels, project(): pl.pallas_call(functools.partial(project_kernel, members, groups), out_sh...  3.12 us
  transfers between devices with their start and end apart: 18, of which 4 were waited for; matrix products, arithmetic and copies ran while one was open for 8% of the time, Pallas kernels for 0%

profile of v1, /device:TPU:0, one launch (start us, length us, event | category | flops | bytes accessed | tf_op | source)
XLA Modules:
  0.0 134.0 jit_solution(6929853315155846872)
XLA Ops:
  0.7 1.7 %copy-done = bf16[312,2,16,128]{3,2,1,0:T(8,128)(2,1)S(1)} copy-done((bf16[312,2,16,128]{3,2,1,0:T(8,128)(2,1)S(1)}, bf16[312,2,16,128]{3,2,1,0:T(8,128)(2,1)}, u32[]{:S(2)}) %copy-start) | copy-done | bytes 2555928
  2.5 0.7 copy-done.5
  3.2 5.4 %pack_pages.1 = (bf16[32,2,16,128]{3,2,1,0:T(8,128)(2,1)}, bf16[32,2,16,128]{3,2,1,0:T(8,128)(2,1)}, bf16[32,2,16,128]{3,2,1,0:T(8,128)(2,1)}, bf16[32,2,16,128]...) custom-call(s32[2]{0:T(128)S(1)} %pad_add_fusion.place, ...), custom_call_target="tpu_custom_call" | custom-call | tf_op jit(solution)/shard_map/pack_pages/pallas_call | solution.py:64
  8.6 1.3 collective-permute-start
  9.9 1.3 collective-permute-start.1
  11.2 1.3 collective-permute-start.2
  12.5 2.0 %collective-permute-start.3 = (bf16[32,2,16,128]{3,2,1,0:T(8,128)(2,1)}, bf16[32,2,16,128]{3,2,1,0:T(8,128)(2,1)}, u32[]{:S(2)}, u32[]{:S(2)}) collective-permute-start(bf16[32,2,16,128]{3,2,1,0:T(8,128)(2,1)} %get-tuple-element.17), channel_id=1, source_target_pairs={{0,7},{2,9},{4,11},{6,13},{8,15},{10,1},{12,3},{14,5},{16,23},{18,... | collective-permute-start | bytes 786440 | tf_op jit(solution)/shard_map/ppermute | solution.py:357
  14.5 2.0 %collective-permute-start.4 = (bf16[32,2,16,128]{3,2,1,0:T(8,128)(2,1)}, bf16[32,2,16,128]{3,2,1,0:T(8,128)(2,1)}, u32[]{:S(2)}, u32[]{:S(2)}) collective-permute-start(bf16[32,2,16,128]{3,2,1,0:T(8,128)(2,1)} %get-tuple-element.18), channel_id=1, source_target_pairs={{0,9},{2,11},{4,13},{6,15},{8,1},{10,3},{12,5},{14,7},{16,25},{18,... | collective-permute-start | bytes 786440 | tf_op jit(solution)/shard_map/ppermute | solution.py:357
  17.2 0.9 reduce-window.6
  18.6 1.7 %convert_reduce_fusion.1 = (f32[16,312]{1,0:T(8,128)S(1)}, f32[16,312]{1,0:T(8,128)S(1)}) fusion(s32[16,128]{1,0:T(8,128)S(1)} %copy-done.13, pred[16,128]{1,0:T(8,128)(4,1)S(1)} %get-tuple-element.31, pred[16,128]{1,0:T(8,128)(4,1)S(1)} %get-tuple-element.30), kind=kLoop, calls=%fused_computation.3 | loop fusion | flops 4462848 | bytes 52224 | tf_op jit(solution)/shard_map/reduce_sum | solution.py:179
  20.3 2.9 %add_log_fusion = f32[16,312,16]{2,1,0:T(8,128)} fusion(f32[16,16]{1,0:T(8,128)S(1)} %fusion.5, f32[16,312]{1,0:T(8,128)S(1)} %get-tuple-element.27, f32[16,312]{1,0:T(8,128)S(1)} %get-tuple-element.26), kind=kLoop, calls=%fused_computation.1 | loop fusion | flops 159744 | bytes 360448 | tf_op jit(solution)/shard_map/log | solution.py:187
  23.3 2.0 %collective-permute-start.5 = (bf16[32,2,16,128]{3,2,1,0:T(8,128)(2,1)}, bf16[32,2,16,128]{3,2,1,0:T(8,128)(2,1)}, u32[]{:S(2)}, u32[]{:S(2)}) collective-permute-start(bf16[32,2,16,128]{3,2,1,0:T(8,128)(2,1)} %get-tuple-element.19), channel_id=1, source_target_pairs={{0,11},{2,13},{4,15},{6,1},{8,3},{10,5},{12,7},{14,9},{16,27},{18,... | collective-permute-start | bytes 786440 | tf_op jit(solution)/shard_map/ppermute | solution.py:357
  25.3 2.0 %collective-permute-start.6 = (bf16[32,2,16,128]{3,2,1,0:T(8,128)(2,1)}, bf16[32,2,16,128]{3,2,1,0:T(8,128)(2,1)}, u32[]{:S(2)}, u32[]{:S(2)}) collective-permute-start(bf16[32,2,16,128]{3,2,1,0:T(8,128)(2,1)} %get-tuple-element.20), channel_id=1, source_target_pairs={{0,13},{2,15},{4,1},{6,3},{8,5},{10,7},{12,9},{14,11},{16,29},{18,... | collective-permute-start | bytes 786440 | tf_op jit(solution)/shard_map/ppermute | solution.py:357
  27.2 0.7 copy-done.3
  28.0 2.0 %collective-permute-start.7 = (bf16[32,2,16,128]{3,2,1,0:T(8,128)(2,1)}, bf16[32,2,16,128]{3,2,1,0:T(8,128)(2,1)}, u32[]{:S(2)}, u32[]{:S(2)}) collective-permute-start(bf16[32,2,16,128]{3,2,1,0:T(8,128)(2,1)} %get-tuple-element.21), channel_id=1, source_target_pairs={{0,15},{2,1},{4,3},{6,5},{8,7},{10,9},{12,11},{14,13},{16,31},{18,... | collective-permute-start | bytes 786440 | tf_op jit(solution)/shard_map/ppermute | solution.py:357
  30.3 2.4 %log.8.bias = f32[16,4992]{1,0:T(8,128)S(1)} reshape(f32[16,312,16]{2,1,0:T(8,128)} %add_log_fusion) | data formatting | bytes 638976 | tf_op jit(solution)/shard_map/log | solution.py:187
  32.8 0.9 reshape.192
  34.4 0.9 copy-done.4
  35.4 2.8 %place_attend.1 = (bf16[312,2,16,128]{3,2,1,0:T(8,128)(2,1)}, bf16[32,1024]{1,0:T(8,128)(2,1)S(1)}) custom-call(s32[2]{0:T(128)S(1)} %pad_add_fusion.place, s32[256]{0:T(256)S(1)} %reshape.191.landing, bf16[312,2,16,128]{3,2,1,0:T(8,128)(2,1)S(1)} %copy-done.1, f32[16,4992]{1,0:T(8,128)S(1)} %log.8.bias, bf16[256,128]{1,0:T(8,128)(2,1)S(1)} %bitcast.30, ...), custom_call_target="tpu_custom_call" | custom-call | tf_op jit(solution)/shard_map/place_attend/pallas_call | solution.py:157
  38.1 0.7 collective-permute-start.8
  43.1 1.3 collective-permute-start.15
  44.4 29.0 %collective-permute-done.15.there = bf16[8,32,1024]{2,1,0:T(8,128)(2,1)S(1)} collective-permute-done((bf16[8,32,1024]{2,1,0:T(8,128)(2,1)S(1)}, bf16[8,32,1024]{2,1,0:T(8,128)(2,1)S(1)}, u32[]{:S(2)}, u32[]{:S(2)}) %collective-permute-start.15) | collective-permute-done | bytes 524320 | tf_op jit(solution)/shard_map/ppermute | solution.py:380
  73.4 3.4 %copy-done.2 = bf16[512,8192]{1,0:T(8,128)(2,1)S(1)} copy-done((bf16[512,8192]{1,0:T(8,128)(2,1)S(1)}, bf16[512,8192]{1,0:T(8,128)(2,1)}, u32[]{:S(2)}) %copy-start.2) | copy-done | bytes 8388632
  76.7 3.1 %out_projection.1 = bf16[32,512]{1,0:T(8,128)(2,1)S(1)} custom-call(s32[2]{0:T(128)S(1)} %pad_add_fusion.place, bf16[512,8192]{1,0:T(8,128)(2,1)S(1)} %copy-done.2, bf16[32,512]{1,0:T(8,128)(2,1)S(1)} %copy-done.7, bf16[8,32,1024]{2,1,0:T(8,128)(2,1)S(1)} %bitcast_dynamic-update-slice_fusion.here, bf16[8,32,1024]{2,1,0:T(8,128)(2,1)S(1)} %collective-permute-done.15.there), custom_call_target="tpu_custom_call" | custom-call | tf_op jit(solution)/shard_map/out_projection/pallas_call | solution.py:235
  79.9 14.4 %all_to_all.10.mine = bf16[8,32,512]{2,1,0:T(8,128)(2,1)S(1)} all-to-all(bf16[8,32,512]{2,1,0:T(8,128)(2,1)S(1)} %broadcast_in_dim.16), channel_id=1, replica_groups=mesh['grp'=2,'tp'=8,'pd'=2] {'tp'}, dimensions={0} | all-to-all | bytes 524288 | tf_op jit(solution)/shard_map/all_to_all | solution.py:386
  94.4 0.7 reshape.194.gain
  95.0 0.8 collective-permute-done.16.sibling
  95.9 0.7 copy-done.10
  96.6 21.2 %feed_forward.1 = (f32[8,32,512]{2,1,0:T(8,128)}, bf16[8,32,512]{2,1,0:T(8,128)(2,1)}) custom-call(s32[2]{0:T(128)} %copy-done.8, bf16[8,32,512]{2,1,0:T(8,128)(2,1)} %copy-done.9, bf16[8,32,512]{2,1,0:T(8,128)(2,1)} %copy-done.10, f32[16,512]{1,0:T(8,128)} %reshape.194.gain, bf16[8192,1024]{1,0:T(8,128)(2,1)} %gate.1, bf16[8192,1024]{1,0:T(8,128)(2,1)} %up.1, ...), custom_call_target="tpu_custom_call" | custom-call | tf_op jit(solution)/shard_map/feed_forward/pallas_call | solution.py:306
  118.0 1.6 %collective-permute-done.17 = bf16[8,32,512]{2,1,0:T(8,128)(2,1)S(1)} collective-permute-done((bf16[8,32,512]{2,1,0:T(8,128)(2,1)}, bf16[8,32,512]{2,1,0:T(8,128)(2,1)S(1)}, u32[]{:S(2)}, u32[]{:S(2)}) %collective-permute-start.17) | collective-permute-done | bytes 262176 | tf_op jit(solution)/shard_map/ppermute | solution.py:360
  119.6 1.1 add_convert_fusion
  120.7 12.6 %all_to_all.11 = bf16[8,32,512]{2,1,0:T(8,128)(2,1)S(1)} all-to-all(bf16[8,32,512]{2,1,0:T(8,128)(2,1)S(1)} %add_convert_fusion), channel_id=1, replica_groups=mesh['grp'=2,'tp'=8,'pd'=2] {'tp'}, dimensions={0} | all-to-all | bytes 524288 | tf_op jit(solution)/shard_map/all_to_all | solution.py:392
  (80 shorter events, 7.3 us)
Async XLA Ops:
  0.6 15.9 %copy-start.6 = (s32[2496]{0:T(1024)S(1)}, s32[2496]{0:T(1024)}, u32[]{:S(2)}) copy-start(s32[2496]{0:T(1024)} %pages.1) | copy-start | bytes 29956
  0.6 17.8 %copy-start.14 = (s32[16]{0:T(128)S(1)}, s32[16]{0:T(128)}, u32[]{:S(2)}) copy-start(s32[16]{0:T(128)} %param.15) | copy-start | bytes 196
  0.7 1.7 %copy-start = (bf16[312,2,16,128]{3,2,1,0:T(8,128)(2,1)S(1)}, bf16[312,2,16,128]{3,2,1,0:T(8,128)(2,1)}, u32[]{:S(2)}) copy-start(bf16[312,2,16,128]{3,2,1,0:T(8,128)(2,1)} %old_pool.1) | copy-start | bytes 7667716
  2.5 0.7 copy-start.5
  3.2 70.2 %copy-start.8 = (s32[2]{0:T(128)}, s32[2]{0:T(128)S(1)}, u32[]{:S(2)}) copy-start(s32[2]{0:T(128)S(1)} %pad_add_fusion.place) | copy-start | bytes 28
  3.2 15.4 %copy-start.13 = (s32[16,128]{1,0:T(8,128)S(1)}, s32[16,128]{1,0:T(8,128)}, u32[]{:S(2)}) copy-start(s32[16,128]{1,0:T(8,128)} %param.14) | copy-start | bytes 24580
  8.6 14.7 %collective-permute-start = (bf16[32,2,16,128]{3,2,1,0:T(8,128)(2,1)}, bf16[32,2,16,128]{3,2,1,0:T(8,128)(2,1)S(1)}, u32[]{:S(2)}, u32[]{:S(2)}) collective-permute-start(bf16[32,2,16,128]{3,2,1,0:T(8,128)(2,1)} %get-tuple-element.14), channel_id=1, source_target_pairs={{0,1},{2,3},{4,5},{6,7},{8,9},{10,11},{12,13},{14,15},{16,17},{18,... | collective-permute-start | bytes 786440 | tf_op jit(solution)/shard_map/ppermute | solution.py:357
  9.9 15.4 %collective-permute-start.1 = (bf16[32,2,16,128]{3,2,1,0:T(8,128)(2,1)}, bf16[32,2,16,128]{3,2,1,0:T(8,128)(2,1)S(1)}, u32[]{:S(2)}, u32[]{:S(2)}) collective-permute-start(bf16[32,2,16,128]{3,2,1,0:T(8,128)(2,1)} %get-tuple-element.15), channel_id=1, source_target_pairs={{0,3},{2,5},{4,7},{6,9},{8,11},{10,13},{12,15},{14,1},{16,19},{18,... | collective-permute-start | bytes 786440 | tf_op jit(solution)/shard_map/ppermute | solution.py:357
  11.2 16.1 %collective-permute-start.2 = (bf16[32,2,16,128]{3,2,1,0:T(8,128)(2,1)}, bf16[32,2,16,128]{3,2,1,0:T(8,128)(2,1)S(1)}, u32[]{:S(2)}, u32[]{:S(2)}) collective-permute-start(bf16[32,2,16,128]{3,2,1,0:T(8,128)(2,1)} %get-tuple-element.16), channel_id=1, source_target_pairs={{0,5},{2,7},{4,9},{6,11},{8,13},{10,15},{12,1},{14,3},{16,21},{18,... | collective-permute-start | bytes 786440 | tf_op jit(solution)/shard_map/ppermute | solution.py:357
  12.5 21.2 %collective-permute-start.3 = (bf16[32,2,16,128]{3,2,1,0:T(8,128)(2,1)}, bf16[32,2,16,128]{3,2,1,0:T(8,128)(2,1)}, u32[]{:S(2)}, u32[]{:S(2)}) collective-permute-start(bf16[32,2,16,128]{3,2,1,0:T(8,128)(2,1)} %get-tuple-element.17), channel_id=1, source_target_pairs={{0,7},{2,9},{4,11},{6,13},{8,15},{10,1},{12,3},{14,5},{16,23},{18,... | collective-permute-start | bytes 786440 | tf_op jit(solution)/shard_map/ppermute | solution.py:357
  14.5 19.2 %collective-permute-start.4 = (bf16[32,2,16,128]{3,2,1,0:T(8,128)(2,1)}, bf16[32,2,16,128]{3,2,1,0:T(8,128)(2,1)}, u32[]{:S(2)}, u32[]{:S(2)}) collective-permute-start(bf16[32,2,16,128]{3,2,1,0:T(8,128)(2,1)} %get-tuple-element.18), channel_id=1, source_target_pairs={{0,9},{2,11},{4,13},{6,15},{8,1},{10,3},{12,5},{14,7},{16,25},{18,... | collective-permute-start | bytes 786440 | tf_op jit(solution)/shard_map/ppermute | solution.py:357
  20.3 12.4 %copy-start.11 = (bf16[16,2,2,128]{3,2,1,0:T(2,128)(2,1)S(1)}, bf16[16,2,2,128]{3,2,1,0:T(2,128)(2,1)}, u32[]{:S(2)}) copy-start(bf16[16,2,2,128]{3,2,1,0:T(2,128)(2,1)} %param.17) | copy-start | bytes 49156
  20.3 14.1 %copy-start.1 = (bf16[312,2,16,128]{3,2,1,0:T(8,128)(2,1)S(1)}, bf16[312,2,16,128]{3,2,1,0:T(8,128)(2,1)}, u32[]{:S(2)}) copy-start(bf16[312,2,16,128]{3,2,1,0:T(8,128)(2,1)} %old_pool.1) | copy-start | bytes 7667716
  23.3 10.5 %collective-permute-start.5 = (bf16[32,2,16,128]{3,2,1,0:T(8,128)(2,1)}, bf16[32,2,16,128]{3,2,1,0:T(8,128)(2,1)}, u32[]{:S(2)}, u32[]{:S(2)}) collective-permute-start(bf16[32,2,16,128]{3,2,1,0:T(8,128)(2,1)} %get-tuple-element.19), channel_id=1, source_target_pairs={{0,11},{2,13},{4,15},{6,1},{8,3},{10,5},{12,7},{14,9},{16,27},{18,... | collective-permute-start | bytes 786440 | tf_op jit(solution)/shard_map/ppermute | solution.py:357
  25.3 8.5 %collective-permute-start.6 = (bf16[32,2,16,128]{3,2,1,0:T(8,128)(2,1)}, bf16[32,2,16,128]{3,2,1,0:T(8,128)(2,1)}, u32[]{:S(2)}, u32[]{:S(2)}) collective-permute-start(bf16[32,2,16,128]{3,2,1,0:T(8,128)(2,1)} %get-tuple-element.20), channel_id=1, source_target_pairs={{0,13},{2,15},{4,1},{6,3},{8,5},{10,7},{12,9},{14,11},{16,29},{18,... | collective-permute-start | bytes 786440 | tf_op jit(solution)/shard_map/ppermute | solution.py:357
  27.2 0.7 copy-start.3
  28.0 6.4 %collective-permute-start.7 = (bf16[32,2,16,128]{3,2,1,0:T(8,128)(2,1)}, bf16[32,2,16,128]{3,2,1,0:T(8,128)(2,1)}, u32[]{:S(2)}, u32[]{:S(2)}) collective-permute-start(bf16[32,2,16,128]{3,2,1,0:T(8,128)(2,1)} %get-tuple-element.21), channel_id=1, source_target_pairs={{0,15},{2,1},{4,3},{6,5},{8,7},{10,9},{12,11},{14,13},{16,31},{18,... | collective-permute-start | bytes 786440 | tf_op jit(solution)/shard_map/ppermute | solution.py:357
  34.4 1.0 copy-start.4
  35.4 38.0 %copy-start.7 = (bf16[32,512]{1,0:T(8,128)(2,1)S(1)}, bf16[32,512]{1,0:T(8,128)(2,1)}, u32[]{:S(2)}) copy-start(bf16[32,512]{1,0:T(8,128)(2,1)} %stream.1) | copy-start | bytes 98308
  38.1 3.4 %collective-permute-start.8 = (bf16[32,1024]{1,0:T(8,128)(2,1)S(1)}, bf16[32,1024]{1,0:T(8,128)(2,1)S(1)}, u32[]{:S(2)}, u32[]{:S(2)}) collective-permute-start(bf16[32,1024]{1,0:T(8,128)(2,1)S(1)} %get-tuple-element.23), channel_id=1, source_target_pairs={{1,3},{3,5},{5,7},{7,9},{9,11},{11,13},{13,15},{15,1},{17,19},{19,... | collective-permute-start | bytes 196616 | tf_op jit(solution)/shard_map/ppermute | solution.py:357
  38.8 3.4 %collective-permute-start.9 = (bf16[32,1024]{1,0:T(8,128)(2,1)S(1)}, bf16[32,1024]{1,0:T(8,128)(2,1)S(1)}, u32[]{:S(2)}, u32[]{:S(2)}) collective-permute-start(bf16[32,1024]{1,0:T(8,128)(2,1)S(1)} %get-tuple-element.23), channel_id=1, source_target_pairs={{1,5},{3,7},{5,9},{7,11},{9,13},{11,15},{13,1},{15,3},{17,21},{19,... | collective-permute-start | bytes 196616 | tf_op jit(solution)/shard_map/ppermute | solution.py:357
  39.5 3.4 %collective-permute-start.10 = (bf16[32,1024]{1,0:T(8,128)(2,1)S(1)}, bf16[32,1024]{1,0:T(8,128)(2,1)S(1)}, u32[]{:S(2)}, u32[]{:S(2)}) collective-permute-start(bf16[32,1024]{1,0:T(8,128)(2,1)S(1)} %get-tuple-element.23), channel_id=1, source_target_pairs={{1,7},{3,9},{5,11},{7,13},{9,15},{11,1},{13,3},{15,5},{17,23},{19,... | collective-permute-start | bytes 196616 | tf_op jit(solution)/shard_map/ppermute | solution.py:357
  40.2 2.8 %collective-permute-start.11 = (bf16[32,1024]{1,0:T(8,128)(2,1)S(1)}, bf16[32,1024]{1,0:T(8,128)(2,1)S(1)}, u32[]{:S(2)}, u32[]{:S(2)}) collective-permute-start(bf16[32,1024]{1,0:T(8,128)(2,1)S(1)} %get-tuple-element.23), channel_id=1, source_target_pairs={{1,9},{3,11},{5,13},{7,15},{9,1},{11,3},{13,5},{15,7},{17,25},{19,... | collective-permute-start | bytes 196616 | tf_op jit(solution)/shard_map/ppermute | solution.py:357
  40.8 2.1 %collective-permute-start.12 = (bf16[32,1024]{1,0:T(8,128)(2,1)S(1)}, bf16[32,1024]{1,0:T(8,128)(2,1)S(1)}, u32[]{:S(2)}, u32[]{:S(2)}) collective-permute-start(bf16[32,1024]{1,0:T(8,128)(2,1)S(1)} %get-tuple-element.23), channel_id=1, source_target_pairs={{1,11},{3,13},{5,15},{7,1},{9,3},{11,5},{13,7},{15,9},{17,27},{19,... | collective-permute-start | bytes 196616 | tf_op jit(solution)/shard_map/ppermute | solution.py:357
  41.5 1.5 %collective-permute-start.13 = (bf16[32,1024]{1,0:T(8,128)(2,1)S(1)}, bf16[32,1024]{1,0:T(8,128)(2,1)S(1)}, u32[]{:S(2)}, u32[]{:S(2)}) collective-permute-start(bf16[32,1024]{1,0:T(8,128)(2,1)S(1)} %get-tuple-element.23), channel_id=1, source_target_pairs={{1,13},{3,15},{5,1},{7,3},{9,5},{11,7},{13,9},{15,11},{17,29},{19,... | collective-permute-start | bytes 196616 | tf_op jit(solution)/shard_map/ppermute | solution.py:357
  42.2 0.8 collective-permute-start.14
  43.0 51.3 %copy-start.12 = (f32[8192]{0:T(1024)S(1)}, f32[8192]{0:T(1024)}, u32[]{:S(2)}) copy-start(f32[8192]{0:T(1024)} %param.20) | copy-start | bytes 98308
  43.1 30.3 %collective-permute-start.15 = (bf16[8,32,1024]{2,1,0:T(8,128)(2,1)S(1)}, bf16[8,32,1024]{2,1,0:T(8,128)(2,1)S(1)}, u32[]{:S(2)}, u32[]{:S(2)}) collective-permute-start(bf16[8,32,1024]{2,1,0:T(8,128)(2,1)S(1)} %bitcast_dynamic-update-slice_fusion.here), channel_id=1, source_target_pairs={{1,0},{3,2},{5,4},{7,6},{9,8},{11,10},{13,12},{15,14},{17,16},{19,... | collective-permute-start | bytes 1572872 | tf_op jit(solution)/shard_map/ppermute | solution.py:380
  73.4 3.4 %copy-start.2 = (bf16[512,8192]{1,0:T(8,128)(2,1)S(1)}, bf16[512,8192]{1,0:T(8,128)(2,1)}, u32[]{:S(2)}) copy-start(bf16[512,8192]{1,0:T(8,128)(2,1)} %weight.1) | copy-start | bytes 25165828
  94.4 1.5 %copy-start.9 = (bf16[8,32,512]{2,1,0:T(8,128)(2,1)}, bf16[8,32,512]{2,1,0:T(8,128)(2,1)S(1)}, u32[]{:S(2)}) copy-start(bf16[8,32,512]{2,1,0:T(8,128)(2,1)S(1)} %all_to_all.10.mine) | copy-start | bytes 786436
  94.4 1.5 %collective-permute-start.16 = (bf16[8,32,512]{2,1,0:T(8,128)(2,1)S(1)}, bf16[8,32,512]{2,1,0:T(8,128)(2,1)S(1)}, u32[]{:S(2)}, u32[]{:S(2)}) collective-permute-start(bf16[8,32,512]{2,1,0:T(8,128)(2,1)S(1)} %all_to_all.10.mine), channel_id=1, source_target_pairs={{0,1},{1,0},{2,3},{3,2},{4,5},{5,4},{6,7},{7,6},{8,9},{9,8},{10,11... | collective-permute-start | bytes 786440 | tf_op jit(solution)/shard_map/ppermute | solution.py:360
  117.8 1.8 %collective-permute-start.17 = (bf16[8,32,512]{2,1,0:T(8,128)(2,1)}, bf16[8,32,512]{2,1,0:T(8,128)(2,1)S(1)}, u32[]{:S(2)}, u32[]{:S(2)}) collective-permute-start(bf16[8,32,512]{2,1,0:T(8,128)(2,1)} %get-tuple-element.25), channel_id=1, source_target_pairs={{0,1},{1,0},{2,3},{3,2},{4,5},{5,4},{6,7},{7,6},{8,9},{9,8},{10,11... | collective-permute-start | bytes 786440 | tf_op jit(solution)/shard_map/ppermute | solution.py:360
  (1 other events, 0.7 us)

commit v2 on v1

--- a/solution.py
+++ b/solution.py
@@ -21,31 +21,77 @@
 VM = pl.BlockSpec(memory_space=pltpu.VMEM)
 SM = pl.BlockSpec(memory_space=pltpu.SMEM)
 ANY = pl.BlockSpec(memory_space=pl.ANY)
+HBM = pl.BlockSpec(memory_space=pltpu.HBM)
+
+
+def in_vmem(x):
+    return pltpu.with_memory_space_constraint(x, pltpu.VMEM)
+
+
+def in_hbm(x):
+    return pltpu.with_memory_space_constraint(x, pltpu.HBM)
 
 
 def pack_kernel(members, place, pages, pool, *refs):
     outs = refs[:members]
-    packed, counts, sems = refs[members:]
+    packed, held, own, counts, sems, load_sems = refs[members:]
     member, half = place[0], place[1]
     slots = pool.shape[0]
     per_peer = ARRIVE // members
+    parts = 4
+    step = slots // parts
 
     @pl.when(half == 0)
     def _():
-        @pl.loop(0, members + 1)
-        def _(i):
-            counts[i] = 0
-
-        @pl.loop(0, slots, unroll=8)
-        def _(i):
-            entry = pages[member * slots + i]
-            target = entry // ARRIVE
-            ahead = lax.rem(target - member + members, members)
-            row = jnp.where(entry >= 0, ahead, members)
-            count = counts[row]
-            counts[row] = count + 1
-            spot = jnp.where(entry >= 0, row * per_peer + count, ARRIVE)
-            packed[spot] = pool[i]
+        own_copy = pltpu.make_async_copy(pages, own, load_sems.at[parts])
+        own_copy.start()
+        loads = []
+        for i in range(parts):
+            window = pl.ds(i * step, step)
+            loads.append(
+                pltpu.make_async_copy(pool.at[window], held.at[window], load_sems.at[i])
+            )
+            loads[-1].start()
+        own_copy.wait()
+        start = member * slots
+
+        if members <= 8:
+            carry = (jnp.int32(0), jnp.int32(0))
+            for i in range(parts):
+                loads[i].wait()
+
+                def body(j, words, base=i * step):
+                    low, high = words
+                    entry = own[start + base + j]
+                    ahead = lax.rem((entry >> 8) - member + members, members)
+                    leaves = entry >= 0
+                    shift = (ahead & 3) * 8
+                    is_low = ahead < 4
+                    count = (jnp.where(is_low, low, high) >> shift) & 255
+                    one = jnp.where(leaves, jnp.int32(1) << shift, 0)
+                    packed[jnp.where(leaves, ahead * per_peer + count, ARRIVE)] = held[base + j]
+                    return (
+                        low + jnp.where(is_low, one, 0),
+                        high + jnp.where(is_low, 0, one),
+                    )
+
+                carry = lax.fori_loop(0, step, body, carry, unroll=6)
+        else:
+            for i in range(parts):
+                loads[i].wait()
+
+            @pl.loop(0, members + 1)
+            def _(i):
+                counts[i] = 0
+
+            @pl.loop(0, slots)
+            def _(i):
+                entry = own[start + i]
+                ahead = lax.rem((entry >> 8) - member + members, members)
+                row = jnp.where(entry >= 0, ahead, members)
+                count = counts[row]
+                counts[row] = count + 1
+                packed[jnp.where(entry >= 0, row * per_peer + count, ARRIVE)] = held[i]
 
         copies = [
             pltpu.make_async_copy(packed.at[pl.ds(k * per_peer, per_peer)], outs[k], sems.at[k])
@@ -64,22 +110,54 @@
     return pl.pallas_call(
         functools.partial(pack_kernel, members),
         out_shape=[shape] * members,
-        in_specs=[SM, SM, VM],
+        in_specs=[SM, HBM, HBM],
         out_specs=[ANY] * members,
         scratch_shapes=[
             pltpu.VMEM((ARRIVE + 1, *pool.shape[1:]), pool.dtype),
+            pltpu.VMEM(pool.shape, pool.dtype),
+            pltpu.SMEM(pages.shape, jnp.int32),
             pltpu.SMEM((members + 1,), jnp.int32),
             pltpu.SemaphoreType.DMA((members,)),
+            pltpu.SemaphoreType.DMA((5,)),
         ],
-        compiler_params=pltpu.CompilerParams(vmem_limit_bytes=16 * MIB),
+        compiler_params=pltpu.CompilerParams(vmem_limit_bytes=61 * MIB),
         name="pack_pages",
-    )(place, pages, pool)
-
-
-def attend_kernel(members, place, landing, old_pool, bias, query, new_k, new_v, *refs):
+    )(place, in_hbm(pages), in_hbm(pool))
+
+
+def hold_kernel(after, *refs):
+    count = (len(refs) - 2) // 2
+    sources, copies_out = refs[:count], refs[count : 2 * count]
+    mark, sems = refs[2 * count :]
+    copies = [
+        pltpu.make_async_copy(sources[i], copies_out[i], sems.at[i]) for i in range(count)
+    ]
+    for copy in copies:
+        copy.start()
+    mark[...] = jnp.zeros_like(mark)
+    for copy in copies:
+        copy.wait()
+
+
+def hold(after, weights):
+    moved = sum(w.size * w.dtype.itemsize for w in weights)
+    return pl.pallas_call(
+        hold_kernel,
+        out_shape=[pltpu.VMEM(w.shape, w.dtype) for w in weights]
+        + [jax.ShapeDtypeStruct((8, 128), jnp.float32)],
+        in_specs=[ANY] + [HBM] * len(weights),
+        out_specs=[VM] * (len(weights) + 1),
+        scratch_shapes=[pltpu.SemaphoreType.DMA((len(weights),))],
+        compiler_params=pltpu.CompilerParams(vmem_limit_bytes=2 * MIB),
+        cost_estimate=pl.CostEstimate(flops=0, bytes_accessed=moved, transcendentals=0),
+        name="hold_weights",
+    )(after, *[in_hbm(w) for w in weights])
+
+
+def attend_kernel(members, place, landing, mark, old_pool, bias, query, new_k, new_v, *refs):
     arrived = refs[:members]
-    kv_out, att_out = refs[members : members + 2]
-    pool, scores, sems = refs[members + 2 :]
+    kv_out, att_low, att_high = refs[members : members + 3]
+    pool, scores, sems = refs[members + 3 :]
     half = place[1]
     slots = pool.shape[0]
     resident = slots - ARRIVE
@@ -92,7 +170,8 @@
     def _():
         copy = pltpu.make_async_copy(old_pool, kv_out, sems.at[0])
         copy.start()
-        att_out[...] = jnp.zeros_like(att_out)
+        att_low[...] = jnp.zeros_like(att_low)
+        att_high[...] = jnp.zeros_like(att_high)
         copy.wait()
 
     @pl.when(half == 1)
@@ -143,12 +222,14 @@
             acc = acc + jnp.dot(p.astype(jnp.bfloat16), values, preferred_element_type=jnp.float32)
         out = (acc / jnp.sum(total, axis=1, keepdims=True)).astype(jnp.bfloat16)
         tokens = rows * steps
-        for j in range(GQ):
-            att_out[:, j * HD : (j + 1) * HD] = out[j * tokens : (j + 1) * tokens]
+        for j in range(GQ // 2):
+            att_low[:, j * HD : (j + 1) * HD] = out[j * tokens : (j + 1) * tokens]
+            other = j + GQ // 2
+            att_high[:, j * HD : (j + 1) * HD] = out[other * tokens : (other + 1) * tokens]
         copy_out.wait()
 
 
-def place_and_attend(place, landing, old_pool, bias, query, new_k, new_v, arrived):
+def place_and_attend(place, landing, mark, old_pool, bias, query, new_k, new_v, arrived):
     members = len(arrived)
     slots = old_pool.shape[0]
     rows = bias.shape[0]
@@ -158,18 +239,19 @@
         functools.partial(attend_kernel, members),
         out_shape=[
             jax.ShapeDtypeStruct(old_pool.shape, old_pool.dtype),
-            jax.ShapeDtypeStruct((tokens, GQ * HD), jnp.bfloat16),
+            jax.ShapeDtypeStruct((tokens, GQ * HD // 2), jnp.bfloat16),
+            jax.ShapeDtypeStruct((tokens, GQ * HD // 2), jnp.bfloat16),
         ],
-        in_specs=[SM, SM, ANY, VM, VM, VM, VM] + [VM] * members,
-        out_specs=[ANY, VM],
+        in_specs=[SM, SM, ANY, HBM, VM, VM, VM, VM] + [VM] * members,
+        out_specs=[HBM, VM, VM],
         scratch_shapes=[
             pltpu.VMEM(old_pool.shape, old_pool.dtype),
             pltpu.VMEM((count, slots * PAGE), jnp.float32),
             pltpu.SemaphoreType.DMA((2,)),
         ],
-        compiler_params=pltpu.CompilerParams(vmem_limit_bytes=28 * MIB),
+        compiler_params=pltpu.CompilerParams(vmem_limit_bytes=9 * MIB),
         name="place_attend",
-    )(place, landing, old_pool, bias, query, new_k, new_v, *arrived)
+    )(place, landing, mark, in_hbm(old_pool), bias, query, new_k, new_v, *arrived)
 
 
 def table_bias(tables, row_lengths, slots):
@@ -194,73 +276,48 @@
     return jnp.sum(jnp.where(pick, (slots_from % ARRIVE)[:, None, :], 0), axis=2)
 
 
-def project_kernel(members, groups, place, weight, stream, here, there, res_out):
-    member, half = place[0], place[1]
-    width = GQ * HD
-    tokens = here.shape[1]
-
-    def run(source):
-        sums = [stream[g * tokens : (g + 1) * tokens].astype(jnp.float32) for g in range(groups)]
-        if groups > 1:
-            res_f32 = jnp.stack(sums)
-        else:
-            res_f32 = sums[0]
-        for k in range(members):
-            owner = lax.rem(member - k + members, members)
-            head = pl.multiple_of(owner // groups * width, width)
-            part = lax.dot_general(
-                source[k],
-                weight[:, pl.ds(head, width)],
+def project_kernel(groups, place, weight, stream, mine, sibling, res_out):
+    half = place[1]
+    members, tokens, width = mine.shape
+    sums = [stream[g * tokens : (g + 1) * tokens].astype(jnp.float32) for g in range(groups)]
+    for h in range(KVH):
+        for g in range(groups):
+            m = h * groups + g
+            first = jnp.where(half == 0, mine[m], sibling[m])
+            second = jnp.where(half == 0, sibling[m], mine[m])
+            sums[g] = sums[g] + lax.dot_general(
+                jnp.concatenate([first, second], axis=1),
+                weight[:, 2 * h * width : 2 * (h + 1) * width],
                 (((1,), (1,)), ((), ())),
                 preferred_element_type=jnp.float32,
             )
-            if groups > 1:
-                mine = lax.broadcasted_iota(jnp.int32, res_f32.shape, 0) == lax.rem(owner, groups)
-                res_f32 = res_f32 + jnp.where(mine, part[None], 0.0)
-            else:
-                res_f32 = res_f32 + part
-        res_out[...] = res_f32.reshape(res_out.shape).astype(res_out.dtype)
-
-    @pl.when(half == 1)
-    def _():
-        run(here)
-
-    @pl.when(half == 0)
-    def _():
-        run(there)
-
-
-def project(place, weight, stream, here, there, groups):
-    members = here.shape[0]
+    for g in range(groups):
+        res_out[g * tokens : (g + 1) * tokens] = sums[g].astype(res_out.dtype)
+
+
+def project(place, weight, stream, mine, sibling, groups):
     return pl.pallas_call(
-        functools.partial(project_kernel, members, groups),
+        functools.partial(project_kernel, groups),
         out_shape=jax.ShapeDtypeStruct(stream.shape, jnp.bfloat16),
         in_specs=[SM, VM, VM, VM, VM],
         out_specs=VM,
-        compiler_params=pltpu.CompilerParams(vmem_limit_bytes=24 * MIB),
+        compiler_params=pltpu.CompilerParams(vmem_limit_bytes=4 * MIB),
         name="out_projection",
-    )(place, weight, stream, here, there)
+    )(place, in_vmem(weight), stream, mine, sibling)
 
 
 def ffn_kernel(place, mine, sibling, gain, gate, up, down, own_out, other_out, *scratch):
-    gate_buf, up_buf, down_buf, normed, gate_sem, up_sem, down_sem = scratch
+    up_buf, down_buf, normed, gated, hidden, up_sem, down_sem = scratch
     half = place[1]
     members, tokens, width = mine.shape
-    features = gate.shape[0]
-    hidden_count = gate.shape[1]
-    blocks = 2 * members
-    order = [(t, p) for p in range(2) for t in range(members)]
-
-    def rows_of(t, p):
-        which = half if p == 0 else 1 - half
-        return pl.ds(pl.multiple_of((t * 2 + which) * width, width), width)
-
-    up_copies, gate_copies, down_copies = [], [], []
-    for i, (t, p) in enumerate(order):
-        rows = rows_of(t, p)
-        gate_copies.append(pltpu.make_async_copy(gate.at[rows], gate_buf.at[rows], gate_sem.at[i]))
-        up_copies.append(pltpu.make_async_copy(up.at[rows], up_buf.at[rows], up_sem.at[i]))
-        gate_copies[-1].start()
+    features, hidden_count = gate.shape
+    tile = min(256, hidden_count)
+    tiles = [slice(f * tile, (f + 1) * tile) for f in range(hidden_count // tile)]
+    up_copies, down_copies = [], []
+    for f, cols in enumerate(tiles):
+        up_copies.append(
+            pltpu.make_async_copy(up.at[:, cols], up_buf.at[:, cols], up_sem.at[f])
+        )
         up_copies[-1].start()
     for t in range(members):
         cols = pl.ds(t * 2 * width, 2 * width)
@@ -275,23 +332,23 @@
             x = block[t].astype(jnp.float32)
             square = square + x * x
     factor = lax.rsqrt(jnp.sum(square, axis=1, keepdims=True) / features + 1e-05)
-    gate_act = jnp.zeros((tokens, hidden_count), jnp.float32)
-    up_act = jnp.zeros((tokens, hidden_count), jnp.float32)
-    for i, (t, p) in enumerate(order):
-        rows = rows_of(t, p)
-        x = (mine if p == 0 else sibling)[t].astype(jnp.float32)
-        which = half if p == 0 else 1 - half
-        g = gain[pl.ds(t * 2 + which, 1), :]
-        n = (x * factor * g).astype(jnp.bfloat16)
-        gate_copies[i].wait()
-        gate_act = gate_act + jnp.dot(n, gate_buf[rows, :], preferred_element_type=jnp.float32)
-        up_copies[i].wait()
-        up_act = up_act + jnp.dot(n, up_buf[rows, :], preferred_element_type=jnp.float32)
-    hidden = (gate_act / (1.0 + jnp.exp(-gate_act)) * up_act).astype(jnp.bfloat16)
+    for t in range(members):
+        first = jnp.where(half == 0, mine[t], sibling[t])
+        second = jnp.where(half == 0, sibling[t], mine[t])
+        x = jnp.concatenate([first, second], axis=1).astype(jnp.float32)
+        n = x * factor * gain[t : t + 1, :]
+        normed[:, 2 * t * width : 2 * (t + 1) * width] = n.astype(jnp.bfloat16)
+    for cols in tiles:
+        act = jnp.dot(normed[...], gate[:, cols], preferred_element_type=jnp.float32)
+        gated[:, cols] = act / (1.0 + jnp.exp(-act))
+    for f, cols in enumerate(tiles):
+        up_copies[f].wait()
+        act = jnp.dot(normed[...], up_buf[:, cols], preferred_element_type=jnp.float32)
+        hidden[:, cols] = (gated[:, cols] * act).astype(jnp.bfloat16)
     for t in range(members):
         down_copies[t].wait()
         part = jnp.dot(
-            hidden,
+            hidden[...],
             down_buf[:, 2 * t * width : 2 * (t + 1) * width],
             preferred_element_type=jnp.float32,
         )
@@ -303,26 +360,35 @@
 def feed_forward(place, mine, sibling, gain, gate, up, down):
     members, tokens, width = mine.shape
     blocks = 2 * members
+    hidden_count = gate.shape[1]
     return pl.pallas_call(
         ffn_kernel,
         out_shape=[
             jax.ShapeDtypeStruct(mine.shape, jnp.float32),
             jax.ShapeDtypeStruct(mine.shape, jnp.bfloat16),
         ],
-        in_specs=[SM, VM, VM, VM, ANY, ANY, ANY],
+        in_specs=[SM, VM, VM, VM, VM, HBM, HBM],
         out_specs=[VM, VM],
         scratch_shapes=[
-            pltpu.VMEM(gate.shape, gate.dtype),
             pltpu.VMEM(up.shape, up.dtype),
             pltpu.VMEM(down.shape, down.dtype),
-            pltpu.VMEM((8, 128), jnp.float32),
-            pltpu.SemaphoreType.DMA((blocks,)),
-            pltpu.SemaphoreType.DMA((blocks,)),
+            pltpu.VMEM((tokens, blocks * width), jnp.bfloat16),
+            pltpu.VMEM((tokens, hidden_count), jnp.float32),
+            pltpu.VMEM((tokens, hidden_count), jnp.bfloat16),
+            pltpu.SemaphoreType.DMA((-(-hidden_count // 256),)),
             pltpu.SemaphoreType.DMA((members,)),
         ],
-        compiler_params=pltpu.CompilerParams(vmem_limit_bytes=56 * MIB),
+        compiler_params=pltpu.CompilerParams(vmem_limit_bytes=36 * MIB),
         name="feed_forward",
-    )(place, mine, sibling, gain.reshape(blocks, width), gate, up, down)
+    )(
+        place,
+        mine,
+        sibling,
+        gain.reshape(members, 2 * width),
+        in_vmem(gate),
+        in_hbm(up),
+        in_hbm(down),
+    )
 
 
 def local(
@@ -360,7 +426,11 @@
         return lax.ppermute(x, "pd", [(0, 1), (1, 0)])
 
     outgoing = pack(place, page_list, kv_pages)
-    arrived = [ahead(outgoing[k], k, 0, 1) for k in range(members)]
+    arrived = [None] * members
+    for k in sorted(range(members), key=lambda k: abs(k - members // 2)):
+        arrived[k] = ahead(outgoing[k], k, 0, 1)
+
+    out_proj, mark = hold(outgoing[0], (out_proj,))
 
     behind = (member - jnp.arange(members)) % members
     landing = landing_slots(page_list.reshape(members, slots)[behind], member, per_peer)
@@ -371,20 +441,22 @@
     new_k = jnp.pad(fresh_kv[:, :, 0].reshape(tokens, HD), padding)
     new_v = jnp.pad(fresh_kv[:, :, 1].reshape(tokens, HD), padding)
 
-    kv_after, attended = place_and_attend(
-        place, landing.reshape(-1), kv_pages, bias, query, new_k, new_v, arrived
-    )
-
-    pieces = [attended] + [ahead(attended, k, 1, 1) for k in range(1, members)]
-    here = jnp.stack(pieces)
-    there = lax.ppermute(here, "pd", [(1, 0)])
+    kv_after, att_low, att_high = place_and_attend(
+        place, landing.reshape(-1), mark, kv_pages, bias, query, new_k, new_v, arrived
+    )
+
+    def everywhere(x):
+        spread = jnp.broadcast_to(x[None], (members, *x.shape))
+        mine = lax.all_to_all(spread, "tp", split_axis=0, concat_axis=0)
+        return mine, swap(mine)
+
+    att_mine = jnp.where(half == 1, att_high, lax.ppermute(att_low, "pd", [(1, 0)]))
+    here, there = everywhere(att_mine)
 
     inner = stream.reshape(steps, groups, rows, -1).transpose(1, 0, 2, 3).reshape(stream.shape)
     residual = project(place, out_proj, inner, here, there, groups)
 
-    spread = jnp.broadcast_to(residual[None], (members, *residual.shape))
-    mine = lax.all_to_all(spread, "tp", split_axis=0, concat_axis=0)
-    sibling = swap(mine)
+    mine, sibling = everywhere(residual)
     own, other = feed_forward(
         place, mine, sibling, norm_gain, gate_weight, up_weight, down_weight
     )

time: 135 us -> 195 us (1.44)
  Pallas kernels: 32.5 us -> 109 us
  waiting for transfers between devices: 32.1 us -> 6.27 us
  blocking collectives: 27.1 us -> 41.3 us
  starting transfers between devices: 20 us -> 12.8 us
  local copies, waits for them, and re-layouts: 13.3 us -> 16 us
    pallas_call x1, Pallas kernels: 2.78 us -> 79.1 us  [place_and_attend(): pl.pallas_call(functools.partial(attend_kernel, members), out_shape=[jax....]
    ppermute x1, waiting for transfers between devices: 29 us -> 1.8 us  [local(): lax.ppermute(att_low, 'pd', [(1, 0)])]
    all_to_all x1 -> x2, blocking collectives: 14.4 us -> 28.7 us  [everywhere(): mine = lax.all_to_all(spread, 'tp', split_axis=0, concat_axis=0)]
    ppermute x15 -> x8, starting transfers between devices: 18.5 us -> 11.3 us  [ahead(): return lax.ppermute(x, BOTH, route)]
    unnamed x39 -> x32, local copies, waits for them, and re-layouts: 8.29 us -> 12.4 us
    pallas_call x1, Pallas kernels: 21.2 us -> 17.6 us  [feed_forward(): pl.pallas_call(ffn_kernel, out_shape=[jax.ShapeDtypeStruct(mine.shape, jn...]
    pallas_call x1 -> x2, Pallas kernels: 3.12 us -> 6.49 us  [the longest x1 3.39 us: hold(): pl.pallas_call(hold_kernel, out_shape=[pltpu.VMEM(w.shape, w.dtype) for w...]
    ppermute x2 -> x3, waiting for transfers between devices: 2.46 us -> 4.45 us  [swap(): return lax.ppermute(x, 'pd', [(0, 1), (1, 0)])]
  transfers between devices with their start and end apart: 18 -> 12, of which waited for: 4 -> 4; matrix products, arithmetic and copies ran while one was open for 8% -> 5% of each run, Pallas kernels for 0% -> 2%
where the time goes in v2:
time: 195 us; the launch traced here: 194 us
  Pallas kernels  109 us (56%)
  blocking collectives  41.3 us (21%)
  local copies, waits for them, and re-layouts  16 us (8%)
  starting transfers between devices  12.8 us (7%)
  other arithmetic  7.38 us (4%)
  waiting for transfers between devices  6.27 us (3%)
    pallas_call x1, Pallas kernels, place_and_attend(): pl.pallas_call(functools.partial(attend_kernel, members), out_shape=[jax....  79.1 us
    all_to_all x2, blocking collectives, everywhere(): mine = lax.all_to_all(spread, 'tp', split_axis=0, concat_axis=0)  28.7 us
    pallas_call x1, Pallas kernels, feed_forward(): pl.pallas_call(ffn_kernel, out_shape=[jax.ShapeDtypeStruct(mine.shape, jn...  17.6 us
    all_to_all x1, blocking collectives, local(): shares = lax.all_to_all(summed, 'tp', split_axis=0, concat_axis=0)  12.6 us
    unnamed x32, local copies, waits for them, and re-layouts  12.4 us
    ppermute x8, starting transfers between devices, ahead(): return lax.ppermute(x, BOTH, route)  11.3 us
    pallas_call x1, Pallas kernels, pack(): pl.pallas_call(functools.partial(pack_kernel, members), out_shape=[shape]...  6.03 us
    ppermute x3, waiting for transfers between devices, swap(): return lax.ppermute(x, 'pd', [(0, 1), (1, 0)])  4.45 us
  transfers between devices with their start and end apart: 12, of which 4 were waited for; matrix products, arithmetic and copies ran while one was open for 5% of the time, Pallas kernels for 2%

profile of v2, /device:TPU:0, one launch (start us, length us, event | category | flops | bytes accessed | tf_op | source)
XLA Modules:
  0.0 194.0 jit_solution(4485215529981297303)
XLA Ops:
  0.7 0.6 pad_add_fusion.place
  1.3 6.0 %pack_pages.1 = (bf16[32,2,16,128]{3,2,1,0:T(8,128)(2,1)}, bf16[32,2,16,128]{3,2,1,0:T(8,128)(2,1)}, bf16[32,2,16,128]{3,2,1,0:T(8,128)(2,1)}, bf16[32,2,16,128]...) custom-call(s32[2]{0:T(128)} %pad_add_fusion.place, ...), custom_call_target="tpu_custom_call" | custom-call | tf_op jit(solution)/shard_map/pack_pages/pallas_call | solution.py:110
  7.3 1.4 collective-permute-start
  8.8 1.3 collective-permute-start.1
  10.1 1.3 collective-permute-start.2
  11.4 1.3 collective-permute-start.3
  12.7 1.3 collective-permute-start.4
  14.2 0.6 gather_fusion
  14.8 0.9 reduce-window.6
  16.2 1.7 convert_reduce_fusion.1
  17.9 2.9 %add_log_fusion = f32[16,312,16]{2,1,0:T(8,128)} fusion(f32[16,16]{1,0:T(8,128)S(1)} %fusion.5, f32[16,312]{1,0:T(8,128)S(1)} %get-tuple-element.33, f32[16,312]{1,0:T(8,128)S(1)} %get-tuple-element.32), kind=kLoop, calls=%fused_computation.1 | loop fusion | flops 159744 | bytes 360448 | tf_op jit(solution)/shard_map/log | solution.py:269
  20.8 1.3 collective-permute-start.5
  22.1 1.3 collective-permute-start.6
  23.5 2.0 %collective-permute-start.7 = (bf16[32,2,16,128]{3,2,1,0:T(8,128)(2,1)S(1)}, bf16[32,2,16,128]{3,2,1,0:T(8,128)(2,1)S(1)}, u32[]{:S(2)}, u32[]{:S(2)}) collective-permute-start(bf16[32,2,16,128]{3,2,1,0:T(8,128)(2,1)S(1)} %copy-done.11), channel_id=1, source_target_pairs={{0,15},{2,1},{4,3},{6,5},{8,7},{10,9},{12,11},{14,13},{16,31},{18,... | collective-permute-start | bytes 786440 | tf_op jit(solution)/shard_map/ppermute | solution.py:423
  25.5 0.2 select_reduce_fusion
  25.8 3.4 %hold_weights.1 = (bf16[512,8192]{1,0:T(8,128)(2,1)S(1)}, f32[8,128]{1,0:T(8,128)S(1)}) custom-call(bf16[32,2,16,128]{3,2,1,0:T(8,128)(2,1)S(1)} %copy-done.3, bf16[512,8192]{1,0:T(8,128)(2,1)} %refs_0_.1), custom_call_target="tpu_custom_call" | custom-call | bytes 8388608 | tf_op jit(solution)/shard_map/hold_weights/pallas_call | solution.py:144
  29.2 3.2 %copy-done.1 = bf16[512,8192]{1,0:T(8,128)(2,1)} copy-done((bf16[512,8192]{1,0:T(8,128)(2,1)}, bf16[512,8192]{1,0:T(8,128)(2,1)S(1)}, u32[]{:S(2)}) %copy-start.1) | copy-done | bytes 8388632
  32.4 2.5 %log.8.bias = f32[16,4992]{1,0:T(8,128)S(1)} reshape(f32[16,312,16]{2,1,0:T(8,128)} %add_log_fusion) | data formatting | bytes 638976 | tf_op jit(solution)/shard_map/log | solution.py:269
  35.1 79.1 %place_attend.1 = (bf16[312,2,16,128]{3,2,1,0:T(8,128)(2,1)}, bf16[32,512]{1,0:T(8,128)(2,1)S(1)}, bf16[32,512]{1,0:T(8,128)(2,1)S(1)}) custom-call(s32[2]{0:T(128)S(1)} %copy-done.5, s32[256]{0:T(256)S(1)} %reshape.192.landing, f32[8,128]{1,0:T(8,128)S(1)} %get-tuple-element.18.mark, bf16[312,2,16,128]{3,2,1,0:T(8,128)(2,1)} %old_pool.1, ...), custom_call_target="tpu_custom_call" | custom-call | tf_op jit(solution)/shard_map/place_attend/pallas_call | solution.py:238
  114.3 1.3 collective-permute-start.8
  115.6 1.8 collective-permute-done.8
  117.4 16.1 %all_to_all.15.mine = bf16[8,32,512]{2,1,0:T(8,128)(2,1)S(1)} all-to-all(bf16[8,32,512]{2,1,0:T(8,128)(2,1)S(1)} %broadcast_in_dim.18), channel_id=1, replica_groups=mesh['grp'=2,'tp'=8,'pd'=2] {'tp'}, dimensions={0} | all-to-all | bytes 524288 | tf_op jit(solution)/shard_map/all_to_all | solution.py:450
  133.5 1.5 collective-permute-done.9.sibling
  135.1 3.4 %copy-done.2 = bf16[512,8192]{1,0:T(8,128)(2,1)S(1)} copy-done((bf16[512,8192]{1,0:T(8,128)(2,1)S(1)}, bf16[512,8192]{1,0:T(8,128)(2,1)}, u32[]{:S(2)}) %copy-start.2) | copy-done | bytes 8388632
  138.5 3.1 %out_projection.1 = bf16[32,512]{1,0:T(8,128)(2,1)S(1)} custom-call(s32[2]{0:T(128)S(1)} %copy-done.5, bf16[512,8192]{1,0:T(8,128)(2,1)S(1)} %copy-done.2, bf16[32,512]{1,0:T(8,128)(2,1)S(1)} %copy-done.4, bf16[8,32,512]{2,1,0:T(8,128)(2,1)S(1)} %all_to_all.15.mine, bf16[8,32,512]{2,1,0:T(8,128)(2,1)S(1)} %collective-permute-done.9.sibling), custom_call_target="tpu_custom_call" | custom-call | tf_op jit(solution)/shard_map/out_projection/pallas_call | solution.py:299
  141.6 12.6 %all_to_all.16.mine = bf16[8,32,512]{2,1,0:T(8,128)(2,1)S(1)} all-to-all(bf16[8,32,512]{2,1,0:T(8,128)(2,1)S(1)} %broadcast_in_dim.19), channel_id=1, replica_groups=mesh['grp'=2,'tp'=8,'pd'=2] {'tp'}, dimensions={0} | all-to-all | bytes 524288 | tf_op jit(solution)/shard_map/all_to_all | solution.py:450
  154.2 1.5 collective-permute-done.10.sibling
  155.7 5.8 %copy-done = bf16[8192,1024]{1,0:T(8,128)(2,1)S(1)} copy-done((bf16[8192,1024]{1,0:T(8,128)(2,1)S(1)}, bf16[8192,1024]{1,0:T(8,128)(2,1)}, u32[]{:S(2)}) %copy-start) | copy-done | bytes 16777240
  161.5 17.6 %feed_forward.1 = (f32[8,32,512]{2,1,0:T(8,128)S(1)}, bf16[8,32,512]{2,1,0:T(8,128)(2,1)S(1)}) custom-call(s32[2]{0:T(128)S(1)} %copy-done.5, bf16[8,32,512]{2,1,0:T(8,128)(2,1)S(1)} %all_to_all.16.mine, bf16[8,32,512]{2,1,0:T(8,128)(2,1)S(1)} %collective-permute-done.10.sibling, f32[8,1024]{1,0:T(8,128)S(1)} %reshape.195.gain, ...), custom_call_target="tpu_custom_call" | custom-call | tf_op jit(solution)/shard_map/feed_forward/pallas_call | solution.py:364
  179.3 1.4 collective-permute-done.11
  180.7 12.6 %all_to_all.17 = bf16[8,32,512]{2,1,0:T(8,128)(2,1)S(1)} all-to-all(bf16[8,32,512]{2,1,0:T(8,128)(2,1)S(1)} %add_convert_fusion), channel_id=1, replica_groups=mesh['grp'=2,'tp'=8,'pd'=2] {'tp'}, dimensions={0} | all-to-all | bytes 524288 | tf_op jit(solution)/shard_map/all_to_all | solution.py:464
  193.4 0.6 add_convert_fusion.1
  (64 shorter events, 1.3 us)
Async XLA Ops:
  0.6 13.4 %copy-start.8 = (s32[2496]{0:T(1024)S(1)}, s32[2496]{0:T(1024)}, u32[]{:S(2)}) copy-start(s32[2496]{0:T(1024)} %pages.1) | copy-start | bytes 29956
  0.6 15.3 %copy-start.14 = (s32[16]{0:T(128)S(1)}, s32[16]{0:T(128)}, u32[]{:S(2)}) copy-start(s32[16]{0:T(128)} %param.15) | copy-start | bytes 196
  0.7 15.5 %copy-start.10 = (s32[16,128]{1,0:T(8,128)S(1)}, s32[16,128]{1,0:T(8,128)}, u32[]{:S(2)}) copy-start(s32[16,128]{1,0:T(8,128)} %param.14) | copy-start | bytes 24580
  7.3 13.5 %copy-start.13 = (bf16[32,2,16,128]{3,2,1,0:T(8,128)(2,1)S(1)}, bf16[32,2,16,128]{3,2,1,0:T(8,128)(2,1)}, u32[]{:S(2)}) copy-start(bf16[32,2,16,128]{3,2,1,0:T(8,128)(2,1)} %get-tuple-element.23) | copy-start | bytes 786436
  7.3 14.8 %copy-start.12 = (bf16[32,2,16,128]{3,2,1,0:T(8,128)(2,1)S(1)}, bf16[32,2,16,128]{3,2,1,0:T(8,128)(2,1)}, u32[]{:S(2)}) copy-start(bf16[32,2,16,128]{3,2,1,0:T(8,128)(2,1)} %get-tuple-element.24) | copy-start | bytes 786436
  7.3 16.1 %copy-start.11 = (bf16[32,2,16,128]{3,2,1,0:T(8,128)(2,1)S(1)}, bf16[32,2,16,128]{3,2,1,0:T(8,128)(2,1)}, u32[]{:S(2)}) copy-start(bf16[32,2,16,128]{3,2,1,0:T(8,128)(2,1)} %get-tuple-element.25) | copy-start | bytes 786436
  7.3 18.5 %copy-start.3 = (bf16[32,2,16,128]{3,2,1,0:T(8,128)(2,1)S(1)}, bf16[32,2,16,128]{3,2,1,0:T(8,128)(2,1)}, u32[]{:S(2)}) copy-start(bf16[32,2,16,128]{3,2,1,0:T(8,128)(2,1)} %get-tuple-element.17.after) | copy-start | bytes 786436
  7.3 13.5 %collective-permute-start = (bf16[32,2,16,128]{3,2,1,0:T(8,128)(2,1)}, bf16[32,2,16,128]{3,2,1,0:T(8,128)(2,1)S(1)}, u32[]{:S(2)}, u32[]{:S(2)}) collective-permute-start(bf16[32,2,16,128]{3,2,1,0:T(8,128)(2,1)} %get-tuple-element.17.after), channel_id=1, source_target_pairs={{0,1},{2,3},{4,5},{6,7},{8,9},{10,11},{12,13},{14,15},{16,17},{18,... | collective-permute-start | bytes 786440 | tf_op jit(solution)/shard_map/ppermute | solution.py:423
  8.8 13.3 %collective-permute-start.1 = (bf16[32,2,16,128]{3,2,1,0:T(8,128)(2,1)}, bf16[32,2,16,128]{3,2,1,0:T(8,128)(2,1)S(1)}, u32[]{:S(2)}, u32[]{:S(2)}) collective-permute-start(bf16[32,2,16,128]{3,2,1,0:T(8,128)(2,1)} %get-tuple-element.19), channel_id=1, source_target_pairs={{0,3},{2,5},{4,7},{6,9},{8,11},{10,13},{12,15},{14,1},{16,19},{18,... | collective-permute-start | bytes 786440 | tf_op jit(solution)/shard_map/ppermute | solution.py:423
  10.1 13.3 %collective-permute-start.2 = (bf16[32,2,16,128]{3,2,1,0:T(8,128)(2,1)}, bf16[32,2,16,128]{3,2,1,0:T(8,128)(2,1)S(1)}, u32[]{:S(2)}, u32[]{:S(2)}) collective-permute-start(bf16[32,2,16,128]{3,2,1,0:T(8,128)(2,1)} %get-tuple-element.20), channel_id=1, source_target_pairs={{0,5},{2,7},{4,9},{6,11},{8,13},{10,15},{12,1},{14,3},{16,21},{18,... | collective-permute-start | bytes 786440 | tf_op jit(solution)/shard_map/ppermute | solution.py:423
  11.4 23.7 %collective-permute-start.3 = (bf16[32,2,16,128]{3,2,1,0:T(8,128)(2,1)}, bf16[32,2,16,128]{3,2,1,0:T(8,128)(2,1)S(1)}, u32[]{:S(2)}, u32[]{:S(2)}) collective-permute-start(bf16[32,2,16,128]{3,2,1,0:T(8,128)(2,1)} %get-tuple-element.21), channel_id=1, source_target_pairs={{0,7},{2,9},{4,11},{6,13},{8,15},{10,1},{12,3},{14,5},{16,23},{18,... | collective-permute-start | bytes 786440 | tf_op jit(solution)/shard_map/ppermute | solution.py:423
  12.7 22.4 %collective-permute-start.4 = (bf16[32,2,16,128]{3,2,1,0:T(8,128)(2,1)}, bf16[32,2,16,128]{3,2,1,0:T(8,128)(2,1)S(1)}, u32[]{:S(2)}, u32[]{:S(2)}) collective-permute-start(bf16[32,2,16,128]{3,2,1,0:T(8,128)(2,1)} %get-tuple-element.22), channel_id=1, source_target_pairs={{0,9},{2,11},{4,13},{6,15},{8,1},{10,3},{12,5},{14,7},{16,25},{18,... | collective-permute-start | bytes 786440 | tf_op jit(solution)/shard_map/ppermute | solution.py:423
  20.8 14.3 %collective-permute-start.5 = (bf16[32,2,16,128]{3,2,1,0:T(8,128)(2,1)S(1)}, bf16[32,2,16,128]{3,2,1,0:T(8,128)(2,1)S(1)}, u32[]{:S(2)}, u32[]{:S(2)}) collective-permute-start(bf16[32,2,16,128]{3,2,1,0:T(8,128)(2,1)S(1)} %copy-done.13), channel_id=1, source_target_pairs={{0,11},{2,13},{4,15},{6,1},{8,3},{10,5},{12,7},{14,9},{16,27},{18,... | collective-permute-start | bytes 786440 | tf_op jit(solution)/shard_map/ppermute | solution.py:423
  22.1 13.0 %collective-permute-start.6 = (bf16[32,2,16,128]{3,2,1,0:T(8,128)(2,1)S(1)}, bf16[32,2,16,128]{3,2,1,0:T(8,128)(2,1)S(1)}, u32[]{:S(2)}, u32[]{:S(2)}) collective-permute-start(bf16[32,2,16,128]{3,2,1,0:T(8,128)(2,1)S(1)} %copy-done.12), channel_id=1, source_target_pairs={{0,13},{2,15},{4,1},{6,3},{8,5},{10,7},{12,9},{14,11},{16,29},{18,... | collective-permute-start | bytes 786440 | tf_op jit(solution)/shard_map/ppermute | solution.py:423
  23.5 11.7 %collective-permute-start.7 = (bf16[32,2,16,128]{3,2,1,0:T(8,128)(2,1)S(1)}, bf16[32,2,16,128]{3,2,1,0:T(8,128)(2,1)S(1)}, u32[]{:S(2)}, u32[]{:S(2)}) collective-permute-start(bf16[32,2,16,128]{3,2,1,0:T(8,128)(2,1)S(1)} %copy-done.11), channel_id=1, source_target_pairs={{0,15},{2,1},{4,3},{6,5},{8,7},{10,9},{12,11},{14,13},{16,31},{18,... | collective-permute-start | bytes 786440 | tf_op jit(solution)/shard_map/ppermute | solution.py:423
  29.2 3.2 %copy-start.1 = (bf16[512,8192]{1,0:T(8,128)(2,1)}, bf16[512,8192]{1,0:T(8,128)(2,1)S(1)}, u32[]{:S(2)}) copy-start(bf16[512,8192]{1,0:T(8,128)(2,1)S(1)} %get-tuple-element.27.weight) | copy-start | bytes 25165828
  32.4 2.5 %copy-start.7 = (bf16[16,2,2,128]{3,2,1,0:T(2,128)(2,1)S(1)}, bf16[16,2,2,128]{3,2,1,0:T(2,128)(2,1)}, u32[]{:S(2)}) copy-start(bf16[16,2,2,128]{3,2,1,0:T(2,128)(2,1)} %param.17) | copy-start | bytes 49156
  32.4 2.6 %copy-start.6 = (bf16[16,2,1024]{2,1,0:T(2,128)(2,1)S(1)}, bf16[16,2,1024]{2,1,0:T(2,128)(2,1)}, u32[]{:S(2)}) copy-start(bf16[16,2,1024]{2,1,0:T(2,128)(2,1)} %param.16) | copy-start | bytes 196612
  32.4 2.7 %copy-start.5 = (s32[2]{0:T(128)S(1)}, s32[2]{0:T(128)}, u32[]{:S(2)}) copy-start(s32[2]{0:T(128)} %pad_add_fusion.place) | copy-start | bytes 28
  35.1 99.9 %copy-start.4 = (bf16[32,512]{1,0:T(8,128)(2,1)S(1)}, bf16[32,512]{1,0:T(8,128)(2,1)}, u32[]{:S(2)}) copy-start(bf16[32,512]{1,0:T(8,128)(2,1)} %stream.1) | copy-start | bytes 98308
  114.3 3.1 %collective-permute-start.8 = (bf16[32,512]{1,0:T(8,128)(2,1)S(1)}, bf16[32,512]{1,0:T(8,128)(2,1)S(1)}, u32[]{:S(2)}, u32[]{:S(2)}) collective-permute-start(bf16[32,512]{1,0:T(8,128)(2,1)S(1)} %get-tuple-element.29), channel_id=1, source_target_pairs={{1,0},{3,2},{5,4},{7,6},{9,8},{11,10},{13,12},{15,14},{17,16},{19,... | collective-permute-start | bytes 98312 | tf_op jit(solution)/shard_map/ppermute | solution.py:453
  133.5 1.5 collective-permute-start.9
  135.1 3.4 %copy-start.2 = (bf16[512,8192]{1,0:T(8,128)(2,1)S(1)}, bf16[512,8192]{1,0:T(8,128)(2,1)}, u32[]{:S(2)}) copy-start(bf16[512,8192]{1,0:T(8,128)(2,1)} %copy-done.1) | copy-start | bytes 25165828
  138.4 15.8 %copy-start.9 = (f32[8192]{0:T(1024)S(1)}, f32[8192]{0:T(1024)}, u32[]{:S(2)}) copy-start(f32[8192]{0:T(1024)} %param.20) | copy-start | bytes 98308
  154.2 1.5 collective-permute-start.10
  155.7 5.8 %copy-start = (bf16[8192,1024]{1,0:T(8,128)(2,1)S(1)}, bf16[8192,1024]{1,0:T(8,128)(2,1)}, u32[]{:S(2)}) copy-start(bf16[8192,1024]{1,0:T(8,128)(2,1)} %gate.1) | copy-start | bytes 50331652
  179.1 1.6 collective-permute-start.11

commit v3 on v2

--- a/solution.py
+++ b/solution.py
@@ -17,6 +17,7 @@
 ARRIVE = REQ_DEV * NEWP
 MIB = 1024 * 1024
 BOTH = ("tp", "pd")
+SPLIT = 2
 
 VM = pl.BlockSpec(memory_space=pltpu.VMEM)
 SM = pl.BlockSpec(memory_space=pltpu.SMEM)
@@ -120,45 +121,120 @@
             pltpu.SemaphoreType.DMA((members,)),
             pltpu.SemaphoreType.DMA((5,)),
         ],
-        compiler_params=pltpu.CompilerParams(vmem_limit_bytes=61 * MIB),
+        compiler_params=pltpu.CompilerParams(vmem_limit_bytes=8 * MIB),
         name="pack_pages",
     )(place, in_hbm(pages), in_hbm(pool))
 
 
-def hold_kernel(after, *refs):
-    count = (len(refs) - 2) // 2
-    sources, copies_out = refs[:count], refs[count : 2 * count]
-    mark, sems = refs[2 * count :]
-    copies = [
-        pltpu.make_async_copy(sources[i], copies_out[i], sems.at[i]) for i in range(count)
-    ]
-    for copy in copies:
-        copy.start()
-    mark[...] = jnp.zeros_like(mark)
+def prepare_kernel(count, parts, place, lens, lens_wide, table, listed, *refs):
+    sources = refs[:count]
+    held = refs[len(refs) - 5 - parts : -5]
+    bias, landing, whole, part, sems = refs[-5:]
+    copies = []
+    for source in sources:
+        done = 0
+        while done < source.shape[0]:
+            part_out = held[len(copies)]
+            window = pl.ds(done, part_out.shape[0])
+            copies.append(
+                pltpu.make_async_copy(source.at[window], part_out, sems.at[len(copies)])
+            )
+            copies[-1].start()
+            done += part_out.shape[0]
+
+    member = place[0]
+    entry = listed[...]
+    members, lanes = entry.shape
+    per_peer = ARRIVE // members
+    wanted = (entry >= 0) & ((entry >> 8) == member)
+    before = lax.broadcasted_iota(jnp.int32, (lanes, lanes), 0) < lax.broadcasted_iota(
+        jnp.int32, (lanes, lanes), 1
+    )
+    rank = jnp.dot(
+        jnp.where(wanted, 1.0, 0.0).astype(jnp.bfloat16),
+        jnp.where(before, 1.0, 0.0).astype(jnp.bfloat16),
+        preferred_element_type=jnp.float32,
+    ).astype(jnp.int32)
+    column = lax.broadcasted_iota(jnp.int32, landing.shape, 1)
+    found = jnp.zeros(landing.shape, jnp.int32)
+    for c in range(per_peer):
+        slot = jnp.sum(jnp.where(wanted & (rank == c), entry & 255, 0), axis=1, keepdims=True)
+        found = jnp.where(column == c, slot, found)
+    landing[...] = found
+
+    rows = bias.shape[0]
+    pages = table.shape[0]
+    wide = whole.shape[1]
+    page_id = lax.broadcasted_iota(jnp.int32, (pages, wide), 0)
+    slot_id = lax.broadcasted_iota(jnp.int32, (pages, wide), 1)
+    for r in range(rows):
+        full = lens[r] // PAGE
+        hit = table[:, r : r + 1] == slot_id
+        in_whole = jnp.where(hit & (page_id < full), 1.0, 0.0)
+        in_part = jnp.where(hit & (page_id == full), 1.0, 0.0)
+        whole[r : r + 1, :] = jnp.sum(in_whole, axis=0, keepdims=True)
+        part[r : r + 1, :] = jnp.sum(in_part, axis=0, keepdims=True)
+    whole_b = whole[...].astype(jnp.bfloat16)
+    part_b = part[...].astype(jnp.bfloat16)
+    lane = lax.broadcasted_iota(jnp.int32, (rows, 128), 1)
+    inside = (lane % PAGE) < (lens_wide[...] % PAGE)
+    per_block = 128 // PAGE
+    slot_in = lax.broadcasted_iota(jnp.int32, (wide, 128), 0)
+    lane_in = lax.broadcasted_iota(jnp.int32, (wide, 128), 1) // PAGE
+    for i in range(bias.shape[1] // 128):
+        expand = jnp.where(slot_in == lane_in + i * per_block, 1.0, 0.0).astype(jnp.bfloat16)
+        times = jnp.dot(whole_b, expand, preferred_element_type=jnp.float32)
+        extra = jnp.dot(part_b, expand, preferred_element_type=jnp.float32)
+        bias[:, i * 128 : (i + 1) * 128] = jnp.log(times + jnp.where(inside, extra, 0.0))
+
     for copy in copies:
         copy.wait()
 
 
-def hold(after, weights):
-    moved = sum(w.size * w.dtype.itemsize for w in weights)
+def prepare(place, lens, tables, listed, slots, weights, first):
+    rows, pages = tables.shape
+    members = listed.shape[0]
+    wide = -(-slots // 128) * 128
+    moved = sum(w.size * w.dtype.itemsize for w, _ in weights)
+    count = len(weights)
+    pieces = [
+        pltpu.VMEM((w.shape[0] // n, w.shape[1]), w.dtype) for w, n in weights for _ in range(n)
+    ]
+    weights = [w for w, _ in weights]
+    parts = len(pieces)
     return pl.pallas_call(
-        hold_kernel,
-        out_shape=[pltpu.VMEM(w.shape, w.dtype) for w in weights]
-        + [jax.ShapeDtypeStruct((8, 128), jnp.float32)],
-        in_specs=[ANY] + [HBM] * len(weights),
-        out_specs=[VM] * (len(weights) + 1),
-        scratch_shapes=[pltpu.SemaphoreType.DMA((len(weights),))],
-        compiler_params=pltpu.CompilerParams(vmem_limit_bytes=2 * MIB),
+        functools.partial(prepare_kernel, count, parts),
+        out_shape=pieces
+        + [
+            jax.ShapeDtypeStruct((rows, slots * PAGE), jnp.float32),
+            jax.ShapeDtypeStruct((members, 128), jnp.int32),
+        ],
+        in_specs=[SM, SM, VM, VM, VM] + [HBM] * count + [ANY] * len(first),
+        out_specs=[VM] * (parts + 2),
+        scratch_shapes=[
+            pltpu.VMEM((rows, wide), jnp.float32),
+            pltpu.VMEM((rows, wide), jnp.float32),
+            pltpu.SemaphoreType.DMA((parts,)),
+        ],
+        compiler_params=pltpu.CompilerParams(vmem_limit_bytes=6 * MIB),
         cost_estimate=pl.CostEstimate(flops=0, bytes_accessed=moved, transcendentals=0),
-        name="hold_weights",
-    )(after, *[in_hbm(w) for w in weights])
-
-
-def attend_kernel(members, place, landing, mark, old_pool, bias, query, new_k, new_v, *refs):
+        name="prepare",
+    )(
+        place,
+        lens,
+        jnp.broadcast_to(lens[:, None], (rows, 128)),
+        tables.T,
+        jnp.pad(listed, ((0, 0), (0, wide - slots)), constant_values=-1),
+        *[in_hbm(w) for w in weights],
+        *first,
+    )
+
+
+def attend_kernel(members, place, landing, old_pool, bias, query, new_k, new_v, *refs):
     arrived = refs[:members]
     kv_out, att_low, att_high = refs[members : members + 3]
     pool, scores, sems = refs[members + 3 :]
-    half = place[1]
+    member, half = place[0], place[1]
     slots = pool.shape[0]
     resident = slots - ARRIVE
     per_peer = ARRIVE // members
@@ -168,11 +244,14 @@
 
     @pl.when(half == 0)
     def _():
-        copy = pltpu.make_async_copy(old_pool, kv_out, sems.at[0])
+        copy = pltpu.make_async_copy(old_pool, pool, sems.at[0])
         copy.start()
         att_low[...] = jnp.zeros_like(att_low)
         att_high[...] = jnp.zeros_like(att_high)
         copy.wait()
+        copy_out = pltpu.make_async_copy(pool, kv_out, sems.at[1])
+        copy_out.start()
+        copy_out.wait()
 
     @pl.when(half == 1)
     def _():
@@ -181,10 +260,11 @@
         )
         copy.start()
         for k in range(members):
+            source = lax.rem(member - k + members, members)
 
             @pl.loop(0, per_peer, unroll=math.gcd(per_peer, 8))
             def _(c):
-                pool[resident + landing[k * per_peer + c]] = arrived[k][c]
+                pool[resident + landing[source, c]] = arrived[k][c]
 
         copy.wait()
         copy_out = pltpu.make_async_copy(pool, kv_out, sems.at[1])
@@ -229,7 +309,7 @@
         copy_out.wait()
 
 
-def place_and_attend(place, landing, mark, old_pool, bias, query, new_k, new_v, arrived):
+def place_and_attend(place, landing, old_pool, bias, query, new_k, new_v, arrived):
     members = len(arrived)
     slots = old_pool.shape[0]
     rows = bias.shape[0]
@@ -242,7 +322,7 @@
             jax.ShapeDtypeStruct((tokens, GQ * HD // 2), jnp.bfloat16),
             jax.ShapeDtypeStruct((tokens, GQ * HD // 2), jnp.bfloat16),
         ],
-        in_specs=[SM, SM, ANY, HBM, VM, VM, VM, VM] + [VM] * members,
+        in_specs=[SM, SM, HBM, VM, VM, VM, VM] + [VM] * members,
         out_specs=[HBM, VM, VM],
         scratch_shapes=[
             pltpu.VMEM(old_pool.shape, old_pool.dtype),
@@ -251,29 +331,7 @@
         ],
         compiler_params=pltpu.CompilerParams(vmem_limit_bytes=9 * MIB),
         name="place_attend",
-    )(place, landing, mark, in_hbm(old_pool), bias, query, new_k, new_v, *arrived)
-
-
-def table_bias(tables, row_lengths, slots):
-    pages = jnp.arange(tables.shape[1])
-    whole_pages = row_lengths // PAGE
-    hit = tables[:, :, None] == jnp.arange(slots)[None, None, :]
-    whole = jnp.sum(
-        (hit & (pages[None, :, None] < whole_pages[:, None, None])).astype(jnp.float32), axis=1
-    )
-    part = jnp.sum(
-        (hit & (pages[None, :, None] == whole_pages[:, None, None])).astype(jnp.float32), axis=1
-    )
-    inside = (jnp.arange(PAGE)[None, :] < (row_lengths % PAGE)[:, None]).astype(jnp.float32)
-    times = whole[:, :, None] + part[:, :, None] * inside[:, None, :]
-    return jnp.log(times).reshape(tables.shape[0], slots * PAGE)
-
-
-def landing_slots(slots_from, member, per_peer):
-    wanted = (slots_from >= 0) & (slots_from // ARRIVE == member)
-    ahead = jnp.cumsum(wanted.astype(jnp.int32), axis=1) - 1
-    pick = wanted[:, None, :] & (ahead[:, None, :] == jnp.arange(per_peer)[None, :, None])
-    return jnp.sum(jnp.where(pick, (slots_from % ARRIVE)[:, None, :], 0), axis=2)
+    )(place, landing, in_hbm(old_pool), bias, query, new_k, new_v, *arrived)
 
 
 def project_kernel(groups, place, weight, stream, mine, sibling, res_out):
@@ -306,19 +364,17 @@
     )(place, in_vmem(weight), stream, mine, sibling)
 
 
-def ffn_kernel(place, mine, sibling, gain, gate, up, down, own_out, other_out, *scratch):
-    up_buf, down_buf, normed, gated, hidden, up_sem, down_sem = scratch
+def ffn_kernel(place, mine, sibling, gain, *refs):
+    gate, up = refs[:SPLIT], refs[SPLIT : 2 * SPLIT]
+    down, own_out, other_out, *scratch = refs[2 * SPLIT :]
+    down_buf, normed, hidden, down_sem = scratch
     half = place[1]
     members, tokens, width = mine.shape
-    features, hidden_count = gate.shape
+    depth, hidden_count = gate[0].shape
+    features = depth * SPLIT
     tile = min(256, hidden_count)
     tiles = [slice(f * tile, (f + 1) * tile) for f in range(hidden_count // tile)]
-    up_copies, down_copies = [], []
-    for f, cols in enumerate(tiles):
-        up_copies.append(
-            pltpu.make_async_copy(up.at[:, cols], up_buf.at[:, cols], up_sem.at[f])
-        )
-        up_copies[-1].start()
+    down_copies = []
     for t in range(members):
         cols = pl.ds(t * 2 * width, 2 * width)
         down_copies.append(
@@ -339,12 +395,13 @@
         n = x * factor * gain[t : t + 1, :]
         normed[:, 2 * t * width : 2 * (t + 1) * width] = n.astype(jnp.bfloat16)
     for cols in tiles:
-        act = jnp.dot(normed[...], gate[:, cols], preferred_element_type=jnp.float32)
-        gated[:, cols] = act / (1.0 + jnp.exp(-act))
-    for f, cols in enumerate(tiles):
-        up_copies[f].wait()
-        act = jnp.dot(normed[...], up_buf[:, cols], preferred_element_type=jnp.float32)
-        hidden[:, cols] = (gated[:, cols] * act).astype(jnp.bfloat16)
+        gate_act = up_act = 0.0
+        for i in range(SPLIT):
+            x = normed[:, i * depth : (i + 1) * depth]
+            gate_act += jnp.dot(x, gate[i][:, cols], preferred_element_type=jnp.float32)
+            up_act += jnp.dot(x, up[i][:, cols], preferred_element_type=jnp.float32)
+        h = gate_act / (1.0 + jnp.exp(-gate_act)) * up_act
+        hidden[:, cols] = h.astype(jnp.bfloat16)
     for t in range(members):
         down_copies[t].wait()
         part = jnp.dot(
@@ -360,35 +417,24 @@
 def feed_forward(place, mine, sibling, gain, gate, up, down):
     members, tokens, width = mine.shape
     blocks = 2 * members
-    hidden_count = gate.shape[1]
+    hidden_count = gate[0].shape[1]
     return pl.pallas_call(
         ffn_kernel,
         out_shape=[
             jax.ShapeDtypeStruct(mine.shape, jnp.float32),
             jax.ShapeDtypeStruct(mine.shape, jnp.bfloat16),
         ],
-        in_specs=[SM, VM, VM, VM, VM, HBM, HBM],
+        in_specs=[SM, VM, VM, VM] + [VM] * (2 * SPLIT) + [HBM],
         out_specs=[VM, VM],
         scratch_shapes=[
-            pltpu.VMEM(up.shape, up.dtype),
             pltpu.VMEM(down.shape, down.dtype),
             pltpu.VMEM((tokens, blocks * width), jnp.bfloat16),
-            pltpu.VMEM((tokens, hidden_count), jnp.float32),
             pltpu.VMEM((tokens, hidden_count), jnp.bfloat16),
-            pltpu.SemaphoreType.DMA((-(-hidden_count // 256),)),
             pltpu.SemaphoreType.DMA((members,)),
         ],
-        compiler_params=pltpu.CompilerParams(vmem_limit_bytes=36 * MIB),
+        compiler_params=pltpu.CompilerParams(vmem_limit_bytes=19 * MIB),
         name="feed_forward",
-    )(
-        place,
-        mine,
-        sibling,
-        gain.reshape(members, 2 * width),
-        in_vmem(gate),
-        in_hbm(up),
-        in_hbm(down),
-    )
+    )(place, mine, sibling, gain, *map(in_vmem, gate), *map(in_vmem, up), in_hbm(down))
 
 
 def local(
@@ -410,7 +456,6 @@
     half = lax.axis_index("pd")
     place = jnp.stack([member, half]).astype(jnp.int32)
     slots = kv_pages.shape[0]
-    per_peer = ARRIVE // members
     groups = members // KVH
     rows = block_tables.shape[0]
     steps = queries.shape[1]
@@ -426,23 +471,33 @@
         return lax.ppermute(x, "pd", [(0, 1), (1, 0)])
 
     outgoing = pack(place, page_list, kv_pages)
+    order = sorted(range(members), key=lambda k: abs(k - members // 2))
     arrived = [None] * members
-    for k in sorted(range(members), key=lambda k: abs(k - members // 2)):
+    for k in order[:5]:
         arrived[k] = ahead(outgoing[k], k, 0, 1)
 
-    out_proj, mark = hold(outgoing[0], (out_proj,))
-
-    behind = (member - jnp.arange(members)) % members
-    landing = landing_slots(page_list.reshape(members, slots)[behind], member, per_peer)
     row_lengths = lax.dynamic_slice_in_dim(lengths, member % groups * rows, rows)
-    bias = table_bias(block_tables, row_lengths, slots)
     query = queries.reshape(rows, steps, GQ, HD).transpose(2, 1, 0, 3).reshape(GQ * tokens, HD)
     padding = ((0, -tokens % 128), (0, 0))
     new_k = jnp.pad(fresh_kv[:, :, 0].reshape(tokens, HD), padding)
     new_v = jnp.pad(fresh_kv[:, :, 1].reshape(tokens, HD), padding)
+    gain = norm_gain.reshape(members, -1)
+    *held, bias, landing = prepare(
+        place,
+        row_lengths,
+        block_tables,
+        page_list.reshape(members, slots),
+        slots,
+        ((out_proj, 1), (gate_weight, SPLIT), (up_weight, SPLIT)),
+        (query, new_k, new_v, gain, outgoing[0]),
+    )
+
+    rest, landing = lax.optimization_barrier(([outgoing[k] for k in order[5:]], landing))
+    for k, block in zip(order[5:], rest):
+        arrived[k] = ahead(block, k, 0, 1)
 
     kv_after, att_low, att_high = place_and_attend(
-        place, landing.reshape(-1), mark, kv_pages, bias, query, new_k, new_v, arrived
+        place, landing, kv_pages, bias, query, new_k, new_v, arrived
     )
 
     def everywhere(x):
@@ -450,15 +505,15 @@
         mine = lax.all_to_all(spread, "tp", split_axis=0, concat_axis=0)
         return mine, swap(mine)
 
-    att_mine = jnp.where(half == 1, att_high, lax.ppermute(att_low, "pd", [(1, 0)]))
+    att_mine = att_high + lax.ppermute(att_low, "pd", [(1, 0)])
     here, there = everywhere(att_mine)
 
     inner = stream.reshape(steps, groups, rows, -1).transpose(1, 0, 2, 3).reshape(stream.shape)
-    residual = project(place, out_proj, inner, here, there, groups)
+    residual = project(place, held[0], inner, here, there, groups)
 
     mine, sibling = everywhere(residual)
     own, other = feed_forward(
-        place, mine, sibling, norm_gain, gate_weight, up_weight, down_weight
+        place, mine, sibling, gain, held[1 : 1 + SPLIT], held[1 + SPLIT :], down_weight
     )
     summed = (own + swap(other).astype(jnp.float32)).astype(jnp.bfloat16)
     shares = lax.all_to_all(summed, "tp", split_axis=0, concat_axis=0)

time: 195 us -> 116 us (0.59)
  Pallas kernels: 109 us -> 39.8 us
  waiting for transfers between devices: 6.27 us -> 15.4 us
  local copies, waits for them, and re-layouts: 16 us -> 6.97 us
  other arithmetic: 7.38 us -> 0.82 us
  blocking collectives: 41.3 us -> 37.7 us
    pallas_call x1, Pallas kernels: 79.1 us -> 4.33 us  [place_and_attend(): pl.pallas_call(functools.partial(attend_kernel, members), out_shape=[jax....]
    pallas_call x1, Pallas kernels: 3.39 us -> 13.8 us  [prepare(): pl.pallas_call(functools.partial(prepare_kernel, count, parts), out_shape...]
    unnamed x32 -> x15, local copies, waits for them, and re-layouts: 12.4 us -> 2.87 us
    ppermute x1, waiting for transfers between devices: 1.8 us -> 7.14 us  [local(): att_mine = att_high + lax.ppermute(att_low, 'pd', [(1, 0)])]
    pallas_call x1, Pallas kernels: 17.6 us -> 13 us  [feed_forward(): pl.pallas_call(ffn_kernel, out_shape=[jax.ShapeDtypeStruct(mine.shape, jn...]
    ppermute x8, waiting for transfers between devices: 0.02 us -> 3.84 us  [ahead(): return lax.ppermute(x, BOTH, route)]
    all_to_all x2, blocking collectives: 28.7 us -> 25.1 us  [everywhere(): mine = lax.all_to_all(spread, 'tp', split_axis=0, concat_axis=0)]
    log x1 -> x0, other arithmetic: 2.91 us -> none  [table_bias(): return jnp.log(times).reshape(tables.shape[0], slots * PAGE)]
  transfers between devices with their start and end apart: 12 -> 12, of which waited for: 4 -> 6; matrix products, arithmetic and copies ran while one was open for 5% -> 4% of each run, Pallas kernels for 2% -> 12%
where the time goes in v3:
time: 116 us
  Pallas kernels  39.8 us (34%)
  blocking collectives  37.7 us (33%)
  waiting for transfers between devices  15.4 us (13%)
  starting transfers between devices  14 us (12%)
  local copies, waits for them, and re-layouts  6.97 us (6%)
    all_to_all x2, blocking collectives, everywhere(): mine = lax.all_to_all(spread, 'tp', split_axis=0, concat_axis=0)  25.1 us
    pallas_call x1, Pallas kernels, prepare(): pl.pallas_call(functools.partial(prepare_kernel, count, parts), out_shape...  13.8 us
    pallas_call x1, Pallas kernels, feed_forward(): pl.pallas_call(ffn_kernel, out_shape=[jax.ShapeDtypeStruct(mine.shape, jn...  13 us
    all_to_all x1, blocking collectives, local(): shares = lax.all_to_all(summed, 'tp', split_axis=0, concat_axis=0)  12.6 us
    ppermute x8, starting transfers between devices, ahead(): return lax.ppermute(x, BOTH, route)  12.5 us
    ppermute x1, waiting for transfers between devices, local(): att_mine = att_high + lax.ppermute(att_low, 'pd', [(1, 0)])  7.14 us
    pallas_call x1, Pallas kernels, pack(): pl.pallas_call(functools.partial(pack_kernel, members), out_shape=[shape]...  5.6 us
    ppermute x3, waiting for transfers between devices, swap(): return lax.ppermute(x, 'pd', [(0, 1), (1, 0)])  4.46 us
  transfers between devices with their start and end apart: 12, of which 6 were waited for; matrix products, arithmetic and copies ran while one was open for 4% of the time, Pallas kernels for 12%

profile of v3, /device:TPU:0, one launch (start us, length us, event | category | flops | bytes accessed | tf_op | source)
XLA Modules:
  0.0 115.6 jit_solution(6531983046622940035)
XLA Ops:
  0.7 5.6 %pack_pages.1 = (bf16[32,2,16,128]{3,2,1,0:T(8,128)(2,1)S(1)}, bf16[32,2,16,128]{3,2,1,0:T(8,128)(2,1)S(1)}, bf16[32,2,16,128]{3,2,1,0:T(8,128)(2,1)}, bf16[32,2...) custom-call(s32[2]{0:T(128)S(1)} %pad_add_fusion.place, ...), custom_call_target="tpu_custom_call" | custom-call | tf_op jit(solution)/shard_map/pack_pages/pallas_call | solution.py:111
  6.3 0.7 copy-done.2
  7.0 0.7 copy-done.4
  7.7 1.3 %collective-permute-start.2 = (bf16[32,2,16,128]{3,2,1,0:T(8,128)(2,1)}, bf16[32,2,16,128]{3,2,1,0:T(8,128)(2,1)S(1)}, u32[]{:S(2)}, u32[]{:S(2)}) collective-permute-start(bf16[32,2,16,128]{3,2,1,0:T(8,128)(2,1)} %get-tuple-element.34), channel_id=1, source_target_pairs={{0,5},{2,7},{4,9},{6,11},{8,13},{10,15},{12,1},{14,3},{16,21},{18,... | collective-permute-start | bytes 786440 | tf_op jit(solution)/shard_map/ppermute | solution.py:468
  9.0 1.3 %collective-permute-start.3 = (bf16[32,2,16,128]{3,2,1,0:T(8,128)(2,1)}, bf16[32,2,16,128]{3,2,1,0:T(8,128)(2,1)S(1)}, u32[]{:S(2)}, u32[]{:S(2)}) collective-permute-start(bf16[32,2,16,128]{3,2,1,0:T(8,128)(2,1)} %get-tuple-element.35), channel_id=1, source_target_pairs={{0,7},{2,9},{4,11},{6,13},{8,15},{10,1},{12,3},{14,5},{16,23},{18,... | collective-permute-start | bytes 786440 | tf_op jit(solution)/shard_map/ppermute | solution.py:468
  10.3 2.0 %collective-permute-start.4 = (bf16[32,2,16,128]{3,2,1,0:T(8,128)(2,1)}, bf16[32,2,16,128]{3,2,1,0:T(8,128)(2,1)}, u32[]{:S(2)}, u32[]{:S(2)}) collective-permute-start(bf16[32,2,16,128]{3,2,1,0:T(8,128)(2,1)} %get-tuple-element.36), channel_id=1, source_target_pairs={{0,9},{2,11},{4,13},{6,15},{8,1},{10,3},{12,5},{14,7},{16,25},{18,... | collective-permute-start | bytes 786440 | tf_op jit(solution)/shard_map/ppermute | solution.py:468
  12.4 2.0 %collective-permute-start.5 = (bf16[32,2,16,128]{3,2,1,0:T(8,128)(2,1)}, bf16[32,2,16,128]{3,2,1,0:T(8,128)(2,1)}, u32[]{:S(2)}, u32[]{:S(2)}) collective-permute-start(bf16[32,2,16,128]{3,2,1,0:T(8,128)(2,1)} %get-tuple-element.37), channel_id=1, source_target_pairs={{0,11},{2,13},{4,15},{6,1},{8,3},{10,5},{12,7},{14,9},{16,27},{18,... | collective-permute-start | bytes 786440 | tf_op jit(solution)/shard_map/ppermute | solution.py:468
  14.3 2.0 %collective-permute-start.6 = (bf16[32,2,16,128]{3,2,1,0:T(8,128)(2,1)}, bf16[32,2,16,128]{3,2,1,0:T(8,128)(2,1)}, u32[]{:S(2)}, u32[]{:S(2)}) collective-permute-start(bf16[32,2,16,128]{3,2,1,0:T(8,128)(2,1)} %get-tuple-element.38), channel_id=1, source_target_pairs={{0,13},{2,15},{4,1},{6,3},{8,5},{10,7},{12,9},{14,11},{16,29},{18,... | collective-permute-start | bytes 786440 | tf_op jit(solution)/shard_map/ppermute | solution.py:468
  16.3 0.8 reshape.19
  17.1 0.8 reshape.22.refs_6_.gain
  17.9 0.8 fusion
  18.8 0.8 copy.16
  19.6 0.9 reshape.20
  20.5 0.7 broadcast_in_dim.6.lens_wide
  21.2 0.7 copy-done.1
  21.9 13.8 %prepare.1 = (bf16[512,8192]{1,0:T(8,128)(2,1)S(1)}, bf16[4096,1024]{1,0:T(8,128)(2,1)S(1)}, bf16[4096,1024]{1,0:T(8,128)(2,1)S(1)}, bf16[4096,1024]{1,0:T(8,128...) custom-call(s32[2]{0:T(128)S(1)} %pad_add_fusion.place, ...), custom_call_target="tpu_custom_call" | custom-call | bytes 41943040 | tf_op jit(solution)/shard_map/prepare/pallas_call | solution.py:205
  35.7 1.3 %collective-permute-start = (bf16[32,2,16,128]{3,2,1,0:T(8,128)(2,1)S(1)}, bf16[32,2,16,128]{3,2,1,0:T(8,128)(2,1)S(1)}, u32[]{:S(2)}, u32[]{:S(2)}) collective-permute-start(bf16[32,2,16,128]{3,2,1,0:T(8,128)(2,1)S(1)} %get-tuple-element.32.refs_7_), channel_id=1, source_target_pairs={{0,1},{2,3},{4,5},{6,7},{8,9},{10,11},{12,13},{14,15},{16,17},{18,... | collective-permute-start | bytes 786440 | tf_op jit(solution)/shard_map/ppermute | solution.py:468
  37.1 1.3 %collective-permute-start.1 = (bf16[32,2,16,128]{3,2,1,0:T(8,128)(2,1)S(1)}, bf16[32,2,16,128]{3,2,1,0:T(8,128)(2,1)S(1)}, u32[]{:S(2)}, u32[]{:S(2)}) collective-permute-start(bf16[32,2,16,128]{3,2,1,0:T(8,128)(2,1)S(1)} %copy-done.5), channel_id=1, source_target_pairs={{0,3},{2,5},{4,7},{6,9},{8,11},{10,13},{12,15},{14,1},{16,19},{18,... | collective-permute-start | bytes 786440 | tf_op jit(solution)/shard_map/ppermute | solution.py:468
  38.4 1.3 %collective-permute-start.7 = (bf16[32,2,16,128]{3,2,1,0:T(8,128)(2,1)S(1)}, bf16[32,2,16,128]{3,2,1,0:T(8,128)(2,1)S(1)}, u32[]{:S(2)}, u32[]{:S(2)}) collective-permute-start(bf16[32,2,16,128]{3,2,1,0:T(8,128)(2,1)S(1)} %copy-done.3), channel_id=1, source_target_pairs={{0,15},{2,1},{4,3},{6,5},{8,7},{10,9},{12,11},{14,13},{16,31},{18,... | collective-permute-start | bytes 786440 | tf_op jit(solution)/shard_map/ppermute | solution.py:468
  39.7 2.5 %collective-permute-done.1.refs_1_ = bf16[32,2,16,128]{3,2,1,0:T(8,128)(2,1)S(1)} collective-permute-done((bf16[32,2,16,128]{3,2,1,0:T(8,128)(2,1)S(1)}, bf16[32,2,16,128]{3,2,1,0:T(8,128)(2,1)S(1)}, u32[]{:S(2)}, u32[]{:S(2)}) %collective-permute-start.1) | collective-permute-done | bytes 262176 | tf_op jit(solution)/shard_map/ppermute | solution.py:468
  42.2 1.3 %collective-permute-done.7.refs_7_ = bf16[32,2,16,128]{3,2,1,0:T(8,128)(2,1)S(1)} collective-permute-done((bf16[32,2,16,128]{3,2,1,0:T(8,128)(2,1)S(1)}, bf16[32,2,16,128]{3,2,1,0:T(8,128)(2,1)S(1)}, u32[]{:S(2)}, u32[]{:S(2)}) %collective-permute-start.7) | collective-permute-done | bytes 262176 | tf_op jit(solution)/shard_map/ppermute | solution.py:468
  43.6 4.3 %place_attend.1 = (bf16[312,2,16,128]{3,2,1,0:T(8,128)(2,1)}, bf16[32,512]{1,0:T(8,128)(2,1)S(1)}, bf16[32,512]{1,0:T(8,128)(2,1)S(1)}) custom-call(s32[2]{0:T(128)S(1)} %pad_add_fusion.place, s32[8,128]{1,0:T(8,128)S(1)} %get-tuple-element.30.landing, bf16[312,2,16,128]{3,2,1,0:T(8,128)(2,1)} %old_pool.1, f32[16,4992]{1,0:T(8,128)S(1)} %get-tuple-element.31.bias, ...), custom_call_target="tpu_custom_call" | custom-call | tf_op jit(solution)/shard_map/place_attend/pallas_call | solution.py:318
  47.9 1.3 %collective-permute-start.8 = (bf16[32,512]{1,0:T(8,128)(2,1)S(1)}, bf16[32,512]{1,0:T(8,128)(2,1)S(1)}, u32[]{:S(2)}, u32[]{:S(2)}) collective-permute-start(bf16[32,512]{1,0:T(8,128)(2,1)S(1)} %get-tuple-element.43), channel_id=1, source_target_pairs={{1,0},{3,2},{5,4},{7,6},{9,8},{11,10},{13,12},{15,14},{17,16},{19,... | collective-permute-start | bytes 98312 | tf_op jit(solution)/shard_map/ppermute | solution.py:508
  49.2 7.1 %collective-permute-done.8 = bf16[32,512]{1,0:T(8,128)(2,1)S(1)} collective-permute-done((bf16[32,512]{1,0:T(8,128)(2,1)S(1)}, bf16[32,512]{1,0:T(8,128)(2,1)S(1)}, u32[]{:S(2)}, u32[]{:S(2)}) %collective-permute-start.8) | collective-permute-done | bytes 32800 | tf_op jit(solution)/shard_map/ppermute | solution.py:508
  56.4 12.5 %all_to_all.15.mine = bf16[8,32,512]{2,1,0:T(8,128)(2,1)S(1)} all-to-all(bf16[8,32,512]{2,1,0:T(8,128)(2,1)S(1)} %broadcast_in_dim.7), channel_id=1, replica_groups=mesh['grp'=2,'tp'=8,'pd'=2] {'tp'}, dimensions={0} | all-to-all | bytes 524288 | tf_op jit(solution)/shard_map/all_to_all | solution.py:505
  68.9 1.5 %collective-permute-done.9.sibling = bf16[8,32,512]{2,1,0:T(8,128)(2,1)S(1)} collective-permute-done((bf16[8,32,512]{2,1,0:T(8,128)(2,1)S(1)}, bf16[8,32,512]{2,1,0:T(8,128)(2,1)S(1)}, u32[]{:S(2)}, u32[]{:S(2)}) %collective-permute-start.9) | collective-permute-done | bytes 262176 | tf_op jit(solution)/shard_map/ppermute | solution.py:471
  70.4 3.1 %out_projection.1 = bf16[32,512]{1,0:T(8,128)(2,1)S(1)} custom-call(s32[2]{0:T(128)S(1)} %pad_add_fusion.place, bf16[512,8192]{1,0:T(8,128)(2,1)S(1)} %get-tuple-element.41.weight, bf16[32,512]{1,0:T(8,128)(2,1)S(1)} %copy-done, bf16[8,32,512]{2,1,0:T(8,128)(2,1)S(1)} %all_to_all.15.mine, bf16[8,32,512]{2,1,0:T(8,128)(2,1)S(1)} %collective-permute-done.9.sibling), custom_call_target="tpu_custom_call" | custom-call | tf_op jit(solution)/shard_map/out_projection/pallas_call | solution.py:357
  73.5 12.6 %all_to_all.16.mine = bf16[8,32,512]{2,1,0:T(8,128)(2,1)S(1)} all-to-all(bf16[8,32,512]{2,1,0:T(8,128)(2,1)S(1)} %broadcast_in_dim.8), channel_id=1, replica_groups=mesh['grp'=2,'tp'=8,'pd'=2] {'tp'}, dimensions={0} | all-to-all | bytes 524288 | tf_op jit(solution)/shard_map/all_to_all | solution.py:505
  86.2 1.5 %collective-permute-done.10.sibling = bf16[8,32,512]{2,1,0:T(8,128)(2,1)S(1)} collective-permute-done((bf16[8,32,512]{2,1,0:T(8,128)(2,1)S(1)}, bf16[8,32,512]{2,1,0:T(8,128)(2,1)S(1)}, u32[]{:S(2)}, u32[]{:S(2)}) %collective-permute-start.10) | collective-permute-done | bytes 262176 | tf_op jit(solution)/shard_map/ppermute | solution.py:471
  87.7 13.0 %feed_forward.1 = (f32[8,32,512]{2,1,0:T(8,128)S(1)}, bf16[8,32,512]{2,1,0:T(8,128)(2,1)S(1)}) custom-call(s32[2]{0:T(128)S(1)} %pad_add_fusion.place, bf16[8,32,512]{2,1,0:T(8,128)(2,1)S(1)} %all_to_all.16.mine, bf16[8,32,512]{2,1,0:T(8,128)(2,1)S(1)} %collective-permute-done.10.sibling, f32[8,1024]{1,0:T(8,128)S(1)} %reshape.22.refs_6_.gain, ...), custom_call_target="tpu_custom_call" | custom-call | tf_op jit(solution)/shard_map/feed_forward/pallas_call | solution.py:421
  100.9 1.4 %collective-permute-done.11 = bf16[8,32,512]{2,1,0:T(8,128)(2,1)S(1)} collective-permute-done((bf16[8,32,512]{2,1,0:T(8,128)(2,1)S(1)}, bf16[8,32,512]{2,1,0:T(8,128)(2,1)S(1)}, u32[]{:S(2)}, u32[]{:S(2)}) %collective-permute-start.11) | collective-permute-done | bytes 262176 | tf_op jit(solution)/shard_map/ppermute | solution.py:471
  102.3 12.6 %all_to_all.17 = bf16[8,32,512]{2,1,0:T(8,128)(2,1)S(1)} all-to-all(bf16[8,32,512]{2,1,0:T(8,128)(2,1)S(1)} %add_convert_fusion), channel_id=1, replica_groups=mesh['grp'=2,'tp'=8,'pd'=2] {'tp'}, dimensions={0} | all-to-all | bytes 524288 | tf_op jit(solution)/shard_map/all_to_all | solution.py:519
  (31 shorter events, 1.2 us)
Async XLA Ops:
  6.3 0.7 copy-start.2
  7.0 0.7 copy-start.4
  7.7 28.0 %collective-permute-start.2 = (bf16[32,2,16,128]{3,2,1,0:T(8,128)(2,1)}, bf16[32,2,16,128]{3,2,1,0:T(8,128)(2,1)S(1)}, u32[]{:S(2)}, u32[]{:S(2)}) collective-permute-start(bf16[32,2,16,128]{3,2,1,0:T(8,128)(2,1)} %get-tuple-element.34), channel_id=1, source_target_pairs={{0,5},{2,7},{4,9},{6,11},{8,13},{10,15},{12,1},{14,3},{16,21},{18,... | collective-permute-start | bytes 786440 | tf_op jit(solution)/shard_map/ppermute | solution.py:468
  9.0 28.0 %collective-permute-start.3 = (bf16[32,2,16,128]{3,2,1,0:T(8,128)(2,1)}, bf16[32,2,16,128]{3,2,1,0:T(8,128)(2,1)S(1)}, u32[]{:S(2)}, u32[]{:S(2)}) collective-permute-start(bf16[32,2,16,128]{3,2,1,0:T(8,128)(2,1)} %get-tuple-element.35), channel_id=1, source_target_pairs={{0,7},{2,9},{4,11},{6,13},{8,15},{10,1},{12,3},{14,5},{16,23},{18,... | collective-permute-start | bytes 786440 | tf_op jit(solution)/shard_map/ppermute | solution.py:468
  10.3 28.1 %collective-permute-start.4 = (bf16[32,2,16,128]{3,2,1,0:T(8,128)(2,1)}, bf16[32,2,16,128]{3,2,1,0:T(8,128)(2,1)}, u32[]{:S(2)}, u32[]{:S(2)}) collective-permute-start(bf16[32,2,16,128]{3,2,1,0:T(8,128)(2,1)} %get-tuple-element.36), channel_id=1, source_target_pairs={{0,9},{2,11},{4,13},{6,15},{8,1},{10,3},{12,5},{14,7},{16,25},{18,... | collective-permute-start | bytes 786440 | tf_op jit(solution)/shard_map/ppermute | solution.py:468
  12.4 27.4 %collective-permute-start.5 = (bf16[32,2,16,128]{3,2,1,0:T(8,128)(2,1)}, bf16[32,2,16,128]{3,2,1,0:T(8,128)(2,1)}, u32[]{:S(2)}, u32[]{:S(2)}) collective-permute-start(bf16[32,2,16,128]{3,2,1,0:T(8,128)(2,1)} %get-tuple-element.37), channel_id=1, source_target_pairs={{0,11},{2,13},{4,15},{6,1},{8,3},{10,5},{12,7},{14,9},{16,27},{18,... | collective-permute-start | bytes 786440 | tf_op jit(solution)/shard_map/ppermute | solution.py:468
  14.3 25.4 %collective-permute-start.6 = (bf16[32,2,16,128]{3,2,1,0:T(8,128)(2,1)}, bf16[32,2,16,128]{3,2,1,0:T(8,128)(2,1)}, u32[]{:S(2)}, u32[]{:S(2)}) collective-permute-start(bf16[32,2,16,128]{3,2,1,0:T(8,128)(2,1)} %get-tuple-element.38), channel_id=1, source_target_pairs={{0,13},{2,15},{4,1},{6,3},{8,5},{10,7},{12,9},{14,11},{16,29},{18,... | collective-permute-start | bytes 786440 | tf_op jit(solution)/shard_map/ppermute | solution.py:468
  21.2 0.7 copy-start.1
  21.9 15.2 %copy-start.5 = (bf16[32,2,16,128]{3,2,1,0:T(8,128)(2,1)S(1)}, bf16[32,2,16,128]{3,2,1,0:T(8,128)(2,1)}, u32[]{:S(2)}) copy-start(bf16[32,2,16,128]{3,2,1,0:T(8,128)(2,1)} %copy-done.4) | copy-start | bytes 786436
  21.9 16.5 %copy-start.3 = (bf16[32,2,16,128]{3,2,1,0:T(8,128)(2,1)S(1)}, bf16[32,2,16,128]{3,2,1,0:T(8,128)(2,1)}, u32[]{:S(2)}) copy-start(bf16[32,2,16,128]{3,2,1,0:T(8,128)(2,1)} %copy-done.2) | copy-start | bytes 786436
  21.9 48.5 %copy-start = (bf16[32,512]{1,0:T(8,128)(2,1)S(1)}, bf16[32,512]{1,0:T(8,128)(2,1)}, u32[]{:S(2)}) copy-start(bf16[32,512]{1,0:T(8,128)(2,1)} %stream.1) | copy-start | bytes 98308
  35.7 4.0 %collective-permute-start = (bf16[32,2,16,128]{3,2,1,0:T(8,128)(2,1)S(1)}, bf16[32,2,16,128]{3,2,1,0:T(8,128)(2,1)S(1)}, u32[]{:S(2)}, u32[]{:S(2)}) collective-permute-start(bf16[32,2,16,128]{3,2,1,0:T(8,128)(2,1)S(1)} %get-tuple-element.32.refs_7_), channel_id=1, source_target_pairs={{0,1},{2,3},{4,5},{6,7},{8,9},{10,11},{12,13},{14,15},{16,17},{18,... | collective-permute-start | bytes 786440 | tf_op jit(solution)/shard_map/ppermute | solution.py:468
  37.1 5.2 %collective-permute-start.1 = (bf16[32,2,16,128]{3,2,1,0:T(8,128)(2,1)S(1)}, bf16[32,2,16,128]{3,2,1,0:T(8,128)(2,1)S(1)}, u32[]{:S(2)}, u32[]{:S(2)}) collective-permute-start(bf16[32,2,16,128]{3,2,1,0:T(8,128)(2,1)S(1)} %copy-done.5), channel_id=1, source_target_pairs={{0,3},{2,5},{4,7},{6,9},{8,11},{10,13},{12,15},{14,1},{16,19},{18,... | collective-permute-start | bytes 786440 | tf_op jit(solution)/shard_map/ppermute | solution.py:468
  38.4 5.2 %collective-permute-start.7 = (bf16[32,2,16,128]{3,2,1,0:T(8,128)(2,1)S(1)}, bf16[32,2,16,128]{3,2,1,0:T(8,128)(2,1)S(1)}, u32[]{:S(2)}, u32[]{:S(2)}) collective-permute-start(bf16[32,2,16,128]{3,2,1,0:T(8,128)(2,1)S(1)} %copy-done.3), channel_id=1, source_target_pairs={{0,15},{2,1},{4,3},{6,5},{8,7},{10,9},{12,11},{14,13},{16,31},{18,... | collective-permute-start | bytes 786440 | tf_op jit(solution)/shard_map/ppermute | solution.py:468
  47.9 8.4 %collective-permute-start.8 = (bf16[32,512]{1,0:T(8,128)(2,1)S(1)}, bf16[32,512]{1,0:T(8,128)(2,1)S(1)}, u32[]{:S(2)}, u32[]{:S(2)}) collective-permute-start(bf16[32,512]{1,0:T(8,128)(2,1)S(1)} %get-tuple-element.43), channel_id=1, source_target_pairs={{1,0},{3,2},{5,4},{7,6},{9,8},{11,10},{13,12},{15,14},{17,16},{19,... | collective-permute-start | bytes 98312 | tf_op jit(solution)/shard_map/ppermute | solution.py:508
  68.9 1.5 %collective-permute-start.9 = (bf16[8,32,512]{2,1,0:T(8,128)(2,1)S(1)}, bf16[8,32,512]{2,1,0:T(8,128)(2,1)S(1)}, u32[]{:S(2)}, u32[]{:S(2)}) collective-permute-start(bf16[8,32,512]{2,1,0:T(8,128)(2,1)S(1)} %all_to_all.15.mine), channel_id=1, source_target_pairs={{0,1},{1,0},{2,3},{3,2},{4,5},{5,4},{6,7},{7,6},{8,9},{9,8},{10,11... | collective-permute-start | bytes 786440 | tf_op jit(solution)/shard_map/ppermute | solution.py:471
  86.2 1.5 %collective-permute-start.10 = (bf16[8,32,512]{2,1,0:T(8,128)(2,1)S(1)}, bf16[8,32,512]{2,1,0:T(8,128)(2,1)S(1)}, u32[]{:S(2)}, u32[]{:S(2)}) collective-permute-start(bf16[8,32,512]{2,1,0:T(8,128)(2,1)S(1)} %all_to_all.16.mine), channel_id=1, source_target_pairs={{0,1},{1,0},{2,3},{3,2},{4,5},{5,4},{6,7},{7,6},{8,9},{9,8},{10,11... | collective-permute-start | bytes 786440 | tf_op jit(solution)/shard_map/ppermute | solution.py:471
  100.7 1.6 %collective-permute-start.11 = (bf16[8,32,512]{2,1,0:T(8,128)(2,1)S(1)}, bf16[8,32,512]{2,1,0:T(8,128)(2,1)S(1)}, u32[]{:S(2)}, u32[]{:S(2)}) collective-permute-start(bf16[8,32,512]{2,1,0:T(8,128)(2,1)S(1)} %get-tuple-element.49), channel_id=1, source_target_pairs={{0,1},{1,0},{2,3},{3,2},{4,5},{5,4},{6,7},{7,6},{8,9},{9,8},{10,11... | collective-permute-start | bytes 786440 | tf_op jit(solution)/shard_map/ppermute | solution.py:471

commit v4 on v3

--- a/solution.py
+++ b/solution.py
@@ -107,12 +107,12 @@
 def pack(place, pages, pool):
     members = lax.axis_size("tp")
     per_peer = ARRIVE // members
-    shape = jax.ShapeDtypeStruct((per_peer, *pool.shape[1:]), pool.dtype)
+    shape = pltpu.HBM((per_peer, *pool.shape[1:]), pool.dtype)
     return pl.pallas_call(
         functools.partial(pack_kernel, members),
         out_shape=[shape] * members,
         in_specs=[SM, HBM, HBM],
-        out_specs=[ANY] * members,
+        out_specs=[HBM] * members,
         scratch_shapes=[
             pltpu.VMEM((ARRIVE + 1, *pool.shape[1:]), pool.dtype),
             pltpu.VMEM(pool.shape, pool.dtype),
@@ -126,10 +126,16 @@
     )(place, in_hbm(pages), in_hbm(pool))
 
 
-def prepare_kernel(count, parts, place, lens, lens_wide, table, listed, *refs):
+def prepare_kernel(count, parts, groups, place, listed, lengths_hbm, table_hbm, *refs):
     sources = refs[:count]
-    held = refs[len(refs) - 5 - parts : -5]
-    bias, landing, whole, part, sems = refs[-5:]
+    held = refs[len(refs) - 8 - parts : -8]
+    bias, landing, entries, whole, part, lengths, table, sems = refs[-8:]
+    small = [
+        pltpu.make_async_copy(lengths_hbm, lengths, sems.at[parts]),
+        pltpu.make_async_copy(table_hbm, table, sems.at[parts + 1]),
+    ]
+    for copy in small:
+        copy.start()
     copies = []
     for source in sources:
         done = 0
@@ -143,7 +149,9 @@
             done += part_out.shape[0]
 
     member = place[0]
-    entry = listed[...]
+    entries[...] = jnp.full(entries.shape, -1, jnp.int32)
+    entries[:, : listed.shape[1]] = listed[...]
+    entry = entries[...]
     members, lanes = entry.shape
     per_peer = ARRIVE // members
     wanted = (entry >= 0) & ((entry >> 8) == member)
@@ -162,14 +170,21 @@
         found = jnp.where(column == c, slot, found)
     landing[...] = found
 
-    rows = bias.shape[0]
-    pages = table.shape[0]
+    for copy in small:
+        copy.wait()
+    rows, pages = table.shape
     wide = whole.shape[1]
+    base = lax.rem(member, groups) * rows
+    columns = table[...].T
     page_id = lax.broadcasted_iota(jnp.int32, (pages, wide), 0)
     slot_id = lax.broadcasted_iota(jnp.int32, (pages, wide), 1)
+    row_id = lax.broadcasted_iota(jnp.int32, (rows, 128), 0)
+    over = jnp.zeros((rows, 128), jnp.int32)
     for r in range(rows):
-        full = lens[r] // PAGE
-        hit = table[:, r : r + 1] == slot_id
+        length = lengths[base + r]
+        full = length // PAGE
+        over = jnp.where(row_id == r, length - full * PAGE, over)
+        hit = columns[:, r : r + 1] == slot_id
         in_whole = jnp.where(hit & (page_id < full), 1.0, 0.0)
         in_part = jnp.where(hit & (page_id == full), 1.0, 0.0)
         whole[r : r + 1, :] = jnp.sum(in_whole, axis=0, keepdims=True)
@@ -177,7 +192,7 @@
     whole_b = whole[...].astype(jnp.bfloat16)
     part_b = part[...].astype(jnp.bfloat16)
     lane = lax.broadcasted_iota(jnp.int32, (rows, 128), 1)
-    inside = (lane % PAGE) < (lens_wide[...] % PAGE)
+    inside = (lane % PAGE) < over
     per_block = 128 // PAGE
     slot_in = lax.broadcasted_iota(jnp.int32, (wide, 128), 0)
     lane_in = lax.broadcasted_iota(jnp.int32, (wide, 128), 1) // PAGE
@@ -191,46 +206,41 @@
         copy.wait()
 
 
-def prepare(place, lens, tables, listed, slots, weights, first):
-    rows, pages = tables.shape
-    members = listed.shape[0]
+def prepare(place, lengths, tables, listed, groups, weights, first):
+    rows = tables.shape[0]
+    members, slots = listed.shape
     wide = -(-slots // 128) * 128
     moved = sum(w.size * w.dtype.itemsize for w, _ in weights)
-    count = len(weights)
     pieces = [
         pltpu.VMEM((w.shape[0] // n, w.shape[1]), w.dtype) for w, n in weights for _ in range(n)
     ]
     weights = [w for w, _ in weights]
-    parts = len(pieces)
+    count, parts = len(weights), len(pieces)
     return pl.pallas_call(
-        functools.partial(prepare_kernel, count, parts),
+        functools.partial(prepare_kernel, count, parts, groups),
         out_shape=pieces
         + [
             jax.ShapeDtypeStruct((rows, slots * PAGE), jnp.float32),
             jax.ShapeDtypeStruct((members, 128), jnp.int32),
         ],
-        in_specs=[SM, SM, VM, VM, VM] + [HBM] * count + [ANY] * len(first),
+        in_specs=[SM, VM] + [HBM] * (2 + count + len(first)),
         out_specs=[VM] * (parts + 2),
         scratch_shapes=[
+            pltpu.VMEM((members, wide), jnp.int32),
             pltpu.VMEM((rows, wide), jnp.float32),
             pltpu.VMEM((rows, wide), jnp.float32),
-            pltpu.SemaphoreType.DMA((parts,)),
+            pltpu.SMEM(lengths.shape, lengths.dtype),
+            pltpu.VMEM(tables.shape, tables.dtype),
+            pltpu.SemaphoreType.DMA((parts + 2,)),
         ],
         compiler_params=pltpu.CompilerParams(vmem_limit_bytes=6 * MIB),
         cost_estimate=pl.CostEstimate(flops=0, bytes_accessed=moved, transcendentals=0),
         name="prepare",
-    )(
-        place,
-        lens,
-        jnp.broadcast_to(lens[:, None], (rows, 128)),
-        tables.T,
-        jnp.pad(listed, ((0, 0), (0, wide - slots)), constant_values=-1),
-        *[in_hbm(w) for w in weights],
-        *first,
-    )
-
-
-def attend_kernel(members, place, landing, old_pool, bias, query, new_k, new_v, *refs):
+    )(place, listed, *[in_hbm(x) for x in (lengths, tables, *weights, *first)])
+
+
+def attend_kernel(members, steps, place, landing, old_pool, bias, new_k, new_v, *refs):
+    asked, refs = refs[:steps], refs[steps:]
     arrived = refs[:members]
     kv_out, att_low, att_high = refs[members : members + 3]
     pool, scores, sems = refs[members + 3 :]
@@ -239,8 +249,7 @@
     resident = slots - ARRIVE
     per_peer = ARRIVE // members
     rows = bias.shape[0]
-    count = query.shape[0]
-    steps = count // (rows * GQ)
+    count = rows * steps * GQ
 
     @pl.when(half == 0)
     def _():
@@ -271,7 +280,9 @@
         copy_out.start()
 
         scale = 1.0 / math.sqrt(HD)
-        q = query[...]
+        q = jnp.concatenate(
+            [ask[:, j * HD : (j + 1) * HD] for j in range(GQ) for ask in asked], axis=0
+        )
         nt = (((1,), (1,)), ((), ()))
         group = 24
         width = group * PAGE
@@ -309,29 +320,29 @@
         copy_out.wait()
 
 
-def place_and_attend(place, landing, old_pool, bias, query, new_k, new_v, arrived):
+def place_and_attend(place, landing, old_pool, bias, new_k, new_v, asked, arrived):
     members = len(arrived)
     slots = old_pool.shape[0]
     rows = bias.shape[0]
-    count = query.shape[0]
-    tokens = count // GQ
+    steps = len(asked)
+    tokens = rows * steps
     return pl.pallas_call(
-        functools.partial(attend_kernel, members),
+        functools.partial(attend_kernel, members, steps),
         out_shape=[
             jax.ShapeDtypeStruct(old_pool.shape, old_pool.dtype),
             jax.ShapeDtypeStruct((tokens, GQ * HD // 2), jnp.bfloat16),
             jax.ShapeDtypeStruct((tokens, GQ * HD // 2), jnp.bfloat16),
         ],
-        in_specs=[SM, SM, HBM, VM, VM, VM, VM] + [VM] * members,
+        in_specs=[SM, SM, HBM, VM, VM, VM] + [VM] * (steps + members),
         out_specs=[HBM, VM, VM],
         scratch_shapes=[
             pltpu.VMEM(old_pool.shape, old_pool.dtype),
-            pltpu.VMEM((count, slots * PAGE), jnp.float32),
+            pltpu.VMEM((tokens * GQ, slots * PAGE), jnp.float32),
             pltpu.SemaphoreType.DMA((2,)),
         ],
         compiler_params=pltpu.CompilerParams(vmem_limit_bytes=9 * MIB),
         name="place_attend",
-    )(place, landing, in_hbm(old_pool), bias, query, new_k, new_v, *arrived)
+    )(place, landing, in_hbm(old_pool), bias, new_k, new_v, *asked, *arrived)
 
 
 def project_kernel(groups, place, weight, stream, mine, sibling, res_out):
@@ -365,16 +376,22 @@
 
 
 def ffn_kernel(place, mine, sibling, gain, *refs):
-    gate, up = refs[:SPLIT], refs[SPLIT : 2 * SPLIT]
-    down, own_out, other_out, *scratch = refs[2 * SPLIT :]
-    down_buf, normed, hidden, down_sem = scratch
+    gate = refs[:SPLIT]
+    up, down, own_out, other_out, *scratch = refs[SPLIT:]
+    up_buf, down_buf, normed, gated, hidden, up_sem, down_sem = scratch
     half = place[1]
     members, tokens, width = mine.shape
     depth, hidden_count = gate[0].shape
     features = depth * SPLIT
-    tile = min(256, hidden_count)
-    tiles = [slice(f * tile, (f + 1) * tile) for f in range(hidden_count // tile)]
-    down_copies = []
+    chunks = up_sem.shape[0]
+    step = features // chunks
+    up_copies, down_copies = [], []
+    for i in range(chunks):
+        window = pl.ds(i * step, step)
+        up_copies.append(
+            pltpu.make_async_copy(up.at[window], up_buf.at[window], up_sem.at[i])
+        )
+        up_copies[-1].start()
     for t in range(members):
         cols = pl.ds(t * 2 * width, 2 * width)
         down_copies.append(
@@ -392,16 +409,22 @@
         first = jnp.where(half == 0, mine[t], sibling[t])
         second = jnp.where(half == 0, sibling[t], mine[t])
         x = jnp.concatenate([first, second], axis=1).astype(jnp.float32)
-        n = x * factor * gain[t : t + 1, :]
-        normed[:, 2 * t * width : 2 * (t + 1) * width] = n.astype(jnp.bfloat16)
-    for cols in tiles:
-        gate_act = up_act = 0.0
+        cols = slice(2 * t * width, 2 * (t + 1) * width)
+        normed[:, cols] = (x * factor * gain[cols][None, :]).astype(jnp.bfloat16)
+    tile = min(256, hidden_count)
+    for f in range(hidden_count // tile):
+        cols = slice(f * tile, (f + 1) * tile)
+        act = 0.0
         for i in range(SPLIT):
             x = normed[:, i * depth : (i + 1) * depth]
-            gate_act += jnp.dot(x, gate[i][:, cols], preferred_element_type=jnp.float32)
-            up_act += jnp.dot(x, up[i][:, cols], preferred_element_type=jnp.float32)
-        h = gate_act / (1.0 + jnp.exp(-gate_act)) * up_act
-        hidden[:, cols] = h.astype(jnp.bfloat16)
+            act += jnp.dot(x, gate[i][:, cols], preferred_element_type=jnp.float32)
+        gated[:, cols] = act / (1.0 + jnp.exp(-act))
+    act = 0.0
+    for i in range(chunks):
+        up_copies[i].wait()
+        rows = slice(i * step, (i + 1) * step)
+        act += jnp.dot(normed[:, rows], up_buf[rows, :], preferred_element_type=jnp.float32)
+    hidden[...] = (gated[...] * act).astype(jnp.bfloat16)
     for t in range(members):
         down_copies[t].wait()
         part = jnp.dot(
@@ -415,26 +438,28 @@
 
 
 def feed_forward(place, mine, sibling, gain, gate, up, down):
-    members, tokens, width = mine.shape
-    blocks = 2 * members
-    hidden_count = gate[0].shape[1]
+    tokens = mine.shape[1]
+    features, hidden_count = up.shape
     return pl.pallas_call(
         ffn_kernel,
         out_shape=[
             jax.ShapeDtypeStruct(mine.shape, jnp.float32),
             jax.ShapeDtypeStruct(mine.shape, jnp.bfloat16),
         ],
-        in_specs=[SM, VM, VM, VM] + [VM] * (2 * SPLIT) + [HBM],
+        in_specs=[SM, VM, VM, VM] + [VM] * SPLIT + [HBM, HBM],
         out_specs=[VM, VM],
         scratch_shapes=[
+            pltpu.VMEM(up.shape, up.dtype),
             pltpu.VMEM(down.shape, down.dtype),
-            pltpu.VMEM((tokens, blocks * width), jnp.bfloat16),
+            pltpu.VMEM((tokens, features), jnp.bfloat16),
+            pltpu.VMEM((tokens, hidden_count), jnp.float32),
             pltpu.VMEM((tokens, hidden_count), jnp.bfloat16),
-            pltpu.SemaphoreType.DMA((members,)),
-        ],
-        compiler_params=pltpu.CompilerParams(vmem_limit_bytes=19 * MIB),
+            pltpu.SemaphoreType.DMA((8,)),
+            pltpu.SemaphoreType.DMA((mine.shape[0],)),
+        ],
+        compiler_params=pltpu.CompilerParams(vmem_limit_bytes=36 * MIB),
         name="feed_forward",
-    )(place, mine, sibling, gain, *map(in_vmem, gate), *map(in_vmem, up), in_hbm(down))
+    )(place, mine, sibling, gain, *map(in_vmem, gate), in_hbm(up), in_hbm(down))
 
 
 def local(
@@ -476,28 +501,26 @@
     for k in order[:5]:
         arrived[k] = ahead(outgoing[k], k, 0, 1)
 
-    row_lengths = lax.dynamic_slice_in_dim(lengths, member % groups * rows, rows)
-    query = queries.reshape(rows, steps, GQ, HD).transpose(2, 1, 0, 3).reshape(GQ * tokens, HD)
+    *held, bias, landing = prepare(
+        place,
+        lengths,
+        block_tables,
+        page_list.reshape(members, slots),
+        groups,
+        ((out_proj, 1), (gate_weight, SPLIT)),
+        (outgoing[0],),
+    )
+
+    rest, landing = lax.optimization_barrier(([outgoing[k] for k in order[5:]], landing))
+    for k, block in zip(order[5:], rest):
+        arrived[k] = ahead(block, k, 0, 1)
+
     padding = ((0, -tokens % 128), (0, 0))
     new_k = jnp.pad(fresh_kv[:, :, 0].reshape(tokens, HD), padding)
     new_v = jnp.pad(fresh_kv[:, :, 1].reshape(tokens, HD), padding)
-    gain = norm_gain.reshape(members, -1)
-    *held, bias, landing = prepare(
-        place,
-        row_lengths,
-        block_tables,
-        page_list.reshape(members, slots),
-        slots,
-        ((out_proj, 1), (gate_weight, SPLIT), (up_weight, SPLIT)),
-        (query, new_k, new_v, gain, outgoing[0]),
-    )
-
-    rest, landing = lax.optimization_barrier(([outgoing[k] for k in order[5:]], landing))
-    for k, block in zip(order[5:], rest):
-        arrived[k] = ahead(block, k, 0, 1)
-
+    asked = [queries[:, st] for st in range(steps)]
     kv_after, att_low, att_high = place_and_attend(
-        place, landing, kv_pages, bias, query, new_k, new_v, arrived
+        place, landing, kv_pages, bias, new_k, new_v, asked, arrived
     )
 
     def everywhere(x):
@@ -513,7 +536,7 @@
 
     mine, sibling = everywhere(residual)
     own, other = feed_forward(
-        place, mine, sibling, gain, held[1 : 1 + SPLIT], held[1 + SPLIT :], down_weight
+        place, mine, sibling, norm_gain, held[1:], up_weight, down_weight
     )
     summed = (own + swap(other).astype(jnp.float32)).astype(jnp.bfloat16)
     shares = lax.all_to_all(summed, "tp", split_axis=0, concat_axis=0)

time: 116 us -> 113 us (0.974)
  starting transfers between devices: 14 us -> 22 us
  local copies, waits for them, and re-layouts: 6.97 us -> 1.06 us
  waiting for transfers between devices: 15.4 us -> 9.96 us
  blocking collectives: 37.7 us -> 39.8 us
  Pallas kernels: 39.8 us -> 38.3 us
    ppermute x8, starting transfers between devices: 12.5 us -> 20.5 us  [ahead(): return lax.ppermute(x, BOTH, route)]
    pallas_call x2, Pallas kernels: 18.1 us -> 12.6 us  [the longest x1 8.76 us: prepare(): pl.pallas_call(functools.partial(prepare_kernel, count, parts, groups), o...]
    ppermute x1, waiting for transfers between devices: 7.14 us -> 1.8 us  [local(): att_mine = att_high + lax.ppermute(att_low, 'pd', [(1, 0)])]
    pallas_call x1, Pallas kernels: 13 us -> 16.8 us  [feed_forward(): pl.pallas_call(ffn_kernel, out_shape=[jax.ShapeDtypeStruct(mine.shape, jn...]
    unnamed x15 -> x16, local copies, waits for them, and re-layouts: 2.87 us -> 0.06 us
    all_to_all x2, blocking collectives: 25.1 us -> 27.2 us  [everywhere(): mine = lax.all_to_all(spread, 'tp', split_axis=0, concat_axis=0)]
    reshape x3 -> x0, local copies, waits for them, and re-layouts: 1.68 us -> none  [the longest x2 0.91 us: local(): queries.reshape(rows, steps, GQ, HD).transpose(2, 1, 0, 3)]
  transfers between devices with their start and end apart: 12 -> 12, of which waited for: 6 -> 5; matrix products, arithmetic and copies ran while one was open for 4% -> 1% of each run, Pallas kernels for 12% -> 8%
where the time goes in v4:
time: 113 us
  blocking collectives  39.8 us (35%)
  Pallas kernels  38.3 us (34%)
  starting transfers between devices  22 us (19%)
  waiting for transfers between devices  9.96 us (9%)
    all_to_all x2, blocking collectives, everywhere(): mine = lax.all_to_all(spread, 'tp', split_axis=0, concat_axis=0)  27.2 us
    ppermute x8, starting transfers between devices, ahead(): return lax.ppermute(x, BOTH, route)  20.5 us
    pallas_call x1, Pallas kernels, feed_forward(): pl.pallas_call(ffn_kernel, out_shape=[jax.ShapeDtypeStruct(mine.shape, jn...  16.8 us
    all_to_all x1, blocking collectives, local(): shares = lax.all_to_all(summed, 'tp', split_axis=0, concat_axis=0)  12.6 us
    pallas_call x1, Pallas kernels, prepare(): pl.pallas_call(functools.partial(prepare_kernel, count, parts, groups), o...  8.76 us
    pallas_call x1, Pallas kernels, pack(): pl.pallas_call(functools.partial(pack_kernel, members), out_shape=[shape]...  5.82 us
    ppermute x3, waiting for transfers between devices, swap(): return lax.ppermute(x, 'pd', [(0, 1), (1, 0)])  4.46 us
    pallas_call x1, Pallas kernels, place_and_attend(): pl.pallas_call(functools.partial(attend_kernel, members, steps), out_shap...  3.81 us
  transfers between devices with their start and end apart: 12, of which 5 were waited for; matrix products, arithmetic and copies ran while one was open for 1% of the time, Pallas kernels for 8%

profile of v4, /device:TPU:0, one launch (start us, length us, event | category | flops | bytes accessed | tf_op | source)
XLA Modules:
  0.0 112.9 jit_solution(9585329177596905875)
XLA Ops:
  0.6 0.1 pad_add_fusion.place
  0.7 5.8 %pack_pages.1 = (bf16[32,2,16,128]{3,2,1,0:T(8,128)(2,1)}, bf16[32,2,16,128]{3,2,1,0:T(8,128)(2,1)}, bf16[32,2,16,128]{3,2,1,0:T(8,128)(2,1)}, bf16[32,2,16,128]...) custom-call(s32[2]{0:T(128)S(1)} %pad_add_fusion.place, ...), custom_call_target="tpu_custom_call" | custom-call | tf_op jit(solution)/shard_map/pack_pages/pallas_call | solution.py:111
  6.5 1.3 %collective-permute-start.2 = (bf16[32,2,16,128]{3,2,1,0:T(8,128)(2,1)}, bf16[32,2,16,128]{3,2,1,0:T(8,128)(2,1)S(1)}, u32[]{:S(2)}, u32[]{:S(2)}) collective-permute-start(bf16[32,2,16,128]{3,2,1,0:T(8,128)(2,1)} %get-tuple-element.32), channel_id=1, source_target_pairs={{0,5},{2,7},{4,9},{6,11},{8,13},{10,15},{12,1},{14,3},{16,21},{18,... | collective-permute-start | bytes 786440 | tf_op jit(solution)/shard_map/ppermute | solution.py:493
  7.8 1.3 %collective-permute-start.3 = (bf16[32,2,16,128]{3,2,1,0:T(8,128)(2,1)}, bf16[32,2,16,128]{3,2,1,0:T(8,128)(2,1)S(1)}, u32[]{:S(2)}, u32[]{:S(2)}) collective-permute-start(bf16[32,2,16,128]{3,2,1,0:T(8,128)(2,1)} %get-tuple-element.33), channel_id=1, source_target_pairs={{0,7},{2,9},{4,11},{6,13},{8,15},{10,1},{12,3},{14,5},{16,23},{18,... | collective-permute-start | bytes 786440 | tf_op jit(solution)/shard_map/ppermute | solution.py:493
  9.2 1.3 %collective-permute-start.4 = (bf16[32,2,16,128]{3,2,1,0:T(8,128)(2,1)}, bf16[32,2,16,128]{3,2,1,0:T(8,128)(2,1)S(1)}, u32[]{:S(2)}, u32[]{:S(2)}) collective-permute-start(bf16[32,2,16,128]{3,2,1,0:T(8,128)(2,1)} %get-tuple-element.34), channel_id=1, source_target_pairs={{0,9},{2,11},{4,13},{6,15},{8,1},{10,3},{12,5},{14,7},{16,25},{18,... | collective-permute-start | bytes 786440 | tf_op jit(solution)/shard_map/ppermute | solution.py:493
  10.5 1.3 %collective-permute-start.5 = (bf16[32,2,16,128]{3,2,1,0:T(8,128)(2,1)}, bf16[32,2,16,128]{3,2,1,0:T(8,128)(2,1)S(1)}, u32[]{:S(2)}, u32[]{:S(2)}) collective-permute-start(bf16[32,2,16,128]{3,2,1,0:T(8,128)(2,1)} %get-tuple-element.35), channel_id=1, source_target_pairs={{0,11},{2,13},{4,15},{6,1},{8,3},{10,5},{12,7},{14,9},{16,27},{18,... | collective-permute-start | bytes 786440 | tf_op jit(solution)/shard_map/ppermute | solution.py:493
  11.8 1.3 %collective-permute-start.6 = (bf16[32,2,16,128]{3,2,1,0:T(8,128)(2,1)}, bf16[32,2,16,128]{3,2,1,0:T(8,128)(2,1)S(1)}, u32[]{:S(2)}, u32[]{:S(2)}) collective-permute-start(bf16[32,2,16,128]{3,2,1,0:T(8,128)(2,1)} %get-tuple-element.36), channel_id=1, source_target_pairs={{0,13},{2,15},{4,1},{6,3},{8,5},{10,7},{12,9},{14,11},{16,29},{18,... | collective-permute-start | bytes 786440 | tf_op jit(solution)/shard_map/ppermute | solution.py:493
  13.1 0.8 reshape.9.listed
  13.9 0.0 copy-start.3
  13.9 0.0 copy-start.2
  13.9 0.0 copy-start.4
  14.0 0.0 copy-start
  14.0 8.8 %prepare.1 = (bf16[512,8192]{1,0:T(8,128)(2,1)S(1)}, bf16[4096,1024]{1,0:T(8,128)(2,1)S(1)}, bf16[4096,1024]{1,0:T(8,128)(2,1)S(1)}, f32[16,4992]{1,0:T(8,128)S(1)}, s32[8,128]{1,0:T(8,128)S(1)}) custom-call(s32[2]{0:T(128)S(1)} %pad_add_fusion.place, s32[8,312]{1,0:T(8,128)S(1)} %reshape.9.listed, s32[16]{0:T(128)} %lengths_hbm.1, s32[16,128]{1,0:T(8,128)} %table_hbm.1, ...), custom_call_target="tpu_custom_call" | custom-call | bytes 25165824 | tf_op jit(solution)/shard_map/prepare/pallas_call | solution.py:219
  22.8 0.1 fusion
  22.9 1.3 %collective-permute-start = (bf16[32,2,16,128]{3,2,1,0:T(8,128)(2,1)S(1)}, bf16[32,2,16,128]{3,2,1,0:T(8,128)(2,1)S(1)}, u32[]{:S(2)}, u32[]{:S(2)}) collective-permute-start(bf16[32,2,16,128]{3,2,1,0:T(8,128)(2,1)S(1)} %copy-done.2), channel_id=1, source_target_pairs={{0,1},{2,3},{4,5},{6,7},{8,9},{10,11},{12,13},{14,15},{16,17},{18,... | collective-permute-start | bytes 786440 | tf_op jit(solution)/shard_map/ppermute | solution.py:493
  24.2 1.3 %collective-permute-start.1 = (bf16[32,2,16,128]{3,2,1,0:T(8,128)(2,1)S(1)}, bf16[32,2,16,128]{3,2,1,0:T(8,128)(2,1)S(1)}, u32[]{:S(2)}, u32[]{:S(2)}) collective-permute-start(bf16[32,2,16,128]{3,2,1,0:T(8,128)(2,1)S(1)} %copy-done.6), channel_id=1, source_target_pairs={{0,3},{2,5},{4,7},{6,9},{8,11},{10,13},{12,15},{14,1},{16,19},{18,... | collective-permute-start | bytes 786440 | tf_op jit(solution)/shard_map/ppermute | solution.py:493
  25.5 11.4 %collective-permute-start.7 = (bf16[32,2,16,128]{3,2,1,0:T(8,128)(2,1)S(1)}, bf16[32,2,16,128]{3,2,1,0:T(8,128)(2,1)S(1)}, u32[]{:S(2)}, u32[]{:S(2)}) collective-permute-start(bf16[32,2,16,128]{3,2,1,0:T(8,128)(2,1)S(1)} %copy-done.5), channel_id=1, source_target_pairs={{0,15},{2,1},{4,3},{6,5},{8,7},{10,9},{12,11},{14,13},{16,31},{18,... | collective-permute-start | bytes 786440 | tf_op jit(solution)/shard_map/ppermute | solution.py:493
  37.1 3.7 %collective-permute-done.7.refs_9_ = bf16[32,2,16,128]{3,2,1,0:T(8,128)(2,1)S(1)} collective-permute-done((bf16[32,2,16,128]{3,2,1,0:T(8,128)(2,1)S(1)}, bf16[32,2,16,128]{3,2,1,0:T(8,128)(2,1)S(1)}, u32[]{:S(2)}, u32[]{:S(2)}) %collective-permute-start.7) | collective-permute-done | bytes 262176 | tf_op jit(solution)/shard_map/ppermute | solution.py:493
  40.8 3.8 %place_attend.1 = (bf16[312,2,16,128]{3,2,1,0:T(8,128)(2,1)}, bf16[32,512]{1,0:T(8,128)(2,1)S(1)}, bf16[32,512]{1,0:T(8,128)(2,1)S(1)}) custom-call(s32[2]{0:T(128)S(1)} %pad_add_fusion.place, s32[8,128]{1,0:T(8,128)S(1)} %get-tuple-element.28.landing, bf16[312,2,16,128]{3,2,1,0:T(8,128)(2,1)} %old_pool.1, f32[16,4992]{1,0:T(8,128)S(1)} %get-tuple-element.29.bias, ...), custom_call_target="tpu_custom_call" | custom-call | tf_op jit(solution)/shard_map/place_attend/pallas_call | solution.py:329
  44.6 1.3 %collective-permute-start.8 = (bf16[32,512]{1,0:T(8,128)(2,1)S(1)}, bf16[32,512]{1,0:T(8,128)(2,1)S(1)}, u32[]{:S(2)}, u32[]{:S(2)}) collective-permute-start(bf16[32,512]{1,0:T(8,128)(2,1)S(1)} %get-tuple-element.41), channel_id=1, source_target_pairs={{1,0},{3,2},{5,4},{7,6},{9,8},{11,10},{13,12},{15,14},{17,16},{19,... | collective-permute-start | bytes 98312 | tf_op jit(solution)/shard_map/ppermute | solution.py:531
  45.9 1.8 %collective-permute-done.8 = bf16[32,512]{1,0:T(8,128)(2,1)S(1)} collective-permute-done((bf16[32,512]{1,0:T(8,128)(2,1)S(1)}, bf16[32,512]{1,0:T(8,128)(2,1)S(1)}, u32[]{:S(2)}, u32[]{:S(2)}) %collective-permute-start.8) | collective-permute-done | bytes 32800 | tf_op jit(solution)/shard_map/ppermute | solution.py:531
  47.7 14.6 %all_to_all.15.mine = bf16[8,32,512]{2,1,0:T(8,128)(2,1)S(1)} all-to-all(bf16[8,32,512]{2,1,0:T(8,128)(2,1)S(1)} %broadcast_in_dim.4), channel_id=1, replica_groups=mesh['grp'=2,'tp'=8,'pd'=2] {'tp'}, dimensions={0} | all-to-all | bytes 524288 | tf_op jit(solution)/shard_map/all_to_all | solution.py:528
  62.3 1.5 %collective-permute-done.9.sibling = bf16[8,32,512]{2,1,0:T(8,128)(2,1)S(1)} collective-permute-done((bf16[8,32,512]{2,1,0:T(8,128)(2,1)S(1)}, bf16[8,32,512]{2,1,0:T(8,128)(2,1)S(1)}, u32[]{:S(2)}, u32[]{:S(2)}) %collective-permute-start.9) | collective-permute-done | bytes 262176 | tf_op jit(solution)/shard_map/ppermute | solution.py:496
  63.8 3.1 %out_projection.1 = bf16[32,512]{1,0:T(8,128)(2,1)S(1)} custom-call(s32[2]{0:T(128)S(1)} %pad_add_fusion.place, bf16[512,8192]{1,0:T(8,128)(2,1)S(1)} %get-tuple-element.39.weight, bf16[32,512]{1,0:T(8,128)(2,1)S(1)} %copy-done, bf16[8,32,512]{2,1,0:T(8,128)(2,1)S(1)} %all_to_all.15.mine, bf16[8,32,512]{2,1,0:T(8,128)(2,1)S(1)} %collective-permute-done.9.sibling), custom_call_target="tpu_custom_call" | custom-call | tf_op jit(solution)/shard_map/out_projection/pallas_call | solution.py:368
  67.0 12.6 %all_to_all.16.mine = bf16[8,32,512]{2,1,0:T(8,128)(2,1)S(1)} all-to-all(bf16[8,32,512]{2,1,0:T(8,128)(2,1)S(1)} %broadcast_in_dim.5), channel_id=1, replica_groups=mesh['grp'=2,'tp'=8,'pd'=2] {'tp'}, dimensions={0} | all-to-all | bytes 524288 | tf_op jit(solution)/shard_map/all_to_all | solution.py:528
  79.6 1.5 %collective-permute-done.10.sibling = bf16[8,32,512]{2,1,0:T(8,128)(2,1)S(1)} collective-permute-done((bf16[8,32,512]{2,1,0:T(8,128)(2,1)S(1)}, bf16[8,32,512]{2,1,0:T(8,128)(2,1)S(1)}, u32[]{:S(2)}, u32[]{:S(2)}) %collective-permute-start.10) | collective-permute-done | bytes 262176 | tf_op jit(solution)/shard_map/ppermute | solution.py:496
  81.1 16.8 %feed_forward.1 = (f32[8,32,512]{2,1,0:T(8,128)S(1)}, bf16[8,32,512]{2,1,0:T(8,128)(2,1)S(1)}) custom-call(s32[2]{0:T(128)S(1)} %pad_add_fusion.place, bf16[8,32,512]{2,1,0:T(8,128)(2,1)S(1)} %all_to_all.16.mine, bf16[8,32,512]{2,1,0:T(8,128)(2,1)S(1)} %collective-permute-done.10.sibling, f32[8192]{0:T(1024)S(1)} %copy-done.1, ...), custom_call_target="tpu_custom_call" | custom-call | tf_op jit(solution)/shard_map/feed_forward/pallas_call | solution.py:443
  97.9 0.2 collective-permute-start.11
  98.1 1.4 %collective-permute-done.11 = bf16[8,32,512]{2,1,0:T(8,128)(2,1)S(1)} collective-permute-done((bf16[8,32,512]{2,1,0:T(8,128)(2,1)S(1)}, bf16[8,32,512]{2,1,0:T(8,128)(2,1)S(1)}, u32[]{:S(2)}, u32[]{:S(2)}) %collective-permute-start.11) | collective-permute-done | bytes 262176 | tf_op jit(solution)/shard_map/ppermute | solution.py:496
  99.5 0.1 add_convert_fusion
  99.6 12.6 %all_to_all.17 = bf16[8,32,512]{2,1,0:T(8,128)(2,1)S(1)} all-to-all(bf16[8,32,512]{2,1,0:T(8,128)(2,1)S(1)} %add_convert_fusion), channel_id=1, replica_groups=mesh['grp'=2,'tp'=8,'pd'=2] {'tp'}, dimensions={0} | all-to-all | bytes 524288 | tf_op jit(solution)/shard_map/all_to_all | solution.py:542
  112.3 0.6 add_convert_fusion.1
  (29 shorter events, 0.2 us)
Async XLA Ops:
  6.5 16.3 %collective-permute-start.2 = (bf16[32,2,16,128]{3,2,1,0:T(8,128)(2,1)}, bf16[32,2,16,128]{3,2,1,0:T(8,128)(2,1)S(1)}, u32[]{:S(2)}, u32[]{:S(2)}) collective-permute-start(bf16[32,2,16,128]{3,2,1,0:T(8,128)(2,1)} %get-tuple-element.32), channel_id=1, source_target_pairs={{0,5},{2,7},{4,9},{6,11},{8,13},{10,15},{12,1},{14,3},{16,21},{18,... | collective-permute-start | bytes 786440 | tf_op jit(solution)/shard_map/ppermute | solution.py:493
  7.8 16.3 %collective-permute-start.3 = (bf16[32,2,16,128]{3,2,1,0:T(8,128)(2,1)}, bf16[32,2,16,128]{3,2,1,0:T(8,128)(2,1)S(1)}, u32[]{:S(2)}, u32[]{:S(2)}) collective-permute-start(bf16[32,2,16,128]{3,2,1,0:T(8,128)(2,1)} %get-tuple-element.33), channel_id=1, source_target_pairs={{0,7},{2,9},{4,11},{6,13},{8,15},{10,1},{12,3},{14,5},{16,23},{18,... | collective-permute-start | bytes 786440 | tf_op jit(solution)/shard_map/ppermute | solution.py:493
  9.2 16.4 %collective-permute-start.4 = (bf16[32,2,16,128]{3,2,1,0:T(8,128)(2,1)}, bf16[32,2,16,128]{3,2,1,0:T(8,128)(2,1)S(1)}, u32[]{:S(2)}, u32[]{:S(2)}) collective-permute-start(bf16[32,2,16,128]{3,2,1,0:T(8,128)(2,1)} %get-tuple-element.34), channel_id=1, source_target_pairs={{0,9},{2,11},{4,13},{6,15},{8,1},{10,3},{12,5},{14,7},{16,25},{18,... | collective-permute-start | bytes 786440 | tf_op jit(solution)/shard_map/ppermute | solution.py:493
  10.5 26.6 %collective-permute-start.5 = (bf16[32,2,16,128]{3,2,1,0:T(8,128)(2,1)}, bf16[32,2,16,128]{3,2,1,0:T(8,128)(2,1)S(1)}, u32[]{:S(2)}, u32[]{:S(2)}) collective-permute-start(bf16[32,2,16,128]{3,2,1,0:T(8,128)(2,1)} %get-tuple-element.35), channel_id=1, source_target_pairs={{0,11},{2,13},{4,15},{6,1},{8,3},{10,5},{12,7},{14,9},{16,27},{18,... | collective-permute-start | bytes 786440 | tf_op jit(solution)/shard_map/ppermute | solution.py:493
  11.8 25.3 %collective-permute-start.6 = (bf16[32,2,16,128]{3,2,1,0:T(8,128)(2,1)}, bf16[32,2,16,128]{3,2,1,0:T(8,128)(2,1)S(1)}, u32[]{:S(2)}, u32[]{:S(2)}) collective-permute-start(bf16[32,2,16,128]{3,2,1,0:T(8,128)(2,1)} %get-tuple-element.36), channel_id=1, source_target_pairs={{0,13},{2,15},{4,1},{6,3},{8,5},{10,7},{12,9},{14,11},{16,29},{18,... | collective-permute-start | bytes 786440 | tf_op jit(solution)/shard_map/ppermute | solution.py:493
  13.9 8.9 %copy-start.3 = (bf16[16,2,1024]{2,1,0:T(2,128)(2,1)S(1)}, bf16[16,2,1024]{2,1,0:T(2,128)(2,1)}, u32[]{:S(2)}) copy-start(bf16[16,2,1024]{2,1,0:T(2,128)(2,1)} %param.16) | copy-start | bytes 196612
  13.9 9.0 %copy-start.2 = (bf16[32,2,16,128]{3,2,1,0:T(8,128)(2,1)S(1)}, bf16[32,2,16,128]{3,2,1,0:T(8,128)(2,1)}, u32[]{:S(2)}) copy-start(bf16[32,2,16,128]{3,2,1,0:T(8,128)(2,1)} %get-tuple-element.30.refs_2_) | copy-start | bytes 786436
  13.9 10.3 %copy-start.6 = (bf16[32,2,16,128]{3,2,1,0:T(8,128)(2,1)S(1)}, bf16[32,2,16,128]{3,2,1,0:T(8,128)(2,1)}, u32[]{:S(2)}) copy-start(bf16[32,2,16,128]{3,2,1,0:T(8,128)(2,1)} %get-tuple-element.31) | copy-start | bytes 786436
  13.9 11.6 %copy-start.5 = (bf16[32,2,16,128]{3,2,1,0:T(8,128)(2,1)S(1)}, bf16[32,2,16,128]{3,2,1,0:T(8,128)(2,1)}, u32[]{:S(2)}) copy-start(bf16[32,2,16,128]{3,2,1,0:T(8,128)(2,1)} %get-tuple-element.37) | copy-start | bytes 786436
  13.9 23.0 %copy-start.4 = (bf16[16,2,2,128]{3,2,1,0:T(2,128)(2,1)S(1)}, bf16[16,2,2,128]{3,2,1,0:T(2,128)(2,1)}, u32[]{:S(2)}) copy-start(bf16[16,2,2,128]{3,2,1,0:T(2,128)(2,1)} %param.17) | copy-start | bytes 49156
  14.0 49.9 %copy-start = (bf16[32,512]{1,0:T(8,128)(2,1)S(1)}, bf16[32,512]{1,0:T(8,128)(2,1)}, u32[]{:S(2)}) copy-start(bf16[32,512]{1,0:T(8,128)(2,1)} %stream.1) | copy-start | bytes 98308
  22.7 58.4 %copy-start.1 = (f32[8192]{0:T(1024)S(1)}, f32[8192]{0:T(1024)}, u32[]{:S(2)}) copy-start(f32[8192]{0:T(1024)} %gain.1) | copy-start | bytes 98308
  22.9 14.2 %collective-permute-start = (bf16[32,2,16,128]{3,2,1,0:T(8,128)(2,1)S(1)}, bf16[32,2,16,128]{3,2,1,0:T(8,128)(2,1)S(1)}, u32[]{:S(2)}, u32[]{:S(2)}) collective-permute-start(bf16[32,2,16,128]{3,2,1,0:T(8,128)(2,1)S(1)} %copy-done.2), channel_id=1, source_target_pairs={{0,1},{2,3},{4,5},{6,7},{8,9},{10,11},{12,13},{14,15},{16,17},{18,... | collective-permute-start | bytes 786440 | tf_op jit(solution)/shard_map/ppermute | solution.py:493
  24.2 12.9 %collective-permute-start.1 = (bf16[32,2,16,128]{3,2,1,0:T(8,128)(2,1)S(1)}, bf16[32,2,16,128]{3,2,1,0:T(8,128)(2,1)S(1)}, u32[]{:S(2)}, u32[]{:S(2)}) collective-permute-start(bf16[32,2,16,128]{3,2,1,0:T(8,128)(2,1)S(1)} %copy-done.6), channel_id=1, source_target_pairs={{0,3},{2,5},{4,7},{6,9},{8,11},{10,13},{12,15},{14,1},{16,19},{18,... | collective-permute-start | bytes 786440 | tf_op jit(solution)/shard_map/ppermute | solution.py:493
  25.5 15.2 %collective-permute-start.7 = (bf16[32,2,16,128]{3,2,1,0:T(8,128)(2,1)S(1)}, bf16[32,2,16,128]{3,2,1,0:T(8,128)(2,1)S(1)}, u32[]{:S(2)}, u32[]{:S(2)}) collective-permute-start(bf16[32,2,16,128]{3,2,1,0:T(8,128)(2,1)S(1)} %copy-done.5), channel_id=1, source_target_pairs={{0,15},{2,1},{4,3},{6,5},{8,7},{10,9},{12,11},{14,13},{16,31},{18,... | collective-permute-start | bytes 786440 | tf_op jit(solution)/shard_map/ppermute | solution.py:493
  44.6 3.1 %collective-permute-start.8 = (bf16[32,512]{1,0:T(8,128)(2,1)S(1)}, bf16[32,512]{1,0:T(8,128)(2,1)S(1)}, u32[]{:S(2)}, u32[]{:S(2)}) collective-permute-start(bf16[32,512]{1,0:T(8,128)(2,1)S(1)} %get-tuple-element.41), channel_id=1, source_target_pairs={{1,0},{3,2},{5,4},{7,6},{9,8},{11,10},{13,12},{15,14},{17,16},{19,... | collective-permute-start | bytes 98312 | tf_op jit(solution)/shard_map/ppermute | solution.py:531
  62.3 1.5 %collective-permute-start.9 = (bf16[8,32,512]{2,1,0:T(8,128)(2,1)S(1)}, bf16[8,32,512]{2,1,0:T(8,128)(2,1)S(1)}, u32[]{:S(2)}, u32[]{:S(2)}) collective-permute-start(bf16[8,32,512]{2,1,0:T(8,128)(2,1)S(1)} %all_to_all.15.mine), channel_id=1, source_target_pairs={{0,1},{1,0},{2,3},{3,2},{4,5},{5,4},{6,7},{7,6},{8,9},{9,8},{10,11... | collective-permute-start | bytes 786440 | tf_op jit(solution)/shard_map/ppermute | solution.py:496
  79.6 1.5 %collective-permute-start.10 = (bf16[8,32,512]{2,1,0:T(8,128)(2,1)S(1)}, bf16[8,32,512]{2,1,0:T(8,128)(2,1)S(1)}, u32[]{:S(2)}, u32[]{:S(2)}) collective-permute-start(bf16[8,32,512]{2,1,0:T(8,128)(2,1)S(1)} %all_to_all.16.mine), channel_id=1, source_target_pairs={{0,1},{1,0},{2,3},{3,2},{4,5},{5,4},{6,7},{7,6},{8,9},{9,8},{10,11... | collective-permute-start | bytes 786440 | tf_op jit(solution)/shard_map/ppermute | solution.py:496
  97.9 1.6 %collective-permute-start.11 = (bf16[8,32,512]{2,1,0:T(8,128)(2,1)S(1)}, bf16[8,32,512]{2,1,0:T(8,128)(2,1)S(1)}, u32[]{:S(2)}, u32[]{:S(2)}) collective-permute-start(bf16[8,32,512]{2,1,0:T(8,128)(2,1)S(1)} %get-tuple-element.45), channel_id=1, source_target_pairs={{0,1},{1,0},{2,3},{3,2},{4,5},{5,4},{6,7},{7,6},{8,9},{9,8},{10,11... | collective-permute-start | bytes 786440 | tf_op jit(solution)/shard_map/ppermute | solution.py:496

commit v5 on v4

--- a/solution.py
+++ b/solution.py
@@ -34,8 +34,9 @@
 
 
 def pack_kernel(members, place, pages, pool, *refs):
-    outs = refs[:members]
-    packed, held, own, counts, sems, load_sems = refs[members:]
+    count = members - 1
+    outs, kept = refs[:count], refs[count]
+    packed, held, own, counts, sems, load_sems, keep_sems = refs[count + 1 :]
     member, half = place[0], place[1]
     slots = pool.shape[0]
     per_peer = ARRIVE // members
@@ -46,12 +47,15 @@
     def _():
         own_copy = pltpu.make_async_copy(pages, own, load_sems.at[parts])
         own_copy.start()
-        loads = []
+        loads, keeps = [], []
         for i in range(parts):
             window = pl.ds(i * step, step)
             loads.append(
                 pltpu.make_async_copy(pool.at[window], held.at[window], load_sems.at[i])
             )
+            keeps.append(
+                pltpu.make_async_copy(held.at[window], kept.at[window], keep_sems.at[i])
+            )
             loads[-1].start()
         own_copy.wait()
         start = member * slots
@@ -64,7 +68,7 @@
                 def body(j, words, base=i * step):
                     low, high = words
                     entry = own[start + base + j]
-                    ahead = lax.rem((entry >> 8) - member + members, members)
+                    ahead = lax.rem((entry >> 8) - member + members + 1, members)
                     leaves = entry >= 0
                     shift = (ahead & 3) * 8
                     is_low = ahead < 4
@@ -88,38 +92,50 @@
             @pl.loop(0, slots)
             def _(i):
                 entry = own[start + i]
-                ahead = lax.rem((entry >> 8) - member + members, members)
+                ahead = lax.rem((entry >> 8) - member + members + 1, members)
                 row = jnp.where(entry >= 0, ahead, members)
                 count = counts[row]
                 counts[row] = count + 1
                 packed[jnp.where(entry >= 0, row * per_peer + count, ARRIVE)] = held[i]
 
-        copies = [
-            pltpu.make_async_copy(packed.at[pl.ds(k * per_peer, per_peer)], outs[k], sems.at[k])
-            for k in range(members)
-        ]
-        for copy in copies:
-            copy.start()
-        for copy in copies:
+        copies = []
+        near, own_chunk, *far = outs
+        moves = [(near, 0, 0), (near, per_peer, 2), (own_chunk, 0, 1)]
+        moves += [(out, 0, 3 + i) for i, out in enumerate(far)]
+        for i, (out, first, row) in enumerate(moves):
+            copies.append(
+                pltpu.make_async_copy(
+                    packed.at[pl.ds(row * per_peer, per_peer)],
+                    out.at[pl.ds(first, per_peer)],
+                    sems.at[i],
+                )
+            )
+            copies[-1].start()
+        for keep in keeps:
+            keep.start()
+        for copy in copies + keeps:
             copy.wait()
 
 
 def pack(place, pages, pool):
     members = lax.axis_size("tp")
     per_peer = ARRIVE // members
-    shape = pltpu.HBM((per_peer, *pool.shape[1:]), pool.dtype)
+    chunk = pool.shape[1:]
     return pl.pallas_call(
         functools.partial(pack_kernel, members),
-        out_shape=[shape] * members,
+        out_shape=[pltpu.HBM((2 * per_peer, *chunk), pool.dtype)]
+        + [pltpu.HBM((per_peer, *chunk), pool.dtype)] * (members - 2)
+        + [pltpu.HBM(pool.shape, pool.dtype)],
         in_specs=[SM, HBM, HBM],
         out_specs=[HBM] * members,
         scratch_shapes=[
-            pltpu.VMEM((ARRIVE + 1, *pool.shape[1:]), pool.dtype),
+            pltpu.VMEM((ARRIVE + 1, *chunk), pool.dtype),
             pltpu.VMEM(pool.shape, pool.dtype),
             pltpu.SMEM(pages.shape, jnp.int32),
             pltpu.SMEM((members + 1,), jnp.int32),
             pltpu.SemaphoreType.DMA((members,)),
             pltpu.SemaphoreType.DMA((5,)),
+            pltpu.SemaphoreType.DMA((4,)),
         ],
         compiler_params=pltpu.CompilerParams(vmem_limit_bytes=8 * MIB),
         name="pack_pages",
@@ -239,11 +255,10 @@
     )(place, listed, *[in_hbm(x) for x in (lengths, tables, *weights, *first)])
 
 
-def attend_kernel(members, steps, place, landing, old_pool, bias, new_k, new_v, *refs):
+def attend_kernel(members, steps, chunks, place, landing, old_pool, _, bias, new_k, new_v, *refs):
     asked, refs = refs[:steps], refs[steps:]
-    arrived = refs[:members]
-    kv_out, att_low, att_high = refs[members : members + 3]
-    pool, scores, sems = refs[members + 3 :]
+    arrived, refs = refs[:-6], refs[-6:]
+    kv_out, att_low, att_high, pool, scores, sems = refs
     member, half = place[0], place[1]
     slots = pool.shape[0]
     resident = slots - ARRIVE
@@ -253,14 +268,8 @@
 
     @pl.when(half == 0)
     def _():
-        copy = pltpu.make_async_copy(old_pool, pool, sems.at[0])
-        copy.start()
         att_low[...] = jnp.zeros_like(att_low)
         att_high[...] = jnp.zeros_like(att_high)
-        copy.wait()
-        copy_out = pltpu.make_async_copy(pool, kv_out, sems.at[1])
-        copy_out.start()
-        copy_out.wait()
 
     @pl.when(half == 1)
     def _():
@@ -268,12 +277,12 @@
             old_pool.at[pl.ds(0, resident)], pool.at[pl.ds(0, resident)], sems.at[0]
         )
         copy.start()
-        for k in range(members):
+        for i, first, k in chunks:
             source = lax.rem(member - k + members, members)
 
             @pl.loop(0, per_peer, unroll=math.gcd(per_peer, 8))
             def _(c):
-                pool[resident + landing[source, c]] = arrived[k][c]
+                pool[resident + landing[source, c]] = arrived[i][first + c]
 
         copy.wait()
         copy_out = pltpu.make_async_copy(pool, kv_out, sems.at[1])
@@ -320,20 +329,20 @@
         copy_out.wait()
 
 
-def place_and_attend(place, landing, old_pool, bias, new_k, new_v, asked, arrived):
-    members = len(arrived)
+def place_and_attend(place, landing, old_pool, kept, bias, new_k, new_v, asked, arrived, chunks):
+    members = landing.shape[0]
     slots = old_pool.shape[0]
     rows = bias.shape[0]
     steps = len(asked)
     tokens = rows * steps
     return pl.pallas_call(
-        functools.partial(attend_kernel, members, steps),
+        functools.partial(attend_kernel, members, steps, chunks),
         out_shape=[
             jax.ShapeDtypeStruct(old_pool.shape, old_pool.dtype),
             jax.ShapeDtypeStruct((tokens, GQ * HD // 2), jnp.bfloat16),
             jax.ShapeDtypeStruct((tokens, GQ * HD // 2), jnp.bfloat16),
         ],
-        in_specs=[SM, SM, HBM, VM, VM, VM] + [VM] * (steps + members),
+        in_specs=[SM, SM, HBM, HBM, VM, VM, VM] + [VM] * (steps + len(arrived)),
         out_specs=[HBM, VM, VM],
         scratch_shapes=[
             pltpu.VMEM(old_pool.shape, old_pool.dtype),
@@ -341,8 +350,19 @@
             pltpu.SemaphoreType.DMA((2,)),
         ],
         compiler_params=pltpu.CompilerParams(vmem_limit_bytes=9 * MIB),
+        input_output_aliases={3: 0},
         name="place_attend",
-    )(place, landing, in_hbm(old_pool), bias, new_k, new_v, *asked, *arrived)
+    )(
+        place,
+        landing,
+        in_hbm(old_pool),
+        in_hbm(kept),
+        bias,
+        new_k,
+        new_v,
+        *asked,
+        *arrived,
+    )
 
 
 def project_kernel(groups, place, weight, stream, mine, sibling, res_out):
@@ -376,22 +396,13 @@
 
 
 def ffn_kernel(place, mine, sibling, gain, *refs):
-    gate = refs[:SPLIT]
-    up, down, own_out, other_out, *scratch = refs[SPLIT:]
-    up_buf, down_buf, normed, gated, hidden, up_sem, down_sem = scratch
+    gate, up = refs[:SPLIT], refs[SPLIT : 2 * SPLIT]
+    down, own_out, other_out, down_buf, normed, hidden, down_sem = refs[2 * SPLIT :]
     half = place[1]
     members, tokens, width = mine.shape
     depth, hidden_count = gate[0].shape
     features = depth * SPLIT
-    chunks = up_sem.shape[0]
-    step = features // chunks
-    up_copies, down_copies = [], []
-    for i in range(chunks):
-        window = pl.ds(i * step, step)
-        up_copies.append(
-            pltpu.make_async_copy(up.at[window], up_buf.at[window], up_sem.at[i])
-        )
-        up_copies[-1].start()
+    down_copies = []
     for t in range(members):
         cols = pl.ds(t * 2 * width, 2 * width)
         down_copies.append(
@@ -414,17 +425,13 @@
     tile = min(256, hidden_count)
     for f in range(hidden_count // tile):
         cols = slice(f * tile, (f + 1) * tile)
-        act = 0.0
+        gate_act = up_act = 0.0
         for i in range(SPLIT):
             x = normed[:, i * depth : (i + 1) * depth]
-            act += jnp.dot(x, gate[i][:, cols], preferred_element_type=jnp.float32)
-        gated[:, cols] = act / (1.0 + jnp.exp(-act))
-    act = 0.0
-    for i in range(chunks):
-        up_copies[i].wait()
-        rows = slice(i * step, (i + 1) * step)
-        act += jnp.dot(normed[:, rows], up_buf[rows, :], preferred_element_type=jnp.float32)
-    hidden[...] = (gated[...] * act).astype(jnp.bfloat16)
+            gate_act += jnp.dot(x, gate[i][:, cols], preferred_element_type=jnp.float32)
+            up_act += jnp.dot(x, up[i][:, cols], preferred_element_type=jnp.float32)
+        h = gate_act / (1.0 + jnp.exp(-gate_act)) * up_act
+        hidden[:, cols] = h.astype(jnp.bfloat16)
     for t in range(members):
         down_copies[t].wait()
         part = jnp.dot(
@@ -439,27 +446,24 @@
 
 def feed_forward(place, mine, sibling, gain, gate, up, down):
     tokens = mine.shape[1]
-    features, hidden_count = up.shape
+    hidden_count, features = down.shape
     return pl.pallas_call(
         ffn_kernel,
         out_shape=[
             jax.ShapeDtypeStruct(mine.shape, jnp.float32),
             jax.ShapeDtypeStruct(mine.shape, jnp.bfloat16),
         ],
-        in_specs=[SM, VM, VM, VM] + [VM] * SPLIT + [HBM, HBM],
+        in_specs=[SM, VM, VM, VM] + [VM] * (2 * SPLIT) + [HBM],
         out_specs=[VM, VM],
         scratch_shapes=[
-            pltpu.VMEM(up.shape, up.dtype),
             pltpu.VMEM(down.shape, down.dtype),
             pltpu.VMEM((tokens, features), jnp.bfloat16),
-            pltpu.VMEM((tokens, hidden_count), jnp.float32),
             pltpu.VMEM((tokens, hidden_count), jnp.bfloat16),
-            pltpu.SemaphoreType.DMA((8,)),
             pltpu.SemaphoreType.DMA((mine.shape[0],)),
         ],
-        compiler_params=pltpu.CompilerParams(vmem_limit_bytes=36 * MIB),
+        compiler_params=pltpu.CompilerParams(vmem_limit_bytes=19 * MIB),
         name="feed_forward",
-    )(place, mine, sibling, gain, *map(in_vmem, gate), in_hbm(up), in_hbm(down))
+    )(place, mine, sibling, gain, *map(in_vmem, (*gate, *up)), in_hbm(down))
 
 
 def local(
@@ -481,25 +485,33 @@
     half = lax.axis_index("pd")
     place = jnp.stack([member, half]).astype(jnp.int32)
     slots = kv_pages.shape[0]
+    per_peer = ARRIVE // members
     groups = members // KVH
     rows = block_tables.shape[0]
     steps = queries.shape[1]
     tokens = rows * steps
 
-    def ahead(x, k, from_half, to_half):
+    def send(x, *hops):
         route = [
-            (2 * t + from_half, 2 * ((t + k) % members) + to_half) for t in range(members)
+            (2 * t + start, 2 * ((t + k) % members) + end)
+            for start, k, end in hops
+            for t in range(members)
         ]
         return lax.ppermute(x, BOTH, route)
 
     def swap(x):
         return lax.ppermute(x, "pd", [(0, 1), (1, 0)])
 
-    outgoing = pack(place, page_list, kv_pages)
-    order = sorted(range(members), key=lambda k: abs(k - members // 2))
-    arrived = [None] * members
-    for k in order[:5]:
-        arrived[k] = ahead(outgoing[k], k, 0, 1)
+    near, own_chunk, *far, kept = pack(place, page_list, kv_pages)
+    far = dict(zip(range(2, members - 1), far))
+    crossed = lax.ppermute(near, "pd", [(0, 1)])
+    behind, ahead = crossed[:per_peer], crossed[per_peer:]
+    hosts = (2, members - 2)
+    middle = sorted(set(far) - set(hosts), key=lambda k: abs(k - members // 2))
+    arrived = {k: send(far[k], (0, k, 1)) for k in middle}
+    for host, k, block in zip(hosts, (1, -1), (ahead, behind)):
+        block = jnp.where(half == 0, far[host], block)
+        arrived[host] = send(block, (0, host, 1), (1, k, 0))
 
     *held, bias, landing = prepare(
         place,
@@ -507,20 +519,23 @@
         block_tables,
         page_list.reshape(members, slots),
         groups,
-        ((out_proj, 1), (gate_weight, SPLIT)),
-        (outgoing[0],),
-    )
-
-    rest, landing = lax.optimization_barrier(([outgoing[k] for k in order[5:]], landing))
-    for k, block in zip(order[5:], rest):
-        arrived[k] = ahead(block, k, 0, 1)
-
+        ((out_proj, 1), (gate_weight, SPLIT), (up_weight, SPLIT)),
+        (near,),
+    )
+
+    arrived, landing = lax.optimization_barrier((arrived, landing))
+    last = lax.ppermute(
+        jnp.concatenate([own_chunk] + [arrived[host] for host in hosts]), "pd", [(0, 1)]
+    )
+    arrays = [last] + [arrived[k] for k in sorted(arrived)]
+    chunks = [(0, 0, 0), (0, per_peer, 1), (0, 2 * per_peer, members - 1)]
+    chunks += [(i + 1, 0, k) for i, k in enumerate(sorted(arrived))]
     padding = ((0, -tokens % 128), (0, 0))
     new_k = jnp.pad(fresh_kv[:, :, 0].reshape(tokens, HD), padding)
     new_v = jnp.pad(fresh_kv[:, :, 1].reshape(tokens, HD), padding)
     asked = [queries[:, st] for st in range(steps)]
     kv_after, att_low, att_high = place_and_attend(
-        place, landing, kv_pages, bias, new_k, new_v, asked, arrived
+        place, landing, kv_pages, kept, bias, new_k, new_v, asked, arrays, chunks
     )
 
     def everywhere(x):
@@ -536,7 +551,7 @@
 
     mine, sibling = everywhere(residual)
     own, other = feed_forward(
-        place, mine, sibling, norm_gain, held[1:], up_weight, down_weight
+        place, mine, sibling, norm_gain, held[1 : 1 + SPLIT], held[1 + SPLIT :], down_weight
     )
     summed = (own + swap(other).astype(jnp.float32)).astype(jnp.bfloat16)
     shares = lax.all_to_all(summed, "tp", split_axis=0, concat_axis=0)

time: 113 us -> 108 us (0.956)
  starting transfers between devices: 22 us -> 14.8 us
  other arithmetic: 0.83 us -> 2.7 us
  Pallas kernels: 38.3 us -> 37 us
    ppermute x8 -> x7, starting transfers between devices: 20.5 us -> 13.3 us  [the longest x5 8.06 us: send(): return lax.ppermute(x, BOTH, route)]
    pallas_call x1, Pallas kernels: 8.76 us -> 13.6 us  [prepare(): pl.pallas_call(functools.partial(prepare_kernel, count, parts, groups), o...]
    pallas_call x1, Pallas kernels: 16.8 us -> 13 us  [feed_forward(): pl.pallas_call(ffn_kernel, out_shape=[jax.ShapeDtypeStruct(mine.shape, jn...]
    ppermute x1, waiting for transfers between devices: 1.8 us -> 4.6 us  [local(): att_mine = att_high + lax.ppermute(att_low, 'pd', [(1, 0)])]
    pallas_call x2, Pallas kernels: 9.63 us -> 7.34 us  [the longest x1 6.71 us: pack(): pl.pallas_call(functools.partial(pack_kernel, members), out_shape=[pltpu....]
    ppermute x8 -> x7, waiting for transfers between devices: 3.7 us -> 1.61 us  [the longest x1 1.59 us: local(): lax.ppermute(jnp.concatenate([own_chunk] + [arrived[host] for host in hos...]
    select_n x0 -> x1, other arithmetic: none -> 1.79 us  [local(): block = jnp.where(half == 0, far[host], block)]
  transfers between devices with their start and end apart: 12 -> 11, of which waited for: 5 -> 5; matrix products, arithmetic and copies ran while one was open for 1% -> 3% of each run, Pallas kernels for 8% -> 13%
where the time goes in v5:
time: 108 us
  blocking collectives  40.5 us (38%)
  Pallas kernels  37 us (34%)
  starting transfers between devices  14.8 us (14%)
  waiting for transfers between devices  10.7 us (10%)
  other arithmetic  2.7 us (2%)
    all_to_all x2, blocking collectives, everywhere(): mine = lax.all_to_all(spread, 'tp', split_axis=0, concat_axis=0)  27.9 us
    pallas_call x1, Pallas kernels, prepare(): pl.pallas_call(functools.partial(prepare_kernel, count, parts, groups), o...  13.6 us
    pallas_call x1, Pallas kernels, feed_forward(): pl.pallas_call(ffn_kernel, out_shape=[jax.ShapeDtypeStruct(mine.shape, jn...  13 us
    all_to_all x1, blocking collectives, local(): shares = lax.all_to_all(summed, 'tp', split_axis=0, concat_axis=0)  12.6 us
    ppermute x5, starting transfers between devices, send(): return lax.ppermute(x, BOTH, route)  8.06 us
    pallas_call x1, Pallas kernels, pack(): pl.pallas_call(functools.partial(pack_kernel, members), out_shape=[pltpu....  6.71 us
    ppermute x1, waiting for transfers between devices, local(): att_mine = att_high + lax.ppermute(att_low, 'pd', [(1, 0)])  4.6 us
    ppermute x3, waiting for transfers between devices, swap(): return lax.ppermute(x, 'pd', [(0, 1), (1, 0)])  4.46 us
  transfers between devices with their start and end apart: 11, of which 5 were waited for; matrix products, arithmetic and copies ran while one was open for 3% of the time, Pallas kernels for 13%

profile of v5, /device:TPU:0, one launch (start us, length us, event | category | flops | bytes accessed | tf_op | source)
XLA Modules:
  0.0 107.6 jit_solution(2744890385775977136)
XLA Ops:
  0.6 0.1 pad_add_fusion.place
  0.7 6.7 %pack_pages.1 = (bf16[64,2,16,128]{3,2,1,0:T(8,128)(2,1)}, bf16[32,2,16,128]{3,2,1,0:T(8,128)(2,1)}, bf16[32,2,16,128]{3,2,1,0:T(8,128)(2,1)}, bf16[32,2,16,128]...) custom-call(s32[2]{0:T(128)S(1)} %pad_add_fusion.place, ...), custom_call_target="tpu_custom_call" | custom-call | tf_op jit(solution)/shard_map/pack_pages/pallas_call | solution.py:124
  7.4 1.3 %collective-permute-start = (bf16[64,2,16,128]{3,2,1,0:T(8,128)(2,1)}, bf16[64,2,16,128]{3,2,1,0:T(8,128)(2,1)S(1)}, u32[]{:S(2)}, u32[]{:S(2)}) collective-permute-start(bf16[64,2,16,128]{3,2,1,0:T(8,128)(2,1)} %get-tuple-element.29.refs_3_), channel_id=1, source_target_pairs={{0,1},{2,3},{4,5},{6,7},{8,9},{10,11},{12,13},{14,15},{16,17},{18,... | collective-permute-start | bytes 1572872 | tf_op jit(solution)/shard_map/ppermute | solution.py:507
  8.8 1.3 %collective-permute-start.2 = (bf16[32,2,16,128]{3,2,1,0:T(8,128)(2,1)}, bf16[32,2,16,128]{3,2,1,0:T(8,128)(2,1)S(1)}, u32[]{:S(2)}, u32[]{:S(2)}) collective-permute-start(bf16[32,2,16,128]{3,2,1,0:T(8,128)(2,1)} %get-tuple-element.30), channel_id=1, source_target_pairs={{0,7},{2,9},{4,11},{6,13},{8,15},{10,1},{12,3},{14,5},{16,23},{18,... | collective-permute-start | bytes 786440 | tf_op jit(solution)/shard_map/ppermute | solution.py:500
  10.1 1.3 %collective-permute-start.3 = (bf16[32,2,16,128]{3,2,1,0:T(8,128)(2,1)}, bf16[32,2,16,128]{3,2,1,0:T(8,128)(2,1)S(1)}, u32[]{:S(2)}, u32[]{:S(2)}) collective-permute-start(bf16[32,2,16,128]{3,2,1,0:T(8,128)(2,1)} %get-tuple-element.31), channel_id=1, source_target_pairs={{0,9},{2,11},{4,13},{6,15},{8,1},{10,3},{12,5},{14,7},{16,25},{18,... | collective-permute-start | bytes 786440 | tf_op jit(solution)/shard_map/ppermute | solution.py:500
  11.4 1.3 %collective-permute-start.4 = (bf16[32,2,16,128]{3,2,1,0:T(8,128)(2,1)}, bf16[32,2,16,128]{3,2,1,0:T(8,128)(2,1)S(1)}, u32[]{:S(2)}, u32[]{:S(2)}) collective-permute-start(bf16[32,2,16,128]{3,2,1,0:T(8,128)(2,1)} %get-tuple-element.32), channel_id=1, source_target_pairs={{0,11},{2,13},{4,15},{6,1},{8,3},{10,5},{12,7},{14,9},{16,27},{18,... | collective-permute-start | bytes 786440 | tf_op jit(solution)/shard_map/ppermute | solution.py:500
  12.7 1.8 %slice_select_fusion = (bf16[32,2,16,128]{3,2,1,0:T(8,128)(2,1)}, bf16[32,2,16,128]{3,2,1,0:T(8,128)(2,1)S(1)}) fusion(bf16[32,2,16,128]{3,2,1,0:T(8,128)(2,1)} %get-tuple-element.33, bf16[64,2,16,128]{3,2,1,0:T(8,128)(2,1)S(1)} %collective-permute-done, pred[]{:T(512)S(6)} %eq.4, bf16[32,2,16,128]{3,2,1,0:T(8,128)(2,1)} %get-tuple-element.28), kind=kLoop, calls=%fused_computation.3 | loop fusion | flops 262144 | bytes 1572865 | tf_op jit(solution)/shard_map/jit(_where)/select_n | solution.py:513
  14.5 1.7 %collective-permute-start.5 = (bf16[32,2,16,128]{3,2,1,0:T(8,128)(2,1)}, bf16[32,2,16,128]{3,2,1,0:T(8,128)(2,1)S(1)}, u32[]{:S(2)}, u32[]{:S(2)}) collective-permute-start(bf16[32,2,16,128]{3,2,1,0:T(8,128)(2,1)} %get-tuple-element.54), channel_id=1, source_target_pairs={{0,13},{2,15},{4,1},{6,3},{8,5},{10,7},{12,9},{14,11},{1,14},{3,0}... | collective-permute-start | bytes 786440 | tf_op jit(solution)/shard_map/ppermute | solution.py:500
  16.2 2.4 %collective-permute-start.1 = (bf16[32,2,16,128]{3,2,1,0:T(8,128)(2,1)S(1)}, bf16[32,2,16,128]{3,2,1,0:T(8,128)(2,1)S(1)}, u32[]{:S(2)}, u32[]{:S(2)}) collective-permute-start(bf16[32,2,16,128]{3,2,1,0:T(8,128)(2,1)S(1)} %get-tuple-element.55), channel_id=1, source_target_pairs={{0,5},{2,7},{4,9},{6,11},{8,13},{10,15},{12,1},{14,3},{1,2},{3,4},... | collective-permute-start | bytes 786440 | tf_op jit(solution)/shard_map/ppermute | solution.py:500
  18.7 0.8 reshape.9.listed
  19.5 0.0 copy-start.4
  19.5 0.0 copy-start.2
  19.5 13.6 %prepare.1 = (bf16[512,8192]{1,0:T(8,128)(2,1)S(1)}, bf16[4096,1024]{1,0:T(8,128)(2,1)S(1)}, bf16[4096,1024]{1,0:T(8,128)(2,1)S(1)}, bf16[4096,1024]{1,0:T(8,128...) custom-call(s32[2]{0:T(128)S(1)} %pad_add_fusion.place, ...), custom_call_target="tpu_custom_call" | custom-call | bytes 41943040 | tf_op jit(solution)/shard_map/prepare/pallas_call | solution.py:235
  33.0 0.0 copy-start
  33.1 0.1 pad_maximum_fusion
  33.2 3.9 %collective-permute-start.6 = (bf16[96,2,16,128]{3,2,1,0:T(8,128)(2,1)S(1)}, bf16[96,2,16,128]{3,2,1,0:T(8,128)(2,1)S(1)}, u32[]{:S(2)}, u32[]{:S(2)}) collective-permute-start(bf16[96,2,16,128]{3,2,1,0:T(8,128)(2,1)S(1)} %pad_maximum_fusion), channel_id=1, source_target_pairs={{0,1},{2,3},{4,5},{6,7},{8,9},{10,11},{12,13},{14,15},{16,17},{18,... | collective-permute-start | bytes 2359304 | tf_op jit(solution)/shard_map/ppermute | solution.py:527
  37.3 0.1 fusion
  37.4 1.6 %collective-permute-done.6.refs_2_ = bf16[96,2,16,128]{3,2,1,0:T(8,128)(2,1)S(1)} collective-permute-done((bf16[96,2,16,128]{3,2,1,0:T(8,128)(2,1)S(1)}, bf16[96,2,16,128]{3,2,1,0:T(8,128)(2,1)S(1)}, u32[]{:S(2)}, u32[]{:S(2)}) %collective-permute-start.6) | collective-permute-done | bytes 786464 | tf_op jit(solution)/shard_map/ppermute | solution.py:527
  39.0 0.6 place_attend.1
  39.6 1.3 %collective-permute-start.7 = (bf16[32,512]{1,0:T(8,128)(2,1)S(1)}, bf16[32,512]{1,0:T(8,128)(2,1)S(1)}, u32[]{:S(2)}, u32[]{:S(2)}) collective-permute-start(bf16[32,512]{1,0:T(8,128)(2,1)S(1)} %get-tuple-element.47), channel_id=1, source_target_pairs={{1,0},{3,2},{5,4},{7,6},{9,8},{11,10},{13,12},{15,14},{17,16},{19,... | collective-permute-start | bytes 98312 | tf_op jit(solution)/shard_map/ppermute | solution.py:546
  40.9 4.6 %collective-permute-done.7 = bf16[32,512]{1,0:T(8,128)(2,1)S(1)} collective-permute-done((bf16[32,512]{1,0:T(8,128)(2,1)S(1)}, bf16[32,512]{1,0:T(8,128)(2,1)S(1)}, u32[]{:S(2)}, u32[]{:S(2)}) %collective-permute-start.7) | collective-permute-done | bytes 32800 | tf_op jit(solution)/shard_map/ppermute | solution.py:546
  45.6 15.3 %all_to_all.15.mine = bf16[8,32,512]{2,1,0:T(8,128)(2,1)S(1)} all-to-all(bf16[8,32,512]{2,1,0:T(8,128)(2,1)S(1)} %broadcast_in_dim.4), channel_id=1, replica_groups=mesh['grp'=2,'tp'=8,'pd'=2] {'tp'}, dimensions={0} | all-to-all | bytes 524288 | tf_op jit(solution)/shard_map/all_to_all | solution.py:543
  60.8 1.5 %collective-permute-done.8.sibling = bf16[8,32,512]{2,1,0:T(8,128)(2,1)S(1)} collective-permute-done((bf16[8,32,512]{2,1,0:T(8,128)(2,1)S(1)}, bf16[8,32,512]{2,1,0:T(8,128)(2,1)S(1)}, u32[]{:S(2)}, u32[]{:S(2)}) %collective-permute-start.8) | collective-permute-done | bytes 262176 | tf_op jit(solution)/shard_map/ppermute | solution.py:503
  62.4 3.1 %out_projection.1 = bf16[32,512]{1,0:T(8,128)(2,1)S(1)} custom-call(s32[2]{0:T(128)S(1)} %pad_add_fusion.place, bf16[512,8192]{1,0:T(8,128)(2,1)S(1)} %get-tuple-element.45.weight, bf16[32,512]{1,0:T(8,128)(2,1)S(1)} %copy-done, bf16[8,32,512]{2,1,0:T(8,128)(2,1)S(1)} %all_to_all.15.mine, bf16[8,32,512]{2,1,0:T(8,128)(2,1)S(1)} %collective-permute-done.8.sibling), custom_call_target="tpu_custom_call" | custom-call | tf_op jit(solution)/shard_map/out_projection/pallas_call | solution.py:388
  65.5 12.6 %all_to_all.16.mine = bf16[8,32,512]{2,1,0:T(8,128)(2,1)S(1)} all-to-all(bf16[8,32,512]{2,1,0:T(8,128)(2,1)S(1)} %broadcast_in_dim.5), channel_id=1, replica_groups=mesh['grp'=2,'tp'=8,'pd'=2] {'tp'}, dimensions={0} | all-to-all | bytes 524288 | tf_op jit(solution)/shard_map/all_to_all | solution.py:543
  78.1 1.5 %collective-permute-done.9.sibling = bf16[8,32,512]{2,1,0:T(8,128)(2,1)S(1)} collective-permute-done((bf16[8,32,512]{2,1,0:T(8,128)(2,1)S(1)}, bf16[8,32,512]{2,1,0:T(8,128)(2,1)S(1)}, u32[]{:S(2)}, u32[]{:S(2)}) %collective-permute-start.9) | collective-permute-done | bytes 262176 | tf_op jit(solution)/shard_map/ppermute | solution.py:503
  79.7 13.0 %feed_forward.1 = (f32[8,32,512]{2,1,0:T(8,128)S(1)}, bf16[8,32,512]{2,1,0:T(8,128)(2,1)S(1)}) custom-call(s32[2]{0:T(128)S(1)} %pad_add_fusion.place, bf16[8,32,512]{2,1,0:T(8,128)(2,1)S(1)} %all_to_all.16.mine, bf16[8,32,512]{2,1,0:T(8,128)(2,1)S(1)} %collective-permute-done.9.sibling, f32[8192]{0:T(1024)S(1)} %copy-done.1, ...), custom_call_target="tpu_custom_call" | custom-call | tf_op jit(solution)/shard_map/feed_forward/pallas_call | solution.py:450
  92.6 0.2 collective-permute-start.10
  92.8 1.4 %collective-permute-done.10 = bf16[8,32,512]{2,1,0:T(8,128)(2,1)S(1)} collective-permute-done((bf16[8,32,512]{2,1,0:T(8,128)(2,1)S(1)}, bf16[8,32,512]{2,1,0:T(8,128)(2,1)S(1)}, u32[]{:S(2)}, u32[]{:S(2)}) %collective-permute-start.10) | collective-permute-done | bytes 262176 | tf_op jit(solution)/shard_map/ppermute | solution.py:503
  94.2 0.1 add_convert_fusion
  94.3 12.6 %all_to_all.17 = bf16[8,32,512]{2,1,0:T(8,128)(2,1)S(1)} all-to-all(bf16[8,32,512]{2,1,0:T(8,128)(2,1)S(1)} %add_convert_fusion), channel_id=1, replica_groups=mesh['grp'=2,'tp'=8,'pd'=2] {'tp'}, dimensions={0} | all-to-all | bytes 524288 | tf_op jit(solution)/shard_map/all_to_all | solution.py:557
  106.9 0.6 add_convert_fusion.1
  (25 shorter events, 0.2 us)
Async XLA Ops:
  7.4 5.3 %collective-permute-start = (bf16[64,2,16,128]{3,2,1,0:T(8,128)(2,1)}, bf16[64,2,16,128]{3,2,1,0:T(8,128)(2,1)S(1)}, u32[]{:S(2)}, u32[]{:S(2)}) collective-permute-start(bf16[64,2,16,128]{3,2,1,0:T(8,128)(2,1)} %get-tuple-element.29.refs_3_), channel_id=1, source_target_pairs={{0,1},{2,3},{4,5},{6,7},{8,9},{10,11},{12,13},{14,15},{16,17},{18,... | collective-permute-start | bytes 1572872 | tf_op jit(solution)/shard_map/ppermute | solution.py:507
  8.8 24.3 %collective-permute-start.2 = (bf16[32,2,16,128]{3,2,1,0:T(8,128)(2,1)}, bf16[32,2,16,128]{3,2,1,0:T(8,128)(2,1)S(1)}, u32[]{:S(2)}, u32[]{:S(2)}) collective-permute-start(bf16[32,2,16,128]{3,2,1,0:T(8,128)(2,1)} %get-tuple-element.30), channel_id=1, source_target_pairs={{0,7},{2,9},{4,11},{6,13},{8,15},{10,1},{12,3},{14,5},{16,23},{18,... | collective-permute-start | bytes 786440 | tf_op jit(solution)/shard_map/ppermute | solution.py:500
  10.1 23.0 %collective-permute-start.3 = (bf16[32,2,16,128]{3,2,1,0:T(8,128)(2,1)}, bf16[32,2,16,128]{3,2,1,0:T(8,128)(2,1)S(1)}, u32[]{:S(2)}, u32[]{:S(2)}) collective-permute-start(bf16[32,2,16,128]{3,2,1,0:T(8,128)(2,1)} %get-tuple-element.31), channel_id=1, source_target_pairs={{0,9},{2,11},{4,13},{6,15},{8,1},{10,3},{12,5},{14,7},{16,25},{18,... | collective-permute-start | bytes 786440 | tf_op jit(solution)/shard_map/ppermute | solution.py:500
  11.4 21.7 %collective-permute-start.4 = (bf16[32,2,16,128]{3,2,1,0:T(8,128)(2,1)}, bf16[32,2,16,128]{3,2,1,0:T(8,128)(2,1)S(1)}, u32[]{:S(2)}, u32[]{:S(2)}) collective-permute-start(bf16[32,2,16,128]{3,2,1,0:T(8,128)(2,1)} %get-tuple-element.32), channel_id=1, source_target_pairs={{0,11},{2,13},{4,15},{6,1},{8,3},{10,5},{12,7},{14,9},{16,27},{18,... | collective-permute-start | bytes 786440 | tf_op jit(solution)/shard_map/ppermute | solution.py:500
  14.5 18.6 %collective-permute-start.5 = (bf16[32,2,16,128]{3,2,1,0:T(8,128)(2,1)}, bf16[32,2,16,128]{3,2,1,0:T(8,128)(2,1)S(1)}, u32[]{:S(2)}, u32[]{:S(2)}) collective-permute-start(bf16[32,2,16,128]{3,2,1,0:T(8,128)(2,1)} %get-tuple-element.54), channel_id=1, source_target_pairs={{0,13},{2,15},{4,1},{6,3},{8,5},{10,7},{12,9},{14,11},{1,14},{3,0}... | collective-permute-start | bytes 786440 | tf_op jit(solution)/shard_map/ppermute | solution.py:500
  16.2 16.9 %collective-permute-start.1 = (bf16[32,2,16,128]{3,2,1,0:T(8,128)(2,1)S(1)}, bf16[32,2,16,128]{3,2,1,0:T(8,128)(2,1)S(1)}, u32[]{:S(2)}, u32[]{:S(2)}) collective-permute-start(bf16[32,2,16,128]{3,2,1,0:T(8,128)(2,1)S(1)} %get-tuple-element.55), channel_id=1, source_target_pairs={{0,5},{2,7},{4,9},{6,11},{8,13},{10,15},{12,1},{14,3},{1,2},{3,4},... | collective-permute-start | bytes 786440 | tf_op jit(solution)/shard_map/ppermute | solution.py:500
  19.4 13.7 %copy-start.3 = (bf16[32,2,16,128]{3,2,1,0:T(8,128)(2,1)S(1)}, bf16[32,2,16,128]{3,2,1,0:T(8,128)(2,1)}, u32[]{:S(2)}) copy-start(bf16[32,2,16,128]{3,2,1,0:T(8,128)(2,1)} %get-tuple-element.38) | copy-start | bytes 786436
  19.5 17.7 %copy-start.4 = (bf16[16,2,2,128]{3,2,1,0:T(2,128)(2,1)S(1)}, bf16[16,2,2,128]{3,2,1,0:T(2,128)(2,1)}, u32[]{:S(2)}) copy-start(bf16[16,2,2,128]{3,2,1,0:T(2,128)(2,1)} %param.17) | copy-start | bytes 49156
  19.5 17.8 %copy-start.2 = (bf16[16,2,1024]{2,1,0:T(2,128)(2,1)S(1)}, bf16[16,2,1024]{2,1,0:T(2,128)(2,1)}, u32[]{:S(2)}) copy-start(bf16[16,2,1024]{2,1,0:T(2,128)(2,1)} %param.16) | copy-start | bytes 196612
  33.0 29.3 %copy-start = (bf16[32,512]{1,0:T(8,128)(2,1)S(1)}, bf16[32,512]{1,0:T(8,128)(2,1)}, u32[]{:S(2)}) copy-start(bf16[32,512]{1,0:T(8,128)(2,1)} %stream.1) | copy-start | bytes 98308
  33.2 5.8 %collective-permute-start.6 = (bf16[96,2,16,128]{3,2,1,0:T(8,128)(2,1)S(1)}, bf16[96,2,16,128]{3,2,1,0:T(8,128)(2,1)S(1)}, u32[]{:S(2)}, u32[]{:S(2)}) collective-permute-start(bf16[96,2,16,128]{3,2,1,0:T(8,128)(2,1)S(1)} %pad_maximum_fusion), channel_id=1, source_target_pairs={{0,1},{2,3},{4,5},{6,7},{8,9},{10,11},{12,13},{14,15},{16,17},{18,... | collective-permute-start | bytes 2359304 | tf_op jit(solution)/shard_map/ppermute | solution.py:527
  39.0 40.7 %copy-start.1 = (f32[8192]{0:T(1024)S(1)}, f32[8192]{0:T(1024)}, u32[]{:S(2)}) copy-start(f32[8192]{0:T(1024)} %gain.1) | copy-start | bytes 98308
  39.6 5.9 %collective-permute-start.7 = (bf16[32,512]{1,0:T(8,128)(2,1)S(1)}, bf16[32,512]{1,0:T(8,128)(2,1)S(1)}, u32[]{:S(2)}, u32[]{:S(2)}) collective-permute-start(bf16[32,512]{1,0:T(8,128)(2,1)S(1)} %get-tuple-element.47), channel_id=1, source_target_pairs={{1,0},{3,2},{5,4},{7,6},{9,8},{11,10},{13,12},{15,14},{17,16},{19,... | collective-permute-start | bytes 98312 | tf_op jit(solution)/shard_map/ppermute | solution.py:546
  60.8 1.5 %collective-permute-start.8 = (bf16[8,32,512]{2,1,0:T(8,128)(2,1)S(1)}, bf16[8,32,512]{2,1,0:T(8,128)(2,1)S(1)}, u32[]{:S(2)}, u32[]{:S(2)}) collective-permute-start(bf16[8,32,512]{2,1,0:T(8,128)(2,1)S(1)} %all_to_all.15.mine), channel_id=1, source_target_pairs={{0,1},{1,0},{2,3},{3,2},{4,5},{5,4},{6,7},{7,6},{8,9},{9,8},{10,11... | collective-permute-start | bytes 786440 | tf_op jit(solution)/shard_map/ppermute | solution.py:503
  78.1 1.5 %collective-permute-start.9 = (bf16[8,32,512]{2,1,0:T(8,128)(2,1)S(1)}, bf16[8,32,512]{2,1,0:T(8,128)(2,1)S(1)}, u32[]{:S(2)}, u32[]{:S(2)}) collective-permute-start(bf16[8,32,512]{2,1,0:T(8,128)(2,1)S(1)} %all_to_all.16.mine), channel_id=1, source_target_pairs={{0,1},{1,0},{2,3},{3,2},{4,5},{5,4},{6,7},{7,6},{8,9},{9,8},{10,11... | collective-permute-start | bytes 786440 | tf_op jit(solution)/shard_map/ppermute | solution.py:503
  92.6 1.6 %collective-permute-start.10 = (bf16[8,32,512]{2,1,0:T(8,128)(2,1)S(1)}, bf16[8,32,512]{2,1,0:T(8,128)(2,1)S(1)}, u32[]{:S(2)}, u32[]{:S(2)}) collective-permute-start(bf16[8,32,512]{2,1,0:T(8,128)(2,1)S(1)} %get-tuple-element.53), channel_id=1, source_target_pairs={{0,1},{1,0},{2,3},{3,2},{4,5},{5,4},{6,7},{7,6},{8,9},{9,8},{10,11... | collective-permute-start | bytes 786440 | tf_op jit(solution)/shard_map/ppermute | solution.py:503

commit v6 on v5

--- a/solution.py
+++ b/solution.py
@@ -17,7 +17,7 @@
 ARRIVE = REQ_DEV * NEWP
 MIB = 1024 * 1024
 BOTH = ("tp", "pd")
-SPLIT = 2
+SPLIT = 4
 
 VM = pl.BlockSpec(memory_space=pltpu.VMEM)
 SM = pl.BlockSpec(memory_space=pltpu.SMEM)
@@ -35,8 +35,8 @@
 
 def pack_kernel(members, place, pages, pool, *refs):
     count = members - 1
-    outs, kept = refs[:count], refs[count]
-    packed, held, own, counts, sems, load_sems, keep_sems = refs[count + 1 :]
+    outs = refs[:count]
+    packed, held, own, counts, sems, load_sems = refs[count:]
     member, half = place[0], place[1]
     slots = pool.shape[0]
     per_peer = ARRIVE // members
@@ -47,14 +47,11 @@
     def _():
         own_copy = pltpu.make_async_copy(pages, own, load_sems.at[parts])
         own_copy.start()
-        loads, keeps = [], []
+        loads = []
         for i in range(parts):
             window = pl.ds(i * step, step)
             loads.append(
                 pltpu.make_async_copy(pool.at[window], held.at[window], load_sems.at[i])
-            )
-            keeps.append(
-                pltpu.make_async_copy(held.at[window], kept.at[window], keep_sems.at[i])
             )
             loads[-1].start()
         own_copy.wait()
@@ -111,9 +108,7 @@
                 )
             )
             copies[-1].start()
-        for keep in keeps:
-            keep.start()
-        for copy in copies + keeps:
+        for copy in copies:
             copy.wait()
 
 
@@ -124,10 +119,9 @@
     return pl.pallas_call(
         functools.partial(pack_kernel, members),
         out_shape=[pltpu.HBM((2 * per_peer, *chunk), pool.dtype)]
-        + [pltpu.HBM((per_peer, *chunk), pool.dtype)] * (members - 2)
-        + [pltpu.HBM(pool.shape, pool.dtype)],
+        + [pltpu.HBM((per_peer, *chunk), pool.dtype)] * (members - 2),
         in_specs=[SM, HBM, HBM],
-        out_specs=[HBM] * members,
+        out_specs=[HBM] * (members - 1),
         scratch_shapes=[
             pltpu.VMEM((ARRIVE + 1, *chunk), pool.dtype),
             pltpu.VMEM(pool.shape, pool.dtype),
@@ -135,7 +129,6 @@
             pltpu.SMEM((members + 1,), jnp.int32),
             pltpu.SemaphoreType.DMA((members,)),
             pltpu.SemaphoreType.DMA((5,)),
-            pltpu.SemaphoreType.DMA((4,)),
         ],
         compiler_params=pltpu.CompilerParams(vmem_limit_bytes=8 * MIB),
         name="pack_pages",
@@ -255,7 +248,7 @@
     )(place, listed, *[in_hbm(x) for x in (lengths, tables, *weights, *first)])
 
 
-def attend_kernel(members, steps, chunks, place, landing, old_pool, _, bias, new_k, new_v, *refs):
+def attend_kernel(members, steps, chunks, place, landing, old_pool, bias, new_k, new_v, *refs):
     asked, refs = refs[:steps], refs[steps:]
     arrived, refs = refs[:-6], refs[-6:]
     kv_out, att_low, att_high, pool, scores, sems = refs
@@ -268,8 +261,14 @@
 
     @pl.when(half == 0)
     def _():
+        copy = pltpu.make_async_copy(old_pool, pool, sems.at[0])
+        copy.start()
         att_low[...] = jnp.zeros_like(att_low)
         att_high[...] = jnp.zeros_like(att_high)
+        copy.wait()
+        copy_out = pltpu.make_async_copy(pool, kv_out, sems.at[1])
+        copy_out.start()
+        copy_out.wait()
 
     @pl.when(half == 1)
     def _():
@@ -329,7 +328,7 @@
         copy_out.wait()
 
 
-def place_and_attend(place, landing, old_pool, kept, bias, new_k, new_v, asked, arrived, chunks):
+def place_and_attend(place, landing, old_pool, bias, new_k, new_v, asked, arrived, chunks):
     members = landing.shape[0]
     slots = old_pool.shape[0]
     rows = bias.shape[0]
@@ -342,7 +341,7 @@
             jax.ShapeDtypeStruct((tokens, GQ * HD // 2), jnp.bfloat16),
             jax.ShapeDtypeStruct((tokens, GQ * HD // 2), jnp.bfloat16),
         ],
-        in_specs=[SM, SM, HBM, HBM, VM, VM, VM] + [VM] * (steps + len(arrived)),
+        in_specs=[SM, SM, HBM, VM, VM, VM] + [VM] * (steps + len(arrived)),
         out_specs=[HBM, VM, VM],
         scratch_shapes=[
             pltpu.VMEM(old_pool.shape, old_pool.dtype),
@@ -350,13 +349,11 @@
             pltpu.SemaphoreType.DMA((2,)),
         ],
         compiler_params=pltpu.CompilerParams(vmem_limit_bytes=9 * MIB),
-        input_output_aliases={3: 0},
         name="place_attend",
     )(
         place,
         landing,
         in_hbm(old_pool),
-        in_hbm(kept),
         bias,
         new_k,
         new_v,
@@ -395,12 +392,12 @@
     )(place, in_vmem(weight), stream, mine, sibling)
 
 
-def ffn_kernel(place, mine, sibling, gain, *refs):
-    gate, up = refs[:SPLIT], refs[SPLIT : 2 * SPLIT]
-    down, own_out, other_out, down_buf, normed, hidden, down_sem = refs[2 * SPLIT :]
+def ffn_kernel(place, mine, sibling, gain, gate, *refs):
+    up = refs[:SPLIT]
+    down, own_out, other_out, down_buf, normed, hidden, down_sem = refs[SPLIT:]
     half = place[1]
     members, tokens, width = mine.shape
-    depth, hidden_count = gate[0].shape
+    depth, hidden_count = up[0].shape
     features = depth * SPLIT
     down_copies = []
     for t in range(members):
@@ -425,10 +422,10 @@
     tile = min(256, hidden_count)
     for f in range(hidden_count // tile):
         cols = slice(f * tile, (f + 1) * tile)
-        gate_act = up_act = 0.0
+        gate_act = jnp.dot(normed[...], gate[:, cols], preferred_element_type=jnp.float32)
+        up_act = 0.0
         for i in range(SPLIT):
             x = normed[:, i * depth : (i + 1) * depth]
-            gate_act += jnp.dot(x, gate[i][:, cols], preferred_element_type=jnp.float32)
             up_act += jnp.dot(x, up[i][:, cols], preferred_element_type=jnp.float32)
         h = gate_act / (1.0 + jnp.exp(-gate_act)) * up_act
         hidden[:, cols] = h.astype(jnp.bfloat16)
@@ -453,7 +450,7 @@
             jax.ShapeDtypeStruct(mine.shape, jnp.float32),
             jax.ShapeDtypeStruct(mine.shape, jnp.bfloat16),
         ],
-        in_specs=[SM, VM, VM, VM] + [VM] * (2 * SPLIT) + [HBM],
+        in_specs=[SM, VM, VM, VM] + [VM] * (1 + SPLIT) + [HBM],
         out_specs=[VM, VM],
         scratch_shapes=[
             pltpu.VMEM(down.shape, down.dtype),
@@ -463,7 +460,7 @@
         ],
         compiler_params=pltpu.CompilerParams(vmem_limit_bytes=19 * MIB),
         name="feed_forward",
-    )(place, mine, sibling, gain, *map(in_vmem, (*gate, *up)), in_hbm(down))
+    )(place, mine, sibling, gain, *map(in_vmem, (gate, *up)), in_hbm(down))
 
 
 def local(
@@ -502,7 +499,7 @@
     def swap(x):
         return lax.ppermute(x, "pd", [(0, 1), (1, 0)])
 
-    near, own_chunk, *far, kept = pack(place, page_list, kv_pages)
+    near, own_chunk, *far = pack(place, page_list, kv_pages)
     far = dict(zip(range(2, members - 1), far))
     crossed = lax.ppermute(near, "pd", [(0, 1)])
     behind, ahead = crossed[:per_peer], crossed[per_peer:]
@@ -519,7 +516,7 @@
         block_tables,
         page_list.reshape(members, slots),
         groups,
-        ((out_proj, 1), (gate_weight, SPLIT), (up_weight, SPLIT)),
+        ((up_weight, SPLIT),),
         (near,),
     )
 
@@ -535,7 +532,7 @@
     new_v = jnp.pad(fresh_kv[:, :, 1].reshape(tokens, HD), padding)
     asked = [queries[:, st] for st in range(steps)]
     kv_after, att_low, att_high = place_and_attend(
-        place, landing, kv_pages, kept, bias, new_k, new_v, asked, arrays, chunks
+        place, landing, kv_pages, bias, new_k, new_v, asked, arrays, chunks
     )
 
     def everywhere(x):
@@ -547,11 +544,11 @@
     here, there = everywhere(att_mine)
 
     inner = stream.reshape(steps, groups, rows, -1).transpose(1, 0, 2, 3).reshape(stream.shape)
-    residual = project(place, held[0], inner, here, there, groups)
+    residual = project(place, out_proj, inner, here, there, groups)
 
     mine, sibling = everywhere(residual)
     own, other = feed_forward(
-        place, mine, sibling, norm_gain, held[1 : 1 + SPLIT], held[1 + SPLIT :], down_weight
+        place, mine, sibling, norm_gain, gate_weight, held, down_weight
     )
     summed = (own + swap(other).astype(jnp.float32)).astype(jnp.bfloat16)
     shares = lax.all_to_all(summed, "tp", split_axis=0, concat_axis=0)

time: 108 us -> 111 us (1.028)
  Pallas kernels: 37 us -> 32.5 us
  starting transfers between devices: 14.8 us -> 18.3 us
  local copies, waits for them, and re-layouts: 1.04 us -> 4.45 us
    pallas_call x1, Pallas kernels: 13.6 us -> 6.77 us  [prepare(): pl.pallas_call(functools.partial(prepare_kernel, count, parts, groups), o...]
    ppermute x1, starting transfers between devices: 3.93 us -> 7.37 us  [local(): lax.ppermute(jnp.concatenate([own_chunk] + [arrived[host] for host in hos...]
    unnamed x12 -> x22, local copies, waits for them, and re-layouts: 0.04 us -> 3.45 us
    pallas_call x1, Pallas kernels: 0.63 us -> 3.81 us  [place_and_attend(): pl.pallas_call(functools.partial(attend_kernel, members, steps, chunks),...]
    ppermute x5, waiting for transfers between devices: 0.01 us -> 2.82 us  [send(): return lax.ppermute(x, BOTH, route)]
    ppermute x1, waiting for transfers between devices: 4.6 us -> 1.8 us  [local(): att_mine = att_high + lax.ppermute(att_low, 'pd', [(1, 0)])]
    all_to_all x2, blocking collectives: 27.9 us -> 29 us  [everywhere(): mine = lax.all_to_all(spread, 'tp', split_axis=0, concat_axis=0)]
  transfers between devices with their start and end apart: 11 -> 11, of which waited for: 5 -> 6; matrix products, arithmetic and copies ran while one was open for 3% -> 2% of each run, Pallas kernels for 13% -> 6%
where the time goes in v6:
time: 111 us; the launch traced here: 110 us
  blocking collectives  41.6 us (37%)
  Pallas kernels  32.5 us (29%)
  starting transfers between devices  18.3 us (16%)
  waiting for transfers between devices  10.7 us (10%)
  local copies, waits for them, and re-layouts  4.45 us (4%)
  other arithmetic  2.01 us (2%)
    all_to_all x2, blocking collectives, everywhere(): mine = lax.all_to_all(spread, 'tp', split_axis=0, concat_axis=0)  29 us
    pallas_call x1, Pallas kernels, feed_forward(): pl.pallas_call(ffn_kernel, out_shape=[jax.ShapeDtypeStruct(mine.shape, jn...  13 us
    all_to_all x1, blocking collectives, local(): shares = lax.all_to_all(summed, 'tp', split_axis=0, concat_axis=0)  12.6 us
    ppermute x5, starting transfers between devices, send(): return lax.ppermute(x, BOTH, route)  8.12 us
    ppermute x1, starting transfers between devices, local(): lax.ppermute(jnp.concatenate([own_chunk] + [arrived[host] for host in hos...  7.37 us
    pallas_call x1, Pallas kernels, prepare(): pl.pallas_call(functools.partial(prepare_kernel, count, parts, groups), o...  6.77 us
    pallas_call x1, Pallas kernels, pack(): pl.pallas_call(functools.partial(pack_kernel, members), out_shape=[pltpu....  5.84 us
    ppermute x3, waiting for transfers between devices, swap(): return lax.ppermute(x, 'pd', [(0, 1), (1, 0)])  4.47 us
  transfers between devices with their start and end apart: 11, of which 6 were waited for; matrix products, arithmetic and copies ran while one was open for 2% of the time, Pallas kernels for 6%

profile of v6, /device:TPU:0, one launch (start us, length us, event | category | flops | bytes accessed | tf_op | source)
XLA Modules:
  0.0 110.5 jit_solution(3471200959516349743)
XLA Ops:
  0.6 0.1 pad_add_fusion.place
  0.7 5.8 %pack_pages.1 = (bf16[64,2,16,128]{3,2,1,0:T(8,128)(2,1)}, bf16[32,2,16,128]{3,2,1,0:T(8,128)(2,1)}, bf16[32,2,16,128]{3,2,1,0:T(8,128)(2,1)}, bf16[32,2,16,128]...) custom-call(s32[2]{0:T(128)S(1)} %pad_add_fusion.place, ...), custom_call_target="tpu_custom_call" | custom-call | tf_op jit(solution)/shard_map/pack_pages/pallas_call | solution.py:119
  6.6 1.3 %collective-permute-start = (bf16[64,2,16,128]{3,2,1,0:T(8,128)(2,1)}, bf16[64,2,16,128]{3,2,1,0:T(8,128)(2,1)S(1)}, u32[]{:S(2)}, u32[]{:S(2)}) collective-permute-start(bf16[64,2,16,128]{3,2,1,0:T(8,128)(2,1)} %get-tuple-element.27.refs_1_), channel_id=1, source_target_pairs={{0,1},{2,3},{4,5},{6,7},{8,9},{10,11},{12,13},{14,15},{16,17},{18,... | collective-permute-start | bytes 1572872 | tf_op jit(solution)/shard_map/ppermute | solution.py:504
  7.9 1.3 %collective-permute-start.2 = (bf16[32,2,16,128]{3,2,1,0:T(8,128)(2,1)}, bf16[32,2,16,128]{3,2,1,0:T(8,128)(2,1)S(1)}, u32[]{:S(2)}, u32[]{:S(2)}) collective-permute-start(bf16[32,2,16,128]{3,2,1,0:T(8,128)(2,1)} %get-tuple-element.28), channel_id=1, source_target_pairs={{0,7},{2,9},{4,11},{6,13},{8,15},{10,1},{12,3},{14,5},{16,23},{18,... | collective-permute-start | bytes 786440 | tf_op jit(solution)/shard_map/ppermute | solution.py:497
  9.2 1.3 %collective-permute-start.3 = (bf16[32,2,16,128]{3,2,1,0:T(8,128)(2,1)}, bf16[32,2,16,128]{3,2,1,0:T(8,128)(2,1)S(1)}, u32[]{:S(2)}, u32[]{:S(2)}) collective-permute-start(bf16[32,2,16,128]{3,2,1,0:T(8,128)(2,1)} %get-tuple-element.29), channel_id=1, source_target_pairs={{0,9},{2,11},{4,13},{6,15},{8,1},{10,3},{12,5},{14,7},{16,25},{18,... | collective-permute-start | bytes 786440 | tf_op jit(solution)/shard_map/ppermute | solution.py:497
  10.5 1.3 %collective-permute-start.4 = (bf16[32,2,16,128]{3,2,1,0:T(8,128)(2,1)}, bf16[32,2,16,128]{3,2,1,0:T(8,128)(2,1)S(1)}, u32[]{:S(2)}, u32[]{:S(2)}) collective-permute-start(bf16[32,2,16,128]{3,2,1,0:T(8,128)(2,1)} %get-tuple-element.30), channel_id=1, source_target_pairs={{0,11},{2,13},{4,15},{6,1},{8,3},{10,5},{12,7},{14,9},{16,27},{18,... | collective-permute-start | bytes 786440 | tf_op jit(solution)/shard_map/ppermute | solution.py:497
  11.8 1.1 slice_select_fusion
  12.9 1.8 %collective-permute-start.5 = (bf16[32,2,16,128]{3,2,1,0:T(8,128)(2,1)S(1)}, bf16[32,2,16,128]{3,2,1,0:T(8,128)(2,1)S(1)}, u32[]{:S(2)}, u32[]{:S(2)}) collective-permute-start(bf16[32,2,16,128]{3,2,1,0:T(8,128)(2,1)S(1)} %get-tuple-element.50), channel_id=1, source_target_pairs={{0,13},{2,15},{4,1},{6,3},{8,5},{10,7},{12,9},{14,11},{1,14},{3,0}... | collective-permute-start | bytes 786440 | tf_op jit(solution)/shard_map/ppermute | solution.py:497
  14.7 2.4 %collective-permute-start.1 = (bf16[32,2,16,128]{3,2,1,0:T(8,128)(2,1)S(1)}, bf16[32,2,16,128]{3,2,1,0:T(8,128)(2,1)S(1)}, u32[]{:S(2)}, u32[]{:S(2)}) collective-permute-start(bf16[32,2,16,128]{3,2,1,0:T(8,128)(2,1)S(1)} %get-tuple-element.51), channel_id=1, source_target_pairs={{0,5},{2,7},{4,9},{6,11},{8,13},{10,15},{12,1},{14,3},{1,2},{3,4},... | collective-permute-start | bytes 786440 | tf_op jit(solution)/shard_map/ppermute | solution.py:497
  17.1 0.8 reshape.9.listed
  18.0 0.0 slice-start
  18.0 6.8 %prepare.1 = (bf16[2048,1024]{1,0:T(8,128)(2,1)S(1)}, bf16[2048,1024]{1,0:T(8,128)(2,1)S(1)}, bf16[2048,1024]{1,0:T(8,128)(2,1)S(1)}, bf16[2048,1024]{1,0:T(8,12...) custom-call(s32[2]{0:T(128)S(1)} %pad_add_fusion.place, s32[8,312]{1,0:T(8,128)S(1)} %reshape.9.listed, ...), custom_call_target="tpu_custom_call" | custom-call | bytes 16777216 | tf_op jit(solution)/shard_map/prepare/pallas_call | solution.py:228
  24.8 2.8 %collective-permute-done.1.refs_3_ = bf16[32,2,16,128]{3,2,1,0:T(8,128)(2,1)S(1)} collective-permute-done((bf16[32,2,16,128]{3,2,1,0:T(8,128)(2,1)S(1)}, bf16[32,2,16,128]{3,2,1,0:T(8,128)(2,1)S(1)}, u32[]{:S(2)}, u32[]{:S(2)}) %collective-permute-start.1) | collective-permute-done | bytes 262176 | tf_op jit(solution)/shard_map/ppermute | solution.py:497
  27.6 0.1 pad_maximum_fusion
  27.7 7.4 %collective-permute-start.6 = (bf16[96,2,16,128]{3,2,1,0:T(8,128)(2,1)S(1)}, bf16[96,2,16,128]{3,2,1,0:T(8,128)(2,1)S(1)}, u32[]{:S(2)}, u32[]{:S(2)}) collective-permute-start(bf16[96,2,16,128]{3,2,1,0:T(8,128)(2,1)S(1)} %pad_maximum_fusion), channel_id=1, source_target_pairs={{0,1},{2,3},{4,5},{6,7},{8,9},{10,11},{12,13},{14,15},{16,17},{18,... | collective-permute-start | bytes 2359304 | tf_op jit(solution)/shard_map/ppermute | solution.py:524
  35.2 0.1 fusion
  35.3 1.6 %collective-permute-done.6.refs_2_ = bf16[96,2,16,128]{3,2,1,0:T(8,128)(2,1)S(1)} collective-permute-done((bf16[96,2,16,128]{3,2,1,0:T(8,128)(2,1)S(1)}, bf16[96,2,16,128]{3,2,1,0:T(8,128)(2,1)S(1)}, u32[]{:S(2)}, u32[]{:S(2)}) %collective-permute-start.6) | collective-permute-done | bytes 786464 | tf_op jit(solution)/shard_map/ppermute | solution.py:524
  36.9 3.8 %place_attend.1 = (bf16[312,2,16,128]{3,2,1,0:T(8,128)(2,1)}, bf16[32,512]{1,0:T(8,128)(2,1)S(1)}, bf16[32,512]{1,0:T(8,128)(2,1)S(1)}) custom-call(s32[2]{0:T(128)S(1)} %pad_add_fusion.place, s32[8,128]{1,0:T(8,128)S(1)} %get-tuple-element.33.landing, bf16[312,2,16,128]{3,2,1,0:T(8,128)(2,1)} %old_pool.1, f32[16,4992]{1,0:T(8,128)S(1)} %get-tuple-element.34.bias, ...), custom_call_target="tpu_custom_call" | custom-call | tf_op jit(solution)/shard_map/place_attend/pallas_call | solution.py:337
  40.8 1.3 %collective-permute-start.7 = (bf16[32,512]{1,0:T(8,128)(2,1)S(1)}, bf16[32,512]{1,0:T(8,128)(2,1)S(1)}, u32[]{:S(2)}, u32[]{:S(2)}) collective-permute-start(bf16[32,512]{1,0:T(8,128)(2,1)S(1)} %get-tuple-element.43), channel_id=1, source_target_pairs={{1,0},{3,2},{5,4},{7,6},{9,8},{11,10},{13,12},{15,14},{17,16},{19,... | collective-permute-start | bytes 98312 | tf_op jit(solution)/shard_map/ppermute | solution.py:543
  42.1 1.8 %collective-permute-done.7 = bf16[32,512]{1,0:T(8,128)(2,1)S(1)} collective-permute-done((bf16[32,512]{1,0:T(8,128)(2,1)S(1)}, bf16[32,512]{1,0:T(8,128)(2,1)S(1)}, u32[]{:S(2)}, u32[]{:S(2)}) %collective-permute-start.7) | collective-permute-done | bytes 32800 | tf_op jit(solution)/shard_map/ppermute | solution.py:543
  43.9 16.4 %all_to_all.15.mine = bf16[8,32,512]{2,1,0:T(8,128)(2,1)S(1)} all-to-all(bf16[8,32,512]{2,1,0:T(8,128)(2,1)S(1)} %broadcast_in_dim.4), channel_id=1, replica_groups=mesh['grp'=2,'tp'=8,'pd'=2] {'tp'}, dimensions={0} | all-to-all | bytes 524288 | tf_op jit(solution)/shard_map/all_to_all | solution.py:540
  60.3 1.5 %collective-permute-done.8.sibling = bf16[8,32,512]{2,1,0:T(8,128)(2,1)S(1)} collective-permute-done((bf16[8,32,512]{2,1,0:T(8,128)(2,1)S(1)}, bf16[8,32,512]{2,1,0:T(8,128)(2,1)S(1)}, u32[]{:S(2)}, u32[]{:S(2)}) %collective-permute-start.8) | collective-permute-done | bytes 262176 | tf_op jit(solution)/shard_map/ppermute | solution.py:500
  61.8 3.4 %copy-done = bf16[512,8192]{1,0:T(8,128)(2,1)S(1)} copy-done((bf16[512,8192]{1,0:T(8,128)(2,1)S(1)}, bf16[512,8192]{1,0:T(8,128)(2,1)}, u32[]{:S(2)}) %copy-start) | copy-done | bytes 8388632
  65.2 3.1 %out_projection.1 = bf16[32,512]{1,0:T(8,128)(2,1)S(1)} custom-call(s32[2]{0:T(128)S(1)} %pad_add_fusion.place, bf16[512,8192]{1,0:T(8,128)(2,1)S(1)} %copy-done, bf16[32,512]{1,0:T(8,128)(2,1)S(1)} %copy-done.1, bf16[8,32,512]{2,1,0:T(8,128)(2,1)S(1)} %all_to_all.15.mine, bf16[8,32,512]{2,1,0:T(8,128)(2,1)S(1)} %collective-permute-done.8.sibling), custom_call_target="tpu_custom_call" | custom-call | tf_op jit(solution)/shard_map/out_projection/pallas_call | solution.py:385
  68.4 12.6 %all_to_all.16.mine = bf16[8,32,512]{2,1,0:T(8,128)(2,1)S(1)} all-to-all(bf16[8,32,512]{2,1,0:T(8,128)(2,1)S(1)} %broadcast_in_dim.5), channel_id=1, replica_groups=mesh['grp'=2,'tp'=8,'pd'=2] {'tp'}, dimensions={0} | all-to-all | bytes 524288 | tf_op jit(solution)/shard_map/all_to_all | solution.py:540
  81.0 1.5 %collective-permute-done.9.sibling = bf16[8,32,512]{2,1,0:T(8,128)(2,1)S(1)} collective-permute-done((bf16[8,32,512]{2,1,0:T(8,128)(2,1)S(1)}, bf16[8,32,512]{2,1,0:T(8,128)(2,1)S(1)}, u32[]{:S(2)}, u32[]{:S(2)}) %collective-permute-start.9) | collective-permute-done | bytes 262176 | tf_op jit(solution)/shard_map/ppermute | solution.py:500
  82.5 13.0 %feed_forward.1 = (f32[8,32,512]{2,1,0:T(8,128)S(1)}, bf16[8,32,512]{2,1,0:T(8,128)(2,1)S(1)}) custom-call(s32[2]{0:T(128)S(1)} %pad_add_fusion.place, bf16[8,32,512]{2,1,0:T(8,128)(2,1)S(1)} %all_to_all.16.mine, bf16[8,32,512]{2,1,0:T(8,128)(2,1)S(1)} %collective-permute-done.9.sibling, f32[8192]{0:T(1024)S(1)} %copy-done.2, ...), custom_call_target="tpu_custom_call" | custom-call | tf_op jit(solution)/shard_map/feed_forward/pallas_call | solution.py:447
  95.5 0.2 collective-permute-start.10
  95.7 1.4 %collective-permute-done.10 = bf16[8,32,512]{2,1,0:T(8,128)(2,1)S(1)} collective-permute-done((bf16[8,32,512]{2,1,0:T(8,128)(2,1)S(1)}, bf16[8,32,512]{2,1,0:T(8,128)(2,1)S(1)}, u32[]{:S(2)}, u32[]{:S(2)}) %collective-permute-start.10) | collective-permute-done | bytes 262176 | tf_op jit(solution)/shard_map/ppermute | solution.py:500
  97.1 0.1 add_convert_fusion
  97.2 12.6 %all_to_all.17 = bf16[8,32,512]{2,1,0:T(8,128)(2,1)S(1)} all-to-all(bf16[8,32,512]{2,1,0:T(8,128)(2,1)S(1)} %add_convert_fusion), channel_id=1, replica_groups=mesh['grp'=2,'tp'=8,'pd'=2] {'tp'}, dimensions={0} | all-to-all | bytes 524288 | tf_op jit(solution)/shard_map/all_to_all | solution.py:554
  109.8 0.6 add_convert_fusion.1
  (36 shorter events, 0.2 us)
Async XLA Ops:
  6.6 5.3 %collective-permute-start = (bf16[64,2,16,128]{3,2,1,0:T(8,128)(2,1)}, bf16[64,2,16,128]{3,2,1,0:T(8,128)(2,1)S(1)}, u32[]{:S(2)}, u32[]{:S(2)}) collective-permute-start(bf16[64,2,16,128]{3,2,1,0:T(8,128)(2,1)} %get-tuple-element.27.refs_1_), channel_id=1, source_target_pairs={{0,1},{2,3},{4,5},{6,7},{8,9},{10,11},{12,13},{14,15},{16,17},{18,... | collective-permute-start | bytes 1572872 | tf_op jit(solution)/shard_map/ppermute | solution.py:504
  7.9 16.9 %collective-permute-start.2 = (bf16[32,2,16,128]{3,2,1,0:T(8,128)(2,1)}, bf16[32,2,16,128]{3,2,1,0:T(8,128)(2,1)S(1)}, u32[]{:S(2)}, u32[]{:S(2)}) collective-permute-start(bf16[32,2,16,128]{3,2,1,0:T(8,128)(2,1)} %get-tuple-element.28), channel_id=1, source_target_pairs={{0,7},{2,9},{4,11},{6,13},{8,15},{10,1},{12,3},{14,5},{16,23},{18,... | collective-permute-start | bytes 786440 | tf_op jit(solution)/shard_map/ppermute | solution.py:497
  9.2 15.6 %collective-permute-start.3 = (bf16[32,2,16,128]{3,2,1,0:T(8,128)(2,1)}, bf16[32,2,16,128]{3,2,1,0:T(8,128)(2,1)S(1)}, u32[]{:S(2)}, u32[]{:S(2)}) collective-permute-start(bf16[32,2,16,128]{3,2,1,0:T(8,128)(2,1)} %get-tuple-element.29), channel_id=1, source_target_pairs={{0,9},{2,11},{4,13},{6,15},{8,1},{10,3},{12,5},{14,7},{16,25},{18,... | collective-permute-start | bytes 786440 | tf_op jit(solution)/shard_map/ppermute | solution.py:497
  10.5 14.3 %collective-permute-start.4 = (bf16[32,2,16,128]{3,2,1,0:T(8,128)(2,1)}, bf16[32,2,16,128]{3,2,1,0:T(8,128)(2,1)S(1)}, u32[]{:S(2)}, u32[]{:S(2)}) collective-permute-start(bf16[32,2,16,128]{3,2,1,0:T(8,128)(2,1)} %get-tuple-element.30), channel_id=1, source_target_pairs={{0,11},{2,13},{4,15},{6,1},{8,3},{10,5},{12,7},{14,9},{16,27},{18,... | collective-permute-start | bytes 786440 | tf_op jit(solution)/shard_map/ppermute | solution.py:497
  12.9 11.9 %collective-permute-start.5 = (bf16[32,2,16,128]{3,2,1,0:T(8,128)(2,1)S(1)}, bf16[32,2,16,128]{3,2,1,0:T(8,128)(2,1)S(1)}, u32[]{:S(2)}, u32[]{:S(2)}) collective-permute-start(bf16[32,2,16,128]{3,2,1,0:T(8,128)(2,1)S(1)} %get-tuple-element.50), channel_id=1, source_target_pairs={{0,13},{2,15},{4,1},{6,3},{8,5},{10,7},{12,9},{14,11},{1,14},{3,0}... | collective-permute-start | bytes 786440 | tf_op jit(solution)/shard_map/ppermute | solution.py:497
  14.7 12.9 %collective-permute-start.1 = (bf16[32,2,16,128]{3,2,1,0:T(8,128)(2,1)S(1)}, bf16[32,2,16,128]{3,2,1,0:T(8,128)(2,1)S(1)}, u32[]{:S(2)}, u32[]{:S(2)}) collective-permute-start(bf16[32,2,16,128]{3,2,1,0:T(8,128)(2,1)S(1)} %get-tuple-element.51), channel_id=1, source_target_pairs={{0,5},{2,7},{4,9},{6,11},{8,13},{10,15},{12,1},{14,3},{1,2},{3,4},... | collective-permute-start | bytes 786440 | tf_op jit(solution)/shard_map/ppermute | solution.py:497
  17.9 9.7 %copy-start.4 = (bf16[32,2,16,128]{3,2,1,0:T(8,128)(2,1)S(1)}, bf16[32,2,16,128]{3,2,1,0:T(8,128)(2,1)}, u32[]{:S(2)}) copy-start(bf16[32,2,16,128]{3,2,1,0:T(8,128)(2,1)} %get-tuple-element.35) | copy-start | bytes 786436
  17.9 17.2 %copy-start.5 = (bf16[16,2,2,128]{3,2,1,0:T(2,128)(2,1)S(1)}, bf16[16,2,2,128]{3,2,1,0:T(2,128)(2,1)}, u32[]{:S(2)}) copy-start(bf16[16,2,2,128]{3,2,1,0:T(2,128)(2,1)} %param.17) | copy-start | bytes 49156
  17.9 17.3 %copy-start.3 = (bf16[16,2,1024]{2,1,0:T(2,128)(2,1)S(1)}, bf16[16,2,1024]{2,1,0:T(2,128)(2,1)}, u32[]{:S(2)}) copy-start(bf16[16,2,1024]{2,1,0:T(2,128)(2,1)} %param.16) | copy-start | bytes 196612
  18.0 64.5 %slice-start = ((s8[16777216]{0:T(1024)(128)(4,1)}), s8[4194304]{0:T(1024)(128)(4,1)S(1)}, s32[]{:S(2)}) async-start(s8[16777216]{0:T(1024)(128)(4,1)} %bitcast.8), calls=%async_computation.3 | async-start | bytes 8388608
  18.0 64.5 %slice-start.1 = ((s8[16777216]{0:T(1024)(128)(4,1)}), s8[4194304]{0:T(1024)(128)(4,1)S(1)}, s32[]{:S(2)}) async-start(s8[16777216]{0:T(1024)(128)(4,1)} %bitcast.8), calls=%async_computation.4 | async-start | bytes 8388608
  24.8 37.1 %copy-start.1 = (bf16[32,512]{1,0:T(8,128)(2,1)S(1)}, bf16[32,512]{1,0:T(8,128)(2,1)}, u32[]{:S(2)}) copy-start(bf16[32,512]{1,0:T(8,128)(2,1)} %stream.1) | copy-start | bytes 98308
  27.6 54.9 %slice-start.2 = ((s8[16777216]{0:T(1024)(128)(4,1)}), s8[4194304]{0:T(1024)(128)(4,1)S(1)}, s32[]{:S(2)}) async-start(s8[16777216]{0:T(1024)(128)(4,1)} %bitcast.8), calls=%async_computation.5 | async-start | bytes 8388608
  27.7 9.2 %collective-permute-start.6 = (bf16[96,2,16,128]{3,2,1,0:T(8,128)(2,1)S(1)}, bf16[96,2,16,128]{3,2,1,0:T(8,128)(2,1)S(1)}, u32[]{:S(2)}, u32[]{:S(2)}) collective-permute-start(bf16[96,2,16,128]{3,2,1,0:T(8,128)(2,1)S(1)} %pad_maximum_fusion), channel_id=1, source_target_pairs={{0,1},{2,3},{4,5},{6,7},{8,9},{10,11},{12,13},{14,15},{16,17},{18,... | collective-permute-start | bytes 2359304 | tf_op jit(solution)/shard_map/ppermute | solution.py:524
  40.8 3.1 %collective-permute-start.7 = (bf16[32,512]{1,0:T(8,128)(2,1)S(1)}, bf16[32,512]{1,0:T(8,128)(2,1)S(1)}, u32[]{:S(2)}, u32[]{:S(2)}) collective-permute-start(bf16[32,512]{1,0:T(8,128)(2,1)S(1)} %get-tuple-element.43), channel_id=1, source_target_pairs={{1,0},{3,2},{5,4},{7,6},{9,8},{11,10},{13,12},{15,14},{17,16},{19,... | collective-permute-start | bytes 98312 | tf_op jit(solution)/shard_map/ppermute | solution.py:543
  43.9 38.6 %copy-start.2 = (f32[8192]{0:T(1024)S(1)}, f32[8192]{0:T(1024)}, u32[]{:S(2)}) copy-start(f32[8192]{0:T(1024)} %gain.1) | copy-start | bytes 98308
  60.3 22.2 %slice-start.3 = ((s8[16777216]{0:T(1024)(128)(4,1)}), s8[4194304]{0:T(1024)(128)(4,1)S(1)}, s32[]{:S(2)}) async-start(s8[16777216]{0:T(1024)(128)(4,1)} %bitcast.8), calls=%async_computation.6 | async-start | bytes 8388608
  60.3 1.5 %collective-permute-start.8 = (bf16[8,32,512]{2,1,0:T(8,128)(2,1)S(1)}, bf16[8,32,512]{2,1,0:T(8,128)(2,1)S(1)}, u32[]{:S(2)}, u32[]{:S(2)}) collective-permute-start(bf16[8,32,512]{2,1,0:T(8,128)(2,1)S(1)} %all_to_all.15.mine), channel_id=1, source_target_pairs={{0,1},{1,0},{2,3},{3,2},{4,5},{5,4},{6,7},{7,6},{8,9},{9,8},{10,11... | collective-permute-start | bytes 786440 | tf_op jit(solution)/shard_map/ppermute | solution.py:500
  61.8 3.4 %copy-start = (bf16[512,8192]{1,0:T(8,128)(2,1)S(1)}, bf16[512,8192]{1,0:T(8,128)(2,1)}, u32[]{:S(2)}) copy-start(bf16[512,8192]{1,0:T(8,128)(2,1)} %weight.1) | copy-start | bytes 25165828
  81.0 1.5 %collective-permute-start.9 = (bf16[8,32,512]{2,1,0:T(8,128)(2,1)S(1)}, bf16[8,32,512]{2,1,0:T(8,128)(2,1)S(1)}, u32[]{:S(2)}, u32[]{:S(2)}) collective-permute-start(bf16[8,32,512]{2,1,0:T(8,128)(2,1)S(1)} %all_to_all.16.mine), channel_id=1, source_target_pairs={{0,1},{1,0},{2,3},{3,2},{4,5},{5,4},{6,7},{7,6},{8,9},{9,8},{10,11... | collective-permute-start | bytes 786440 | tf_op jit(solution)/shard_map/ppermute | solution.py:500
  95.5 1.6 %collective-permute-start.10 = (bf16[8,32,512]{2,1,0:T(8,128)(2,1)S(1)}, bf16[8,32,512]{2,1,0:T(8,128)(2,1)S(1)}, u32[]{:S(2)}, u32[]{:S(2)}) collective-permute-start(bf16[8,32,512]{2,1,0:T(8,128)(2,1)S(1)} %get-tuple-element.49), channel_id=1, source_target_pairs={{0,1},{1,0},{2,3},{3,2},{4,5},{5,4},{6,7},{7,6},{8,9},{9,8},{10,11... | collective-permute-start | bytes 786440 | tf_op jit(solution)/shard_map/ppermute | solution.py:500

commit v7 on v6

--- a/solution.py
+++ b/solution.py
@@ -57,7 +57,7 @@
         own_copy.wait()
         start = member * slots
 
-        if members <= 8:
+        if members in (4, 8):
             carry = (jnp.int32(0), jnp.int32(0))
             for i in range(parts):
                 loads[i].wait()
@@ -65,7 +65,7 @@
                 def body(j, words, base=i * step):
                     low, high = words
                     entry = own[start + base + j]
-                    ahead = lax.rem((entry >> 8) - member + members + 1, members)
+                    ahead = ((entry >> 8) - member + 1) & (members - 1)
                     leaves = entry >= 0
                     shift = (ahead & 3) * 8
                     is_low = ahead < 4
@@ -77,7 +77,7 @@
                         high + jnp.where(is_low, 0, one),
                     )
 
-                carry = lax.fori_loop(0, step, body, carry, unroll=6)
+                carry = lax.fori_loop(0, step, body, carry, unroll=13)
         else:
             for i in range(parts):
                 loads[i].wait()
@@ -362,34 +362,60 @@
     )
 
 
-def project_kernel(groups, place, weight, stream, mine, sibling, res_out):
-    half = place[1]
+def member_bits(members):
+    offsets = [0]
+    for bit in reversed(range(members.bit_length() - 1)):
+        offsets += [o ^ (1 << bit) for o in offsets]
+    return offsets
+
+
+def project_kernel(groups, place, *refs):
+    *weight, stream, mine, sibling, res_out = refs
+    member, half = place[0], place[1]
     members, tokens, width = mine.shape
-    sums = [stream[g * tokens : (g + 1) * tokens].astype(jnp.float32) for g in range(groups)]
-    for h in range(KVH):
-        for g in range(groups):
-            m = h * groups + g
-            first = jnp.where(half == 0, mine[m], sibling[m])
-            second = jnp.where(half == 0, sibling[m], mine[m])
-            sums[g] = sums[g] + lax.dot_general(
-                jnp.concatenate([first, second], axis=1),
-                weight[:, 2 * h * width : 2 * (h + 1) * width],
+    rows = weight[0].shape[0]
+    sums = [
+        [
+            stream[g * tokens : (g + 1) * tokens, i * rows : (i + 1) * rows].astype(jnp.float32)
+            for g in range(groups)
+        ]
+        for i in range(len(weight))
+    ]
+    for m, offset in enumerate(member_bits(members)):
+        owner = member ^ offset
+        first = jnp.where(half == 0, mine[m], sibling[m])
+        second = jnp.where(half == 0, sibling[m], mine[m])
+        x = jnp.concatenate([first, second], axis=1)
+        head = pl.ds(pl.multiple_of(owner // groups * 2 * width, 2 * width), 2 * width)
+        for i in range(len(weight)):
+            part = lax.dot_general(
+                x,
+                weight[i][:, head],
                 (((1,), (1,)), ((), ())),
                 preferred_element_type=jnp.float32,
             )
-    for g in range(groups):
-        res_out[g * tokens : (g + 1) * tokens] = sums[g].astype(res_out.dtype)
+            for g in range(groups):
+                if groups > 1:
+                    part_g = jnp.where(lax.rem(owner, groups) == g, part, 0.0)
+                else:
+                    part_g = part
+                sums[i][g] = sums[i][g] + part_g
+    for i in range(len(weight)):
+        for g in range(groups):
+            res_out[g * tokens : (g + 1) * tokens, i * rows : (i + 1) * rows] = sums[i][g].astype(
+                res_out.dtype
+            )
 
 
 def project(place, weight, stream, mine, sibling, groups):
     return pl.pallas_call(
         functools.partial(project_kernel, groups),
         out_shape=jax.ShapeDtypeStruct(stream.shape, jnp.bfloat16),
-        in_specs=[SM, VM, VM, VM, VM],
+        in_specs=[SM] + [VM] * (len(weight) + 3),
         out_specs=VM,
-        compiler_params=pltpu.CompilerParams(vmem_limit_bytes=4 * MIB),
+        compiler_params=pltpu.CompilerParams(vmem_limit_bytes=9 * MIB),
         name="out_projection",
-    )(place, in_vmem(weight), stream, mine, sibling)
+    )(place, *map(in_vmem, weight), stream, mine, sibling)
 
 
 def ffn_kernel(place, mine, sibling, gain, gate, *refs):
@@ -413,11 +439,12 @@
             x = block[t].astype(jnp.float32)
             square = square + x * x
     factor = lax.rsqrt(jnp.sum(square, axis=1, keepdims=True) / features + 1e-05)
-    for t in range(members):
+    for t, offset in enumerate(member_bits(members)):
         first = jnp.where(half == 0, mine[t], sibling[t])
         second = jnp.where(half == 0, sibling[t], mine[t])
         x = jnp.concatenate([first, second], axis=1).astype(jnp.float32)
-        cols = slice(2 * t * width, 2 * (t + 1) * width)
+        owner = place[0] ^ offset
+        cols = pl.ds(pl.multiple_of(owner * 2 * width, 2 * width), 2 * width)
         normed[:, cols] = (x * factor * gain[cols][None, :]).astype(jnp.bfloat16)
     tile = min(256, hidden_count)
     for f in range(hidden_count // tile):
@@ -516,7 +543,7 @@
         block_tables,
         page_list.reshape(members, slots),
         groups,
-        ((up_weight, SPLIT),),
+        ((out_proj, 2), (up_weight, SPLIT)),
         (near,),
     )
 
@@ -536,19 +563,21 @@
     )
 
     def everywhere(x):
-        spread = jnp.broadcast_to(x[None], (members, *x.shape))
-        mine = lax.all_to_all(spread, "tp", split_axis=0, concat_axis=0)
-        return mine, swap(mine)
+        blocks = x[None]
+        for bit in reversed(range(members.bit_length() - 1)):
+            route = [(t, t ^ (1 << bit)) for t in range(members)]
+            blocks = jnp.concatenate([blocks, lax.ppermute(blocks, "tp", route)])
+        return blocks, swap(blocks)
 
     att_mine = att_high + lax.ppermute(att_low, "pd", [(1, 0)])
     here, there = everywhere(att_mine)
 
     inner = stream.reshape(steps, groups, rows, -1).transpose(1, 0, 2, 3).reshape(stream.shape)
-    residual = project(place, out_proj, inner, here, there, groups)
+    residual = project(place, held[:2], inner, here, there, groups)
 
     mine, sibling = everywhere(residual)
     own, other = feed_forward(
-        place, mine, sibling, norm_gain, gate_weight, held, down_weight
+        place, mine, sibling, norm_gain, gate_weight, held[2:], down_weight
     )
     summed = (own + swap(other).astype(jnp.float32)).astype(jnp.bfloat16)
     shares = lax.all_to_all(summed, "tp", split_axis=0, concat_axis=0)

time: 111 us -> 111 us (level)
  blocking collectives: 41.6 us -> 12.4 us
  waiting for transfers between devices: 10.7 us -> 26.6 us
  starting transfers between devices: 18.3 us -> 30.4 us
  Pallas kernels: 32.5 us -> 34.9 us
  local copies, waits for them, and re-layouts: 4.45 us -> 3.14 us
    all_to_all x2 -> x0, blocking collectives: 29 us -> none  [everywhere(): mine = lax.all_to_all(spread, 'tp', split_axis=0, concat_axis=0)]
    ppermute x0 -> x6, waiting for transfers between devices: none -> 18.9 us  [everywhere(): blocks = jnp.concatenate([blocks, lax.ppermute(blocks, 'tp', route)])]
    ppermute x0 -> x6, starting transfers between devices: none -> 13.5 us  [everywhere(): blocks = jnp.concatenate([blocks, lax.ppermute(blocks, 'tp', route)])]
    ppermute x5, waiting for transfers between devices: 2.82 us -> 0.01 us  [send(): return lax.ppermute(x, BOTH, route)]
    pallas_call x1, Pallas kernels: 6.77 us -> 9.18 us  [prepare(): pl.pallas_call(functools.partial(prepare_kernel, count, parts, groups), o...]
    ppermute x1, starting transfers between devices: 7.37 us -> 5.62 us  [local(): lax.ppermute(jnp.concatenate([own_chunk] + [arrived[host] for host in hos...]
    unnamed x22 -> x24, local copies, waits for them, and re-layouts: 3.45 us -> 2.19 us
  transfers between devices with their start and end apart: 11 -> 17, of which waited for: 6 -> 11; matrix products, arithmetic and copies ran while one was open for 2% -> 2% of each run, Pallas kernels for 6% -> 8%
where the time goes in v7:
time: 111 us
  Pallas kernels  34.9 us (31%)
  starting transfers between devices  30.4 us (27%)
  waiting for transfers between devices  26.6 us (24%)
  blocking collectives  12.4 us (11%)
  local copies, waits for them, and re-layouts  3.14 us (3%)
  other arithmetic  2.11 us (2%)
    ppermute x6, waiting for transfers between devices, everywhere(): blocks = jnp.concatenate([blocks, lax.ppermute(blocks, 'tp', route)])  18.9 us
    ppermute x6, starting transfers between devices, everywhere(): blocks = jnp.concatenate([blocks, lax.ppermute(blocks, 'tp', route)])  13.5 us
    pallas_call x1, Pallas kernels, feed_forward(): pl.pallas_call(ffn_kernel, out_shape=[jax.ShapeDtypeStruct(mine.shape, jn...  13.1 us
    all_to_all x1, blocking collectives, local(): shares = lax.all_to_all(summed, 'tp', split_axis=0, concat_axis=0)  12.4 us
    pallas_call x1, Pallas kernels, prepare(): pl.pallas_call(functools.partial(prepare_kernel, count, parts, groups), o...  9.18 us
    ppermute x5, starting transfers between devices, send(): return lax.ppermute(x, BOTH, route)  8.12 us
    ppermute x1, starting transfers between devices, local(): lax.ppermute(jnp.concatenate([own_chunk] + [arrived[host] for host in hos...  5.62 us
    pallas_call x1, Pallas kernels, pack(): pl.pallas_call(functools.partial(pack_kernel, members), out_shape=[pltpu....  5.45 us
  transfers between devices with their start and end apart: 17, of which 11 were waited for; matrix products, arithmetic and copies ran while one was open for 2% of the time, Pallas kernels for 8%

profile of v7, /device:TPU:0, one launch (start us, length us, event | category | flops | bytes accessed | tf_op | source)
XLA Modules:
  0.0 110.6 jit_solution(12428123543699967027)
XLA Ops:
  0.7 5.4 %pack_pages.1 = (bf16[64,2,16,128]{3,2,1,0:T(8,128)(2,1)}, bf16[32,2,16,128]{3,2,1,0:T(8,128)(2,1)}, bf16[32,2,16,128]{3,2,1,0:T(8,128)(2,1)}, bf16[32,2,16,128]...) custom-call(s32[2]{0:T(128)S(1)} %pad_add_fusion.place, ...), custom_call_target="tpu_custom_call" | custom-call | tf_op jit(solution)/shard_map/pack_pages/pallas_call | solution.py:119
  6.2 1.3 %collective-permute-start = (bf16[64,2,16,128]{3,2,1,0:T(8,128)(2,1)}, bf16[64,2,16,128]{3,2,1,0:T(8,128)(2,1)S(1)}, u32[]{:S(2)}, u32[]{:S(2)}) collective-permute-start(bf16[64,2,16,128]{3,2,1,0:T(8,128)(2,1)} %get-tuple-element.29.refs_2_), channel_id=1, source_target_pairs={{0,1},{2,3},{4,5},{6,7},{8,9},{10,11},{12,13},{14,15},{16,17},{18,... | collective-permute-start | bytes 1572872 | tf_op jit(solution)/shard_map/ppermute | solution.py:531
  7.5 1.3 %collective-permute-start.2 = (bf16[32,2,16,128]{3,2,1,0:T(8,128)(2,1)}, bf16[32,2,16,128]{3,2,1,0:T(8,128)(2,1)S(1)}, u32[]{:S(2)}, u32[]{:S(2)}) collective-permute-start(bf16[32,2,16,128]{3,2,1,0:T(8,128)(2,1)} %get-tuple-element.30), channel_id=1, source_target_pairs={{0,7},{2,9},{4,11},{6,13},{8,15},{10,1},{12,3},{14,5},{16,23},{18,... | collective-permute-start | bytes 786440 | tf_op jit(solution)/shard_map/ppermute | solution.py:524
  8.8 1.3 %collective-permute-start.3 = (bf16[32,2,16,128]{3,2,1,0:T(8,128)(2,1)}, bf16[32,2,16,128]{3,2,1,0:T(8,128)(2,1)S(1)}, u32[]{:S(2)}, u32[]{:S(2)}) collective-permute-start(bf16[32,2,16,128]{3,2,1,0:T(8,128)(2,1)} %get-tuple-element.31), channel_id=1, source_target_pairs={{0,9},{2,11},{4,13},{6,15},{8,1},{10,3},{12,5},{14,7},{16,25},{18,... | collective-permute-start | bytes 786440 | tf_op jit(solution)/shard_map/ppermute | solution.py:524
  10.1 1.5 %collective-permute-start.4 = (bf16[32,2,16,128]{3,2,1,0:T(8,128)(2,1)}, bf16[32,2,16,128]{3,2,1,0:T(8,128)(2,1)S(1)}, u32[]{:S(2)}, u32[]{:S(2)}) collective-permute-start(bf16[32,2,16,128]{3,2,1,0:T(8,128)(2,1)} %get-tuple-element.32), channel_id=1, source_target_pairs={{0,11},{2,13},{4,15},{6,1},{8,3},{10,5},{12,7},{14,9},{16,27},{18,... | collective-permute-start | bytes 786440 | tf_op jit(solution)/shard_map/ppermute | solution.py:524
  11.7 1.1 slice_select_fusion
  12.8 1.6 %collective-permute-start.5 = (bf16[32,2,16,128]{3,2,1,0:T(8,128)(2,1)S(1)}, bf16[32,2,16,128]{3,2,1,0:T(8,128)(2,1)S(1)}, u32[]{:S(2)}, u32[]{:S(2)}) collective-permute-start(bf16[32,2,16,128]{3,2,1,0:T(8,128)(2,1)S(1)} %get-tuple-element.54), channel_id=1, source_target_pairs={{0,13},{2,15},{4,1},{6,3},{8,5},{10,7},{12,9},{14,11},{1,14},{3,0}... | collective-permute-start | bytes 786440 | tf_op jit(solution)/shard_map/ppermute | solution.py:524
  14.3 2.4 %collective-permute-start.1 = (bf16[32,2,16,128]{3,2,1,0:T(8,128)(2,1)S(1)}, bf16[32,2,16,128]{3,2,1,0:T(8,128)(2,1)S(1)}, u32[]{:S(2)}, u32[]{:S(2)}) collective-permute-start(bf16[32,2,16,128]{3,2,1,0:T(8,128)(2,1)S(1)} %get-tuple-element.55), channel_id=1, source_target_pairs={{0,5},{2,7},{4,9},{6,11},{8,13},{10,15},{12,1},{14,3},{1,2},{3,4},... | collective-permute-start | bytes 786440 | tf_op jit(solution)/shard_map/ppermute | solution.py:524
  16.7 0.8 reshape.7.listed
  17.6 9.2 %prepare.1 = (bf16[256,8192]{1,0:T(8,128)(2,1)S(1)}, bf16[256,8192]{1,0:T(8,128)(2,1)S(1)}, bf16[2048,1024]{1,0:T(8,128)(2,1)S(1)}, bf16[2048,1024]{1,0:T(8,128)...) custom-call(s32[2]{0:T(128)S(1)} %pad_add_fusion.place, ...), custom_call_target="tpu_custom_call" | custom-call | bytes 25165824 | tf_op jit(solution)/shard_map/prepare/pallas_call | solution.py:228
  26.8 2.1 %copy-done = bf16[256,8192]{1,0:T(8,128)(2,1)} copy-done((bf16[256,8192]{1,0:T(8,128)(2,1)}, bf16[256,8192]{1,0:T(8,128)(2,1)S(1)}, u32[]{:S(2)}) %copy-start) | copy-done | bytes 4194328
  29.1 5.6 %collective-permute-start.6 = (bf16[96,2,16,128]{3,2,1,0:T(8,128)(2,1)S(1)}, bf16[96,2,16,128]{3,2,1,0:T(8,128)(2,1)S(1)}, u32[]{:S(2)}, u32[]{:S(2)}) collective-permute-start(bf16[96,2,16,128]{3,2,1,0:T(8,128)(2,1)S(1)} %pad_maximum_fusion), channel_id=1, source_target_pairs={{0,1},{2,3},{4,5},{6,7},{8,9},{10,11},{12,13},{14,15},{16,17},{18,... | collective-permute-start | bytes 2359304 | tf_op jit(solution)/shard_map/ppermute | solution.py:551
  35.0 1.6 %collective-permute-done.6.refs_2_ = bf16[96,2,16,128]{3,2,1,0:T(8,128)(2,1)S(1)} collective-permute-done((bf16[96,2,16,128]{3,2,1,0:T(8,128)(2,1)S(1)}, bf16[96,2,16,128]{3,2,1,0:T(8,128)(2,1)S(1)}, u32[]{:S(2)}, u32[]{:S(2)}) %collective-permute-start.6) | collective-permute-done | bytes 786464 | tf_op jit(solution)/shard_map/ppermute | solution.py:551
  36.6 4.1 %place_attend.1 = (bf16[312,2,16,128]{3,2,1,0:T(8,128)(2,1)}, bf16[32,512]{1,0:T(8,128)(2,1)S(1)}, bf16[32,512]{1,0:T(8,128)(2,1)S(1)}) custom-call(s32[2]{0:T(128)S(1)} %pad_add_fusion.place, s32[8,128]{1,0:T(8,128)S(1)} %get-tuple-element.35.landing, bf16[312,2,16,128]{3,2,1,0:T(8,128)(2,1)} %old_pool.1, f32[16,4992]{1,0:T(8,128)S(1)} %get-tuple-element.36.bias, ...), custom_call_target="tpu_custom_call" | custom-call | tf_op jit(solution)/shard_map/place_attend/pallas_call | solution.py:337
  40.7 1.5 %collective-permute-start.7 = (bf16[32,512]{1,0:T(8,128)(2,1)S(1)}, bf16[32,512]{1,0:T(8,128)(2,1)S(1)}, u32[]{:S(2)}, u32[]{:S(2)}) collective-permute-start(bf16[32,512]{1,0:T(8,128)(2,1)S(1)} %get-tuple-element.47), channel_id=1, source_target_pairs={{1,0},{3,2},{5,4},{7,6},{9,8},{11,10},{13,12},{15,14},{17,16},{19,... | collective-permute-start | bytes 98312 | tf_op jit(solution)/shard_map/ppermute | solution.py:572
  42.2 1.6 %collective-permute-done.7 = bf16[32,512]{1,0:T(8,128)(2,1)S(1)} collective-permute-done((bf16[32,512]{1,0:T(8,128)(2,1)S(1)}, bf16[32,512]{1,0:T(8,128)(2,1)S(1)}, u32[]{:S(2)}, u32[]{:S(2)}) %collective-permute-start.7) | collective-permute-done | bytes 32800 | tf_op jit(solution)/shard_map/ppermute | solution.py:572
  43.8 5.2 %collective-permute-start.8 = (bf16[1,32,512]{2,1,0:T(8,128)(2,1)S(1)}, bf16[1,32,512]{2,1,0:T(8,128)(2,1)S(1)}, u32[]{:S(2)}, u32[]{:S(2)}) collective-permute-start(bf16[1,32,512]{2,1,0:T(8,128)(2,1)S(1)} %add_bitcast_fusion), channel_id=1, source_target_pairs={{0,8},{2,10},{4,12},{6,14},{8,0},{10,2},{12,4},{14,6},{1,9},{3,11}... | collective-permute-start | bytes 98312 | tf_op jit(solution)/shard_map/ppermute | solution.py:569
  49.0 1.9 %collective-permute-done.8 = bf16[1,32,512]{2,1,0:T(8,128)(2,1)S(1)} collective-permute-done((bf16[1,32,512]{2,1,0:T(8,128)(2,1)S(1)}, bf16[1,32,512]{2,1,0:T(8,128)(2,1)S(1)}, u32[]{:S(2)}, u32[]{:S(2)}) %collective-permute-start.8) | collective-permute-done | bytes 32800 | tf_op jit(solution)/shard_map/ppermute | solution.py:569
  50.9 3.9 %collective-permute-start.9 = (bf16[2,32,512]{2,1,0:T(8,128)(2,1)S(1)}, bf16[2,32,512]{2,1,0:T(8,128)(2,1)S(1)}, u32[]{:S(2)}, u32[]{:S(2)}) collective-permute-start(bf16[2,32,512]{2,1,0:T(8,128)(2,1)S(1)} %pad_maximum_fusion.5), channel_id=1, source_target_pairs={{0,4},{2,6},{4,0},{6,2},{8,12},{10,14},{12,8},{14,10},{1,5},{3,7},... | collective-permute-start | bytes 196616 | tf_op jit(solution)/shard_map/ppermute | solution.py:569
  54.7 2.2 %collective-permute-done.9 = bf16[2,32,512]{2,1,0:T(8,128)(2,1)S(1)} collective-permute-done((bf16[2,32,512]{2,1,0:T(8,128)(2,1)S(1)}, bf16[2,32,512]{2,1,0:T(8,128)(2,1)S(1)}, u32[]{:S(2)}, u32[]{:S(2)}) %collective-permute-start.9) | collective-permute-done | bytes 65568 | tf_op jit(solution)/shard_map/ppermute | solution.py:569
  57.6 4.4 %collective-permute-done.10 = bf16[4,32,512]{2,1,0:T(8,128)(2,1)S(1)} collective-permute-done((bf16[4,32,512]{2,1,0:T(8,128)(2,1)S(1)}, bf16[4,32,512]{2,1,0:T(8,128)(2,1)S(1)}, u32[]{:S(2)}, u32[]{:S(2)}) %collective-permute-start.10) | collective-permute-done | bytes 131104 | tf_op jit(solution)/shard_map/ppermute | solution.py:569
  62.1 1.5 %collective-permute-done.11.refs_4_ = bf16[8,32,512]{2,1,0:T(8,128)(2,1)S(1)} collective-permute-done((bf16[8,32,512]{2,1,0:T(8,128)(2,1)S(1)}, bf16[8,32,512]{2,1,0:T(8,128)(2,1)S(1)}, u32[]{:S(2)}, u32[]{:S(2)}) %collective-permute-start.11) | collective-permute-done | bytes 262176 | tf_op jit(solution)/shard_map/ppermute | solution.py:527
  63.7 3.1 %out_projection.1 = bf16[32,512]{1,0:T(8,128)(2,1)S(1)} custom-call(s32[2]{0:T(128)S(1)} %pad_add_fusion.place, bf16[256,8192]{1,0:T(8,128)(2,1)S(1)} %get-tuple-element.44.refs_0_, bf16[256,8192]{1,0:T(8,128)(2,1)S(1)} %copy-done.1, bf16[32,512]{1,0:T(8,128)(2,1)S(1)} %copy-done.2, bf16[8,32,512]{2,1,0:T(8,128)(2,1)S(1)} %pad_maximum_fusion.1.refs_3_, ...), custom_call_target="tpu_custom_call" | custom-call | tf_op jit(solution)/shard_map/out_projection/pallas_call | solution.py:411
  66.8 1.2 %collective-permute-start.12 = (bf16[1,32,512]{2,1,0:T(8,128)(2,1)S(1)}, bf16[1,32,512]{2,1,0:T(8,128)(2,1)S(1)}, u32[]{:S(2)}, u32[]{:S(2)}) collective-permute-start(bf16[1,32,512]{2,1,0:T(8,128)(2,1)S(1)} %bitcast.13), channel_id=1, source_target_pairs={{0,8},{2,10},{4,12},{6,14},{8,0},{10,2},{12,4},{14,6},{1,9},{3,11}... | collective-permute-start | bytes 98312 | tf_op jit(solution)/shard_map/ppermute | solution.py:569
  68.0 3.7 %collective-permute-done.12 = bf16[1,32,512]{2,1,0:T(8,128)(2,1)S(1)} collective-permute-done((bf16[1,32,512]{2,1,0:T(8,128)(2,1)S(1)}, bf16[1,32,512]{2,1,0:T(8,128)(2,1)S(1)}, u32[]{:S(2)}, u32[]{:S(2)}) %collective-permute-start.12) | collective-permute-done | bytes 32800 | tf_op jit(solution)/shard_map/ppermute | solution.py:569
  71.6 2.1 %collective-permute-start.13 = (bf16[2,32,512]{2,1,0:T(8,128)(2,1)S(1)}, bf16[2,32,512]{2,1,0:T(8,128)(2,1)S(1)}, u32[]{:S(2)}, u32[]{:S(2)}) collective-permute-start(bf16[2,32,512]{2,1,0:T(8,128)(2,1)S(1)} %pad_maximum_fusion.6), channel_id=1, source_target_pairs={{0,4},{2,6},{4,0},{6,2},{8,12},{10,14},{12,8},{14,10},{1,5},{3,7},... | collective-permute-start | bytes 196616 | tf_op jit(solution)/shard_map/ppermute | solution.py:569
  73.7 2.2 %collective-permute-done.13 = bf16[2,32,512]{2,1,0:T(8,128)(2,1)S(1)} collective-permute-done((bf16[2,32,512]{2,1,0:T(8,128)(2,1)S(1)}, bf16[2,32,512]{2,1,0:T(8,128)(2,1)S(1)}, u32[]{:S(2)}, u32[]{:S(2)}) %collective-permute-start.13) | collective-permute-done | bytes 65568 | tf_op jit(solution)/shard_map/ppermute | solution.py:569
  76.6 4.4 %collective-permute-done.14 = bf16[4,32,512]{2,1,0:T(8,128)(2,1)S(1)} collective-permute-done((bf16[4,32,512]{2,1,0:T(8,128)(2,1)S(1)}, bf16[4,32,512]{2,1,0:T(8,128)(2,1)S(1)}, u32[]{:S(2)}, u32[]{:S(2)}) %collective-permute-start.14) | collective-permute-done | bytes 131104 | tf_op jit(solution)/shard_map/ppermute | solution.py:569
  81.1 1.5 %collective-permute-done.15.sibling = bf16[8,32,512]{2,1,0:T(8,128)(2,1)S(1)} collective-permute-done((bf16[8,32,512]{2,1,0:T(8,128)(2,1)S(1)}, bf16[8,32,512]{2,1,0:T(8,128)(2,1)S(1)}, u32[]{:S(2)}, u32[]{:S(2)}) %collective-permute-start.15) | collective-permute-done | bytes 262176 | tf_op jit(solution)/shard_map/ppermute | solution.py:527
  82.7 13.1 %feed_forward.1 = (f32[8,32,512]{2,1,0:T(8,128)S(1)}, bf16[8,32,512]{2,1,0:T(8,128)(2,1)S(1)}) custom-call(s32[2]{0:T(128)S(1)} %pad_add_fusion.place, bf16[8,32,512]{2,1,0:T(8,128)(2,1)S(1)} %pad_maximum_fusion.2.mine, bf16[8,32,512]{2,1,0:T(8,128)(2,1)S(1)} %collective-permute-done.15.sibling, f32[8192]{0:T(1024)S(1)} %copy-done.3, ...), custom_call_target="tpu_custom_call" | custom-call | tf_op jit(solution)/shard_map/feed_forward/pallas_call | solution.py:474
  96.0 1.4 %collective-permute-done.16 = bf16[8,32,512]{2,1,0:T(8,128)(2,1)S(1)} collective-permute-done((bf16[8,32,512]{2,1,0:T(8,128)(2,1)S(1)}, bf16[8,32,512]{2,1,0:T(8,128)(2,1)S(1)}, u32[]{:S(2)}, u32[]{:S(2)}) %collective-permute-start.16) | collective-permute-done | bytes 262176 | tf_op jit(solution)/shard_map/ppermute | solution.py:527
  97.5 12.4 %all_to_all.5 = bf16[8,32,512]{2,1,0:T(8,128)(2,1)S(1)} all-to-all(bf16[8,32,512]{2,1,0:T(8,128)(2,1)S(1)} %add_convert_fusion), channel_id=1, replica_groups=mesh['grp'=2,'tp'=8,'pd'=2] {'tp'}, dimensions={0} | all-to-all | bytes 524288 | tf_op jit(solution)/shard_map/all_to_all | solution.py:583
  (52 shorter events, 2.8 us)
Async XLA Ops:
  6.2 5.5 %collective-permute-start = (bf16[64,2,16,128]{3,2,1,0:T(8,128)(2,1)}, bf16[64,2,16,128]{3,2,1,0:T(8,128)(2,1)S(1)}, u32[]{:S(2)}, u32[]{:S(2)}) collective-permute-start(bf16[64,2,16,128]{3,2,1,0:T(8,128)(2,1)} %get-tuple-element.29.refs_2_), channel_id=1, source_target_pairs={{0,1},{2,3},{4,5},{6,7},{8,9},{10,11},{12,13},{14,15},{16,17},{18,... | collective-permute-start | bytes 1572872 | tf_op jit(solution)/shard_map/ppermute | solution.py:531
  7.5 21.4 %collective-permute-start.2 = (bf16[32,2,16,128]{3,2,1,0:T(8,128)(2,1)}, bf16[32,2,16,128]{3,2,1,0:T(8,128)(2,1)S(1)}, u32[]{:S(2)}, u32[]{:S(2)}) collective-permute-start(bf16[32,2,16,128]{3,2,1,0:T(8,128)(2,1)} %get-tuple-element.30), channel_id=1, source_target_pairs={{0,7},{2,9},{4,11},{6,13},{8,15},{10,1},{12,3},{14,5},{16,23},{18,... | collective-permute-start | bytes 786440 | tf_op jit(solution)/shard_map/ppermute | solution.py:524
  8.8 20.1 %collective-permute-start.3 = (bf16[32,2,16,128]{3,2,1,0:T(8,128)(2,1)}, bf16[32,2,16,128]{3,2,1,0:T(8,128)(2,1)S(1)}, u32[]{:S(2)}, u32[]{:S(2)}) collective-permute-start(bf16[32,2,16,128]{3,2,1,0:T(8,128)(2,1)} %get-tuple-element.31), channel_id=1, source_target_pairs={{0,9},{2,11},{4,13},{6,15},{8,1},{10,3},{12,5},{14,7},{16,25},{18,... | collective-permute-start | bytes 786440 | tf_op jit(solution)/shard_map/ppermute | solution.py:524
  10.1 18.8 %collective-permute-start.4 = (bf16[32,2,16,128]{3,2,1,0:T(8,128)(2,1)}, bf16[32,2,16,128]{3,2,1,0:T(8,128)(2,1)S(1)}, u32[]{:S(2)}, u32[]{:S(2)}) collective-permute-start(bf16[32,2,16,128]{3,2,1,0:T(8,128)(2,1)} %get-tuple-element.32), channel_id=1, source_target_pairs={{0,11},{2,13},{4,15},{6,1},{8,3},{10,5},{12,7},{14,9},{16,27},{18,... | collective-permute-start | bytes 786440 | tf_op jit(solution)/shard_map/ppermute | solution.py:524
  12.8 16.2 %collective-permute-start.5 = (bf16[32,2,16,128]{3,2,1,0:T(8,128)(2,1)S(1)}, bf16[32,2,16,128]{3,2,1,0:T(8,128)(2,1)S(1)}, u32[]{:S(2)}, u32[]{:S(2)}) collective-permute-start(bf16[32,2,16,128]{3,2,1,0:T(8,128)(2,1)S(1)} %get-tuple-element.54), channel_id=1, source_target_pairs={{0,13},{2,15},{4,1},{6,3},{8,5},{10,7},{12,9},{14,11},{1,14},{3,0}... | collective-permute-start | bytes 786440 | tf_op jit(solution)/shard_map/ppermute | solution.py:524
  14.3 14.6 %collective-permute-start.1 = (bf16[32,2,16,128]{3,2,1,0:T(8,128)(2,1)S(1)}, bf16[32,2,16,128]{3,2,1,0:T(8,128)(2,1)S(1)}, u32[]{:S(2)}, u32[]{:S(2)}) collective-permute-start(bf16[32,2,16,128]{3,2,1,0:T(8,128)(2,1)S(1)} %get-tuple-element.55), channel_id=1, source_target_pairs={{0,5},{2,7},{4,9},{6,11},{8,13},{10,15},{12,1},{14,3},{1,2},{3,4},... | collective-permute-start | bytes 786440 | tf_op jit(solution)/shard_map/ppermute | solution.py:524
  17.5 11.4 %copy-start.5 = (bf16[32,2,16,128]{3,2,1,0:T(8,128)(2,1)S(1)}, bf16[32,2,16,128]{3,2,1,0:T(8,128)(2,1)}, u32[]{:S(2)}) copy-start(bf16[32,2,16,128]{3,2,1,0:T(8,128)(2,1)} %get-tuple-element.37) | copy-start | bytes 786436
  17.5 17.2 %copy-start.6 = (bf16[16,2,2,128]{3,2,1,0:T(2,128)(2,1)S(1)}, bf16[16,2,2,128]{3,2,1,0:T(2,128)(2,1)}, u32[]{:S(2)}) copy-start(bf16[16,2,2,128]{3,2,1,0:T(2,128)(2,1)} %param.17) | copy-start | bytes 49156
  17.6 17.3 %copy-start.4 = (bf16[16,2,1024]{2,1,0:T(2,128)(2,1)S(1)}, bf16[16,2,1024]{2,1,0:T(2,128)(2,1)}, u32[]{:S(2)}) copy-start(bf16[16,2,1024]{2,1,0:T(2,128)(2,1)} %param.16) | copy-start | bytes 196612
  17.6 65.1 %slice-start = ((s8[16777216]{0:T(1024)(128)(4,1)}), s8[4194304]{0:T(1024)(128)(4,1)S(1)}, s32[]{:S(2)}) async-start(s8[16777216]{0:T(1024)(128)(4,1)} %bitcast.11), calls=%async_computation.1 | async-start | bytes 8388608
  17.6 65.1 %slice-start.1 = ((s8[16777216]{0:T(1024)(128)(4,1)}), s8[4194304]{0:T(1024)(128)(4,1)S(1)}, s32[]{:S(2)}) async-start(s8[16777216]{0:T(1024)(128)(4,1)} %bitcast.11), calls=%async_computation.2 | async-start | bytes 8388608
  17.6 65.1 %slice-start.2 = ((s8[16777216]{0:T(1024)(128)(4,1)}), s8[4194304]{0:T(1024)(128)(4,1)S(1)}, s32[]{:S(2)}) async-start(s8[16777216]{0:T(1024)(128)(4,1)} %bitcast.11), calls=%async_computation.3 | async-start | bytes 8388608
  26.8 2.1 %copy-start = (bf16[256,8192]{1,0:T(8,128)(2,1)}, bf16[256,8192]{1,0:T(8,128)(2,1)S(1)}, u32[]{:S(2)}) copy-start(bf16[256,8192]{1,0:T(8,128)(2,1)S(1)} %get-tuple-element.45.refs_1_) | copy-start | bytes 12582916
  28.9 34.7 %copy-start.2 = (bf16[32,512]{1,0:T(8,128)(2,1)S(1)}, bf16[32,512]{1,0:T(8,128)(2,1)}, u32[]{:S(2)}) copy-start(bf16[32,512]{1,0:T(8,128)(2,1)} %refs_2_.1) | copy-start | bytes 98308
  29.1 34.6 %copy-start.1 = (bf16[256,8192]{1,0:T(8,128)(2,1)S(1)}, bf16[256,8192]{1,0:T(8,128)(2,1)}, u32[]{:S(2)}) copy-start(bf16[256,8192]{1,0:T(8,128)(2,1)} %copy-done) | copy-start | bytes 12582916
  29.1 7.5 %collective-permute-start.6 = (bf16[96,2,16,128]{3,2,1,0:T(8,128)(2,1)S(1)}, bf16[96,2,16,128]{3,2,1,0:T(8,128)(2,1)S(1)}, u32[]{:S(2)}, u32[]{:S(2)}) collective-permute-start(bf16[96,2,16,128]{3,2,1,0:T(8,128)(2,1)S(1)} %pad_maximum_fusion), channel_id=1, source_target_pairs={{0,1},{2,3},{4,5},{6,7},{8,9},{10,11},{12,13},{14,15},{16,17},{18,... | collective-permute-start | bytes 2359304 | tf_op jit(solution)/shard_map/ppermute | solution.py:551
  36.6 46.1 %slice-start.3 = ((s8[16777216]{0:T(1024)(128)(4,1)}), s8[4194304]{0:T(1024)(128)(4,1)S(1)}, s32[]{:S(2)}) async-start(s8[16777216]{0:T(1024)(128)(4,1)} %bitcast.11), calls=%async_computation.4 | async-start | bytes 8388608
  40.7 3.1 %collective-permute-start.7 = (bf16[32,512]{1,0:T(8,128)(2,1)S(1)}, bf16[32,512]{1,0:T(8,128)(2,1)S(1)}, u32[]{:S(2)}, u32[]{:S(2)}) collective-permute-start(bf16[32,512]{1,0:T(8,128)(2,1)S(1)} %get-tuple-element.47), channel_id=1, source_target_pairs={{1,0},{3,2},{5,4},{7,6},{9,8},{11,10},{13,12},{15,14},{17,16},{19,... | collective-permute-start | bytes 98312 | tf_op jit(solution)/shard_map/ppermute | solution.py:572
  43.8 7.1 %collective-permute-start.8 = (bf16[1,32,512]{2,1,0:T(8,128)(2,1)S(1)}, bf16[1,32,512]{2,1,0:T(8,128)(2,1)S(1)}, u32[]{:S(2)}, u32[]{:S(2)}) collective-permute-start(bf16[1,32,512]{2,1,0:T(8,128)(2,1)S(1)} %add_bitcast_fusion), channel_id=1, source_target_pairs={{0,8},{2,10},{4,12},{6,14},{8,0},{10,2},{12,4},{14,6},{1,9},{3,11}... | collective-permute-start | bytes 98312 | tf_op jit(solution)/shard_map/ppermute | solution.py:569
  50.9 6.1 %collective-permute-start.9 = (bf16[2,32,512]{2,1,0:T(8,128)(2,1)S(1)}, bf16[2,32,512]{2,1,0:T(8,128)(2,1)S(1)}, u32[]{:S(2)}, u32[]{:S(2)}) collective-permute-start(bf16[2,32,512]{2,1,0:T(8,128)(2,1)S(1)} %pad_maximum_fusion.5), channel_id=1, source_target_pairs={{0,4},{2,6},{4,0},{6,2},{8,12},{10,14},{12,8},{14,10},{1,5},{3,7},... | collective-permute-start | bytes 196616 | tf_op jit(solution)/shard_map/ppermute | solution.py:569
  57.0 5.0 %collective-permute-start.10 = (bf16[4,32,512]{2,1,0:T(8,128)(2,1)S(1)}, bf16[4,32,512]{2,1,0:T(8,128)(2,1)S(1)}, u32[]{:S(2)}, u32[]{:S(2)}) collective-permute-start(bf16[4,32,512]{2,1,0:T(8,128)(2,1)S(1)} %pad_maximum_fusion.3), channel_id=1, source_target_pairs={{0,2},{2,0},{4,6},{6,4},{8,10},{10,8},{12,14},{14,12},{1,3},{3,1},... | collective-permute-start | bytes 393224 | tf_op jit(solution)/shard_map/ppermute | solution.py:569
  62.1 1.6 %collective-permute-start.11 = (bf16[8,32,512]{2,1,0:T(8,128)(2,1)S(1)}, bf16[8,32,512]{2,1,0:T(8,128)(2,1)S(1)}, u32[]{:S(2)}, u32[]{:S(2)}) collective-permute-start(bf16[8,32,512]{2,1,0:T(8,128)(2,1)S(1)} %pad_maximum_fusion.1.refs_3_), channel_id=1, source_target_pairs={{0,1},{1,0},{2,3},{3,2},{4,5},{5,4},{6,7},{7,6},{8,9},{9,8},{10,11... | collective-permute-start | bytes 786440 | tf_op jit(solution)/shard_map/ppermute | solution.py:527
  63.7 19.0 %copy-start.3 = (f32[8192]{0:T(1024)S(1)}, f32[8192]{0:T(1024)}, u32[]{:S(2)}) copy-start(f32[8192]{0:T(1024)} %gain.1) | copy-start | bytes 98308
  66.8 4.9 %collective-permute-start.12 = (bf16[1,32,512]{2,1,0:T(8,128)(2,1)S(1)}, bf16[1,32,512]{2,1,0:T(8,128)(2,1)S(1)}, u32[]{:S(2)}, u32[]{:S(2)}) collective-permute-start(bf16[1,32,512]{2,1,0:T(8,128)(2,1)S(1)} %bitcast.13), channel_id=1, source_target_pairs={{0,8},{2,10},{4,12},{6,14},{8,0},{10,2},{12,4},{14,6},{1,9},{3,11}... | collective-permute-start | bytes 98312 | tf_op jit(solution)/shard_map/ppermute | solution.py:569
  71.6 4.3 %collective-permute-start.13 = (bf16[2,32,512]{2,1,0:T(8,128)(2,1)S(1)}, bf16[2,32,512]{2,1,0:T(8,128)(2,1)S(1)}, u32[]{:S(2)}, u32[]{:S(2)}) collective-permute-start(bf16[2,32,512]{2,1,0:T(8,128)(2,1)S(1)} %pad_maximum_fusion.6), channel_id=1, source_target_pairs={{0,4},{2,6},{4,0},{6,2},{8,12},{10,14},{12,8},{14,10},{1,5},{3,7},... | collective-permute-start | bytes 196616 | tf_op jit(solution)/shard_map/ppermute | solution.py:569
  76.0 5.0 %collective-permute-start.14 = (bf16[4,32,512]{2,1,0:T(8,128)(2,1)S(1)}, bf16[4,32,512]{2,1,0:T(8,128)(2,1)S(1)}, u32[]{:S(2)}, u32[]{:S(2)}) collective-permute-start(bf16[4,32,512]{2,1,0:T(8,128)(2,1)S(1)} %pad_maximum_fusion.4), channel_id=1, source_target_pairs={{0,2},{2,0},{4,6},{6,4},{8,10},{10,8},{12,14},{14,12},{1,3},{3,1},... | collective-permute-start | bytes 393224 | tf_op jit(solution)/shard_map/ppermute | solution.py:569
  81.1 1.6 %collective-permute-start.15 = (bf16[8,32,512]{2,1,0:T(8,128)(2,1)S(1)}, bf16[8,32,512]{2,1,0:T(8,128)(2,1)S(1)}, u32[]{:S(2)}, u32[]{:S(2)}) collective-permute-start(bf16[8,32,512]{2,1,0:T(8,128)(2,1)S(1)} %pad_maximum_fusion.2.mine), channel_id=1, source_target_pairs={{0,1},{1,0},{2,3},{3,2},{4,5},{5,4},{6,7},{7,6},{8,9},{9,8},{10,11... | collective-permute-start | bytes 786440 | tf_op jit(solution)/shard_map/ppermute | solution.py:527
  95.8 1.6 %collective-permute-start.16 = (bf16[8,32,512]{2,1,0:T(8,128)(2,1)S(1)}, bf16[8,32,512]{2,1,0:T(8,128)(2,1)S(1)}, u32[]{:S(2)}, u32[]{:S(2)}) collective-permute-start(bf16[8,32,512]{2,1,0:T(8,128)(2,1)S(1)} %get-tuple-element.53), channel_id=1, source_target_pairs={{0,1},{1,0},{2,3},{3,2},{4,5},{5,4},{6,7},{7,6},{8,9},{9,8},{10,11... | collective-permute-start | bytes 786440 | tf_op jit(solution)/shard_map/ppermute | solution.py:527

commit v8 on v6

--- a/solution.py
+++ b/solution.py
@@ -57,7 +57,7 @@
         own_copy.wait()
         start = member * slots
 
-        if members <= 8:
+        if members in (4, 8):
             carry = (jnp.int32(0), jnp.int32(0))
             for i in range(parts):
                 loads[i].wait()
@@ -65,7 +65,7 @@
                 def body(j, words, base=i * step):
                     low, high = words
                     entry = own[start + base + j]
-                    ahead = lax.rem((entry >> 8) - member + members + 1, members)
+                    ahead = ((entry >> 8) - member + 1) & (members - 1)
                     leaves = entry >= 0
                     shift = (ahead & 3) * 8
                     is_low = ahead < 4
@@ -77,7 +77,7 @@
                         high + jnp.where(is_low, 0, one),
                     )
 
-                carry = lax.fori_loop(0, step, body, carry, unroll=6)
+                carry = lax.fori_loop(0, step, body, carry, unroll=13)
         else:
             for i in range(parts):
                 loads[i].wait()
@@ -248,10 +248,12 @@
     )(place, listed, *[in_hbm(x) for x in (lengths, tables, *weights, *first)])
 
 
-def attend_kernel(members, steps, chunks, place, landing, old_pool, bias, new_k, new_v, *refs):
+def attend_kernel(members, steps, chunks, place, landing, old_pool, weight, bias, new_k, new_v, *refs):
     asked, refs = refs[:steps], refs[steps:]
-    arrived, refs = refs[:-6], refs[-6:]
-    kv_out, att_low, att_high, pool, scores, sems = refs
+    arrived, refs = refs[:-7], refs[-7:]
+    kv_out, att_low, att_high, held, pool, scores, sems = refs
+    fetch = pltpu.make_async_copy(weight, held, sems.at[2])
+    fetch.start()
     member, half = place[0], place[1]
     slots = pool.shape[0]
     resident = slots - ARRIVE
@@ -327,8 +329,10 @@
             att_high[:, j * HD : (j + 1) * HD] = out[other * tokens : (other + 1) * tokens]
         copy_out.wait()
 
-
-def place_and_attend(place, landing, old_pool, bias, new_k, new_v, asked, arrived, chunks):
+    fetch.wait()
+
+
+def place_and_attend(place, landing, old_pool, weight, bias, new_k, new_v, asked, arrived, chunks):
     members = landing.shape[0]
     slots = old_pool.shape[0]
     rows = bias.shape[0]
@@ -340,13 +344,14 @@
             jax.ShapeDtypeStruct(old_pool.shape, old_pool.dtype),
             jax.ShapeDtypeStruct((tokens, GQ * HD // 2), jnp.bfloat16),
             jax.ShapeDtypeStruct((tokens, GQ * HD // 2), jnp.bfloat16),
-        ],
-        in_specs=[SM, SM, HBM, VM, VM, VM] + [VM] * (steps + len(arrived)),
-        out_specs=[HBM, VM, VM],
+            pltpu.VMEM(weight.shape, weight.dtype),
+        ],
+        in_specs=[SM, SM, HBM, HBM, VM, VM, VM] + [VM] * (steps + len(arrived)),
+        out_specs=[HBM, VM, VM, VM],
         scratch_shapes=[
             pltpu.VMEM(old_pool.shape, old_pool.dtype),
             pltpu.VMEM((tokens * GQ, slots * PAGE), jnp.float32),
-            pltpu.SemaphoreType.DMA((2,)),
+            pltpu.SemaphoreType.DMA((3,)),
         ],
         compiler_params=pltpu.CompilerParams(vmem_limit_bytes=9 * MIB),
         name="place_attend",
@@ -354,6 +359,7 @@
         place,
         landing,
         in_hbm(old_pool),
+        in_hbm(weight),
         bias,
         new_k,
         new_v,
@@ -419,7 +425,7 @@
         x = jnp.concatenate([first, second], axis=1).astype(jnp.float32)
         cols = slice(2 * t * width, 2 * (t + 1) * width)
         normed[:, cols] = (x * factor * gain[cols][None, :]).astype(jnp.bfloat16)
-    tile = min(256, hidden_count)
+    tile = min(1024, hidden_count)
     for f in range(hidden_count // tile):
         cols = slice(f * tile, (f + 1) * tile)
         gate_act = jnp.dot(normed[...], gate[:, cols], preferred_element_type=jnp.float32)
@@ -531,8 +537,8 @@
     new_k = jnp.pad(fresh_kv[:, :, 0].reshape(tokens, HD), padding)
     new_v = jnp.pad(fresh_kv[:, :, 1].reshape(tokens, HD), padding)
     asked = [queries[:, st] for st in range(steps)]
-    kv_after, att_low, att_high = place_and_attend(
-        place, landing, kv_pages, bias, new_k, new_v, asked, arrays, chunks
+    kv_after, att_low, att_high, out_proj = place_and_attend(
+        place, landing, kv_pages, out_proj, bias, new_k, new_v, asked, arrays, chunks
     )
 
     def everywhere(x):

time: 111 us -> 110 us (level)
  local copies, waits for them, and re-layouts: 4.45 us -> 1.06 us
  Pallas kernels: 32.5 us -> 34.7 us
    unnamed x22 -> x20, local copies, waits for them, and re-layouts: 3.45 us -> 0.06 us
    pallas_call x1, Pallas kernels: 3.81 us -> 6.5 us  [place_and_attend(): pl.pallas_call(functools.partial(attend_kernel, members, steps, chunks),...]
where the time goes in v8:
time: 110 us; the launch traced here: 109 us
  blocking collectives  41.6 us (38%)
  Pallas kernels  34.7 us (32%)
  starting transfers between devices  18 us (16%)
  waiting for transfers between devices  10.7 us (10%)
  other arithmetic  2.01 us (2%)
    all_to_all x2, blocking collectives, everywhere(): mine = lax.all_to_all(spread, 'tp', split_axis=0, concat_axis=0)  29 us
    pallas_call x1, Pallas kernels, feed_forward(): pl.pallas_call(ffn_kernel, out_shape=[jax.ShapeDtypeStruct(mine.shape, jn...  12.9 us
    all_to_all x1, blocking collectives, local(): shares = lax.all_to_all(summed, 'tp', split_axis=0, concat_axis=0)  12.6 us
    ppermute x5, starting transfers between devices, send(): return lax.ppermute(x, BOTH, route)  8.12 us
    ppermute x1, starting transfers between devices, local(): lax.ppermute(jnp.concatenate([own_chunk] + [arrived[host] for host in hos...  7.11 us
    pallas_call x1, Pallas kernels, prepare(): pl.pallas_call(functools.partial(prepare_kernel, count, parts, groups), o...  6.77 us
    pallas_call x1, Pallas kernels, place_and_attend(): pl.pallas_call(functools.partial(attend_kernel, members, steps, chunks),...  6.5 us
    pallas_call x1, Pallas kernels, pack(): pl.pallas_call(functools.partial(pack_kernel, members), out_shape=[pltpu....  5.45 us
  transfers between devices with their start and end apart: 11, of which 6 were waited for; matrix products, arithmetic and copies ran while one was open for 2% of the time, Pallas kernels for 6%

profile of v8, /device:TPU:0, one launch (start us, length us, event | category | flops | bytes accessed | tf_op | source)
XLA Modules:
  0.0 109.1 jit_solution(15179443101541086565)
XLA Ops:
  0.6 0.1 pad_add_fusion.place
  0.7 5.4 %pack_pages.1 = (bf16[64,2,16,128]{3,2,1,0:T(8,128)(2,1)}, bf16[32,2,16,128]{3,2,1,0:T(8,128)(2,1)}, bf16[32,2,16,128]{3,2,1,0:T(8,128)(2,1)}, bf16[32,2,16,128]...) custom-call(s32[2]{0:T(128)S(1)} %pad_add_fusion.place, ...), custom_call_target="tpu_custom_call" | custom-call | tf_op jit(solution)/shard_map/pack_pages/pallas_call | solution.py:119
  6.2 1.3 %collective-permute-start = (bf16[64,2,16,128]{3,2,1,0:T(8,128)(2,1)}, bf16[64,2,16,128]{3,2,1,0:T(8,128)(2,1)S(1)}, u32[]{:S(2)}, u32[]{:S(2)}) collective-permute-start(bf16[64,2,16,128]{3,2,1,0:T(8,128)(2,1)} %get-tuple-element.28.refs_1_), channel_id=1, source_target_pairs={{0,1},{2,3},{4,5},{6,7},{8,9},{10,11},{12,13},{14,15},{16,17},{18,... | collective-permute-start | bytes 1572872 | tf_op jit(solution)/shard_map/ppermute | solution.py:510
  7.5 1.3 %collective-permute-start.2 = (bf16[32,2,16,128]{3,2,1,0:T(8,128)(2,1)}, bf16[32,2,16,128]{3,2,1,0:T(8,128)(2,1)S(1)}, u32[]{:S(2)}, u32[]{:S(2)}) collective-permute-start(bf16[32,2,16,128]{3,2,1,0:T(8,128)(2,1)} %get-tuple-element.29), channel_id=1, source_target_pairs={{0,7},{2,9},{4,11},{6,13},{8,15},{10,1},{12,3},{14,5},{16,23},{18,... | collective-permute-start | bytes 786440 | tf_op jit(solution)/shard_map/ppermute | solution.py:503
  8.8 1.3 %collective-permute-start.3 = (bf16[32,2,16,128]{3,2,1,0:T(8,128)(2,1)}, bf16[32,2,16,128]{3,2,1,0:T(8,128)(2,1)S(1)}, u32[]{:S(2)}, u32[]{:S(2)}) collective-permute-start(bf16[32,2,16,128]{3,2,1,0:T(8,128)(2,1)} %get-tuple-element.30), channel_id=1, source_target_pairs={{0,9},{2,11},{4,13},{6,15},{8,1},{10,3},{12,5},{14,7},{16,25},{18,... | collective-permute-start | bytes 786440 | tf_op jit(solution)/shard_map/ppermute | solution.py:503
  10.1 1.5 %collective-permute-start.4 = (bf16[32,2,16,128]{3,2,1,0:T(8,128)(2,1)}, bf16[32,2,16,128]{3,2,1,0:T(8,128)(2,1)S(1)}, u32[]{:S(2)}, u32[]{:S(2)}) collective-permute-start(bf16[32,2,16,128]{3,2,1,0:T(8,128)(2,1)} %get-tuple-element.31), channel_id=1, source_target_pairs={{0,11},{2,13},{4,15},{6,1},{8,3},{10,5},{12,7},{14,9},{16,27},{18,... | collective-permute-start | bytes 786440 | tf_op jit(solution)/shard_map/ppermute | solution.py:503
  11.7 1.1 %slice_select_fusion = (bf16[32,2,16,128]{3,2,1,0:T(8,128)(2,1)S(1)}, bf16[32,2,16,128]{3,2,1,0:T(8,128)(2,1)S(1)}) fusion(bf16[32,2,16,128]{3,2,1,0:T(8,128)(2,1)} %get-tuple-element.32, bf16[64,2,16,128]{3,2,1,0:T(8,128)(2,1)S(1)} %collective-permute-done, pred[]{:T(512)S(6)} %eq.4, bf16[32,2,16,128]{3,2,1,0:T(8,128)(2,1)} %get-tuple-element.27), kind=kLoop, calls=%fused_computation.3 | loop fusion | flops 262144 | bytes 1572865 | tf_op jit(solution)/shard_map/jit(_where)/select_n | solution.py:516
  12.8 1.6 %collective-permute-start.5 = (bf16[32,2,16,128]{3,2,1,0:T(8,128)(2,1)S(1)}, bf16[32,2,16,128]{3,2,1,0:T(8,128)(2,1)S(1)}, u32[]{:S(2)}, u32[]{:S(2)}) collective-permute-start(bf16[32,2,16,128]{3,2,1,0:T(8,128)(2,1)S(1)} %get-tuple-element.52), channel_id=1, source_target_pairs={{0,13},{2,15},{4,1},{6,3},{8,5},{10,7},{12,9},{14,11},{1,14},{3,0}... | collective-permute-start | bytes 786440 | tf_op jit(solution)/shard_map/ppermute | solution.py:503
  14.3 2.4 %collective-permute-start.1 = (bf16[32,2,16,128]{3,2,1,0:T(8,128)(2,1)S(1)}, bf16[32,2,16,128]{3,2,1,0:T(8,128)(2,1)S(1)}, u32[]{:S(2)}, u32[]{:S(2)}) collective-permute-start(bf16[32,2,16,128]{3,2,1,0:T(8,128)(2,1)S(1)} %get-tuple-element.53), channel_id=1, source_target_pairs={{0,5},{2,7},{4,9},{6,11},{8,13},{10,15},{12,1},{14,3},{1,2},{3,4},... | collective-permute-start | bytes 786440 | tf_op jit(solution)/shard_map/ppermute | solution.py:503
  16.7 0.8 reshape.9.listed
  17.5 0.0 copy-start.4
  17.6 0.0 slice-start
  17.6 6.8 %prepare.1 = (bf16[2048,1024]{1,0:T(8,128)(2,1)S(1)}, bf16[2048,1024]{1,0:T(8,128)(2,1)S(1)}, bf16[2048,1024]{1,0:T(8,128)(2,1)S(1)}, bf16[2048,1024]{1,0:T(8,12...) custom-call(s32[2]{0:T(128)S(1)} %pad_add_fusion.place, s32[8,312]{1,0:T(8,128)S(1)} %reshape.9.listed, ...), custom_call_target="tpu_custom_call" | custom-call | bytes 16777216 | tf_op jit(solution)/shard_map/prepare/pallas_call | solution.py:228
  24.4 2.8 %collective-permute-done.1.refs_3_ = bf16[32,2,16,128]{3,2,1,0:T(8,128)(2,1)S(1)} collective-permute-done((bf16[32,2,16,128]{3,2,1,0:T(8,128)(2,1)S(1)}, bf16[32,2,16,128]{3,2,1,0:T(8,128)(2,1)S(1)}, u32[]{:S(2)}, u32[]{:S(2)}) %collective-permute-start.1) | collective-permute-done | bytes 262176 | tf_op jit(solution)/shard_map/ppermute | solution.py:503
  27.2 0.1 pad_maximum_fusion
  27.3 7.1 %collective-permute-start.6 = (bf16[96,2,16,128]{3,2,1,0:T(8,128)(2,1)S(1)}, bf16[96,2,16,128]{3,2,1,0:T(8,128)(2,1)S(1)}, u32[]{:S(2)}, u32[]{:S(2)}) collective-permute-start(bf16[96,2,16,128]{3,2,1,0:T(8,128)(2,1)S(1)} %pad_maximum_fusion), channel_id=1, source_target_pairs={{0,1},{2,3},{4,5},{6,7},{8,9},{10,11},{12,13},{14,15},{16,17},{18,... | collective-permute-start | bytes 2359304 | tf_op jit(solution)/shard_map/ppermute | solution.py:530
  34.6 0.1 fusion
  34.7 1.6 %collective-permute-done.6.refs_2_ = bf16[96,2,16,128]{3,2,1,0:T(8,128)(2,1)S(1)} collective-permute-done((bf16[96,2,16,128]{3,2,1,0:T(8,128)(2,1)S(1)}, bf16[96,2,16,128]{3,2,1,0:T(8,128)(2,1)S(1)}, u32[]{:S(2)}, u32[]{:S(2)}) %collective-permute-start.6) | collective-permute-done | bytes 786464 | tf_op jit(solution)/shard_map/ppermute | solution.py:530
  36.3 6.5 %place_attend.1 = (bf16[312,2,16,128]{3,2,1,0:T(8,128)(2,1)}, bf16[32,512]{1,0:T(8,128)(2,1)S(1)}, bf16[32,512]{1,0:T(8,128)(2,1)S(1)}, bf16[512,8192]{1,0:T(8,128)(2,1)S(1)}) custom-call(s32[2]{0:T(128)S(1)} %pad_add_fusion.place, s32[8,128]{1,0:T(8,128)S(1)} %get-tuple-element.34.landing, bf16[312,2,16,128]{3,2,1,0:T(8,128)(2,1)} %old_pool.1, ...), custom_call_target="tpu_custom_call" | custom-call | tf_op jit(solution)/shard_map/place_attend/pallas_call | solution.py:341
  42.8 1.3 %collective-permute-start.7 = (bf16[32,512]{1,0:T(8,128)(2,1)S(1)}, bf16[32,512]{1,0:T(8,128)(2,1)S(1)}, u32[]{:S(2)}, u32[]{:S(2)}) collective-permute-start(bf16[32,512]{1,0:T(8,128)(2,1)S(1)} %get-tuple-element.45), channel_id=1, source_target_pairs={{1,0},{3,2},{5,4},{7,6},{9,8},{11,10},{13,12},{15,14},{17,16},{19,... | collective-permute-start | bytes 98312 | tf_op jit(solution)/shard_map/ppermute | solution.py:549
  44.1 1.8 %collective-permute-done.7 = bf16[32,512]{1,0:T(8,128)(2,1)S(1)} collective-permute-done((bf16[32,512]{1,0:T(8,128)(2,1)S(1)}, bf16[32,512]{1,0:T(8,128)(2,1)S(1)}, u32[]{:S(2)}, u32[]{:S(2)}) %collective-permute-start.7) | collective-permute-done | bytes 32800 | tf_op jit(solution)/shard_map/ppermute | solution.py:549
  46.0 16.4 %all_to_all.15.mine = bf16[8,32,512]{2,1,0:T(8,128)(2,1)S(1)} all-to-all(bf16[8,32,512]{2,1,0:T(8,128)(2,1)S(1)} %broadcast_in_dim.4), channel_id=1, replica_groups=mesh['grp'=2,'tp'=8,'pd'=2] {'tp'}, dimensions={0} | all-to-all | bytes 524288 | tf_op jit(solution)/shard_map/all_to_all | solution.py:546
  62.3 1.5 %collective-permute-done.8.sibling = bf16[8,32,512]{2,1,0:T(8,128)(2,1)S(1)} collective-permute-done((bf16[8,32,512]{2,1,0:T(8,128)(2,1)S(1)}, bf16[8,32,512]{2,1,0:T(8,128)(2,1)S(1)}, u32[]{:S(2)}, u32[]{:S(2)}) %collective-permute-start.8) | collective-permute-done | bytes 262176 | tf_op jit(solution)/shard_map/ppermute | solution.py:506
  63.9 3.1 %out_projection.1 = bf16[32,512]{1,0:T(8,128)(2,1)S(1)} custom-call(s32[2]{0:T(128)S(1)} %pad_add_fusion.place, bf16[512,8192]{1,0:T(8,128)(2,1)S(1)} %get-tuple-element.43.weight, bf16[32,512]{1,0:T(8,128)(2,1)S(1)} %copy-done, bf16[8,32,512]{2,1,0:T(8,128)(2,1)S(1)} %all_to_all.15.mine, bf16[8,32,512]{2,1,0:T(8,128)(2,1)S(1)} %collective-permute-done.8.sibling), custom_call_target="tpu_custom_call" | custom-call | tf_op jit(solution)/shard_map/out_projection/pallas_call | solution.py:391
  67.0 12.6 %all_to_all.16.mine = bf16[8,32,512]{2,1,0:T(8,128)(2,1)S(1)} all-to-all(bf16[8,32,512]{2,1,0:T(8,128)(2,1)S(1)} %broadcast_in_dim.5), channel_id=1, replica_groups=mesh['grp'=2,'tp'=8,'pd'=2] {'tp'}, dimensions={0} | all-to-all | bytes 524288 | tf_op jit(solution)/shard_map/all_to_all | solution.py:546
  79.6 1.5 %collective-permute-done.9.sibling = bf16[8,32,512]{2,1,0:T(8,128)(2,1)S(1)} collective-permute-done((bf16[8,32,512]{2,1,0:T(8,128)(2,1)S(1)}, bf16[8,32,512]{2,1,0:T(8,128)(2,1)S(1)}, u32[]{:S(2)}, u32[]{:S(2)}) %collective-permute-start.9) | collective-permute-done | bytes 262176 | tf_op jit(solution)/shard_map/ppermute | solution.py:506
  81.2 12.9 %feed_forward.1 = (f32[8,32,512]{2,1,0:T(8,128)S(1)}, bf16[8,32,512]{2,1,0:T(8,128)(2,1)S(1)}) custom-call(s32[2]{0:T(128)S(1)} %pad_add_fusion.place, bf16[8,32,512]{2,1,0:T(8,128)(2,1)S(1)} %all_to_all.16.mine, bf16[8,32,512]{2,1,0:T(8,128)(2,1)S(1)} %collective-permute-done.9.sibling, f32[8192]{0:T(1024)S(1)} %copy-done.1, ...), custom_call_target="tpu_custom_call" | custom-call | tf_op jit(solution)/shard_map/feed_forward/pallas_call | solution.py:453
  94.1 0.2 collective-permute-start.10
  94.3 1.4 %collective-permute-done.10 = bf16[8,32,512]{2,1,0:T(8,128)(2,1)S(1)} collective-permute-done((bf16[8,32,512]{2,1,0:T(8,128)(2,1)S(1)}, bf16[8,32,512]{2,1,0:T(8,128)(2,1)S(1)}, u32[]{:S(2)}, u32[]{:S(2)}) %collective-permute-start.10) | collective-permute-done | bytes 262176 | tf_op jit(solution)/shard_map/ppermute | solution.py:506
  95.7 0.1 add_convert_fusion
  95.8 12.6 %all_to_all.17 = bf16[8,32,512]{2,1,0:T(8,128)(2,1)S(1)} all-to-all(bf16[8,32,512]{2,1,0:T(8,128)(2,1)S(1)} %add_convert_fusion), channel_id=1, replica_groups=mesh['grp'=2,'tp'=8,'pd'=2] {'tp'}, dimensions={0} | all-to-all | bytes 524288 | tf_op jit(solution)/shard_map/all_to_all | solution.py:560
  108.4 0.6 add_convert_fusion.1
  (34 shorter events, 0.2 us)
Async XLA Ops:
  6.2 5.5 %collective-permute-start = (bf16[64,2,16,128]{3,2,1,0:T(8,128)(2,1)}, bf16[64,2,16,128]{3,2,1,0:T(8,128)(2,1)S(1)}, u32[]{:S(2)}, u32[]{:S(2)}) collective-permute-start(bf16[64,2,16,128]{3,2,1,0:T(8,128)(2,1)} %get-tuple-element.28.refs_1_), channel_id=1, source_target_pairs={{0,1},{2,3},{4,5},{6,7},{8,9},{10,11},{12,13},{14,15},{16,17},{18,... | collective-permute-start | bytes 1572872 | tf_op jit(solution)/shard_map/ppermute | solution.py:510
  7.5 16.9 %collective-permute-start.2 = (bf16[32,2,16,128]{3,2,1,0:T(8,128)(2,1)}, bf16[32,2,16,128]{3,2,1,0:T(8,128)(2,1)S(1)}, u32[]{:S(2)}, u32[]{:S(2)}) collective-permute-start(bf16[32,2,16,128]{3,2,1,0:T(8,128)(2,1)} %get-tuple-element.29), channel_id=1, source_target_pairs={{0,7},{2,9},{4,11},{6,13},{8,15},{10,1},{12,3},{14,5},{16,23},{18,... | collective-permute-start | bytes 786440 | tf_op jit(solution)/shard_map/ppermute | solution.py:503
  8.8 15.6 %collective-permute-start.3 = (bf16[32,2,16,128]{3,2,1,0:T(8,128)(2,1)}, bf16[32,2,16,128]{3,2,1,0:T(8,128)(2,1)S(1)}, u32[]{:S(2)}, u32[]{:S(2)}) collective-permute-start(bf16[32,2,16,128]{3,2,1,0:T(8,128)(2,1)} %get-tuple-element.30), channel_id=1, source_target_pairs={{0,9},{2,11},{4,13},{6,15},{8,1},{10,3},{12,5},{14,7},{16,25},{18,... | collective-permute-start | bytes 786440 | tf_op jit(solution)/shard_map/ppermute | solution.py:503
  10.1 14.3 %collective-permute-start.4 = (bf16[32,2,16,128]{3,2,1,0:T(8,128)(2,1)}, bf16[32,2,16,128]{3,2,1,0:T(8,128)(2,1)S(1)}, u32[]{:S(2)}, u32[]{:S(2)}) collective-permute-start(bf16[32,2,16,128]{3,2,1,0:T(8,128)(2,1)} %get-tuple-element.31), channel_id=1, source_target_pairs={{0,11},{2,13},{4,15},{6,1},{8,3},{10,5},{12,7},{14,9},{16,27},{18,... | collective-permute-start | bytes 786440 | tf_op jit(solution)/shard_map/ppermute | solution.py:503
  12.8 11.7 %collective-permute-start.5 = (bf16[32,2,16,128]{3,2,1,0:T(8,128)(2,1)S(1)}, bf16[32,2,16,128]{3,2,1,0:T(8,128)(2,1)S(1)}, u32[]{:S(2)}, u32[]{:S(2)}) collective-permute-start(bf16[32,2,16,128]{3,2,1,0:T(8,128)(2,1)S(1)} %get-tuple-element.52), channel_id=1, source_target_pairs={{0,13},{2,15},{4,1},{6,3},{8,5},{10,7},{12,9},{14,11},{1,14},{3,0}... | collective-permute-start | bytes 786440 | tf_op jit(solution)/shard_map/ppermute | solution.py:503
  14.3 12.9 %collective-permute-start.1 = (bf16[32,2,16,128]{3,2,1,0:T(8,128)(2,1)S(1)}, bf16[32,2,16,128]{3,2,1,0:T(8,128)(2,1)S(1)}, u32[]{:S(2)}, u32[]{:S(2)}) collective-permute-start(bf16[32,2,16,128]{3,2,1,0:T(8,128)(2,1)S(1)} %get-tuple-element.53), channel_id=1, source_target_pairs={{0,5},{2,7},{4,9},{6,11},{8,13},{10,15},{12,1},{14,3},{1,2},{3,4},... | collective-permute-start | bytes 786440 | tf_op jit(solution)/shard_map/ppermute | solution.py:503
  17.5 9.7 %copy-start.3 = (bf16[32,2,16,128]{3,2,1,0:T(8,128)(2,1)S(1)}, bf16[32,2,16,128]{3,2,1,0:T(8,128)(2,1)}, u32[]{:S(2)}) copy-start(bf16[32,2,16,128]{3,2,1,0:T(8,128)(2,1)} %get-tuple-element.36) | copy-start | bytes 786436
  17.5 16.9 %copy-start.4 = (bf16[16,2,2,128]{3,2,1,0:T(2,128)(2,1)S(1)}, bf16[16,2,2,128]{3,2,1,0:T(2,128)(2,1)}, u32[]{:S(2)}) copy-start(bf16[16,2,2,128]{3,2,1,0:T(2,128)(2,1)} %param.17) | copy-start | bytes 49156
  17.6 17.0 %copy-start.2 = (bf16[16,2,1024]{2,1,0:T(2,128)(2,1)S(1)}, bf16[16,2,1024]{2,1,0:T(2,128)(2,1)}, u32[]{:S(2)}) copy-start(bf16[16,2,1024]{2,1,0:T(2,128)(2,1)} %param.16) | copy-start | bytes 196612
  17.6 63.6 %slice-start = ((s8[16777216]{0:T(1024)(128)(4,1)}), s8[4194304]{0:T(1024)(128)(4,1)S(1)}, s32[]{:S(2)}) async-start(s8[16777216]{0:T(1024)(128)(4,1)} %bitcast.8), calls=%async_computation.3 | async-start | bytes 8388608
  17.6 63.6 %slice-start.1 = ((s8[16777216]{0:T(1024)(128)(4,1)}), s8[4194304]{0:T(1024)(128)(4,1)S(1)}, s32[]{:S(2)}) async-start(s8[16777216]{0:T(1024)(128)(4,1)} %bitcast.8), calls=%async_computation.4 | async-start | bytes 8388608
  27.3 9.0 %collective-permute-start.6 = (bf16[96,2,16,128]{3,2,1,0:T(8,128)(2,1)S(1)}, bf16[96,2,16,128]{3,2,1,0:T(8,128)(2,1)S(1)}, u32[]{:S(2)}, u32[]{:S(2)}) collective-permute-start(bf16[96,2,16,128]{3,2,1,0:T(8,128)(2,1)S(1)} %pad_maximum_fusion), channel_id=1, source_target_pairs={{0,1},{2,3},{4,5},{6,7},{8,9},{10,11},{12,13},{14,15},{16,17},{18,... | collective-permute-start | bytes 2359304 | tf_op jit(solution)/shard_map/ppermute | solution.py:530
  36.3 27.6 %copy-start = (bf16[32,512]{1,0:T(8,128)(2,1)S(1)}, bf16[32,512]{1,0:T(8,128)(2,1)}, u32[]{:S(2)}) copy-start(bf16[32,512]{1,0:T(8,128)(2,1)} %stream.1) | copy-start | bytes 98308
  36.3 44.9 %slice-start.2 = ((s8[16777216]{0:T(1024)(128)(4,1)}), s8[4194304]{0:T(1024)(128)(4,1)S(1)}, s32[]{:S(2)}) async-start(s8[16777216]{0:T(1024)(128)(4,1)} %bitcast.8), calls=%async_computation.5 | async-start | bytes 8388608
  36.3 44.9 %slice-start.3 = ((s8[16777216]{0:T(1024)(128)(4,1)}), s8[4194304]{0:T(1024)(128)(4,1)S(1)}, s32[]{:S(2)}) async-start(s8[16777216]{0:T(1024)(128)(4,1)} %bitcast.8), calls=%async_computation.6 | async-start | bytes 8388608
  42.8 3.1 %collective-permute-start.7 = (bf16[32,512]{1,0:T(8,128)(2,1)S(1)}, bf16[32,512]{1,0:T(8,128)(2,1)S(1)}, u32[]{:S(2)}, u32[]{:S(2)}) collective-permute-start(bf16[32,512]{1,0:T(8,128)(2,1)S(1)} %get-tuple-element.45), channel_id=1, source_target_pairs={{1,0},{3,2},{5,4},{7,6},{9,8},{11,10},{13,12},{15,14},{17,16},{19,... | collective-permute-start | bytes 98312 | tf_op jit(solution)/shard_map/ppermute | solution.py:549
  62.3 1.5 %collective-permute-start.8 = (bf16[8,32,512]{2,1,0:T(8,128)(2,1)S(1)}, bf16[8,32,512]{2,1,0:T(8,128)(2,1)S(1)}, u32[]{:S(2)}, u32[]{:S(2)}) collective-permute-start(bf16[8,32,512]{2,1,0:T(8,128)(2,1)S(1)} %all_to_all.15.mine), channel_id=1, source_target_pairs={{0,1},{1,0},{2,3},{3,2},{4,5},{5,4},{6,7},{7,6},{8,9},{9,8},{10,11... | collective-permute-start | bytes 786440 | tf_op jit(solution)/shard_map/ppermute | solution.py:506
  63.9 17.3 %copy-start.1 = (f32[8192]{0:T(1024)S(1)}, f32[8192]{0:T(1024)}, u32[]{:S(2)}) copy-start(f32[8192]{0:T(1024)} %gain.1) | copy-start | bytes 98308
  79.6 1.5 %collective-permute-start.9 = (bf16[8,32,512]{2,1,0:T(8,128)(2,1)S(1)}, bf16[8,32,512]{2,1,0:T(8,128)(2,1)S(1)}, u32[]{:S(2)}, u32[]{:S(2)}) collective-permute-start(bf16[8,32,512]{2,1,0:T(8,128)(2,1)S(1)} %all_to_all.16.mine), channel_id=1, source_target_pairs={{0,1},{1,0},{2,3},{3,2},{4,5},{5,4},{6,7},{7,6},{8,9},{9,8},{10,11... | collective-permute-start | bytes 786440 | tf_op jit(solution)/shard_map/ppermute | solution.py:506
  94.1 1.6 %collective-permute-start.10 = (bf16[8,32,512]{2,1,0:T(8,128)(2,1)S(1)}, bf16[8,32,512]{2,1,0:T(8,128)(2,1)S(1)}, u32[]{:S(2)}, u32[]{:S(2)}) collective-permute-start(bf16[8,32,512]{2,1,0:T(8,128)(2,1)S(1)} %get-tuple-element.51), channel_id=1, source_target_pairs={{0,1},{1,0},{2,3},{3,2},{4,5},{5,4},{6,7},{7,6},{8,9},{9,8},{10,11... | collective-permute-start | bytes 786440 | tf_op jit(solution)/shard_map/ppermute | solution.py:506

commit v9 on v6

--- a/solution.py
+++ b/solution.py
@@ -17,7 +17,7 @@
 ARRIVE = REQ_DEV * NEWP
 MIB = 1024 * 1024
 BOTH = ("tp", "pd")
-SPLIT = 4
+SPLIT = 2
 
 VM = pl.BlockSpec(memory_space=pltpu.VMEM)
 SM = pl.BlockSpec(memory_space=pltpu.SMEM)
@@ -57,7 +57,7 @@
         own_copy.wait()
         start = member * slots
 
-        if members <= 8:
+        if members in (4, 8):
             carry = (jnp.int32(0), jnp.int32(0))
             for i in range(parts):
                 loads[i].wait()
@@ -65,7 +65,7 @@
                 def body(j, words, base=i * step):
                     low, high = words
                     entry = own[start + base + j]
-                    ahead = lax.rem((entry >> 8) - member + members + 1, members)
+                    ahead = ((entry >> 8) - member + 1) & (members - 1)
                     leaves = entry >= 0
                     shift = (ahead & 3) * 8
                     is_low = ahead < 4
@@ -77,7 +77,7 @@
                         high + jnp.where(is_low, 0, one),
                     )
 
-                carry = lax.fori_loop(0, step, body, carry, unroll=6)
+                carry = lax.fori_loop(0, step, body, carry, unroll=13)
         else:
             for i in range(parts):
                 loads[i].wait()
@@ -174,10 +174,18 @@
     ).astype(jnp.int32)
     column = lax.broadcasted_iota(jnp.int32, landing.shape, 1)
     found = jnp.zeros(landing.shape, jnp.int32)
+    distance = member - lax.broadcasted_iota(jnp.int32, entry.shape, 0)
+    distance = jnp.where(distance < 0, distance + members, distance)
+    is_near = (distance <= 1) | (distance == members - 1)
+    slot_lane = lax.broadcasted_iota(jnp.int32, entry.shape, 1) - (listed.shape[1] - ARRIVE)
+    near = jnp.zeros(entry.shape, jnp.float32)
     for c in range(per_peer):
         slot = jnp.sum(jnp.where(wanted & (rank == c), entry & 255, 0), axis=1, keepdims=True)
         found = jnp.where(column == c, slot, found)
+        near = jnp.where(is_near & (slot == slot_lane), 1.0, near)
     landing[...] = found
+    near = jnp.max(near, axis=0, keepdims=True)
+    present = jnp.where(place[1] == 0, near, 1.0 - near)
 
     for copy in small:
         copy.wait()
@@ -198,8 +206,8 @@
         in_part = jnp.where(hit & (page_id == full), 1.0, 0.0)
         whole[r : r + 1, :] = jnp.sum(in_whole, axis=0, keepdims=True)
         part[r : r + 1, :] = jnp.sum(in_part, axis=0, keepdims=True)
-    whole_b = whole[...].astype(jnp.bfloat16)
-    part_b = part[...].astype(jnp.bfloat16)
+    whole_b = (whole[...] * present).astype(jnp.bfloat16)
+    part_b = (part[...] * present).astype(jnp.bfloat16)
     lane = lax.broadcasted_iota(jnp.int32, (rows, 128), 1)
     inside = (lane % PAGE) < over
     per_block = 128 // PAGE
@@ -242,7 +250,7 @@
             pltpu.VMEM(tables.shape, tables.dtype),
             pltpu.SemaphoreType.DMA((parts + 2,)),
         ],
-        compiler_params=pltpu.CompilerParams(vmem_limit_bytes=6 * MIB),
+        compiler_params=pltpu.CompilerParams(vmem_limit_bytes=16 * MIB),
         cost_estimate=pl.CostEstimate(flops=0, bytes_accessed=moved, transcendentals=0),
         name="prepare",
     )(place, listed, *[in_hbm(x) for x in (lengths, tables, *weights, *first)])
@@ -251,24 +259,27 @@
 def attend_kernel(members, steps, chunks, place, landing, old_pool, bias, new_k, new_v, *refs):
     asked, refs = refs[:steps], refs[steps:]
     arrived, refs = refs[:-6], refs[-6:]
-    kv_out, att_low, att_high, pool, scores, sems = refs
+    kv_out, keep, give, pool, scores, sems = refs
     member, half = place[0], place[1]
     slots = pool.shape[0]
     resident = slots - ARRIVE
     per_peer = ARRIVE // members
     rows = bias.shape[0]
     count = rows * steps * GQ
+    pool[resident:] = jnp.zeros((ARRIVE, *pool.shape[1:]), pool.dtype)
+
+    def place_pages(which):
+        for i, k in chunks[which]:
+            source = lax.rem(member - k + members, members)
+
+            @pl.loop(0, per_peer, unroll=math.gcd(per_peer, 8))
+            def _(c):
+                pool[resident + landing[source, c]] = arrived[i][c]
 
     @pl.when(half == 0)
     def _():
-        copy = pltpu.make_async_copy(old_pool, pool, sems.at[0])
-        copy.start()
-        att_low[...] = jnp.zeros_like(att_low)
-        att_high[...] = jnp.zeros_like(att_high)
-        copy.wait()
-        copy_out = pltpu.make_async_copy(pool, kv_out, sems.at[1])
-        copy_out.start()
-        copy_out.wait()
+        pool[:resident] = jnp.zeros((resident, *pool.shape[1:]), pool.dtype)
+        place_pages(0)
 
     @pl.when(half == 1)
     def _():
@@ -276,97 +287,121 @@
             old_pool.at[pl.ds(0, resident)], pool.at[pl.ds(0, resident)], sems.at[0]
         )
         copy.start()
-        for i, first, k in chunks:
-            source = lax.rem(member - k + members, members)
-
-            @pl.loop(0, per_peer, unroll=math.gcd(per_peer, 8))
-            def _(c):
-                pool[resident + landing[source, c]] = arrived[i][first + c]
-
+        place_pages(1)
         copy.wait()
-        copy_out = pltpu.make_async_copy(pool, kv_out, sems.at[1])
-        copy_out.start()
-
-        scale = 1.0 / math.sqrt(HD)
-        q = jnp.concatenate(
-            [ask[:, j * HD : (j + 1) * HD] for j in range(GQ) for ask in asked], axis=0
+        pltpu.make_async_copy(pool, kv_out, sems.at[1]).start()
+
+    scale = 1.0 / math.sqrt(HD)
+    q = jnp.concatenate(
+        [ask[:, j * HD : (j + 1) * HD] for j in range(GQ) for ask in asked], axis=0
+    )
+    nt = (((1,), (1,)), ((), ()))
+    group = 24
+    width = group * PAGE
+    lanes = 128
+    fresh = lax.dot_general(q, new_k[...], nt, preferred_element_type=jnp.float32) * scale
+    q_id = lax.broadcasted_iota(jnp.int32, fresh.shape, 0)
+    t_id = lax.broadcasted_iota(jnp.int32, fresh.shape, 1)
+    allowed = (q_id % rows == t_id // steps) & (t_id % steps <= (q_id // rows) % steps)
+    fresh = jnp.where(allowed & (half == 1), fresh, -jnp.inf)
+    peak = fresh
+    for c in range(slots // group):
+        keys = pool[c * group : (c + 1) * group, 0].reshape(width, HD)
+        s = lax.dot_general(q, keys, nt, preferred_element_type=jnp.float32) * scale
+        b = bias[:, c * width : (c + 1) * width]
+        s = (s.reshape(count // rows, rows, width) + b[None]).reshape(count, width)
+        scores[:, c * width : (c + 1) * width] = s
+        for i in range(width // lanes):
+            peak = jnp.maximum(peak, s[:, i * lanes : (i + 1) * lanes])
+    top = jnp.maximum(jnp.max(peak, axis=1, keepdims=True), -1e30)
+    p = jnp.exp(fresh - top)
+    total = p
+    acc = jnp.dot(p.astype(jnp.bfloat16), new_v[...], preferred_element_type=jnp.float32)
+    for c in range(slots // group):
+        p = jnp.exp(scores[:, c * width : (c + 1) * width] - top)
+        for i in range(width // lanes):
+            total = total + p[:, i * lanes : (i + 1) * lanes]
+        values = pool[c * group : (c + 1) * group, 1].reshape(width, HD)
+        acc = acc + jnp.dot(p.astype(jnp.bfloat16), values, preferred_element_type=jnp.float32)
+    total = jnp.sum(total, axis=1, keepdims=True)
+    middle = count // 2
+    for out, first in ((keep, half == 0), (give, half == 1)):
+        out[:, :HD] = jnp.where(first, acc[:middle], acc[middle:])
+        out[:, HD : 2 * HD] = jnp.broadcast_to(
+            jnp.where(first, top[:middle], top[middle:]), (middle, HD)
         )
-        nt = (((1,), (1,)), ((), ()))
-        group = 24
-        width = group * PAGE
-        lanes = 128
-        fresh = lax.dot_general(q, new_k[...], nt, preferred_element_type=jnp.float32) * scale
-        q_id = lax.broadcasted_iota(jnp.int32, fresh.shape, 0)
-        t_id = lax.broadcasted_iota(jnp.int32, fresh.shape, 1)
-        allowed = (q_id % rows == t_id // steps) & (t_id % steps <= (q_id // rows) % steps)
-        fresh = jnp.where(allowed, fresh, -jnp.inf)
-        peak = fresh
-        for c in range(slots // group):
-            keys = pool[c * group : (c + 1) * group, 0].reshape(width, HD)
-            s = lax.dot_general(q, keys, nt, preferred_element_type=jnp.float32) * scale
-            b = bias[:, c * width : (c + 1) * width]
-            s = (s.reshape(count // rows, rows, width) + b[None]).reshape(count, width)
-            scores[:, c * width : (c + 1) * width] = s
-            for i in range(width // lanes):
-                peak = jnp.maximum(peak, s[:, i * lanes : (i + 1) * lanes])
-        top = jnp.max(peak, axis=1, keepdims=True)
-        p = jnp.exp(fresh - top)
-        total = p
-        acc = jnp.dot(p.astype(jnp.bfloat16), new_v[...], preferred_element_type=jnp.float32)
-        for c in range(slots // group):
-            p = jnp.exp(scores[:, c * width : (c + 1) * width] - top)
-            for i in range(width // lanes):
-                total = total + p[:, i * lanes : (i + 1) * lanes]
-            values = pool[c * group : (c + 1) * group, 1].reshape(width, HD)
-            acc = acc + jnp.dot(p.astype(jnp.bfloat16), values, preferred_element_type=jnp.float32)
-        out = (acc / jnp.sum(total, axis=1, keepdims=True)).astype(jnp.bfloat16)
-        tokens = rows * steps
-        for j in range(GQ // 2):
-            att_low[:, j * HD : (j + 1) * HD] = out[j * tokens : (j + 1) * tokens]
-            other = j + GQ // 2
-            att_high[:, j * HD : (j + 1) * HD] = out[other * tokens : (other + 1) * tokens]
-        copy_out.wait()
+        out[:, 2 * HD :] = jnp.broadcast_to(
+            jnp.where(first, total[:middle], total[middle:]), (middle, HD)
+        )
+
+    @pl.when(half == 1)
+    def _():
+        pltpu.make_async_copy(pool, kv_out, sems.at[1]).wait()
 
 
 def place_and_attend(place, landing, old_pool, bias, new_k, new_v, asked, arrived, chunks):
     members = landing.shape[0]
     slots = old_pool.shape[0]
-    rows = bias.shape[0]
     steps = len(asked)
-    tokens = rows * steps
+    count = bias.shape[0] * steps * GQ
+    part = jax.ShapeDtypeStruct((count // 2, 3 * HD), jnp.float32)
     return pl.pallas_call(
         functools.partial(attend_kernel, members, steps, chunks),
-        out_shape=[
-            jax.ShapeDtypeStruct(old_pool.shape, old_pool.dtype),
-            jax.ShapeDtypeStruct((tokens, GQ * HD // 2), jnp.bfloat16),
-            jax.ShapeDtypeStruct((tokens, GQ * HD // 2), jnp.bfloat16),
-        ],
+        out_shape=[jax.ShapeDtypeStruct(old_pool.shape, old_pool.dtype), part, part],
         in_specs=[SM, SM, HBM, VM, VM, VM] + [VM] * (steps + len(arrived)),
         out_specs=[HBM, VM, VM],
         scratch_shapes=[
             pltpu.VMEM(old_pool.shape, old_pool.dtype),
-            pltpu.VMEM((tokens * GQ, slots * PAGE), jnp.float32),
+            pltpu.VMEM((count, slots * PAGE), jnp.float32),
             pltpu.SemaphoreType.DMA((2,)),
         ],
         compiler_params=pltpu.CompilerParams(vmem_limit_bytes=9 * MIB),
         name="place_attend",
-    )(
-        place,
-        landing,
-        in_hbm(old_pool),
-        bias,
-        new_k,
-        new_v,
-        *asked,
-        *arrived,
-    )
-
-
-def project_kernel(groups, place, weight, stream, mine, sibling, res_out):
+    )(place, landing, in_hbm(old_pool), bias, new_k, new_v, *asked, *arrived)
+
+
+def combine_kernel(mine, other, out):
+    tokens = out.shape[0]
+    for j in range(out.shape[1] // HD):
+        rows = slice(j * tokens, (j + 1) * tokens)
+        a, b = mine[rows, :], other[rows, :]
+        top_a, top_b = a[:, HD : 2 * HD], b[:, HD : 2 * HD]
+        top = jnp.maximum(top_a, top_b)
+        scale_a, scale_b = jnp.exp(top_a - top), jnp.exp(top_b - top)
+        total = a[:, 2 * HD :] * scale_a + b[:, 2 * HD :] * scale_b
+        value = (a[:, :HD] * scale_a + b[:, :HD] * scale_b) / total
+        out[:, j * HD : (j + 1) * HD] = value.astype(out.dtype)
+
+
+def combine(mine, other, tokens):
+    return pl.pallas_call(
+        combine_kernel,
+        out_shape=jax.ShapeDtypeStruct((tokens, GQ // 2 * HD), jnp.bfloat16),
+        in_specs=[VM, VM],
+        out_specs=VM,
+        compiler_params=pltpu.CompilerParams(vmem_limit_bytes=2 * MIB),
+        name="combine",
+    )(mine, other)
+
+
+def project_kernel(groups, place, weight, stream, mine, sibling, old_pool, _, *refs):
+    res_out, kv_out, pool, sems = refs
     half = place[1]
+
+    @pl.when(half == 0)
+    def _():
+        pltpu.make_async_copy(old_pool, pool, sems.at[0]).start()
+
     members, tokens, width = mine.shape
     sums = [stream[g * tokens : (g + 1) * tokens].astype(jnp.float32) for g in range(groups)]
     for h in range(KVH):
+        if h == KVH // 2:
+
+            @pl.when(half == 0)
+            def _():
+                pltpu.make_async_copy(old_pool, pool, sems.at[0]).wait()
+                pltpu.make_async_copy(pool, kv_out, sems.at[1]).start()
+
         for g in range(groups):
             m = h * groups + g
             first = jnp.where(half == 0, mine[m], sibling[m])
@@ -380,23 +415,56 @@
     for g in range(groups):
         res_out[g * tokens : (g + 1) * tokens] = sums[g].astype(res_out.dtype)
 
-
-def project(place, weight, stream, mine, sibling, groups):
+    @pl.when(half == 0)
+    def _():
+        pltpu.make_async_copy(pool, kv_out, sems.at[1]).wait()
+
+
+def project(place, weight, stream, mine, sibling, old_pool, kv, groups):
     return pl.pallas_call(
         functools.partial(project_kernel, groups),
-        out_shape=jax.ShapeDtypeStruct(stream.shape, jnp.bfloat16),
-        in_specs=[SM, VM, VM, VM, VM],
-        out_specs=VM,
-        compiler_params=pltpu.CompilerParams(vmem_limit_bytes=4 * MIB),
+        out_shape=[
+            jax.ShapeDtypeStruct(stream.shape, jnp.bfloat16),
+            jax.ShapeDtypeStruct(kv.shape, kv.dtype),
+        ],
+        in_specs=[SM, VM, VM, VM, VM, HBM, HBM],
+        out_specs=[VM, HBM],
+        scratch_shapes=[
+            pltpu.VMEM(kv.shape, kv.dtype),
+            pltpu.SemaphoreType.DMA((2,)),
+        ],
+        input_output_aliases={6: 1},
+        compiler_params=pltpu.CompilerParams(vmem_limit_bytes=6 * MIB),
         name="out_projection",
-    )(place, in_vmem(weight), stream, mine, sibling)
-
-
-def ffn_kernel(place, mine, sibling, gain, gate, *refs):
-    up = refs[:SPLIT]
-    down, own_out, other_out, down_buf, normed, hidden, down_sem = refs[SPLIT:]
-    half = place[1]
+    )(place, in_vmem(weight), stream, mine, sibling, in_hbm(old_pool), in_hbm(kv))
+
+
+def ffn_kernel(place, landing, mine, sibling, gain, *refs):
+    gate, up, refs = refs[:SPLIT], refs[SPLIT : 2 * SPLIT], refs[2 * SPLIT :]
+    down, late, _, own_out, other_out, kv_out = refs[:6]
+    down_buf, normed, hidden, down_sem, late_sem = refs[6:]
+    member, half = place[0], place[1]
     members, tokens, width = mine.shape
+    per_peer = ARRIVE // members
+    resident = kv_out.shape[0] - ARRIVE
+
+    def late_copy(i, k, c):
+        source = lax.rem(member - k + members, members)
+        spot = i * per_peer + c
+        return pltpu.make_async_copy(
+            late.at[spot], kv_out.at[resident + landing[source, c]], late_sem.at[spot]
+        )
+
+    late_chunks = [(0, 0), (1, 1), (2, members - 1)]
+
+    @pl.when(half == 1)
+    def _():
+        for i, k in late_chunks:
+
+            @pl.loop(0, per_peer)
+            def _(c):
+                late_copy(i, k, c).start()
+
     depth, hidden_count = up[0].shape
     features = depth * SPLIT
     down_copies = []
@@ -419,13 +487,13 @@
         x = jnp.concatenate([first, second], axis=1).astype(jnp.float32)
         cols = slice(2 * t * width, 2 * (t + 1) * width)
         normed[:, cols] = (x * factor * gain[cols][None, :]).astype(jnp.bfloat16)
-    tile = min(256, hidden_count)
+    tile = min(1024, hidden_count)
     for f in range(hidden_count // tile):
         cols = slice(f * tile, (f + 1) * tile)
-        gate_act = jnp.dot(normed[...], gate[:, cols], preferred_element_type=jnp.float32)
-        up_act = 0.0
+        gate_act = up_act = 0.0
         for i in range(SPLIT):
             x = normed[:, i * depth : (i + 1) * depth]
+            gate_act += jnp.dot(x, gate[i][:, cols], preferred_element_type=jnp.float32)
             up_act += jnp.dot(x, up[i][:, cols], preferred_element_type=jnp.float32)
         h = gate_act / (1.0 + jnp.exp(-gate_act)) * up_act
         hidden[:, cols] = h.astype(jnp.bfloat16)
@@ -440,8 +508,16 @@
         own_out[t] = jnp.where(half == 0, first, second)
         other_out[t] = jnp.where(half == 0, second, first).astype(jnp.bfloat16)
 
-
-def feed_forward(place, mine, sibling, gain, gate, up, down):
+    @pl.when(half == 1)
+    def _():
+        for i, k in late_chunks:
+
+            @pl.loop(0, per_peer)
+            def _(c):
+                late_copy(i, k, c).wait()
+
+
+def feed_forward(place, landing, mine, sibling, gain, gate, up, down, late, kv):
     tokens = mine.shape[1]
     hidden_count, features = down.shape
     return pl.pallas_call(
@@ -449,18 +525,29 @@
         out_shape=[
             jax.ShapeDtypeStruct(mine.shape, jnp.float32),
             jax.ShapeDtypeStruct(mine.shape, jnp.bfloat16),
-        ],
-        in_specs=[SM, VM, VM, VM] + [VM] * (1 + SPLIT) + [HBM],
-        out_specs=[VM, VM],
+            jax.ShapeDtypeStruct(kv.shape, kv.dtype),
+        ],
+        in_specs=[SM, SM, VM, VM, VM] + [VM] * (2 * SPLIT) + [HBM] * 3,
+        out_specs=[VM, VM, HBM],
+        input_output_aliases={5 + 2 * SPLIT + 2: 2},
         scratch_shapes=[
             pltpu.VMEM(down.shape, down.dtype),
             pltpu.VMEM((tokens, features), jnp.bfloat16),
             pltpu.VMEM((tokens, hidden_count), jnp.bfloat16),
             pltpu.SemaphoreType.DMA((mine.shape[0],)),
+            pltpu.SemaphoreType.DMA((late.shape[0],)),
         ],
         compiler_params=pltpu.CompilerParams(vmem_limit_bytes=19 * MIB),
         name="feed_forward",
-    )(place, mine, sibling, gain, *map(in_vmem, (gate, *up)), in_hbm(down))
+    )(
+        place,
+        landing,
+        mine,
+        sibling,
+        gain,
+        *map(in_vmem, (*gate, *up)),
+        *map(in_hbm, (down, late, kv)),
+    )
 
 
 def local(
@@ -516,22 +603,24 @@
         block_tables,
         page_list.reshape(members, slots),
         groups,
-        ((up_weight, SPLIT),),
+        ((out_proj, 1), (gate_weight, SPLIT), (up_weight, SPLIT)),
         (near,),
     )
 
-    arrived, landing = lax.optimization_barrier((arrived, landing))
-    last = lax.ppermute(
+    late = lax.ppermute(
         jnp.concatenate([own_chunk] + [arrived[host] for host in hosts]), "pd", [(0, 1)]
     )
-    arrays = [last] + [arrived[k] for k in sorted(arrived)]
-    chunks = [(0, 0, 0), (0, per_peer, 1), (0, 2 * per_peer, members - 1)]
-    chunks += [(i + 1, 0, k) for i, k in enumerate(sorted(arrived))]
+    order = sorted(arrived)
+    arrays = [own_chunk] + [arrived[k] for k in order]
+    chunks = (
+        [(0, 0)] + [(1 + order.index(host), k % members) for host, k in zip(hosts, (1, -1))],
+        [(1 + i, k) for i, k in enumerate(order)],
+    )
     padding = ((0, -tokens % 128), (0, 0))
     new_k = jnp.pad(fresh_kv[:, :, 0].reshape(tokens, HD), padding)
     new_v = jnp.pad(fresh_kv[:, :, 1].reshape(tokens, HD), padding)
     asked = [queries[:, st] for st in range(steps)]
-    kv_after, att_low, att_high = place_and_attend(
+    kv_part, keep, give = place_and_attend(
         place, landing, kv_pages, bias, new_k, new_v, asked, arrays, chunks
     )
 
@@ -540,15 +629,17 @@
         mine = lax.all_to_all(spread, "tp", split_axis=0, concat_axis=0)
         return mine, swap(mine)
 
-    att_mine = att_high + lax.ppermute(att_low, "pd", [(1, 0)])
+    att_mine = combine(keep, swap(give), tokens)
     here, there = everywhere(att_mine)
 
     inner = stream.reshape(steps, groups, rows, -1).transpose(1, 0, 2, 3).reshape(stream.shape)
-    residual = project(place, out_proj, inner, here, there, groups)
+    residual, kv_part = project(
+        place, held[0], inner, here, there, kv_pages, kv_part, groups
+    )
 
     mine, sibling = everywhere(residual)
-    own, other = feed_forward(
-        place, mine, sibling, norm_gain, gate_weight, held, down_weight
+    own, other, kv_after = feed_forward(
+        place, landing, mine, sibling, norm_gain, held[1 : 1 + SPLIT], held[1 + SPLIT :], down_weight, late, kv_part
     )
     summed = (own + swap(other).astype(jnp.float32)).astype(jnp.bfloat16)
     shares = lax.all_to_all(summed, "tp", split_axis=0, concat_axis=0)

time: 111 us -> 134 us (1.21)
  local copies, waits for them, and re-layouts: 4.45 us -> 19.9 us
  Pallas kernels: 32.5 us -> 42.1 us
  starting transfers between devices: 18.3 us -> 27.6 us
  waiting for transfers between devices: 10.7 us -> 3.78 us
  blocking collectives: 41.6 us -> 37.1 us
    ppermute x3 -> x4, starting transfers between devices: 0.2 us -> 15.7 us  [swap(): return lax.ppermute(x, 'pd', [(0, 1), (1, 0)])]
    unnamed x22 -> x42, local copies, waits for them, and re-layouts: 3.45 us -> 16.6 us
    pallas_call x1, Pallas kernels: 6.77 us -> 14.5 us  [prepare(): pl.pallas_call(functools.partial(prepare_kernel, count, parts, groups), o...]
    ppermute x1, starting transfers between devices: 7.37 us -> 2.46 us  [local(): lax.ppermute(jnp.concatenate([own_chunk] + [arrived[host] for host in hos...]
    all_to_all x2, blocking collectives: 29 us -> 25 us  [everywhere(): mine = lax.all_to_all(spread, 'tp', split_axis=0, concat_axis=0)]
    ppermute x5, waiting for transfers between devices: 2.82 us -> 0.01 us  [send(): return lax.ppermute(x, BOTH, route)]
    ppermute x1 -> x0, waiting for transfers between devices: 1.8 us -> none  [local(): att_mine = att_high + lax.ppermute(att_low, 'pd', [(1, 0)])]
    ppermute x1, waiting for transfers between devices: 1.59 us -> 0.01 us  [local(): lax.ppermute(jnp.concatenate([own_chunk] + [arrived[host] for host in hos...]
  transfers between devices with their start and end apart: 11 -> 11, of which waited for: 6 -> 3; matrix products, arithmetic and copies ran while one was open for 2% -> 3% of each run, Pallas kernels for 6% -> 14%
where the time goes in v9:
time: 134 us
  Pallas kernels  42.1 us (31%)
  blocking collectives  37.1 us (28%)
  starting transfers between devices  27.6 us (21%)
  local copies, waits for them, and re-layouts  19.9 us (15%)
  waiting for transfers between devices  3.78 us (3%)
  other arithmetic  2 us (1%)
    all_to_all x2, blocking collectives, everywhere(): mine = lax.all_to_all(spread, 'tp', split_axis=0, concat_axis=0)  25 us
    unnamed x42, local copies, waits for them, and re-layouts  16.6 us
    ppermute x4, starting transfers between devices, swap(): return lax.ppermute(x, 'pd', [(0, 1), (1, 0)])  15.7 us
    pallas_call x1, Pallas kernels, prepare(): pl.pallas_call(functools.partial(prepare_kernel, count, parts, groups), o...  14.5 us
    pallas_call x1, Pallas kernels, feed_forward(): pl.pallas_call(ffn_kernel, out_shape=[jax.ShapeDtypeStruct(mine.shape, jn...  14 us
    all_to_all x1, blocking collectives, local(): shares = lax.all_to_all(summed, 'tp', split_axis=0, concat_axis=0)  12.2 us
    ppermute x5, starting transfers between devices, send(): return lax.ppermute(x, BOTH, route)  8.12 us
    pallas_call x1, Pallas kernels, pack(): pl.pallas_call(functools.partial(pack_kernel, members), out_shape=[pltpu....  5.44 us
  transfers between devices with their start and end apart: 11, of which 3 were waited for; matrix products, arithmetic and copies ran while one was open for 3% of the time, Pallas kernels for 14%

profile of v9, /device:TPU:0, one launch (start us, length us, event | category | flops | bytes accessed | tf_op | source)
XLA Modules:
  0.0 133.5 jit_solution(16487341206585824108)
XLA Ops:
  0.7 5.4 %pack_pages.1 = (bf16[64,2,16,128]{3,2,1,0:T(8,128)(2,1)}, bf16[32,2,16,128]{3,2,1,0:T(8,128)(2,1)}, bf16[32,2,16,128]{3,2,1,0:T(8,128)(2,1)}, bf16[32,2,16,128]...) custom-call(s32[2]{0:T(128)S(1)} %pad_add_fusion.place, ...), custom_call_target="tpu_custom_call" | custom-call | tf_op jit(solution)/shard_map/pack_pages/pallas_call | solution.py:119
  6.2 1.3 collective-permute-start
  7.5 1.3 collective-permute-start.2
  8.8 1.3 collective-permute-start.3
  10.1 1.5 %collective-permute-start.4 = (bf16[32,2,16,128]{3,2,1,0:T(8,128)(2,1)}, bf16[32,2,16,128]{3,2,1,0:T(8,128)(2,1)S(1)}, u32[]{:S(2)}, u32[]{:S(2)}) collective-permute-start(bf16[32,2,16,128]{3,2,1,0:T(8,128)(2,1)} %get-tuple-element.32), channel_id=1, source_target_pairs={{0,11},{2,13},{4,15},{6,1},{8,3},{10,5},{12,7},{14,9},{16,27},{18,... | collective-permute-start | bytes 786440 | tf_op jit(solution)/shard_map/ppermute | solution.py:584
  11.6 1.0 fusion
  12.7 1.1 slice_select_fusion
  14.3 3.4 %collective-permute-start.1 = (bf16[32,2,16,128]{3,2,1,0:T(8,128)(2,1)S(1)}, bf16[32,2,16,128]{3,2,1,0:T(8,128)(2,1)S(1)}, u32[]{:S(2)}, u32[]{:S(2)}) collective-permute-start(bf16[32,2,16,128]{3,2,1,0:T(8,128)(2,1)S(1)} %get-tuple-element.47), channel_id=1, source_target_pairs={{0,5},{2,7},{4,9},{6,11},{8,13},{10,15},{12,1},{14,3},{1,2},{3,4},... | collective-permute-start | bytes 786440 | tf_op jit(solution)/shard_map/ppermute | solution.py:584
  17.8 0.8 fusion.1
  18.6 1.4 %reshape.9.listed = s32[8,312]{1,0:T(8,128)} reshape(s32[2496]{0:T(1024)} %pages.1) | data formatting | bytes 19968 | tf_op jit(solution)/shard_map/reshape | solution.py:604
  20.1 14.5 %prepare.1 = (bf16[512,8192]{1,0:T(8,128)(2,1)S(1)}, bf16[4096,1024]{1,0:T(8,128)(2,1)S(1)}, bf16[4096,1024]{1,0:T(8,128)(2,1)S(1)}, bf16[4096,1024]{1,0:T(8,128...) custom-call(s32[2]{0:T(128)} %copy-done.13, s32[8,312]{1,0:T(8,128)} %reshape.9.listed, ...), custom_call_target="tpu_custom_call" | custom-call | bytes 41943040 | tf_op jit(solution)/shard_map/prepare/pallas_call | solution.py:236
  34.6 3.3 %copy-done.4 = bf16[4096,1024]{1,0:T(8,128)(2,1)} copy-done((bf16[4096,1024]{1,0:T(8,128)(2,1)}, bf16[4096,1024]{1,0:T(8,128)(2,1)S(1)}, u32[]{:S(2)}) %copy-start.4) | copy-done | bytes 8388632
  37.9 3.2 %copy-done.5 = bf16[4096,1024]{1,0:T(8,128)(2,1)} copy-done((bf16[4096,1024]{1,0:T(8,128)(2,1)}, bf16[4096,1024]{1,0:T(8,128)(2,1)S(1)}, u32[]{:S(2)}) %copy-start.5) | copy-done | bytes 8388632
  41.3 1.2 copy-done.8
  42.5 0.7 copy-done.11
  43.2 0.7 copy-done.14
  43.8 4.0 %place_attend.1 = (bf16[312,2,16,128]{3,2,1,0:T(8,128)(2,1)}, f32[128,384]{1,0:T(8,128)S(1)}, f32[128,384]{1,0:T(8,128)S(1)}) custom-call(s32[2]{0:T(128)S(1)} %copy-done.14, s32[8,128]{1,0:T(8,128)S(1)} %copy-done.11, bf16[312,2,16,128]{3,2,1,0:T(8,128)(2,1)} %old_pool.3, f32[16,4992]{1,0:T(8,128)S(1)} %copy-done.8, bf16[128,128]{1,0:T(8,128)(2,1)S(1)} %pad.7.new_k, ...), custom_call_target="tpu_custom_call" | custom-call | tf_op jit(solution)/shard_map/place_attend/pallas_call | solution.py:348
  47.9 3.0 %collective-permute-start.6 = (f32[128,384]{1,0:T(8,128)S(1)}, f32[128,384]{1,0:T(8,128)S(1)}, u32[]{:S(2)}, u32[]{:S(2)}) collective-permute-start(f32[128,384]{1,0:T(8,128)S(1)} %get-tuple-element.35), channel_id=1, source_target_pairs={{0,1},{1,0},{2,3},{3,2},{4,5},{5,4},{6,7},{7,6},{8,9},{9,8},{10,11... | collective-permute-start | bytes 589832 | tf_op jit(solution)/shard_map/ppermute | solution.py:587
  50.9 1.1 collective-permute-done.6.other
  52.1 13.4 %all_to_all.15.mine = bf16[8,32,512]{2,1,0:T(8,128)(2,1)S(1)} all-to-all(bf16[8,32,512]{2,1,0:T(8,128)(2,1)S(1)} %broadcast_in_dim.4), channel_id=1, replica_groups=mesh['grp'=2,'tp'=8,'pd'=2] {'tp'}, dimensions={0} | all-to-all | bytes 524288 | tf_op jit(solution)/shard_map/all_to_all | solution.py:629
  65.6 2.5 %collective-permute-start.9 = (bf16[96,2,16,128]{3,2,1,0:T(8,128)(2,1)S(1)}, bf16[96,2,16,128]{3,2,1,0:T(8,128)(2,1)S(1)}, u32[]{:S(2)}, u32[]{:S(2)}) collective-permute-start(bf16[96,2,16,128]{3,2,1,0:T(8,128)(2,1)S(1)} %pad_maximum_fusion), channel_id=1, source_target_pairs={{0,1},{2,3},{4,5},{6,7},{8,9},{10,11},{12,13},{14,15},{16,17},{18,... | collective-permute-start | bytes 2359304 | tf_op jit(solution)/shard_map/ppermute | solution.py:610
  68.1 0.7 copy-done.15
  68.7 4.0 %out_projection.1 = (bf16[32,512]{1,0:T(8,128)(2,1)S(1)}, bf16[312,2,16,128]{3,2,1,0:T(8,128)(2,1)}) custom-call(s32[2]{0:T(128)S(1)} %copy-done.15, bf16[512,8192]{1,0:T(8,128)(2,1)S(1)} %get-tuple-element.26.weight, bf16[32,512]{1,0:T(8,128)(2,1)S(1)} %copy-done.9, bf16[8,32,512]{2,1,0:T(8,128)(2,1)S(1)} %all_to_all.15.mine, ...), custom_call_target="tpu_custom_call", output_to_operand_aliasing={{1}: (6, {})} | custom-call | tf_op jit(solution)/shard_map/out_projection/pallas_call | solution.py:424
  72.8 11.6 %all_to_all.16.mine = bf16[8,32,512]{2,1,0:T(8,128)(2,1)S(1)} all-to-all(bf16[8,32,512]{2,1,0:T(8,128)(2,1)S(1)} %broadcast_in_dim.5), channel_id=1, replica_groups=mesh['grp'=2,'tp'=8,'pd'=2] {'tp'}, dimensions={0} | all-to-all | bytes 524288 | tf_op jit(solution)/shard_map/all_to_all | solution.py:629
  84.4 1.5 %collective-permute-done.8.sibling = bf16[8,32,512]{2,1,0:T(8,128)(2,1)S(1)} collective-permute-done((bf16[8,32,512]{2,1,0:T(8,128)(2,1)S(1)}, bf16[8,32,512]{2,1,0:T(8,128)(2,1)S(1)}, u32[]{:S(2)}, u32[]{:S(2)}) %collective-permute-start.8) | collective-permute-done | bytes 262176 | tf_op jit(solution)/shard_map/ppermute | solution.py:587
  86.0 3.4 %copy-done.1 = bf16[4096,1024]{1,0:T(8,128)(2,1)S(1)} copy-done((bf16[4096,1024]{1,0:T(8,128)(2,1)S(1)}, bf16[4096,1024]{1,0:T(8,128)(2,1)}, u32[]{:S(2)}) %copy-start.1) | copy-done | bytes 8388632
  89.4 3.4 %copy-done.3 = bf16[4096,1024]{1,0:T(8,128)(2,1)S(1)} copy-done((bf16[4096,1024]{1,0:T(8,128)(2,1)S(1)}, bf16[4096,1024]{1,0:T(8,128)(2,1)}, u32[]{:S(2)}) %copy-start.3) | copy-done | bytes 8388632
  92.8 14.0 %feed_forward.1 = (f32[8,32,512]{2,1,0:T(8,128)S(1)}, bf16[8,32,512]{2,1,0:T(8,128)(2,1)S(1)}, bf16[312,2,16,128]{3,2,1,0:T(8,128)(2,1)}) custom-call(s32[2]{0:T(128)S(1)} %copy-done.16, s32[8,128]{1,0:T(8,128)S(1)} %copy-done.12, bf16[8,32,512]{2,1,0:T(8,128)(2,1)S(1)} %all_to_all.16.mine, ...), custom_call_target="tpu_custom_call", output_to_operand_aliasing={{2}: (11, {})} | custom-call | tf_op jit(solution)/shard_map/feed_forward/pallas_call | solution.py:523
  106.8 12.7 %collective-permute-start.10 = (bf16[8,32,512]{2,1,0:T(8,128)(2,1)S(1)}, bf16[8,32,512]{2,1,0:T(8,128)(2,1)S(1)}, u32[]{:S(2)}, u32[]{:S(2)}) collective-permute-start(bf16[8,32,512]{2,1,0:T(8,128)(2,1)S(1)} %get-tuple-element.45), channel_id=1, source_target_pairs={{0,1},{1,0},{2,3},{3,2},{4,5},{5,4},{6,7},{7,6},{8,9},{9,8},{10,11... | collective-permute-start | bytes 786440 | tf_op jit(solution)/shard_map/ppermute | solution.py:587
  119.5 1.2 collective-permute-done.10
  120.7 12.2 %all_to_all.17 = bf16[8,32,512]{2,1,0:T(8,128)(2,1)S(1)} all-to-all(bf16[8,32,512]{2,1,0:T(8,128)(2,1)S(1)} %add_convert_fusion), channel_id=1, replica_groups=mesh['grp'=2,'tp'=8,'pd'=2] {'tp'}, dimensions={0} | all-to-all | bytes 524288 | tf_op jit(solution)/shard_map/all_to_all | solution.py:645
  132.9 0.6 add_convert_fusion.1
  (56 shorter events, 1.1 us)
Async XLA Ops:
  0.7 19.3 %copy-start.13 = (s32[2]{0:T(128)}, s32[2]{0:T(128)S(1)}, u32[]{:S(2)}) copy-start(s32[2]{0:T(128)S(1)} %pad_add_fusion.place) | copy-start | bytes 28
  6.2 6.5 %collective-permute-start = (bf16[64,2,16,128]{3,2,1,0:T(8,128)(2,1)}, bf16[64,2,16,128]{3,2,1,0:T(8,128)(2,1)S(1)}, u32[]{:S(2)}, u32[]{:S(2)}) collective-permute-start(bf16[64,2,16,128]{3,2,1,0:T(8,128)(2,1)} %get-tuple-element.24.refs_3_), channel_id=1, source_target_pairs={{0,1},{2,3},{4,5},{6,7},{8,9},{10,11},{12,13},{14,15},{16,17},{18,... | collective-permute-start | bytes 1572872 | tf_op jit(solution)/shard_map/ppermute | solution.py:591
  7.5 33.7 %collective-permute-start.2 = (bf16[32,2,16,128]{3,2,1,0:T(8,128)(2,1)}, bf16[32,2,16,128]{3,2,1,0:T(8,128)(2,1)S(1)}, u32[]{:S(2)}, u32[]{:S(2)}) collective-permute-start(bf16[32,2,16,128]{3,2,1,0:T(8,128)(2,1)} %get-tuple-element.30), channel_id=1, source_target_pairs={{0,7},{2,9},{4,11},{6,13},{8,15},{10,1},{12,3},{14,5},{16,23},{18,... | collective-permute-start | bytes 786440 | tf_op jit(solution)/shard_map/ppermute | solution.py:584
  8.8 32.4 %collective-permute-start.3 = (bf16[32,2,16,128]{3,2,1,0:T(8,128)(2,1)}, bf16[32,2,16,128]{3,2,1,0:T(8,128)(2,1)S(1)}, u32[]{:S(2)}, u32[]{:S(2)}) collective-permute-start(bf16[32,2,16,128]{3,2,1,0:T(8,128)(2,1)} %get-tuple-element.31), channel_id=1, source_target_pairs={{0,9},{2,11},{4,13},{6,15},{8,1},{10,3},{12,5},{14,7},{16,25},{18,... | collective-permute-start | bytes 786440 | tf_op jit(solution)/shard_map/ppermute | solution.py:584
  10.1 31.1 %collective-permute-start.4 = (bf16[32,2,16,128]{3,2,1,0:T(8,128)(2,1)}, bf16[32,2,16,128]{3,2,1,0:T(8,128)(2,1)S(1)}, u32[]{:S(2)}, u32[]{:S(2)}) collective-permute-start(bf16[32,2,16,128]{3,2,1,0:T(8,128)(2,1)} %get-tuple-element.32), channel_id=1, source_target_pairs={{0,11},{2,13},{4,15},{6,1},{8,3},{10,5},{12,7},{14,9},{16,27},{18,... | collective-permute-start | bytes 786440 | tf_op jit(solution)/shard_map/ppermute | solution.py:584
  13.8 27.4 %collective-permute-start.5 = (bf16[32,2,16,128]{3,2,1,0:T(8,128)(2,1)S(1)}, bf16[32,2,16,128]{3,2,1,0:T(8,128)(2,1)S(1)}, u32[]{:S(2)}, u32[]{:S(2)}) collective-permute-start(bf16[32,2,16,128]{3,2,1,0:T(8,128)(2,1)S(1)} %get-tuple-element.46), channel_id=1, source_target_pairs={{0,13},{2,15},{4,1},{6,3},{8,5},{10,7},{12,9},{14,11},{1,14},{3,0}... | collective-permute-start | bytes 786440 | tf_op jit(solution)/shard_map/ppermute | solution.py:584
  14.3 26.9 %collective-permute-start.1 = (bf16[32,2,16,128]{3,2,1,0:T(8,128)(2,1)S(1)}, bf16[32,2,16,128]{3,2,1,0:T(8,128)(2,1)S(1)}, u32[]{:S(2)}, u32[]{:S(2)}) collective-permute-start(bf16[32,2,16,128]{3,2,1,0:T(8,128)(2,1)S(1)} %get-tuple-element.47), channel_id=1, source_target_pairs={{0,5},{2,7},{4,9},{6,11},{8,13},{10,15},{12,1},{14,3},{1,2},{3,4},... | collective-permute-start | bytes 786440 | tf_op jit(solution)/shard_map/ppermute | solution.py:584
  20.1 21.2 %copy-start.7 = (bf16[32,2,16,128]{3,2,1,0:T(8,128)(2,1)S(1)}, bf16[32,2,16,128]{3,2,1,0:T(8,128)(2,1)}, u32[]{:S(2)}) copy-start(bf16[32,2,16,128]{3,2,1,0:T(8,128)(2,1)} %get-tuple-element.28.refs_2_) | copy-start | bytes 786436
  20.1 48.0 %copy-start.9 = (bf16[32,512]{1,0:T(8,128)(2,1)S(1)}, bf16[32,512]{1,0:T(8,128)(2,1)}, u32[]{:S(2)}) copy-start(bf16[32,512]{1,0:T(8,128)(2,1)} %stream.1) | copy-start | bytes 98308
  34.6 3.3 %copy-start.4 = (bf16[4096,1024]{1,0:T(8,128)(2,1)}, bf16[4096,1024]{1,0:T(8,128)(2,1)S(1)}, u32[]{:S(2)}) copy-start(bf16[4096,1024]{1,0:T(8,128)(2,1)S(1)} %get-tuple-element.40.refs_2_) | copy-start | bytes 25165828
  37.9 3.2 %copy-start.5 = (bf16[4096,1024]{1,0:T(8,128)(2,1)}, bf16[4096,1024]{1,0:T(8,128)(2,1)S(1)}, u32[]{:S(2)}) copy-start(bf16[4096,1024]{1,0:T(8,128)(2,1)S(1)} %get-tuple-element.41.refs_3_) | copy-start | bytes 25165828
  41.1 31.6 %copy-start = (bf16[4096,1024]{1,0:T(8,128)(2,1)}, bf16[4096,1024]{1,0:T(8,128)(2,1)S(1)}, u32[]{:S(2)}) copy-start(bf16[4096,1024]{1,0:T(8,128)(2,1)S(1)} %get-tuple-element.38.refs_0_) | copy-start | bytes 25165828
  41.2 31.6 %copy-start.2 = (bf16[4096,1024]{1,0:T(8,128)(2,1)}, bf16[4096,1024]{1,0:T(8,128)(2,1)S(1)}, u32[]{:S(2)}) copy-start(bf16[4096,1024]{1,0:T(8,128)(2,1)S(1)} %get-tuple-element.39.refs_1_) | copy-start | bytes 25165828
  41.2 1.2 copy-start.8
  42.5 0.7 copy-start.11
  43.2 0.7 copy-start.14
  47.9 4.1 %collective-permute-start.6 = (f32[128,384]{1,0:T(8,128)S(1)}, f32[128,384]{1,0:T(8,128)S(1)}, u32[]{:S(2)}, u32[]{:S(2)}) collective-permute-start(f32[128,384]{1,0:T(8,128)S(1)} %get-tuple-element.35), channel_id=1, source_target_pairs={{0,1},{1,0},{2,3},{3,2},{4,5},{5,4},{6,7},{7,6},{8,9},{9,8},{10,11... | collective-permute-start | bytes 589832 | tf_op jit(solution)/shard_map/ppermute | solution.py:587
  52.0 33.9 %copy-start.16 = (s32[2]{0:T(128)S(1)}, s32[2]{0:T(128)}, u32[]{:S(2)}) copy-start(s32[2]{0:T(128)} %copy-done.13) | copy-start | bytes 28
  52.1 33.9 %slice-start = ((s8[8388608]{0:T(1024)(128)(4,1)}), s8[4194304]{0:T(1024)(128)(4,1)S(1)}, s32[]{:S(2)}) async-start(s8[8388608]{0:T(1024)(128)(4,1)} %bitcast.8), calls=%async_computation.3 | async-start | bytes 8388608
  52.1 33.9 %copy-start.6 = (bf16[4096,1024]{1,0:T(8,128)(2,1)S(1)}, bf16[4096,1024]{1,0:T(8,128)(2,1)}, u32[]{:S(2)}) copy-start(bf16[4096,1024]{1,0:T(8,128)(2,1)} %copy-done.5) | copy-start | bytes 25165828
  52.1 33.9 %copy-start.10 = (f32[8192]{0:T(1024)S(1)}, f32[8192]{0:T(1024)}, u32[]{:S(2)}) copy-start(f32[8192]{0:T(1024)} %gain.1) | copy-start | bytes 98308
  52.1 33.9 %copy-start.12 = (s32[8,128]{1,0:T(8,128)S(1)}, s32[8,128]{1,0:T(8,128)}, u32[]{:S(2)}) copy-start(s32[8,128]{1,0:T(8,128)} %get-tuple-element.25.landing) | copy-start | bytes 12292
  65.5 2.6 %collective-permute-start.7 = (bf16[8,32,512]{2,1,0:T(8,128)(2,1)S(1)}, bf16[8,32,512]{2,1,0:T(8,128)(2,1)S(1)}, u32[]{:S(2)}, u32[]{:S(2)}) collective-permute-start(bf16[8,32,512]{2,1,0:T(8,128)(2,1)S(1)} %all_to_all.15.mine), channel_id=1, source_target_pairs={{0,1},{1,0},{2,3},{3,2},{4,5},{5,4},{6,7},{7,6},{8,9},{9,8},{10,11... | collective-permute-start | bytes 786440 | tf_op jit(solution)/shard_map/ppermute | solution.py:587
  65.6 18.8 %collective-permute-start.9 = (bf16[96,2,16,128]{3,2,1,0:T(8,128)(2,1)S(1)}, bf16[96,2,16,128]{3,2,1,0:T(8,128)(2,1)S(1)}, u32[]{:S(2)}, u32[]{:S(2)}) collective-permute-start(bf16[96,2,16,128]{3,2,1,0:T(8,128)(2,1)S(1)} %pad_maximum_fusion), channel_id=1, source_target_pairs={{0,1},{2,3},{4,5},{6,7},{8,9},{10,11},{12,13},{14,15},{16,17},{18,... | collective-permute-start | bytes 2359304 | tf_op jit(solution)/shard_map/ppermute | solution.py:610
  68.1 0.7 copy-start.15
  68.7 17.3 %slice-start.1 = ((s8[8388608]{0:T(1024)(128)(4,1)}), s8[4194304]{0:T(1024)(128)(4,1)S(1)}, s32[]{:S(2)}) async-start(s8[8388608]{0:T(1024)(128)(4,1)} %bitcast.8), calls=%async_computation.4 | async-start | bytes 8388608
  84.4 1.5 %collective-permute-start.8 = (bf16[8,32,512]{2,1,0:T(8,128)(2,1)S(1)}, bf16[8,32,512]{2,1,0:T(8,128)(2,1)S(1)}, u32[]{:S(2)}, u32[]{:S(2)}) collective-permute-start(bf16[8,32,512]{2,1,0:T(8,128)(2,1)S(1)} %all_to_all.16.mine), channel_id=1, source_target_pairs={{0,1},{1,0},{2,3},{3,2},{4,5},{5,4},{6,7},{7,6},{8,9},{9,8},{10,11... | collective-permute-start | bytes 786440 | tf_op jit(solution)/shard_map/ppermute | solution.py:587
  84.4 1.5 %copy-start.17 = (bf16[96,2,16,128]{3,2,1,0:T(8,128)(2,1)}, bf16[96,2,16,128]{3,2,1,0:T(8,128)(2,1)S(1)}, u32[]{:S(2)}) copy-start(bf16[96,2,16,128]{3,2,1,0:T(8,128)(2,1)S(1)} %collective-permute-done.9.refs_5_) | copy-start | bytes 2359300
  86.0 3.4 %copy-start.1 = (bf16[4096,1024]{1,0:T(8,128)(2,1)S(1)}, bf16[4096,1024]{1,0:T(8,128)(2,1)}, u32[]{:S(2)}) copy-start(bf16[4096,1024]{1,0:T(8,128)(2,1)} %copy-done) | copy-start | bytes 25165828
  89.4 3.4 %copy-start.3 = (bf16[4096,1024]{1,0:T(8,128)(2,1)S(1)}, bf16[4096,1024]{1,0:T(8,128)(2,1)}, u32[]{:S(2)}) copy-start(bf16[4096,1024]{1,0:T(8,128)(2,1)} %copy-done.2) | copy-start | bytes 25165828
  106.8 13.8 %collective-permute-start.10 = (bf16[8,32,512]{2,1,0:T(8,128)(2,1)S(1)}, bf16[8,32,512]{2,1,0:T(8,128)(2,1)S(1)}, u32[]{:S(2)}, u32[]{:S(2)}) collective-permute-start(bf16[8,32,512]{2,1,0:T(8,128)(2,1)S(1)} %get-tuple-element.45), channel_id=1, source_target_pairs={{0,1},{1,0},{2,3},{3,2},{4,5},{5,4},{6,7},{7,6},{8,9},{9,8},{10,11... | collective-permute-start | bytes 786440 | tf_op jit(solution)/shard_map/ppermute | solution.py:587

commit v10 on v9

--- a/solution.py
+++ b/solution.py
@@ -17,7 +17,7 @@
 ARRIVE = REQ_DEV * NEWP
 MIB = 1024 * 1024
 BOTH = ("tp", "pd")
-SPLIT = 2
+SPLIT = 4
 
 VM = pl.BlockSpec(memory_space=pltpu.VMEM)
 SM = pl.BlockSpec(memory_space=pltpu.SMEM)
@@ -250,7 +250,7 @@
             pltpu.VMEM(tables.shape, tables.dtype),
             pltpu.SemaphoreType.DMA((parts + 2,)),
         ],
-        compiler_params=pltpu.CompilerParams(vmem_limit_bytes=16 * MIB),
+        compiler_params=pltpu.CompilerParams(vmem_limit_bytes=14 * MIB),
         cost_estimate=pl.CostEstimate(flops=0, bytes_accessed=moved, transcendentals=0),
         name="prepare",
     )(place, listed, *[in_hbm(x) for x in (lengths, tables, *weights, *first)])
@@ -258,8 +258,8 @@
 
 def attend_kernel(members, steps, chunks, place, landing, old_pool, bias, new_k, new_v, *refs):
     asked, refs = refs[:steps], refs[steps:]
-    arrived, refs = refs[:-6], refs[-6:]
-    kv_out, keep, give, pool, scores, sems = refs
+    arrived, refs = refs[:-7], refs[-7:]
+    kv_out, keep, give, late, pool, scores, sems = refs
     member, half = place[0], place[1]
     slots = pool.shape[0]
     resident = slots - ARRIVE
@@ -276,8 +276,17 @@
             def _(c):
                 pool[resident + landing[source, c]] = arrived[i][c]
 
+    late_copies = [
+        pltpu.make_async_copy(
+            arrived[i], late.at[pl.ds(n * per_peer, per_peer)], sems.at[2 + n]
+        )
+        for n, (i, _) in enumerate(chunks[0])
+    ]
+
     @pl.when(half == 0)
     def _():
+        for copy in late_copies:
+            copy.start()
         pool[:resident] = jnp.zeros((resident, *pool.shape[1:]), pool.dtype)
         place_pages(0)
 
@@ -338,6 +347,11 @@
     def _():
         pltpu.make_async_copy(pool, kv_out, sems.at[1]).wait()
 
+    @pl.when(half == 0)
+    def _():
+        for copy in late_copies:
+            copy.wait()
+
 
 def place_and_attend(place, landing, old_pool, bias, new_k, new_v, asked, arrived, chunks):
     members = landing.shape[0]
@@ -347,13 +361,18 @@
     part = jax.ShapeDtypeStruct((count // 2, 3 * HD), jnp.float32)
     return pl.pallas_call(
         functools.partial(attend_kernel, members, steps, chunks),
-        out_shape=[jax.ShapeDtypeStruct(old_pool.shape, old_pool.dtype), part, part],
+        out_shape=[
+            jax.ShapeDtypeStruct(old_pool.shape, old_pool.dtype),
+            part,
+            part,
+            jax.ShapeDtypeStruct((3 * ARRIVE // members, *old_pool.shape[1:]), old_pool.dtype),
+        ],
         in_specs=[SM, SM, HBM, VM, VM, VM] + [VM] * (steps + len(arrived)),
-        out_specs=[HBM, VM, VM],
+        out_specs=[HBM, VM, VM, HBM],
         scratch_shapes=[
             pltpu.VMEM(old_pool.shape, old_pool.dtype),
             pltpu.VMEM((count, slots * PAGE), jnp.float32),
-            pltpu.SemaphoreType.DMA((2,)),
+            pltpu.SemaphoreType.DMA((5,)),
         ],
         compiler_params=pltpu.CompilerParams(vmem_limit_bytes=9 * MIB),
         name="place_attend",
@@ -384,24 +403,11 @@
     )(mine, other)
 
 
-def project_kernel(groups, place, weight, stream, mine, sibling, old_pool, _, *refs):
-    res_out, kv_out, pool, sems = refs
+def project_kernel(groups, place, weight, stream, mine, sibling, res_out):
     half = place[1]
-
-    @pl.when(half == 0)
-    def _():
-        pltpu.make_async_copy(old_pool, pool, sems.at[0]).start()
-
     members, tokens, width = mine.shape
     sums = [stream[g * tokens : (g + 1) * tokens].astype(jnp.float32) for g in range(groups)]
     for h in range(KVH):
-        if h == KVH // 2:
-
-            @pl.when(half == 0)
-            def _():
-                pltpu.make_async_copy(old_pool, pool, sems.at[0]).wait()
-                pltpu.make_async_copy(pool, kv_out, sems.at[1]).start()
-
         for g in range(groups):
             m = h * groups + g
             first = jnp.where(half == 0, mine[m], sibling[m])
@@ -415,34 +421,22 @@
     for g in range(groups):
         res_out[g * tokens : (g + 1) * tokens] = sums[g].astype(res_out.dtype)
 
-    @pl.when(half == 0)
-    def _():
-        pltpu.make_async_copy(pool, kv_out, sems.at[1]).wait()
-
-
-def project(place, weight, stream, mine, sibling, old_pool, kv, groups):
+
+def project(place, weight, stream, mine, sibling, groups):
     return pl.pallas_call(
         functools.partial(project_kernel, groups),
-        out_shape=[
-            jax.ShapeDtypeStruct(stream.shape, jnp.bfloat16),
-            jax.ShapeDtypeStruct(kv.shape, kv.dtype),
-        ],
-        in_specs=[SM, VM, VM, VM, VM, HBM, HBM],
-        out_specs=[VM, HBM],
-        scratch_shapes=[
-            pltpu.VMEM(kv.shape, kv.dtype),
-            pltpu.SemaphoreType.DMA((2,)),
-        ],
-        input_output_aliases={6: 1},
-        compiler_params=pltpu.CompilerParams(vmem_limit_bytes=6 * MIB),
+        out_shape=jax.ShapeDtypeStruct(stream.shape, jnp.bfloat16),
+        in_specs=[SM, VM, VM, VM, VM],
+        out_specs=VM,
+        compiler_params=pltpu.CompilerParams(vmem_limit_bytes=4 * MIB),
         name="out_projection",
-    )(place, in_vmem(weight), stream, mine, sibling, in_hbm(old_pool), in_hbm(kv))
-
-
-def ffn_kernel(place, landing, mine, sibling, gain, *refs):
-    gate, up, refs = refs[:SPLIT], refs[SPLIT : 2 * SPLIT], refs[2 * SPLIT :]
-    down, late, _, own_out, other_out, kv_out = refs[:6]
-    down_buf, normed, hidden, down_sem, late_sem = refs[6:]
+    )(place, in_vmem(weight), stream, mine, sibling)
+
+
+def ffn_kernel(place, landing, mine, sibling, gain, gate, *refs):
+    up, refs = refs[:SPLIT], refs[SPLIT:]
+    down, late, old_pool, _, own_out, other_out, kv_out = refs[:7]
+    down_buf, normed, hidden, pool, down_sem, late_sem, pool_sem = refs[7:]
     member, half = place[0], place[1]
     members, tokens, width = mine.shape
     per_peer = ARRIVE // members
@@ -456,6 +450,13 @@
         )
 
     late_chunks = [(0, 0), (1, 1), (2, members - 1)]
+
+    pool_in = pltpu.make_async_copy(old_pool, pool, pool_sem.at[0])
+    pool_out = pltpu.make_async_copy(pool, kv_out, pool_sem.at[1])
+
+    @pl.when(half == 0)
+    def _():
+        pool_in.start()
 
     @pl.when(half == 1)
     def _():
@@ -490,13 +491,18 @@
     tile = min(1024, hidden_count)
     for f in range(hidden_count // tile):
         cols = slice(f * tile, (f + 1) * tile)
-        gate_act = up_act = 0.0
+        gate_act = jnp.dot(normed[...], gate[:, cols], preferred_element_type=jnp.float32)
+        up_act = 0.0
         for i in range(SPLIT):
             x = normed[:, i * depth : (i + 1) * depth]
-            gate_act += jnp.dot(x, gate[i][:, cols], preferred_element_type=jnp.float32)
             up_act += jnp.dot(x, up[i][:, cols], preferred_element_type=jnp.float32)
         h = gate_act / (1.0 + jnp.exp(-gate_act)) * up_act
         hidden[:, cols] = h.astype(jnp.bfloat16)
+    @pl.when(half == 0)
+    def _():
+        pool_in.wait()
+        pool_out.start()
+
     for t in range(members):
         down_copies[t].wait()
         part = jnp.dot(
@@ -508,6 +514,10 @@
         own_out[t] = jnp.where(half == 0, first, second)
         other_out[t] = jnp.where(half == 0, second, first).astype(jnp.bfloat16)
 
+    @pl.when(half == 0)
+    def _():
+        pool_out.wait()
+
     @pl.when(half == 1)
     def _():
         for i, k in late_chunks:
@@ -517,7 +527,7 @@
                 late_copy(i, k, c).wait()
 
 
-def feed_forward(place, landing, mine, sibling, gain, gate, up, down, late, kv):
+def feed_forward(place, landing, mine, sibling, gain, gate, up, down, late, old_pool, kv):
     tokens = mine.shape[1]
     hidden_count, features = down.shape
     return pl.pallas_call(
@@ -527,17 +537,19 @@
             jax.ShapeDtypeStruct(mine.shape, jnp.bfloat16),
             jax.ShapeDtypeStruct(kv.shape, kv.dtype),
         ],
-        in_specs=[SM, SM, VM, VM, VM] + [VM] * (2 * SPLIT) + [HBM] * 3,
+        in_specs=[SM, SM, VM, VM, VM] + [VM] * (1 + SPLIT) + [HBM, VM, HBM, HBM],
         out_specs=[VM, VM, HBM],
-        input_output_aliases={5 + 2 * SPLIT + 2: 2},
+        input_output_aliases={5 + 1 + SPLIT + 3: 2},
         scratch_shapes=[
             pltpu.VMEM(down.shape, down.dtype),
             pltpu.VMEM((tokens, features), jnp.bfloat16),
             pltpu.VMEM((tokens, hidden_count), jnp.bfloat16),
+            pltpu.VMEM(kv.shape, kv.dtype),
             pltpu.SemaphoreType.DMA((mine.shape[0],)),
             pltpu.SemaphoreType.DMA((late.shape[0],)),
+            pltpu.SemaphoreType.DMA((2,)),
         ],
-        compiler_params=pltpu.CompilerParams(vmem_limit_bytes=19 * MIB),
+        compiler_params=pltpu.CompilerParams(vmem_limit_bytes=21 * MIB),
         name="feed_forward",
     )(
         place,
@@ -545,8 +557,11 @@
         mine,
         sibling,
         gain,
-        *map(in_vmem, (*gate, *up)),
-        *map(in_hbm, (down, late, kv)),
+        *map(in_vmem, (gate, *up)),
+        in_hbm(down),
+        late,
+        in_hbm(old_pool),
+        in_hbm(kv),
     )
 
 
@@ -603,13 +618,10 @@
         block_tables,
         page_list.reshape(members, slots),
         groups,
-        ((out_proj, 1), (gate_weight, SPLIT), (up_weight, SPLIT)),
+        ((out_proj, 1), (up_weight, SPLIT)),
         (near,),
     )
 
-    late = lax.ppermute(
-        jnp.concatenate([own_chunk] + [arrived[host] for host in hosts]), "pd", [(0, 1)]
-    )
     order = sorted(arrived)
     arrays = [own_chunk] + [arrived[k] for k in order]
     chunks = (
@@ -620,9 +632,10 @@
     new_k = jnp.pad(fresh_kv[:, :, 0].reshape(tokens, HD), padding)
     new_v = jnp.pad(fresh_kv[:, :, 1].reshape(tokens, HD), padding)
     asked = [queries[:, st] for st in range(steps)]
-    kv_part, keep, give = place_and_attend(
+    kv_part, keep, give, late = place_and_attend(
         place, landing, kv_pages, bias, new_k, new_v, asked, arrays, chunks
     )
+    late = lax.ppermute(late, "pd", [(0, 1)])
 
     def everywhere(x):
         spread = jnp.broadcast_to(x[None], (members, *x.shape))
@@ -633,13 +646,11 @@
     here, there = everywhere(att_mine)
 
     inner = stream.reshape(steps, groups, rows, -1).transpose(1, 0, 2, 3).reshape(stream.shape)
-    residual, kv_part = project(
-        place, held[0], inner, here, there, kv_pages, kv_part, groups
-    )
+    residual = project(place, held[0], inner, here, there, groups)
 
     mine, sibling = everywhere(residual)
     own, other, kv_after = feed_forward(
-        place, landing, mine, sibling, norm_gain, held[1 : 1 + SPLIT], held[1 + SPLIT :], down_weight, late, kv_part
+        place, landing, mine, sibling, norm_gain, gate_weight, held[1:], down_weight, late, kv_pages, kv_part
     )
     summed = (own + swap(other).astype(jnp.float32)).astype(jnp.bfloat16)
     shares = lax.all_to_all(summed, "tp", split_axis=0, concat_axis=0)

time: 134 us -> 108 us (0.81)
  local copies, waits for them, and re-layouts: 19.9 us -> 1.3 us
  starting transfers between devices: 27.6 us -> 18.7 us
  blocking collectives: 37.1 us -> 42.1 us
  Pallas kernels: 42.1 us -> 38.2 us
    unnamed x42 -> x22, local copies, waits for them, and re-layouts: 16.6 us -> 0.07 us
    ppermute x4, starting transfers between devices: 15.7 us -> 6.77 us  [swap(): return lax.ppermute(x, 'pd', [(0, 1), (1, 0)])]
    pallas_call x1, Pallas kernels: 14.5 us -> 9.07 us  [prepare(): pl.pallas_call(functools.partial(prepare_kernel, count, parts, groups), o...]
    all_to_all x2, blocking collectives: 25 us -> 29.4 us  [everywhere(): mine = lax.all_to_all(spread, 'tp', split_axis=0, concat_axis=0)]
    pallas_call x1, Pallas kernels: 14 us -> 16.3 us  [feed_forward(): pl.pallas_call(ffn_kernel, out_shape=[jax.ShapeDtypeStruct(mine.shape, jn...]
  transfers between devices with their start and end apart: 11 -> 11, of which waited for: 3 -> 3; matrix products, arithmetic and copies ran while one was open for 3% -> 2% of each run, Pallas kernels for 14% -> 11%
where the time goes in v10:
time: 108 us
  blocking collectives  42.1 us (39%)
  Pallas kernels  38.2 us (35%)
  starting transfers between devices  18.7 us (17%)
  waiting for transfers between devices  3.78 us (4%)
  other arithmetic  2.95 us (3%)
  local copies, waits for them, and re-layouts  1.3 us (1%)
    all_to_all x2, blocking collectives, everywhere(): mine = lax.all_to_all(spread, 'tp', split_axis=0, concat_axis=0)  29.4 us
    pallas_call x1, Pallas kernels, feed_forward(): pl.pallas_call(ffn_kernel, out_shape=[jax.ShapeDtypeStruct(mine.shape, jn...  16.3 us
    all_to_all x1, blocking collectives, local(): shares = lax.all_to_all(summed, 'tp', split_axis=0, concat_axis=0)  12.7 us
    pallas_call x1, Pallas kernels, prepare(): pl.pallas_call(functools.partial(prepare_kernel, count, parts, groups), o...  9.07 us
    ppermute x5, starting transfers between devices, send(): return lax.ppermute(x, BOTH, route)  8.12 us
    ppermute x4, starting transfers between devices, swap(): return lax.ppermute(x, 'pd', [(0, 1), (1, 0)])  6.77 us
    pallas_call x1, Pallas kernels, pack(): pl.pallas_call(functools.partial(pack_kernel, members), out_shape=[pltpu....  5.46 us
    pallas_call x1, Pallas kernels, place_and_attend(): pl.pallas_call(functools.partial(attend_kernel, members, steps, chunks),...  4.13 us
  transfers between devices with their start and end apart: 11, of which 3 were waited for; matrix products, arithmetic and copies ran while one was open for 2% of the time, Pallas kernels for 11%

profile of v10, /device:TPU:0, one launch (start us, length us, event | category | flops | bytes accessed | tf_op | source)
XLA Modules:
  0.0 108.0 jit_solution(5930770534079557384)
XLA Ops:
  0.6 0.0 copy-start.5
  0.7 0.1 pad_add_fusion.place
  0.7 5.5 %pack_pages.1 = (bf16[64,2,16,128]{3,2,1,0:T(8,128)(2,1)}, bf16[32,2,16,128]{3,2,1,0:T(8,128)(2,1)}, bf16[32,2,16,128]{3,2,1,0:T(8,128)(2,1)}, bf16[32,2,16,128]...) custom-call(s32[2]{0:T(128)S(1)} %pad_add_fusion.place, ...), custom_call_target="tpu_custom_call" | custom-call | tf_op jit(solution)/shard_map/pack_pages/pallas_call | solution.py:119
  6.2 1.3 %collective-permute-start = (bf16[64,2,16,128]{3,2,1,0:T(8,128)(2,1)}, bf16[64,2,16,128]{3,2,1,0:T(8,128)(2,1)S(1)}, u32[]{:S(2)}, u32[]{:S(2)}) collective-permute-start(bf16[64,2,16,128]{3,2,1,0:T(8,128)(2,1)} %get-tuple-element.23.refs_2_), channel_id=1, source_target_pairs={{0,1},{2,3},{4,5},{6,7},{8,9},{10,11},{12,13},{14,15},{16,17},{18,... | collective-permute-start | bytes 1572872 | tf_op jit(solution)/shard_map/ppermute | solution.py:606
  7.5 1.3 %collective-permute-start.2 = (bf16[32,2,16,128]{3,2,1,0:T(8,128)(2,1)}, bf16[32,2,16,128]{3,2,1,0:T(8,128)(2,1)S(1)}, u32[]{:S(2)}, u32[]{:S(2)}) collective-permute-start(bf16[32,2,16,128]{3,2,1,0:T(8,128)(2,1)} %get-tuple-element.29), channel_id=1, source_target_pairs={{0,7},{2,9},{4,11},{6,13},{8,15},{10,1},{12,3},{14,5},{16,23},{18,... | collective-permute-start | bytes 786440 | tf_op jit(solution)/shard_map/ppermute | solution.py:599
  8.8 1.3 %collective-permute-start.3 = (bf16[32,2,16,128]{3,2,1,0:T(8,128)(2,1)}, bf16[32,2,16,128]{3,2,1,0:T(8,128)(2,1)S(1)}, u32[]{:S(2)}, u32[]{:S(2)}) collective-permute-start(bf16[32,2,16,128]{3,2,1,0:T(8,128)(2,1)} %get-tuple-element.30), channel_id=1, source_target_pairs={{0,9},{2,11},{4,13},{6,15},{8,1},{10,3},{12,5},{14,7},{16,25},{18,... | collective-permute-start | bytes 786440 | tf_op jit(solution)/shard_map/ppermute | solution.py:599
  10.2 1.5 %collective-permute-start.4 = (bf16[32,2,16,128]{3,2,1,0:T(8,128)(2,1)}, bf16[32,2,16,128]{3,2,1,0:T(8,128)(2,1)S(1)}, u32[]{:S(2)}, u32[]{:S(2)}) collective-permute-start(bf16[32,2,16,128]{3,2,1,0:T(8,128)(2,1)} %get-tuple-element.31), channel_id=1, source_target_pairs={{0,11},{2,13},{4,15},{6,1},{8,3},{10,5},{12,7},{14,9},{16,27},{18,... | collective-permute-start | bytes 786440 | tf_op jit(solution)/shard_map/ppermute | solution.py:599
  11.7 1.0 fusion
  12.7 1.1 %slice_select_fusion = (bf16[32,2,16,128]{3,2,1,0:T(8,128)(2,1)S(1)}, bf16[32,2,16,128]{3,2,1,0:T(8,128)(2,1)S(1)}) fusion(bf16[32,2,16,128]{3,2,1,0:T(8,128)(2,1)} %get-tuple-element.32, bf16[64,2,16,128]{3,2,1,0:T(8,128)(2,1)S(1)} %collective-permute-done, pred[]{:T(512)S(6)} %eq.4, bf16[32,2,16,128]{3,2,1,0:T(8,128)(2,1)} %get-tuple-element.28), kind=kLoop, calls=%fused_computation.2 | loop fusion | flops 262144 | bytes 1572865 | tf_op jit(solution)/shard_map/jit(_where)/select_n | solution.py:612
  13.8 0.6 collective-permute-start.5
  14.4 3.4 %collective-permute-start.1 = (bf16[32,2,16,128]{3,2,1,0:T(8,128)(2,1)S(1)}, bf16[32,2,16,128]{3,2,1,0:T(8,128)(2,1)S(1)}, u32[]{:S(2)}, u32[]{:S(2)}) collective-permute-start(bf16[32,2,16,128]{3,2,1,0:T(8,128)(2,1)S(1)} %get-tuple-element.45), channel_id=1, source_target_pairs={{0,5},{2,7},{4,9},{6,11},{8,13},{10,15},{12,1},{14,3},{1,2},{3,4},... | collective-permute-start | bytes 786440 | tf_op jit(solution)/shard_map/ppermute | solution.py:599
  17.9 0.1 reshape.9.listed
  18.0 0.0 slice-start
  18.1 9.1 %prepare.1 = (bf16[512,8192]{1,0:T(8,128)(2,1)S(1)}, bf16[2048,1024]{1,0:T(8,128)(2,1)S(1)}, bf16[2048,1024]{1,0:T(8,128)(2,1)S(1)}, bf16[2048,1024]{1,0:T(8,128...) custom-call(s32[2]{0:T(128)S(1)} %pad_add_fusion.place, ...), custom_call_target="tpu_custom_call" | custom-call | bytes 25165824 | tf_op jit(solution)/shard_map/prepare/pallas_call | solution.py:236
  27.1 0.0 copy-start.1
  27.2 4.1 %place_attend.1 = (bf16[312,2,16,128]{3,2,1,0:T(8,128)(2,1)}, f32[128,384]{1,0:T(8,128)S(1)}, f32[128,384]{1,0:T(8,128)S(1)}, bf16[96,2,16,128]{3,2,1,0:T(8,128)(2,1)S(1)}) custom-call(s32[2]{0:T(128)S(1)} %pad_add_fusion.place, s32[8,128]{1,0:T(8,128)S(1)} %get-tuple-element.24.landing, bf16[312,2,16,128]{3,2,1,0:T(8,128)(2,1)} %refs_6_.1, ...), custom_call_target="tpu_custom_call" | custom-call | tf_op jit(solution)/shard_map/place_attend/pallas_call | solution.py:362
  31.4 5.8 %collective-permute-start.6 = (f32[128,384]{1,0:T(8,128)S(1)}, f32[128,384]{1,0:T(8,128)S(1)}, u32[]{:S(2)}, u32[]{:S(2)}) collective-permute-start(f32[128,384]{1,0:T(8,128)S(1)} %get-tuple-element.34), channel_id=1, source_target_pairs={{0,1},{1,0},{2,3},{3,2},{4,5},{5,4},{6,7},{7,6},{8,9},{9,8},{10,11... | collective-permute-start | bytes 589832 | tf_op jit(solution)/shard_map/ppermute | solution.py:602
  37.2 1.1 collective-permute-done.6.other
  38.3 0.1 combine.1
  38.3 0.0 slice-start.3
  38.4 17.5 %all_to_all.15.mine = bf16[8,32,512]{2,1,0:T(8,128)(2,1)S(1)} all-to-all(bf16[8,32,512]{2,1,0:T(8,128)(2,1)S(1)} %broadcast_in_dim.4), channel_id=1, replica_groups=mesh['grp'=2,'tp'=8,'pd'=2] {'tp'}, dimensions={0} | all-to-all | bytes 524288 | tf_op jit(solution)/shard_map/all_to_all | solution.py:642
  55.9 2.4 %collective-permute-start.9 = (bf16[96,2,16,128]{3,2,1,0:T(8,128)(2,1)S(1)}, bf16[96,2,16,128]{3,2,1,0:T(8,128)(2,1)S(1)}, u32[]{:S(2)}, u32[]{:S(2)}) collective-permute-start(bf16[96,2,16,128]{3,2,1,0:T(8,128)(2,1)S(1)} %get-tuple-element.39), channel_id=1, source_target_pairs={{0,1},{2,3},{4,5},{6,7},{8,9},{10,11},{12,13},{14,15},{16,17},{18,... | collective-permute-start | bytes 2359304 | tf_op jit(solution)/shard_map/ppermute | solution.py:638
  58.3 0.0 copy-start.2
  58.4 3.1 %out_projection.1 = bf16[32,512]{1,0:T(8,128)(2,1)S(1)} custom-call(s32[2]{0:T(128)S(1)} %pad_add_fusion.place, bf16[512,8192]{1,0:T(8,128)(2,1)S(1)} %get-tuple-element.25.weight, bf16[32,512]{1,0:T(8,128)(2,1)S(1)} %copy-done.1, bf16[8,32,512]{2,1,0:T(8,128)(2,1)S(1)} %all_to_all.15.mine, bf16[8,32,512]{2,1,0:T(8,128)(2,1)S(1)} %collective-permute-done.7.sibling), custom_call_target="tpu_custom_call" | custom-call | tf_op jit(solution)/shard_map/out_projection/pallas_call | solution.py:426
  61.5 11.9 %all_to_all.16.mine = bf16[8,32,512]{2,1,0:T(8,128)(2,1)S(1)} all-to-all(bf16[8,32,512]{2,1,0:T(8,128)(2,1)S(1)} %broadcast_in_dim.5), channel_id=1, replica_groups=mesh['grp'=2,'tp'=8,'pd'=2] {'tp'}, dimensions={0} | all-to-all | bytes 524288 | tf_op jit(solution)/shard_map/all_to_all | solution.py:642
  73.4 1.5 %collective-permute-done.8.sibling = bf16[8,32,512]{2,1,0:T(8,128)(2,1)S(1)} collective-permute-done((bf16[8,32,512]{2,1,0:T(8,128)(2,1)S(1)}, bf16[8,32,512]{2,1,0:T(8,128)(2,1)S(1)}, u32[]{:S(2)}, u32[]{:S(2)}) %collective-permute-start.8) | collective-permute-done | bytes 262176 | tf_op jit(solution)/shard_map/ppermute | solution.py:602
  75.0 16.3 %feed_forward.1 = (f32[8,32,512]{2,1,0:T(8,128)}, bf16[8,32,512]{2,1,0:T(8,128)(2,1)S(1)}, bf16[312,2,16,128]{3,2,1,0:T(8,128)(2,1)}) custom-call(s32[2]{0:T(128)S(1)} %pad_add_fusion.place, s32[8,128]{1,0:T(8,128)S(1)} %get-tuple-element.24.landing, bf16[8,32,512]{2,1,0:T(8,128)(2,1)S(1)} %all_to_all.16.mine, ...), custom_call_target="tpu_custom_call", output_to_operand_aliasing={{2}: (13, {})} | custom-call | tf_op jit(solution)/shard_map/feed_forward/pallas_call | solution.py:533
  91.4 0.9 collective-permute-start.10
  92.3 1.2 %collective-permute-done.10 = bf16[8,32,512]{2,1,0:T(8,128)(2,1)S(1)} collective-permute-done((bf16[8,32,512]{2,1,0:T(8,128)(2,1)S(1)}, bf16[8,32,512]{2,1,0:T(8,128)(2,1)S(1)}, u32[]{:S(2)}, u32[]{:S(2)}) %collective-permute-start.10) | collective-permute-done | bytes 262176 | tf_op jit(solution)/shard_map/ppermute | solution.py:602
  93.4 1.1 %add_convert_fusion = bf16[8,32,512]{2,1,0:T(8,128)(2,1)S(1)} fusion(f32[8,32,512]{2,1,0:T(8,128)} %get-tuple-element.42, bf16[8,32,512]{2,1,0:T(8,128)(2,1)S(1)} %collective-permute-done.10), kind=kLoop, calls=%fused_computation.1 | loop fusion | flops 393216 | bytes 1048576 | tf_op jit(solution)/shard_map/convert_element_type | solution.py:655
  94.6 12.7 %all_to_all.17 = bf16[8,32,512]{2,1,0:T(8,128)(2,1)S(1)} all-to-all(bf16[8,32,512]{2,1,0:T(8,128)(2,1)S(1)} %add_convert_fusion), channel_id=1, replica_groups=mesh['grp'=2,'tp'=8,'pd'=2] {'tp'}, dimensions={0} | all-to-all | bytes 524288 | tf_op jit(solution)/shard_map/all_to_all | solution.py:656
  107.3 0.6 add_convert_fusion.1
  (35 shorter events, 0.2 us)
Async XLA Ops:
  0.6 17.2 %copy-start.5 = (s32[2496]{0:T(1024)S(1)}, s32[2496]{0:T(1024)}, u32[]{:S(2)}) copy-start(s32[2496]{0:T(1024)} %pages.1) | copy-start | bytes 29956
  0.6 17.2 %copy-start.4 = (bf16[16,2,2,128]{3,2,1,0:T(2,128)(2,1)S(1)}, bf16[16,2,2,128]{3,2,1,0:T(2,128)(2,1)}, u32[]{:S(2)}) copy-start(bf16[16,2,2,128]{3,2,1,0:T(2,128)(2,1)} %param.17) | copy-start | bytes 49156
  6.2 6.5 %collective-permute-start = (bf16[64,2,16,128]{3,2,1,0:T(8,128)(2,1)}, bf16[64,2,16,128]{3,2,1,0:T(8,128)(2,1)S(1)}, u32[]{:S(2)}, u32[]{:S(2)}) collective-permute-start(bf16[64,2,16,128]{3,2,1,0:T(8,128)(2,1)} %get-tuple-element.23.refs_2_), channel_id=1, source_target_pairs={{0,1},{2,3},{4,5},{6,7},{8,9},{10,11},{12,13},{14,15},{16,17},{18,... | collective-permute-start | bytes 1572872 | tf_op jit(solution)/shard_map/ppermute | solution.py:606
  7.5 19.6 %collective-permute-start.2 = (bf16[32,2,16,128]{3,2,1,0:T(8,128)(2,1)}, bf16[32,2,16,128]{3,2,1,0:T(8,128)(2,1)S(1)}, u32[]{:S(2)}, u32[]{:S(2)}) collective-permute-start(bf16[32,2,16,128]{3,2,1,0:T(8,128)(2,1)} %get-tuple-element.29), channel_id=1, source_target_pairs={{0,7},{2,9},{4,11},{6,13},{8,15},{10,1},{12,3},{14,5},{16,23},{18,... | collective-permute-start | bytes 786440 | tf_op jit(solution)/shard_map/ppermute | solution.py:599
  8.8 18.3 %collective-permute-start.3 = (bf16[32,2,16,128]{3,2,1,0:T(8,128)(2,1)}, bf16[32,2,16,128]{3,2,1,0:T(8,128)(2,1)S(1)}, u32[]{:S(2)}, u32[]{:S(2)}) collective-permute-start(bf16[32,2,16,128]{3,2,1,0:T(8,128)(2,1)} %get-tuple-element.30), channel_id=1, source_target_pairs={{0,9},{2,11},{4,13},{6,15},{8,1},{10,3},{12,5},{14,7},{16,25},{18,... | collective-permute-start | bytes 786440 | tf_op jit(solution)/shard_map/ppermute | solution.py:599
  10.2 17.0 %collective-permute-start.4 = (bf16[32,2,16,128]{3,2,1,0:T(8,128)(2,1)}, bf16[32,2,16,128]{3,2,1,0:T(8,128)(2,1)S(1)}, u32[]{:S(2)}, u32[]{:S(2)}) collective-permute-start(bf16[32,2,16,128]{3,2,1,0:T(8,128)(2,1)} %get-tuple-element.31), channel_id=1, source_target_pairs={{0,11},{2,13},{4,15},{6,1},{8,3},{10,5},{12,7},{14,9},{16,27},{18,... | collective-permute-start | bytes 786440 | tf_op jit(solution)/shard_map/ppermute | solution.py:599
  13.8 13.4 %collective-permute-start.5 = (bf16[32,2,16,128]{3,2,1,0:T(8,128)(2,1)S(1)}, bf16[32,2,16,128]{3,2,1,0:T(8,128)(2,1)S(1)}, u32[]{:S(2)}, u32[]{:S(2)}) collective-permute-start(bf16[32,2,16,128]{3,2,1,0:T(8,128)(2,1)S(1)} %get-tuple-element.44), channel_id=1, source_target_pairs={{0,13},{2,15},{4,1},{6,3},{8,5},{10,7},{12,9},{14,11},{1,14},{3,0}... | collective-permute-start | bytes 786440 | tf_op jit(solution)/shard_map/ppermute | solution.py:599
  14.4 12.8 %collective-permute-start.1 = (bf16[32,2,16,128]{3,2,1,0:T(8,128)(2,1)S(1)}, bf16[32,2,16,128]{3,2,1,0:T(8,128)(2,1)S(1)}, u32[]{:S(2)}, u32[]{:S(2)}) collective-permute-start(bf16[32,2,16,128]{3,2,1,0:T(8,128)(2,1)S(1)} %get-tuple-element.45), channel_id=1, source_target_pairs={{0,5},{2,7},{4,9},{6,11},{8,13},{10,15},{12,1},{14,3},{1,2},{3,4},... | collective-permute-start | bytes 786440 | tf_op jit(solution)/shard_map/ppermute | solution.py:599
  18.0 9.2 %copy-start = (bf16[32,2,16,128]{3,2,1,0:T(8,128)(2,1)S(1)}, bf16[32,2,16,128]{3,2,1,0:T(8,128)(2,1)}, u32[]{:S(2)}) copy-start(bf16[32,2,16,128]{3,2,1,0:T(8,128)(2,1)} %get-tuple-element.27.refs_2_) | copy-start | bytes 786436
  18.0 56.9 %slice-start = ((s8[16777216]{0:T(1024)(128)(4,1)}), s8[4194304]{0:T(1024)(128)(4,1)S(1)}, s32[]{:S(2)}) async-start(s8[16777216]{0:T(1024)(128)(4,1)} %bitcast.8), calls=%async_computation.3 | async-start | bytes 8388608
  18.0 56.9 %slice-start.1 = ((s8[16777216]{0:T(1024)(128)(4,1)}), s8[4194304]{0:T(1024)(128)(4,1)S(1)}, s32[]{:S(2)}) async-start(s8[16777216]{0:T(1024)(128)(4,1)} %bitcast.8), calls=%async_computation.4 | async-start | bytes 8388608
  18.0 56.9 %slice-start.2 = ((s8[16777216]{0:T(1024)(128)(4,1)}), s8[4194304]{0:T(1024)(128)(4,1)S(1)}, s32[]{:S(2)}) async-start(s8[16777216]{0:T(1024)(128)(4,1)} %bitcast.8), calls=%async_computation.5 | async-start | bytes 8388608
  27.1 31.2 %copy-start.1 = (bf16[32,512]{1,0:T(8,128)(2,1)S(1)}, bf16[32,512]{1,0:T(8,128)(2,1)}, u32[]{:S(2)}) copy-start(bf16[32,512]{1,0:T(8,128)(2,1)} %stream.1) | copy-start | bytes 98308
  31.4 6.9 %collective-permute-start.6 = (f32[128,384]{1,0:T(8,128)S(1)}, f32[128,384]{1,0:T(8,128)S(1)}, u32[]{:S(2)}, u32[]{:S(2)}) collective-permute-start(f32[128,384]{1,0:T(8,128)S(1)} %get-tuple-element.34), channel_id=1, source_target_pairs={{0,1},{1,0},{2,3},{3,2},{4,5},{5,4},{6,7},{7,6},{8,9},{9,8},{10,11... | collective-permute-start | bytes 589832 | tf_op jit(solution)/shard_map/ppermute | solution.py:602
  38.3 36.6 %slice-start.3 = ((s8[16777216]{0:T(1024)(128)(4,1)}), s8[4194304]{0:T(1024)(128)(4,1)S(1)}, s32[]{:S(2)}) async-start(s8[16777216]{0:T(1024)(128)(4,1)} %bitcast.8), calls=%async_computation.6 | async-start | bytes 8388608
  55.9 2.5 %collective-permute-start.7 = (bf16[8,32,512]{2,1,0:T(8,128)(2,1)S(1)}, bf16[8,32,512]{2,1,0:T(8,128)(2,1)S(1)}, u32[]{:S(2)}, u32[]{:S(2)}) collective-permute-start(bf16[8,32,512]{2,1,0:T(8,128)(2,1)S(1)} %all_to_all.15.mine), channel_id=1, source_target_pairs={{0,1},{1,0},{2,3},{3,2},{4,5},{5,4},{6,7},{7,6},{8,9},{9,8},{10,11... | collective-permute-start | bytes 786440 | tf_op jit(solution)/shard_map/ppermute | solution.py:602
  55.9 17.6 %collective-permute-start.9 = (bf16[96,2,16,128]{3,2,1,0:T(8,128)(2,1)S(1)}, bf16[96,2,16,128]{3,2,1,0:T(8,128)(2,1)S(1)}, u32[]{:S(2)}, u32[]{:S(2)}) collective-permute-start(bf16[96,2,16,128]{3,2,1,0:T(8,128)(2,1)S(1)} %get-tuple-element.39), channel_id=1, source_target_pairs={{0,1},{2,3},{4,5},{6,7},{8,9},{10,11},{12,13},{14,15},{16,17},{18,... | collective-permute-start | bytes 2359304 | tf_op jit(solution)/shard_map/ppermute | solution.py:638
  58.3 16.6 %copy-start.2 = (f32[8192]{0:T(1024)S(1)}, f32[8192]{0:T(1024)}, u32[]{:S(2)}) copy-start(f32[8192]{0:T(1024)} %gain.1) | copy-start | bytes 98308
  73.4 1.5 %collective-permute-start.8 = (bf16[8,32,512]{2,1,0:T(8,128)(2,1)S(1)}, bf16[8,32,512]{2,1,0:T(8,128)(2,1)S(1)}, u32[]{:S(2)}, u32[]{:S(2)}) collective-permute-start(bf16[8,32,512]{2,1,0:T(8,128)(2,1)S(1)} %all_to_all.16.mine), channel_id=1, source_target_pairs={{0,1},{1,0},{2,3},{3,2},{4,5},{5,4},{6,7},{7,6},{8,9},{9,8},{10,11... | collective-permute-start | bytes 786440 | tf_op jit(solution)/shard_map/ppermute | solution.py:602
  73.4 1.5 %copy-start.3 = (bf16[96,2,16,128]{3,2,1,0:T(8,128)(2,1)}, bf16[96,2,16,128]{3,2,1,0:T(8,128)(2,1)S(1)}, u32[]{:S(2)}) copy-start(bf16[96,2,16,128]{3,2,1,0:T(8,128)(2,1)S(1)} %collective-permute-done.9.refs_5_) | copy-start | bytes 2359300
  91.4 2.1 %collective-permute-start.10 = (bf16[8,32,512]{2,1,0:T(8,128)(2,1)S(1)}, bf16[8,32,512]{2,1,0:T(8,128)(2,1)S(1)}, u32[]{:S(2)}, u32[]{:S(2)}) collective-permute-start(bf16[8,32,512]{2,1,0:T(8,128)(2,1)S(1)} %get-tuple-element.43), channel_id=1, source_target_pairs={{0,1},{1,0},{2,3},{3,2},{4,5},{5,4},{6,7},{7,6},{8,9},{9,8},{10,11... | collective-permute-start | bytes 786440 | tf_op jit(solution)/shard_map/ppermute | solution.py:602

commit v11 on v10

--- a/solution.py
+++ b/solution.py
@@ -250,7 +250,7 @@
             pltpu.VMEM(tables.shape, tables.dtype),
             pltpu.SemaphoreType.DMA((parts + 2,)),
         ],
-        compiler_params=pltpu.CompilerParams(vmem_limit_bytes=14 * MIB),
+        compiler_params=pltpu.CompilerParams(vmem_limit_bytes=13 * MIB),
         cost_estimate=pl.CostEstimate(flops=0, bytes_accessed=moved, transcendentals=0),
         name="prepare",
     )(place, listed, *[in_hbm(x) for x in (lengths, tables, *weights, *first)])
@@ -258,8 +258,8 @@
 
 def attend_kernel(members, steps, chunks, place, landing, old_pool, bias, new_k, new_v, *refs):
     asked, refs = refs[:steps], refs[steps:]
-    arrived, refs = refs[:-7], refs[-7:]
-    kv_out, keep, give, late, pool, scores, sems = refs
+    arrived, refs = refs[:-8], refs[-8:]
+    kv_out, keep, give, late, pool, spare, scores, sems = refs
     member, half = place[0], place[1]
     slots = pool.shape[0]
     resident = slots - ARRIVE
@@ -276,6 +276,9 @@
             def _(c):
                 pool[resident + landing[source, c]] = arrived[i][c]
 
+    spare_in = pltpu.make_async_copy(old_pool, spare, sems.at[0])
+    spare_out = pltpu.make_async_copy(spare, kv_out, sems.at[1])
+
     late_copies = [
         pltpu.make_async_copy(
             arrived[i], late.at[pl.ds(n * per_peer, per_peer)], sems.at[2 + n]
@@ -285,10 +288,13 @@
 
     @pl.when(half == 0)
     def _():
+        spare_in.start()
         for copy in late_copies:
             copy.start()
         pool[:resident] = jnp.zeros((resident, *pool.shape[1:]), pool.dtype)
         place_pages(0)
+        spare_in.wait()
+        spare_out.start()
 
     @pl.when(half == 1)
     def _():
@@ -349,6 +355,7 @@
 
     @pl.when(half == 0)
     def _():
+        spare_out.wait()
         for copy in late_copies:
             copy.wait()
 
@@ -371,10 +378,11 @@
         out_specs=[HBM, VM, VM, HBM],
         scratch_shapes=[
             pltpu.VMEM(old_pool.shape, old_pool.dtype),
+            pltpu.VMEM(old_pool.shape, old_pool.dtype),
             pltpu.VMEM((count, slots * PAGE), jnp.float32),
             pltpu.SemaphoreType.DMA((5,)),
         ],
-        compiler_params=pltpu.CompilerParams(vmem_limit_bytes=9 * MIB),
+        compiler_params=pltpu.CompilerParams(vmem_limit_bytes=12 * MIB),
         name="place_attend",
     )(place, landing, in_hbm(old_pool), bias, new_k, new_v, *asked, *arrived)
 
@@ -435,8 +443,8 @@
 
 def ffn_kernel(place, landing, mine, sibling, gain, gate, *refs):
     up, refs = refs[:SPLIT], refs[SPLIT:]
-    down, late, old_pool, _, own_out, other_out, kv_out = refs[:7]
-    down_buf, normed, hidden, pool, down_sem, late_sem, pool_sem = refs[7:]
+    down, late, _, own_out, other_out, kv_out = refs[:6]
+    down_buf, normed, hidden, down_sem, late_sem = refs[6:]
     member, half = place[0], place[1]
     members, tokens, width = mine.shape
     per_peer = ARRIVE // members
@@ -450,13 +458,6 @@
         )
 
     late_chunks = [(0, 0), (1, 1), (2, members - 1)]
-
-    pool_in = pltpu.make_async_copy(old_pool, pool, pool_sem.at[0])
-    pool_out = pltpu.make_async_copy(pool, kv_out, pool_sem.at[1])
-
-    @pl.when(half == 0)
-    def _():
-        pool_in.start()
 
     @pl.when(half == 1)
     def _():
@@ -498,11 +499,6 @@
             up_act += jnp.dot(x, up[i][:, cols], preferred_element_type=jnp.float32)
         h = gate_act / (1.0 + jnp.exp(-gate_act)) * up_act
         hidden[:, cols] = h.astype(jnp.bfloat16)
-    @pl.when(half == 0)
-    def _():
-        pool_in.wait()
-        pool_out.start()
-
     for t in range(members):
         down_copies[t].wait()
         part = jnp.dot(
@@ -514,10 +510,6 @@
         own_out[t] = jnp.where(half == 0, first, second)
         other_out[t] = jnp.where(half == 0, second, first).astype(jnp.bfloat16)
 
-    @pl.when(half == 0)
-    def _():
-        pool_out.wait()
-
     @pl.when(half == 1)
     def _():
         for i, k in late_chunks:
@@ -527,7 +519,7 @@
                 late_copy(i, k, c).wait()
 
 
-def feed_forward(place, landing, mine, sibling, gain, gate, up, down, late, old_pool, kv):
+def feed_forward(place, landing, mine, sibling, gain, gate, up, down, late, kv):
     tokens = mine.shape[1]
     hidden_count, features = down.shape
     return pl.pallas_call(
@@ -537,19 +529,17 @@
             jax.ShapeDtypeStruct(mine.shape, jnp.bfloat16),
             jax.ShapeDtypeStruct(kv.shape, kv.dtype),
         ],
-        in_specs=[SM, SM, VM, VM, VM] + [VM] * (1 + SPLIT) + [HBM, VM, HBM, HBM],
+        in_specs=[SM, SM, VM, VM, VM] + [VM] * (1 + SPLIT) + [HBM, VM, HBM],
         out_specs=[VM, VM, HBM],
-        input_output_aliases={5 + 1 + SPLIT + 3: 2},
+        input_output_aliases={5 + 1 + SPLIT + 2: 2},
         scratch_shapes=[
             pltpu.VMEM(down.shape, down.dtype),
             pltpu.VMEM((tokens, features), jnp.bfloat16),
             pltpu.VMEM((tokens, hidden_count), jnp.bfloat16),
-            pltpu.VMEM(kv.shape, kv.dtype),
             pltpu.SemaphoreType.DMA((mine.shape[0],)),
             pltpu.SemaphoreType.DMA((late.shape[0],)),
-            pltpu.SemaphoreType.DMA((2,)),
         ],
-        compiler_params=pltpu.CompilerParams(vmem_limit_bytes=21 * MIB),
+        compiler_params=pltpu.CompilerParams(vmem_limit_bytes=19 * MIB),
         name="feed_forward",
     )(
         place,
@@ -560,7 +550,6 @@
         *map(in_vmem, (gate, *up)),
         in_hbm(down),
         late,
-        in_hbm(old_pool),
         in_hbm(kv),
     )
 
@@ -650,7 +639,7 @@
 
     mine, sibling = everywhere(residual)
     own, other, kv_after = feed_forward(
-        place, landing, mine, sibling, norm_gain, gate_weight, held[1:], down_weight, late, kv_pages, kv_part
+        place, landing, mine, sibling, norm_gain, gate_weight, held[1:], down_weight, late, kv_part
     )
     summed = (own + swap(other).astype(jnp.float32)).astype(jnp.bfloat16)
     shares = lax.all_to_all(summed, "tp", split_axis=0, concat_axis=0)

time: 108 us -> 107 us (level)
  starting transfers between devices: 18.7 us -> 17.5 us
    pallas_call x1, Pallas kernels: 16.3 us -> 14 us  [feed_forward(): pl.pallas_call(ffn_kernel, out_shape=[jax.ShapeDtypeStruct(mine.shape, jn...]
    pallas_call x1, Pallas kernels: 4.13 us -> 6.19 us  [place_and_attend(): pl.pallas_call(functools.partial(attend_kernel, members, steps, chunks),...]
    ppermute x4, starting transfers between devices: 6.77 us -> 5.63 us  [swap(): return lax.ppermute(x, 'pd', [(0, 1), (1, 0)])]
where the time goes in v11:
time: 107 us; the launch traced here: 106 us
  blocking collectives  43 us (40%)
  Pallas kernels  37.9 us (35%)
  starting transfers between devices  17.5 us (16%)
  waiting for transfers between devices  3.78 us (4%)
  other arithmetic  1.91 us (2%)
  local copies, waits for them, and re-layouts  1.3 us (1%)
    all_to_all x2, blocking collectives, everywhere(): mine = lax.all_to_all(spread, 'tp', split_axis=0, concat_axis=0)  30.2 us
    pallas_call x1, Pallas kernels, feed_forward(): pl.pallas_call(ffn_kernel, out_shape=[jax.ShapeDtypeStruct(mine.shape, jn...  14 us
    all_to_all x1, blocking collectives, local(): shares = lax.all_to_all(summed, 'tp', split_axis=0, concat_axis=0)  12.7 us
    pallas_call x1, Pallas kernels, prepare(): pl.pallas_call(functools.partial(prepare_kernel, count, parts, groups), o...  9.07 us
    ppermute x5, starting transfers between devices, send(): return lax.ppermute(x, BOTH, route)  8.12 us
    pallas_call x1, Pallas kernels, place_and_attend(): pl.pallas_call(functools.partial(attend_kernel, members, steps, chunks),...  6.19 us
    ppermute x4, starting transfers between devices, swap(): return lax.ppermute(x, 'pd', [(0, 1), (1, 0)])  5.63 us
    pallas_call x1, Pallas kernels, pack(): pl.pallas_call(functools.partial(pack_kernel, members), out_shape=[pltpu....  5.45 us
  transfers between devices with their start and end apart: 11, of which 3 were waited for; matrix products, arithmetic and copies ran while one was open for 2% of the time, Pallas kernels for 11%

profile of v11, /device:TPU:0, one launch (start us, length us, event | category | flops | bytes accessed | tf_op | source)
XLA Modules:
  0.0 106.3 jit_solution(8446321593620598855)
XLA Ops:
  0.6 0.0 copy-start.4
  0.7 0.1 pad_add_fusion.place
  0.7 5.4 %pack_pages.1 = (bf16[64,2,16,128]{3,2,1,0:T(8,128)(2,1)}, bf16[32,2,16,128]{3,2,1,0:T(8,128)(2,1)}, bf16[32,2,16,128]{3,2,1,0:T(8,128)(2,1)}, bf16[32,2,16,128]...) custom-call(s32[2]{0:T(128)S(1)} %pad_add_fusion.place, ...), custom_call_target="tpu_custom_call" | custom-call | tf_op jit(solution)/shard_map/pack_pages/pallas_call | solution.py:119
  6.2 1.3 %collective-permute-start = (bf16[64,2,16,128]{3,2,1,0:T(8,128)(2,1)}, bf16[64,2,16,128]{3,2,1,0:T(8,128)(2,1)S(1)}, u32[]{:S(2)}, u32[]{:S(2)}) collective-permute-start(bf16[64,2,16,128]{3,2,1,0:T(8,128)(2,1)} %get-tuple-element.23.refs_2_), channel_id=1, source_target_pairs={{0,1},{2,3},{4,5},{6,7},{8,9},{10,11},{12,13},{14,15},{16,17},{18,... | collective-permute-start | bytes 1572872 | tf_op jit(solution)/shard_map/ppermute | solution.py:595
  7.5 1.3 %collective-permute-start.2 = (bf16[32,2,16,128]{3,2,1,0:T(8,128)(2,1)}, bf16[32,2,16,128]{3,2,1,0:T(8,128)(2,1)S(1)}, u32[]{:S(2)}, u32[]{:S(2)}) collective-permute-start(bf16[32,2,16,128]{3,2,1,0:T(8,128)(2,1)} %get-tuple-element.29), channel_id=1, source_target_pairs={{0,7},{2,9},{4,11},{6,13},{8,15},{10,1},{12,3},{14,5},{16,23},{18,... | collective-permute-start | bytes 786440 | tf_op jit(solution)/shard_map/ppermute | solution.py:588
  8.8 1.3 %collective-permute-start.3 = (bf16[32,2,16,128]{3,2,1,0:T(8,128)(2,1)}, bf16[32,2,16,128]{3,2,1,0:T(8,128)(2,1)S(1)}, u32[]{:S(2)}, u32[]{:S(2)}) collective-permute-start(bf16[32,2,16,128]{3,2,1,0:T(8,128)(2,1)} %get-tuple-element.30), channel_id=1, source_target_pairs={{0,9},{2,11},{4,13},{6,15},{8,1},{10,3},{12,5},{14,7},{16,25},{18,... | collective-permute-start | bytes 786440 | tf_op jit(solution)/shard_map/ppermute | solution.py:588
  10.1 1.5 %collective-permute-start.4 = (bf16[32,2,16,128]{3,2,1,0:T(8,128)(2,1)}, bf16[32,2,16,128]{3,2,1,0:T(8,128)(2,1)S(1)}, u32[]{:S(2)}, u32[]{:S(2)}) collective-permute-start(bf16[32,2,16,128]{3,2,1,0:T(8,128)(2,1)} %get-tuple-element.31), channel_id=1, source_target_pairs={{0,11},{2,13},{4,15},{6,1},{8,3},{10,5},{12,7},{14,9},{16,27},{18,... | collective-permute-start | bytes 786440 | tf_op jit(solution)/shard_map/ppermute | solution.py:588
  11.7 1.0 fusion
  12.7 1.1 %slice_select_fusion = (bf16[32,2,16,128]{3,2,1,0:T(8,128)(2,1)S(1)}, bf16[32,2,16,128]{3,2,1,0:T(8,128)(2,1)S(1)}) fusion(bf16[32,2,16,128]{3,2,1,0:T(8,128)(2,1)} %get-tuple-element.32, bf16[64,2,16,128]{3,2,1,0:T(8,128)(2,1)S(1)} %collective-permute-done, pred[]{:T(512)S(6)} %eq.4, bf16[32,2,16,128]{3,2,1,0:T(8,128)(2,1)} %get-tuple-element.28), kind=kLoop, calls=%fused_computation.2 | loop fusion | flops 262144 | bytes 1572865 | tf_op jit(solution)/shard_map/jit(_where)/select_n | solution.py:601
  13.8 0.5 collective-permute-start.5
  14.4 3.4 %collective-permute-start.1 = (bf16[32,2,16,128]{3,2,1,0:T(8,128)(2,1)S(1)}, bf16[32,2,16,128]{3,2,1,0:T(8,128)(2,1)S(1)}, u32[]{:S(2)}, u32[]{:S(2)}) collective-permute-start(bf16[32,2,16,128]{3,2,1,0:T(8,128)(2,1)S(1)} %get-tuple-element.45), channel_id=1, source_target_pairs={{0,5},{2,7},{4,9},{6,11},{8,13},{10,15},{12,1},{14,3},{1,2},{3,4},... | collective-permute-start | bytes 786440 | tf_op jit(solution)/shard_map/ppermute | solution.py:588
  17.9 0.1 reshape.9.listed
  18.0 0.0 slice-start
  18.0 9.1 %prepare.1 = (bf16[512,8192]{1,0:T(8,128)(2,1)S(1)}, bf16[2048,1024]{1,0:T(8,128)(2,1)S(1)}, bf16[2048,1024]{1,0:T(8,128)(2,1)S(1)}, bf16[2048,1024]{1,0:T(8,128...) custom-call(s32[2]{0:T(128)S(1)} %pad_add_fusion.place, ...), custom_call_target="tpu_custom_call" | custom-call | bytes 25165824 | tf_op jit(solution)/shard_map/prepare/pallas_call | solution.py:236
  27.1 0.0 copy-start.1
  27.2 6.2 %place_attend.1 = (bf16[312,2,16,128]{3,2,1,0:T(8,128)(2,1)}, f32[128,384]{1,0:T(8,128)S(1)}, f32[128,384]{1,0:T(8,128)S(1)}, bf16[96,2,16,128]{3,2,1,0:T(8,128)(2,1)S(1)}) custom-call(s32[2]{0:T(128)S(1)} %pad_add_fusion.place, s32[8,128]{1,0:T(8,128)S(1)} %get-tuple-element.24.landing, bf16[312,2,16,128]{3,2,1,0:T(8,128)(2,1)} %old_pool.1, ...), custom_call_target="tpu_custom_call" | custom-call | tf_op jit(solution)/shard_map/place_attend/pallas_call | solution.py:369
  33.4 3.8 %collective-permute-start.6 = (f32[128,384]{1,0:T(8,128)S(1)}, f32[128,384]{1,0:T(8,128)S(1)}, u32[]{:S(2)}, u32[]{:S(2)}) collective-permute-start(f32[128,384]{1,0:T(8,128)S(1)} %get-tuple-element.34), channel_id=1, source_target_pairs={{0,1},{1,0},{2,3},{3,2},{4,5},{5,4},{6,7},{7,6},{8,9},{9,8},{10,11... | collective-permute-start | bytes 589832 | tf_op jit(solution)/shard_map/ppermute | solution.py:591
  37.2 1.1 %collective-permute-done.6.other = f32[128,384]{1,0:T(8,128)S(1)} collective-permute-done((f32[128,384]{1,0:T(8,128)S(1)}, f32[128,384]{1,0:T(8,128)S(1)}, u32[]{:S(2)}, u32[]{:S(2)}) %collective-permute-start.6) | collective-permute-done | bytes 196640 | tf_op jit(solution)/shard_map/ppermute | solution.py:591
  38.3 0.1 combine.1
  38.3 0.0 slice-start.3
  38.4 18.3 %all_to_all.15.mine = bf16[8,32,512]{2,1,0:T(8,128)(2,1)S(1)} all-to-all(bf16[8,32,512]{2,1,0:T(8,128)(2,1)S(1)} %broadcast_in_dim.4), channel_id=1, replica_groups=mesh['grp'=2,'tp'=8,'pd'=2] {'tp'}, dimensions={0} | all-to-all | bytes 524288 | tf_op jit(solution)/shard_map/all_to_all | solution.py:631
  56.7 2.4 %collective-permute-start.9 = (bf16[96,2,16,128]{3,2,1,0:T(8,128)(2,1)S(1)}, bf16[96,2,16,128]{3,2,1,0:T(8,128)(2,1)S(1)}, u32[]{:S(2)}, u32[]{:S(2)}) collective-permute-start(bf16[96,2,16,128]{3,2,1,0:T(8,128)(2,1)S(1)} %get-tuple-element.39), channel_id=1, source_target_pairs={{0,1},{2,3},{4,5},{6,7},{8,9},{10,11},{12,13},{14,15},{16,17},{18,... | collective-permute-start | bytes 2359304 | tf_op jit(solution)/shard_map/ppermute | solution.py:627
  59.2 0.0 copy-start.2
  59.2 3.1 %out_projection.1 = bf16[32,512]{1,0:T(8,128)(2,1)S(1)} custom-call(s32[2]{0:T(128)S(1)} %pad_add_fusion.place, bf16[512,8192]{1,0:T(8,128)(2,1)S(1)} %get-tuple-element.25.weight, bf16[32,512]{1,0:T(8,128)(2,1)S(1)} %copy-done.1, bf16[8,32,512]{2,1,0:T(8,128)(2,1)S(1)} %all_to_all.15.mine, bf16[8,32,512]{2,1,0:T(8,128)(2,1)S(1)} %collective-permute-done.7.sibling), custom_call_target="tpu_custom_call" | custom-call | tf_op jit(solution)/shard_map/out_projection/pallas_call | solution.py:434
  62.3 11.9 %all_to_all.16.mine = bf16[8,32,512]{2,1,0:T(8,128)(2,1)S(1)} all-to-all(bf16[8,32,512]{2,1,0:T(8,128)(2,1)S(1)} %broadcast_in_dim.5), channel_id=1, replica_groups=mesh['grp'=2,'tp'=8,'pd'=2] {'tp'}, dimensions={0} | all-to-all | bytes 524288 | tf_op jit(solution)/shard_map/all_to_all | solution.py:631
  74.2 1.5 %collective-permute-done.8.sibling = bf16[8,32,512]{2,1,0:T(8,128)(2,1)S(1)} collective-permute-done((bf16[8,32,512]{2,1,0:T(8,128)(2,1)S(1)}, bf16[8,32,512]{2,1,0:T(8,128)(2,1)S(1)}, u32[]{:S(2)}, u32[]{:S(2)}) %collective-permute-start.8) | collective-permute-done | bytes 262176 | tf_op jit(solution)/shard_map/ppermute | solution.py:591
  75.8 14.0 %feed_forward.1 = (f32[8,32,512]{2,1,0:T(8,128)S(1)}, bf16[8,32,512]{2,1,0:T(8,128)(2,1)S(1)}, bf16[312,2,16,128]{3,2,1,0:T(8,128)(2,1)}) custom-call(s32[2]{0:T(128)S(1)} %pad_add_fusion.place, s32[8,128]{1,0:T(8,128)S(1)} %get-tuple-element.24.landing, bf16[8,32,512]{2,1,0:T(8,128)(2,1)S(1)} %all_to_all.16.mine, ...), custom_call_target="tpu_custom_call", output_to_operand_aliasing={{2}: (12, {})} | custom-call | tf_op jit(solution)/shard_map/feed_forward/pallas_call | solution.py:525
  89.8 1.9 %collective-permute-start.10 = (bf16[8,32,512]{2,1,0:T(8,128)(2,1)S(1)}, bf16[8,32,512]{2,1,0:T(8,128)(2,1)S(1)}, u32[]{:S(2)}, u32[]{:S(2)}) collective-permute-start(bf16[8,32,512]{2,1,0:T(8,128)(2,1)S(1)} %get-tuple-element.43), channel_id=1, source_target_pairs={{0,1},{1,0},{2,3},{3,2},{4,5},{5,4},{6,7},{7,6},{8,9},{9,8},{10,11... | collective-permute-start | bytes 786440 | tf_op jit(solution)/shard_map/ppermute | solution.py:591
  91.7 1.2 %collective-permute-done.10 = bf16[8,32,512]{2,1,0:T(8,128)(2,1)S(1)} collective-permute-done((bf16[8,32,512]{2,1,0:T(8,128)(2,1)S(1)}, bf16[8,32,512]{2,1,0:T(8,128)(2,1)S(1)}, u32[]{:S(2)}, u32[]{:S(2)}) %collective-permute-start.10) | collective-permute-done | bytes 262176 | tf_op jit(solution)/shard_map/ppermute | solution.py:591
  92.8 0.1 add_convert_fusion
  92.9 12.7 %all_to_all.17 = bf16[8,32,512]{2,1,0:T(8,128)(2,1)S(1)} all-to-all(bf16[8,32,512]{2,1,0:T(8,128)(2,1)S(1)} %add_convert_fusion), channel_id=1, replica_groups=mesh['grp'=2,'tp'=8,'pd'=2] {'tp'}, dimensions={0} | all-to-all | bytes 524288 | tf_op jit(solution)/shard_map/all_to_all | solution.py:645
  105.7 0.6 add_convert_fusion.1
  (33 shorter events, 0.2 us)
Async XLA Ops:
  0.6 17.2 %copy-start.4 = (s32[2496]{0:T(1024)S(1)}, s32[2496]{0:T(1024)}, u32[]{:S(2)}) copy-start(s32[2496]{0:T(1024)} %pages.1) | copy-start | bytes 29956
  0.6 17.2 %copy-start.3 = (bf16[16,2,2,128]{3,2,1,0:T(2,128)(2,1)S(1)}, bf16[16,2,2,128]{3,2,1,0:T(2,128)(2,1)}, u32[]{:S(2)}) copy-start(bf16[16,2,2,128]{3,2,1,0:T(2,128)(2,1)} %param.17) | copy-start | bytes 49156
  6.2 6.5 %collective-permute-start = (bf16[64,2,16,128]{3,2,1,0:T(8,128)(2,1)}, bf16[64,2,16,128]{3,2,1,0:T(8,128)(2,1)S(1)}, u32[]{:S(2)}, u32[]{:S(2)}) collective-permute-start(bf16[64,2,16,128]{3,2,1,0:T(8,128)(2,1)} %get-tuple-element.23.refs_2_), channel_id=1, source_target_pairs={{0,1},{2,3},{4,5},{6,7},{8,9},{10,11},{12,13},{14,15},{16,17},{18,... | collective-permute-start | bytes 1572872 | tf_op jit(solution)/shard_map/ppermute | solution.py:595
  7.5 19.6 %collective-permute-start.2 = (bf16[32,2,16,128]{3,2,1,0:T(8,128)(2,1)}, bf16[32,2,16,128]{3,2,1,0:T(8,128)(2,1)S(1)}, u32[]{:S(2)}, u32[]{:S(2)}) collective-permute-start(bf16[32,2,16,128]{3,2,1,0:T(8,128)(2,1)} %get-tuple-element.29), channel_id=1, source_target_pairs={{0,7},{2,9},{4,11},{6,13},{8,15},{10,1},{12,3},{14,5},{16,23},{18,... | collective-permute-start | bytes 786440 | tf_op jit(solution)/shard_map/ppermute | solution.py:588
  8.8 18.3 %collective-permute-start.3 = (bf16[32,2,16,128]{3,2,1,0:T(8,128)(2,1)}, bf16[32,2,16,128]{3,2,1,0:T(8,128)(2,1)S(1)}, u32[]{:S(2)}, u32[]{:S(2)}) collective-permute-start(bf16[32,2,16,128]{3,2,1,0:T(8,128)(2,1)} %get-tuple-element.30), channel_id=1, source_target_pairs={{0,9},{2,11},{4,13},{6,15},{8,1},{10,3},{12,5},{14,7},{16,25},{18,... | collective-permute-start | bytes 786440 | tf_op jit(solution)/shard_map/ppermute | solution.py:588
  10.1 17.0 %collective-permute-start.4 = (bf16[32,2,16,128]{3,2,1,0:T(8,128)(2,1)}, bf16[32,2,16,128]{3,2,1,0:T(8,128)(2,1)S(1)}, u32[]{:S(2)}, u32[]{:S(2)}) collective-permute-start(bf16[32,2,16,128]{3,2,1,0:T(8,128)(2,1)} %get-tuple-element.31), channel_id=1, source_target_pairs={{0,11},{2,13},{4,15},{6,1},{8,3},{10,5},{12,7},{14,9},{16,27},{18,... | collective-permute-start | bytes 786440 | tf_op jit(solution)/shard_map/ppermute | solution.py:588
  13.8 13.4 %collective-permute-start.5 = (bf16[32,2,16,128]{3,2,1,0:T(8,128)(2,1)S(1)}, bf16[32,2,16,128]{3,2,1,0:T(8,128)(2,1)S(1)}, u32[]{:S(2)}, u32[]{:S(2)}) collective-permute-start(bf16[32,2,16,128]{3,2,1,0:T(8,128)(2,1)S(1)} %get-tuple-element.44), channel_id=1, source_target_pairs={{0,13},{2,15},{4,1},{6,3},{8,5},{10,7},{12,9},{14,11},{1,14},{3,0}... | collective-permute-start | bytes 786440 | tf_op jit(solution)/shard_map/ppermute | solution.py:588
  14.4 12.8 %collective-permute-start.1 = (bf16[32,2,16,128]{3,2,1,0:T(8,128)(2,1)S(1)}, bf16[32,2,16,128]{3,2,1,0:T(8,128)(2,1)S(1)}, u32[]{:S(2)}, u32[]{:S(2)}) collective-permute-start(bf16[32,2,16,128]{3,2,1,0:T(8,128)(2,1)S(1)} %get-tuple-element.45), channel_id=1, source_target_pairs={{0,5},{2,7},{4,9},{6,11},{8,13},{10,15},{12,1},{14,3},{1,2},{3,4},... | collective-permute-start | bytes 786440 | tf_op jit(solution)/shard_map/ppermute | solution.py:588
  18.0 9.2 %copy-start = (bf16[32,2,16,128]{3,2,1,0:T(8,128)(2,1)S(1)}, bf16[32,2,16,128]{3,2,1,0:T(8,128)(2,1)}, u32[]{:S(2)}) copy-start(bf16[32,2,16,128]{3,2,1,0:T(8,128)(2,1)} %get-tuple-element.27.refs_2_) | copy-start | bytes 786436
  18.0 57.8 %slice-start = ((s8[16777216]{0:T(1024)(128)(4,1)}), s8[4194304]{0:T(1024)(128)(4,1)S(1)}, s32[]{:S(2)}) async-start(s8[16777216]{0:T(1024)(128)(4,1)} %bitcast.8), calls=%async_computation.3 | async-start | bytes 8388608
  18.0 57.7 %slice-start.1 = ((s8[16777216]{0:T(1024)(128)(4,1)}), s8[4194304]{0:T(1024)(128)(4,1)S(1)}, s32[]{:S(2)}) async-start(s8[16777216]{0:T(1024)(128)(4,1)} %bitcast.8), calls=%async_computation.4 | async-start | bytes 8388608
  18.0 57.7 %slice-start.2 = ((s8[16777216]{0:T(1024)(128)(4,1)}), s8[4194304]{0:T(1024)(128)(4,1)S(1)}, s32[]{:S(2)}) async-start(s8[16777216]{0:T(1024)(128)(4,1)} %bitcast.8), calls=%async_computation.5 | async-start | bytes 8388608
  27.1 32.0 %copy-start.1 = (bf16[32,512]{1,0:T(8,128)(2,1)S(1)}, bf16[32,512]{1,0:T(8,128)(2,1)}, u32[]{:S(2)}) copy-start(bf16[32,512]{1,0:T(8,128)(2,1)} %stream.1) | copy-start | bytes 98308
  33.4 4.8 %collective-permute-start.6 = (f32[128,384]{1,0:T(8,128)S(1)}, f32[128,384]{1,0:T(8,128)S(1)}, u32[]{:S(2)}, u32[]{:S(2)}) collective-permute-start(f32[128,384]{1,0:T(8,128)S(1)} %get-tuple-element.34), channel_id=1, source_target_pairs={{0,1},{1,0},{2,3},{3,2},{4,5},{5,4},{6,7},{7,6},{8,9},{9,8},{10,11... | collective-permute-start | bytes 589832 | tf_op jit(solution)/shard_map/ppermute | solution.py:591
  38.3 37.4 %slice-start.3 = ((s8[16777216]{0:T(1024)(128)(4,1)}), s8[4194304]{0:T(1024)(128)(4,1)S(1)}, s32[]{:S(2)}) async-start(s8[16777216]{0:T(1024)(128)(4,1)} %bitcast.8), calls=%async_computation.6 | async-start | bytes 8388608
  56.7 2.5 %collective-permute-start.7 = (bf16[8,32,512]{2,1,0:T(8,128)(2,1)S(1)}, bf16[8,32,512]{2,1,0:T(8,128)(2,1)S(1)}, u32[]{:S(2)}, u32[]{:S(2)}) collective-permute-start(bf16[8,32,512]{2,1,0:T(8,128)(2,1)S(1)} %all_to_all.15.mine), channel_id=1, source_target_pairs={{0,1},{1,0},{2,3},{3,2},{4,5},{5,4},{6,7},{7,6},{8,9},{9,8},{10,11... | collective-permute-start | bytes 786440 | tf_op jit(solution)/shard_map/ppermute | solution.py:591
  56.7 17.6 %collective-permute-start.9 = (bf16[96,2,16,128]{3,2,1,0:T(8,128)(2,1)S(1)}, bf16[96,2,16,128]{3,2,1,0:T(8,128)(2,1)S(1)}, u32[]{:S(2)}, u32[]{:S(2)}) collective-permute-start(bf16[96,2,16,128]{3,2,1,0:T(8,128)(2,1)S(1)} %get-tuple-element.39), channel_id=1, source_target_pairs={{0,1},{2,3},{4,5},{6,7},{8,9},{10,11},{12,13},{14,15},{16,17},{18,... | collective-permute-start | bytes 2359304 | tf_op jit(solution)/shard_map/ppermute | solution.py:627
  59.2 16.6 %copy-start.2 = (f32[8192]{0:T(1024)S(1)}, f32[8192]{0:T(1024)}, u32[]{:S(2)}) copy-start(f32[8192]{0:T(1024)} %gain.1) | copy-start | bytes 98308
  74.2 1.5 %collective-permute-start.8 = (bf16[8,32,512]{2,1,0:T(8,128)(2,1)S(1)}, bf16[8,32,512]{2,1,0:T(8,128)(2,1)S(1)}, u32[]{:S(2)}, u32[]{:S(2)}) collective-permute-start(bf16[8,32,512]{2,1,0:T(8,128)(2,1)S(1)} %all_to_all.16.mine), channel_id=1, source_target_pairs={{0,1},{1,0},{2,3},{3,2},{4,5},{5,4},{6,7},{7,6},{8,9},{9,8},{10,11... | collective-permute-start | bytes 786440 | tf_op jit(solution)/shard_map/ppermute | solution.py:591
  89.8 3.0 %collective-permute-start.10 = (bf16[8,32,512]{2,1,0:T(8,128)(2,1)S(1)}, bf16[8,32,512]{2,1,0:T(8,128)(2,1)S(1)}, u32[]{:S(2)}, u32[]{:S(2)}) collective-permute-start(bf16[8,32,512]{2,1,0:T(8,128)(2,1)S(1)} %get-tuple-element.43), channel_id=1, source_target_pairs={{0,1},{1,0},{2,3},{3,2},{4,5},{5,4},{6,7},{7,6},{8,9},{9,8},{10,11... | collective-permute-start | bytes 786440 | tf_op jit(solution)/shard_map/ppermute | solution.py:591

commit v12 on v11

--- a/solution.py
+++ b/solution.py
@@ -441,32 +441,11 @@
     )(place, in_vmem(weight), stream, mine, sibling)
 
 
-def ffn_kernel(place, landing, mine, sibling, gain, gate, *refs):
+def ffn_kernel(place, mine, sibling, gain, gate, *refs):
     up, refs = refs[:SPLIT], refs[SPLIT:]
-    down, late, _, own_out, other_out, kv_out = refs[:6]
-    down_buf, normed, hidden, down_sem, late_sem = refs[6:]
-    member, half = place[0], place[1]
+    down, own_out, other_out, down_buf, normed, hidden, down_sem = refs
+    half = place[1]
     members, tokens, width = mine.shape
-    per_peer = ARRIVE // members
-    resident = kv_out.shape[0] - ARRIVE
-
-    def late_copy(i, k, c):
-        source = lax.rem(member - k + members, members)
-        spot = i * per_peer + c
-        return pltpu.make_async_copy(
-            late.at[spot], kv_out.at[resident + landing[source, c]], late_sem.at[spot]
-        )
-
-    late_chunks = [(0, 0), (1, 1), (2, members - 1)]
-
-    @pl.when(half == 1)
-    def _():
-        for i, k in late_chunks:
-
-            @pl.loop(0, per_peer)
-            def _(c):
-                late_copy(i, k, c).start()
-
     depth, hidden_count = up[0].shape
     features = depth * SPLIT
     down_copies = []
@@ -510,16 +489,8 @@
         own_out[t] = jnp.where(half == 0, first, second)
         other_out[t] = jnp.where(half == 0, second, first).astype(jnp.bfloat16)
 
-    @pl.when(half == 1)
-    def _():
-        for i, k in late_chunks:
-
-            @pl.loop(0, per_peer)
-            def _(c):
-                late_copy(i, k, c).wait()
-
-
-def feed_forward(place, landing, mine, sibling, gain, gate, up, down, late, kv):
+
+def feed_forward(place, mine, sibling, gain, gate, up, down):
     tokens = mine.shape[1]
     hidden_count, features = down.shape
     return pl.pallas_call(
@@ -527,31 +498,60 @@
         out_shape=[
             jax.ShapeDtypeStruct(mine.shape, jnp.float32),
             jax.ShapeDtypeStruct(mine.shape, jnp.bfloat16),
-            jax.ShapeDtypeStruct(kv.shape, kv.dtype),
         ],
-        in_specs=[SM, SM, VM, VM, VM] + [VM] * (1 + SPLIT) + [HBM, VM, HBM],
-        out_specs=[VM, VM, HBM],
-        input_output_aliases={5 + 1 + SPLIT + 2: 2},
+        in_specs=[SM, VM, VM, VM] + [VM] * (1 + SPLIT) + [HBM],
+        out_specs=[VM, VM],
         scratch_shapes=[
             pltpu.VMEM(down.shape, down.dtype),
             pltpu.VMEM((tokens, features), jnp.bfloat16),
             pltpu.VMEM((tokens, hidden_count), jnp.bfloat16),
             pltpu.SemaphoreType.DMA((mine.shape[0],)),
-            pltpu.SemaphoreType.DMA((late.shape[0],)),
         ],
         compiler_params=pltpu.CompilerParams(vmem_limit_bytes=19 * MIB),
         name="feed_forward",
-    )(
-        place,
-        landing,
-        mine,
-        sibling,
-        gain,
-        *map(in_vmem, (gate, *up)),
-        in_hbm(down),
-        late,
-        in_hbm(kv),
-    )
+    )(place, mine, sibling, gain, *map(in_vmem, (gate, *up)), in_hbm(down))
+
+
+def late_kernel(members, place, landing, late, _, __, kv_out, sems):
+    member, half = place[0], place[1]
+    per_peer = ARRIVE // members
+    resident = kv_out.shape[0] - ARRIVE
+
+    def page(i, k, c):
+        source = lax.rem(member - k + members, members)
+        spot = i * per_peer + c
+        return pltpu.make_async_copy(
+            late.at[spot], kv_out.at[resident + landing[source, c]], sems.at[spot]
+        )
+
+    chunks = [(0, 0), (1, 1), (2, members - 1)]
+
+    @pl.when(half == 1)
+    def _():
+        for i, k in chunks:
+
+            @pl.loop(0, per_peer, unroll=math.gcd(per_peer, 8))
+            def _(c):
+                page(i, k, c).start()
+
+        for i, k in chunks:
+
+            @pl.loop(0, per_peer, unroll=math.gcd(per_peer, 8))
+            def _(c):
+                page(i, k, c).wait()
+
+
+def place_late(place, landing, late, after, kv):
+    return pl.pallas_call(
+        functools.partial(late_kernel, landing.shape[0]),
+        out_shape=jax.ShapeDtypeStruct(kv.shape, kv.dtype),
+        in_specs=[SM, SM, VM, ANY, HBM],
+        out_specs=HBM,
+        scratch_shapes=[pltpu.SemaphoreType.DMA((late.shape[0],))],
+        input_output_aliases={4: 0},
+        compiler_params=pltpu.CompilerParams(vmem_limit_bytes=2 * MIB),
+        name="place_late",
+    )(place, landing, late, after, in_hbm(kv))
 
 
 def local(
@@ -626,21 +626,22 @@
     )
     late = lax.ppermute(late, "pd", [(0, 1)])
 
-    def everywhere(x):
+    def all_members(x):
         spread = jnp.broadcast_to(x[None], (members, *x.shape))
-        mine = lax.all_to_all(spread, "tp", split_axis=0, concat_axis=0)
-        return mine, swap(mine)
+        return lax.all_to_all(spread, "tp", split_axis=0, concat_axis=0)
 
     att_mine = combine(keep, swap(give), tokens)
-    here, there = everywhere(att_mine)
+    here = all_members(att_mine)
+    there = swap(here)
 
     inner = stream.reshape(steps, groups, rows, -1).transpose(1, 0, 2, 3).reshape(stream.shape)
     residual = project(place, held[0], inner, here, there, groups)
 
-    mine, sibling = everywhere(residual)
-    own, other, kv_after = feed_forward(
-        place, landing, mine, sibling, norm_gain, gate_weight, held[1:], down_weight, late, kv_part
-    )
+    mine = all_members(residual)
+    kv_after = place_late(place, landing, late, mine, kv_part)
+    mine, kv_after = lax.optimization_barrier((mine, kv_after))
+    sibling = swap(mine)
+    own, other = feed_forward(place, mine, sibling, norm_gain, gate_weight, held[1:], down_weight)
     summed = (own + swap(other).astype(jnp.float32)).astype(jnp.bfloat16)
     shares = lax.all_to_all(summed, "tp", split_axis=0, concat_axis=0)
     layer = residual.astype(jnp.float32) + jnp.sum(shares.astype(jnp.float32), axis=0)

time: 107 us -> 128 us (1.20)
  blocking collectives: 43 us -> 13 us
  local copies, waits for them, and re-layouts: 1.3 us -> 29.6 us
  waiting for transfers between devices: 3.78 us -> 22.2 us
  starting transfers between devices: 17.5 us -> 22.2 us
    all_to_all x2 -> x0, blocking collectives: 30.2 us -> none  [everywhere(): mine = lax.all_to_all(spread, 'tp', split_axis=0, concat_axis=0)]
    unnamed x20 -> x34, local copies, waits for them, and re-layouts: 0.07 us -> 27 us
    all_to_all x0 -> x2, waiting for transfers between devices: none -> 16.7 us  [all_members(): return lax.all_to_all(spread, 'tp', split_axis=0, concat_axis=0)]
    all_to_all x0 -> x2, starting transfers between devices: none -> 9.37 us  [all_members(): return lax.all_to_all(spread, 'tp', split_axis=0, concat_axis=0)]
    ppermute x4, starting transfers between devices: 5.63 us -> 1.61 us  [swap(): return lax.ppermute(x, 'pd', [(0, 1), (1, 0)])]
    ppermute x4, waiting for transfers between devices: 3.76 us -> 5.52 us  [swap(): return lax.ppermute(x, 'pd', [(0, 1), (1, 0)])]
    pallas_call x0 -> x1, Pallas kernels: none -> 1.65 us  [place_late(): pl.pallas_call(functools.partial(late_kernel, landing.shape[0]), out_shap...]
    broadcast_in_dim x2, local copies, waits for them, and re-layouts: 0.05 us -> 1.46 us  [all_members(): spread = jnp.broadcast_to(x[None], (members, *x.shape))]
  transfers between devices with their start and end apart: 11 -> 13, of which waited for: 3 -> 6; matrix products, arithmetic and copies ran while one was open for 2% -> 2% of each run, Pallas kernels for 11% -> 9%
where the time goes in v12:
time: 128 us; the launch traced here: 127 us
  Pallas kernels  37.4 us (29%)
  local copies, waits for them, and re-layouts  29.6 us (23%)
  starting transfers between devices  22.2 us (17%)
  waiting for transfers between devices  22.2 us (17%)
  blocking collectives  13 us (10%)
  other arithmetic  1.9 us (1%)
    unnamed x34, local copies, waits for them, and re-layouts  27 us
    all_to_all x2, waiting for transfers between devices, all_members(): return lax.all_to_all(spread, 'tp', split_axis=0, concat_axis=0)  16.7 us
    all_to_all x1, blocking collectives, local(): shares = lax.all_to_all(summed, 'tp', split_axis=0, concat_axis=0)  13 us
    pallas_call x1, Pallas kernels, feed_forward(): pl.pallas_call(ffn_kernel, out_shape=[jax.ShapeDtypeStruct(mine.shape, jn...  12.9 us
    all_to_all x2, starting transfers between devices, all_members(): return lax.all_to_all(spread, 'tp', split_axis=0, concat_axis=0)  9.37 us
    pallas_call x1, Pallas kernels, prepare(): pl.pallas_call(functools.partial(prepare_kernel, count, parts, groups), o...  8.78 us
    ppermute x5, starting transfers between devices, send(): return lax.ppermute(x, BOTH, route)  8.12 us
    ppermute x4, waiting for transfers between devices, swap(): return lax.ppermute(x, 'pd', [(0, 1), (1, 0)])  5.52 us
  transfers between devices with their start and end apart: 13, of which 6 were waited for; matrix products, arithmetic and copies ran while one was open for 2% of the time, Pallas kernels for 9%

profile of v12, /device:TPU:0, one launch (start us, length us, event | category | flops | bytes accessed | tf_op | source)
XLA Modules:
  0.0 127.2 jit_solution(18113012368446796328)
XLA Ops:
  0.7 5.4 %pack_pages.1 = (bf16[64,2,16,128]{3,2,1,0:T(8,128)(2,1)}, bf16[32,2,16,128]{3,2,1,0:T(8,128)(2,1)}, bf16[32,2,16,128]{3,2,1,0:T(8,128)(2,1)}, bf16[32,2,16,128]...) custom-call(s32[2]{0:T(128)S(1)} %pad_add_fusion.place, ...), custom_call_target="tpu_custom_call" | custom-call | tf_op jit(solution)/shard_map/pack_pages/pallas_call | solution.py:119
  6.2 1.3 %collective-permute-start = (bf16[64,2,16,128]{3,2,1,0:T(8,128)(2,1)}, bf16[64,2,16,128]{3,2,1,0:T(8,128)(2,1)S(1)}, u32[]{:S(2)}, u32[]{:S(2)}) collective-permute-start(bf16[64,2,16,128]{3,2,1,0:T(8,128)(2,1)} %get-tuple-element.24.refs_2_), channel_id=1, source_target_pairs={{0,1},{2,3},{4,5},{6,7},{8,9},{10,11},{12,13},{14,15},{16,17},{18,... | collective-permute-start | bytes 1572872 | tf_op jit(solution)/shard_map/ppermute | solution.py:595
  7.5 1.3 %collective-permute-start.2 = (bf16[32,2,16,128]{3,2,1,0:T(8,128)(2,1)}, bf16[32,2,16,128]{3,2,1,0:T(8,128)(2,1)S(1)}, u32[]{:S(2)}, u32[]{:S(2)}) collective-permute-start(bf16[32,2,16,128]{3,2,1,0:T(8,128)(2,1)} %get-tuple-element.30), channel_id=1, source_target_pairs={{0,7},{2,9},{4,11},{6,13},{8,15},{10,1},{12,3},{14,5},{16,23},{18,... | collective-permute-start | bytes 786440 | tf_op jit(solution)/shard_map/ppermute | solution.py:588
  8.8 1.3 %collective-permute-start.3 = (bf16[32,2,16,128]{3,2,1,0:T(8,128)(2,1)}, bf16[32,2,16,128]{3,2,1,0:T(8,128)(2,1)S(1)}, u32[]{:S(2)}, u32[]{:S(2)}) collective-permute-start(bf16[32,2,16,128]{3,2,1,0:T(8,128)(2,1)} %get-tuple-element.31), channel_id=1, source_target_pairs={{0,9},{2,11},{4,13},{6,15},{8,1},{10,3},{12,5},{14,7},{16,25},{18,... | collective-permute-start | bytes 786440 | tf_op jit(solution)/shard_map/ppermute | solution.py:588
  10.1 1.5 %collective-permute-start.4 = (bf16[32,2,16,128]{3,2,1,0:T(8,128)(2,1)}, bf16[32,2,16,128]{3,2,1,0:T(8,128)(2,1)S(1)}, u32[]{:S(2)}, u32[]{:S(2)}) collective-permute-start(bf16[32,2,16,128]{3,2,1,0:T(8,128)(2,1)} %get-tuple-element.32), channel_id=1, source_target_pairs={{0,11},{2,13},{4,15},{6,1},{8,3},{10,5},{12,7},{14,9},{16,27},{18,... | collective-permute-start | bytes 786440 | tf_op jit(solution)/shard_map/ppermute | solution.py:588
  12.7 1.1 slice_select_fusion
  14.4 3.4 %collective-permute-start.1 = (bf16[32,2,16,128]{3,2,1,0:T(8,128)(2,1)S(1)}, bf16[32,2,16,128]{3,2,1,0:T(8,128)(2,1)S(1)}, u32[]{:S(2)}, u32[]{:S(2)}) collective-permute-start(bf16[32,2,16,128]{3,2,1,0:T(8,128)(2,1)S(1)} %get-tuple-element.47), channel_id=1, source_target_pairs={{0,5},{2,7},{4,9},{6,11},{8,13},{10,15},{12,1},{14,3},{1,2},{3,4},... | collective-permute-start | bytes 786440 | tf_op jit(solution)/shard_map/ppermute | solution.py:588
  18.0 8.8 %prepare.1 = (bf16[512,8192]{1,0:T(8,128)(2,1)S(1)}, bf16[2048,1024]{1,0:T(8,128)(2,1)S(1)}, bf16[2048,1024]{1,0:T(8,128)(2,1)S(1)}, bf16[2048,1024]{1,0:T(8,128...) custom-call(s32[2]{0:T(128)S(1)} %pad_add_fusion.place, ...), custom_call_target="tpu_custom_call" | custom-call | bytes 25165824 | tf_op jit(solution)/shard_map/prepare/pallas_call | solution.py:236
  26.8 3.3 %copy-done.1 = bf16[512,8192]{1,0:T(8,128)(2,1)} copy-done((bf16[512,8192]{1,0:T(8,128)(2,1)}, bf16[512,8192]{1,0:T(8,128)(2,1)S(1)}, u32[]{:S(2)}) %copy-start.1) | copy-done | bytes 8388632
  30.1 2.0 %copy-done.3 = bf16[2048,1024]{1,0:T(8,128)(2,1)} copy-done((bf16[2048,1024]{1,0:T(8,128)(2,1)}, bf16[2048,1024]{1,0:T(8,128)(2,1)S(1)}, u32[]{:S(2)}) %copy-start.3) | copy-done | bytes 4194328
  32.1 1.9 %copy-done.5 = bf16[2048,1024]{1,0:T(8,128)(2,1)} copy-done((bf16[2048,1024]{1,0:T(8,128)(2,1)}, bf16[2048,1024]{1,0:T(8,128)(2,1)S(1)}, u32[]{:S(2)}) %copy-start.5) | copy-done | bytes 4194328
  34.0 2.0 %copy-done.7 = bf16[2048,1024]{1,0:T(8,128)(2,1)} copy-done((bf16[2048,1024]{1,0:T(8,128)(2,1)}, bf16[2048,1024]{1,0:T(8,128)(2,1)S(1)}, u32[]{:S(2)}) %copy-start.7) | copy-done | bytes 4194328
  36.0 2.0 %copy-done.9 = bf16[2048,1024]{1,0:T(8,128)(2,1)} copy-done((bf16[2048,1024]{1,0:T(8,128)(2,1)}, bf16[2048,1024]{1,0:T(8,128)(2,1)S(1)}, u32[]{:S(2)}) %copy-start.9) | copy-done | bytes 4194328
  38.1 5.4 %place_attend.1 = (bf16[312,2,16,128]{3,2,1,0:T(8,128)(2,1)}, f32[128,384]{1,0:T(8,128)S(1)}, f32[128,384]{1,0:T(8,128)S(1)}, bf16[96,2,16,128]{3,2,1,0:T(8,128)(2,1)S(1)}) custom-call(s32[2]{0:T(128)S(1)} %pad_add_fusion.place, s32[8,128]{1,0:T(8,128)S(1)} %get-tuple-element.26.landing, bf16[312,2,16,128]{3,2,1,0:T(8,128)(2,1)} %old_pool.1, ...), custom_call_target="tpu_custom_call" | custom-call | tf_op jit(solution)/shard_map/place_attend/pallas_call | solution.py:369
  43.5 1.3 %collective-permute-start.6 = (f32[128,384]{1,0:T(8,128)S(1)}, f32[128,384]{1,0:T(8,128)S(1)}, u32[]{:S(2)}, u32[]{:S(2)}) collective-permute-start(f32[128,384]{1,0:T(8,128)S(1)} %get-tuple-element.35), channel_id=1, source_target_pairs={{0,1},{1,0},{2,3},{3,2},{4,5},{5,4},{6,7},{7,6},{8,9},{9,8},{10,11... | collective-permute-start | bytes 589832 | tf_op jit(solution)/shard_map/ppermute | solution.py:591
  46.7 5.8 %all-to-all-start = ((bf16[8,32,512]{2,1,0:T(8,128)(2,1)}), bf16[8,32,512]{2,1,0:T(8,128)(2,1)S(1)}, u32[]{:S(2)}, u32[]{:S(2)}) async-start(bf16[8,32,512]{2,1,0:T(8,128)(2,1)} %broadcast_in_dim.4), calls=%async_computation | async-start | bytes 524288 | tf_op jit(solution)/shard_map/all_to_all | solution.py:631
  52.5 1.8 %collective-permute-start.8 = (bf16[96,2,16,128]{3,2,1,0:T(8,128)(2,1)S(1)}, bf16[96,2,16,128]{3,2,1,0:T(8,128)(2,1)S(1)}, u32[]{:S(2)}, u32[]{:S(2)}) collective-permute-start(bf16[96,2,16,128]{3,2,1,0:T(8,128)(2,1)S(1)} %get-tuple-element.36), channel_id=1, source_target_pairs={{0,1},{2,3},{4,5},{6,7},{8,9},{10,11},{12,13},{14,15},{16,17},{18,... | collective-permute-start | bytes 2359304 | tf_op jit(solution)/shard_map/ppermute | solution.py:627
  54.3 7.4 %all-to-all-done.mine = bf16[8,32,512]{2,1,0:T(8,128)(2,1)S(1)} async-done(((bf16[8,32,512]{2,1,0:T(8,128)(2,1)}), bf16[8,32,512]{2,1,0:T(8,128)(2,1)S(1)}, u32[]{:S(2)}, u32[]{:S(2)}) %all-to-all-start) | async-done | bytes 262176 | tf_op jit(solution)/shard_map/all_to_all | solution.py:631
  61.7 1.5 %collective-permute-done.7.sibling = bf16[8,32,512]{2,1,0:T(8,128)(2,1)S(1)} collective-permute-done((bf16[8,32,512]{2,1,0:T(8,128)(2,1)S(1)}, bf16[8,32,512]{2,1,0:T(8,128)(2,1)S(1)}, u32[]{:S(2)}, u32[]{:S(2)}) %collective-permute-start.7) | collective-permute-done | bytes 262176 | tf_op jit(solution)/shard_map/ppermute | solution.py:591
  63.3 3.4 %copy-done.2 = bf16[512,8192]{1,0:T(8,128)(2,1)S(1)} copy-done((bf16[512,8192]{1,0:T(8,128)(2,1)S(1)}, bf16[512,8192]{1,0:T(8,128)(2,1)}, u32[]{:S(2)}) %copy-start.2) | copy-done | bytes 8388632
  66.7 3.1 %out_projection.1 = bf16[32,512]{1,0:T(8,128)(2,1)S(1)} custom-call(s32[2]{0:T(128)S(1)} %pad_add_fusion.place, bf16[512,8192]{1,0:T(8,128)(2,1)S(1)} %copy-done.2, bf16[32,512]{1,0:T(8,128)(2,1)S(1)} %copy-done.12, bf16[8,32,512]{2,1,0:T(8,128)(2,1)S(1)} %all-to-all-done.mine, bf16[8,32,512]{2,1,0:T(8,128)(2,1)S(1)} %collective-permute-done.7.sibling), custom_call_target="tpu_custom_call" | custom-call | tf_op jit(solution)/shard_map/out_projection/pallas_call | solution.py:434
  70.5 3.6 %all-to-all-start.1 = ((bf16[8,32,512]{2,1,0:T(8,128)(2,1)}), bf16[8,32,512]{2,1,0:T(8,128)(2,1)S(1)}, u32[]{:S(2)}, u32[]{:S(2)}) async-start(bf16[8,32,512]{2,1,0:T(8,128)(2,1)} %broadcast_in_dim.5), calls=%async_computation.1 | async-start | bytes 524288 | tf_op jit(solution)/shard_map/all_to_all | solution.py:631
  74.1 9.3 %all-to-all-done.1._.mine = bf16[8,32,512]{2,1,0:T(8,128)(2,1)S(1)} async-done(((bf16[8,32,512]{2,1,0:T(8,128)(2,1)}), bf16[8,32,512]{2,1,0:T(8,128)(2,1)S(1)}, u32[]{:S(2)}, u32[]{:S(2)}) %all-to-all-start.1) | async-done | bytes 262176 | tf_op jit(solution)/shard_map/all_to_all | solution.py:631
  83.4 1.6 %place_late.1 = bf16[312,2,16,128]{3,2,1,0:T(8,128)(2,1)} custom-call(s32[2]{0:T(128)S(1)} %pad_add_fusion.place, s32[8,128]{1,0:T(8,128)S(1)} %get-tuple-element.26.landing, bf16[96,2,16,128]{3,2,1,0:T(8,128)(2,1)S(1)} %collective-permute-done.8.late, bf16[8,32,512]{2,1,0:T(8,128)(2,1)S(1)} %all-to-all-done.1._.mine, ...), custom_call_target="tpu_custom_call", output_to_operand_aliasing={{}: (4, {})} | custom-call | tf_op jit(solution)/shard_map/place_late/pallas_call | solution.py:545
  85.1 1.5 %collective-permute-done.9.sibling = bf16[8,32,512]{2,1,0:T(8,128)(2,1)S(1)} collective-permute-done((bf16[8,32,512]{2,1,0:T(8,128)(2,1)S(1)}, bf16[8,32,512]{2,1,0:T(8,128)(2,1)S(1)}, u32[]{:S(2)}, u32[]{:S(2)}) %collective-permute-start.9) | collective-permute-done | bytes 262176 | tf_op jit(solution)/shard_map/ppermute | solution.py:591
  86.6 5.8 %copy-done = bf16[8192,1024]{1,0:T(8,128)(2,1)S(1)} copy-done((bf16[8192,1024]{1,0:T(8,128)(2,1)S(1)}, bf16[8192,1024]{1,0:T(8,128)(2,1)}, u32[]{:S(2)}) %copy-start) | copy-done | bytes 16777240
  92.4 2.2 %copy-done.6 = bf16[2048,1024]{1,0:T(8,128)(2,1)S(1)} copy-done((bf16[2048,1024]{1,0:T(8,128)(2,1)S(1)}, bf16[2048,1024]{1,0:T(8,128)(2,1)}, u32[]{:S(2)}) %copy-start.6) | copy-done | bytes 4194328
  94.6 2.2 %copy-done.8 = bf16[2048,1024]{1,0:T(8,128)(2,1)S(1)} copy-done((bf16[2048,1024]{1,0:T(8,128)(2,1)S(1)}, bf16[2048,1024]{1,0:T(8,128)(2,1)}, u32[]{:S(2)}) %copy-start.8) | copy-done | bytes 4194328
  96.8 2.2 %copy-done.10 = bf16[2048,1024]{1,0:T(8,128)(2,1)S(1)} copy-done((bf16[2048,1024]{1,0:T(8,128)(2,1)S(1)}, bf16[2048,1024]{1,0:T(8,128)(2,1)}, u32[]{:S(2)}) %copy-start.10) | copy-done | bytes 4194328
  99.0 12.9 %feed_forward.1 = (f32[8,32,512]{2,1,0:T(8,128)S(1)}, bf16[8,32,512]{2,1,0:T(8,128)(2,1)S(1)}) custom-call(s32[2]{0:T(128)S(1)} %pad_add_fusion.place, bf16[8,32,512]{2,1,0:T(8,128)(2,1)S(1)} %all-to-all-done.1._.mine, bf16[8,32,512]{2,1,0:T(8,128)(2,1)S(1)} %collective-permute-done.9.sibling, f32[8192]{0:T(1024)S(1)} %copy-done.13, ...), custom_call_target="tpu_custom_call" | custom-call | tf_op jit(solution)/shard_map/feed_forward/pallas_call | solution.py:496
  112.1 1.4 %collective-permute-done.10 = bf16[8,32,512]{2,1,0:T(8,128)(2,1)S(1)} collective-permute-done((bf16[8,32,512]{2,1,0:T(8,128)(2,1)S(1)}, bf16[8,32,512]{2,1,0:T(8,128)(2,1)S(1)}, u32[]{:S(2)}, u32[]{:S(2)}) %collective-permute-start.10) | collective-permute-done | bytes 262176 | tf_op jit(solution)/shard_map/ppermute | solution.py:591
  113.6 13.0 %all_to_all.15 = bf16[8,32,512]{2,1,0:T(8,128)(2,1)S(1)} all-to-all(bf16[8,32,512]{2,1,0:T(8,128)(2,1)S(1)} %add_convert_fusion), channel_id=1, replica_groups=mesh['grp'=2,'tp'=8,'pd'=2] {'tp'}, dimensions={0} | all-to-all | bytes 524288 | tf_op jit(solution)/shard_map/all_to_all | solution.py:646
  (49 shorter events, 5.5 us)
Async XLA Ops:
  0.6 17.2 %copy-start.15 = (s32[2496]{0:T(1024)S(1)}, s32[2496]{0:T(1024)}, u32[]{:S(2)}) copy-start(s32[2496]{0:T(1024)} %pages.1) | copy-start | bytes 29956
  0.6 17.2 %copy-start.14 = (bf16[16,2,2,128]{3,2,1,0:T(2,128)(2,1)S(1)}, bf16[16,2,2,128]{3,2,1,0:T(2,128)(2,1)}, u32[]{:S(2)}) copy-start(bf16[16,2,2,128]{3,2,1,0:T(2,128)(2,1)} %param.17) | copy-start | bytes 49156
  6.2 6.5 %collective-permute-start = (bf16[64,2,16,128]{3,2,1,0:T(8,128)(2,1)}, bf16[64,2,16,128]{3,2,1,0:T(8,128)(2,1)S(1)}, u32[]{:S(2)}, u32[]{:S(2)}) collective-permute-start(bf16[64,2,16,128]{3,2,1,0:T(8,128)(2,1)} %get-tuple-element.24.refs_2_), channel_id=1, source_target_pairs={{0,1},{2,3},{4,5},{6,7},{8,9},{10,11},{12,13},{14,15},{16,17},{18,... | collective-permute-start | bytes 1572872 | tf_op jit(solution)/shard_map/ppermute | solution.py:595
  7.5 30.5 %collective-permute-start.2 = (bf16[32,2,16,128]{3,2,1,0:T(8,128)(2,1)}, bf16[32,2,16,128]{3,2,1,0:T(8,128)(2,1)S(1)}, u32[]{:S(2)}, u32[]{:S(2)}) collective-permute-start(bf16[32,2,16,128]{3,2,1,0:T(8,128)(2,1)} %get-tuple-element.30), channel_id=1, source_target_pairs={{0,7},{2,9},{4,11},{6,13},{8,15},{10,1},{12,3},{14,5},{16,23},{18,... | collective-permute-start | bytes 786440 | tf_op jit(solution)/shard_map/ppermute | solution.py:588
  8.8 29.2 %collective-permute-start.3 = (bf16[32,2,16,128]{3,2,1,0:T(8,128)(2,1)}, bf16[32,2,16,128]{3,2,1,0:T(8,128)(2,1)S(1)}, u32[]{:S(2)}, u32[]{:S(2)}) collective-permute-start(bf16[32,2,16,128]{3,2,1,0:T(8,128)(2,1)} %get-tuple-element.31), channel_id=1, source_target_pairs={{0,9},{2,11},{4,13},{6,15},{8,1},{10,3},{12,5},{14,7},{16,25},{18,... | collective-permute-start | bytes 786440 | tf_op jit(solution)/shard_map/ppermute | solution.py:588
  10.1 27.9 %collective-permute-start.4 = (bf16[32,2,16,128]{3,2,1,0:T(8,128)(2,1)}, bf16[32,2,16,128]{3,2,1,0:T(8,128)(2,1)S(1)}, u32[]{:S(2)}, u32[]{:S(2)}) collective-permute-start(bf16[32,2,16,128]{3,2,1,0:T(8,128)(2,1)} %get-tuple-element.32), channel_id=1, source_target_pairs={{0,11},{2,13},{4,15},{6,1},{8,3},{10,5},{12,7},{14,9},{16,27},{18,... | collective-permute-start | bytes 786440 | tf_op jit(solution)/shard_map/ppermute | solution.py:588
  13.8 24.2 %collective-permute-start.5 = (bf16[32,2,16,128]{3,2,1,0:T(8,128)(2,1)S(1)}, bf16[32,2,16,128]{3,2,1,0:T(8,128)(2,1)S(1)}, u32[]{:S(2)}, u32[]{:S(2)}) collective-permute-start(bf16[32,2,16,128]{3,2,1,0:T(8,128)(2,1)S(1)} %get-tuple-element.46), channel_id=1, source_target_pairs={{0,13},{2,15},{4,1},{6,3},{8,5},{10,7},{12,9},{14,11},{1,14},{3,0}... | collective-permute-start | bytes 786440 | tf_op jit(solution)/shard_map/ppermute | solution.py:588
  14.4 23.7 %collective-permute-start.1 = (bf16[32,2,16,128]{3,2,1,0:T(8,128)(2,1)S(1)}, bf16[32,2,16,128]{3,2,1,0:T(8,128)(2,1)S(1)}, u32[]{:S(2)}, u32[]{:S(2)}) collective-permute-start(bf16[32,2,16,128]{3,2,1,0:T(8,128)(2,1)S(1)} %get-tuple-element.47), channel_id=1, source_target_pairs={{0,5},{2,7},{4,9},{6,11},{8,13},{10,15},{12,1},{14,3},{1,2},{3,4},... | collective-permute-start | bytes 786440 | tf_op jit(solution)/shard_map/ppermute | solution.py:588
  18.0 20.1 %copy-start.11 = (bf16[32,2,16,128]{3,2,1,0:T(8,128)(2,1)S(1)}, bf16[32,2,16,128]{3,2,1,0:T(8,128)(2,1)}, u32[]{:S(2)}) copy-start(bf16[32,2,16,128]{3,2,1,0:T(8,128)(2,1)} %get-tuple-element.28.refs_2_) | copy-start | bytes 786436
  26.8 3.3 %copy-start.1 = (bf16[512,8192]{1,0:T(8,128)(2,1)}, bf16[512,8192]{1,0:T(8,128)(2,1)S(1)}, u32[]{:S(2)}) copy-start(bf16[512,8192]{1,0:T(8,128)(2,1)S(1)} %get-tuple-element.25.weight) | copy-start | bytes 25165828
  30.1 2.0 %copy-start.3 = (bf16[2048,1024]{1,0:T(8,128)(2,1)}, bf16[2048,1024]{1,0:T(8,128)(2,1)S(1)}, u32[]{:S(2)}) copy-start(bf16[2048,1024]{1,0:T(8,128)(2,1)S(1)} %get-tuple-element.40.refs_0_) | copy-start | bytes 12582916
  32.1 1.9 %copy-start.5 = (bf16[2048,1024]{1,0:T(8,128)(2,1)}, bf16[2048,1024]{1,0:T(8,128)(2,1)S(1)}, u32[]{:S(2)}) copy-start(bf16[2048,1024]{1,0:T(8,128)(2,1)S(1)} %get-tuple-element.41.refs_1_) | copy-start | bytes 12582916
  34.0 2.0 %copy-start.7 = (bf16[2048,1024]{1,0:T(8,128)(2,1)}, bf16[2048,1024]{1,0:T(8,128)(2,1)S(1)}, u32[]{:S(2)}) copy-start(bf16[2048,1024]{1,0:T(8,128)(2,1)S(1)} %get-tuple-element.42.refs_2_) | copy-start | bytes 12582916
  36.0 2.0 %copy-start.9 = (bf16[2048,1024]{1,0:T(8,128)(2,1)}, bf16[2048,1024]{1,0:T(8,128)(2,1)S(1)}, u32[]{:S(2)}) copy-start(bf16[2048,1024]{1,0:T(8,128)(2,1)S(1)} %get-tuple-element.43.refs_3_) | copy-start | bytes 12582916
  38.0 25.3 %copy-start.12 = (bf16[32,512]{1,0:T(8,128)(2,1)S(1)}, bf16[32,512]{1,0:T(8,128)(2,1)}, u32[]{:S(2)}) copy-start(bf16[32,512]{1,0:T(8,128)(2,1)} %stream.1) | copy-start | bytes 98308
  43.5 2.4 %collective-permute-start.6 = (f32[128,384]{1,0:T(8,128)S(1)}, f32[128,384]{1,0:T(8,128)S(1)}, u32[]{:S(2)}, u32[]{:S(2)}) collective-permute-start(f32[128,384]{1,0:T(8,128)S(1)} %get-tuple-element.35), channel_id=1, source_target_pairs={{0,1},{1,0},{2,3},{3,2},{4,5},{5,4},{6,7},{7,6},{8,9},{9,8},{10,11... | collective-permute-start | bytes 589832 | tf_op jit(solution)/shard_map/ppermute | solution.py:591
  46.7 15.0 %all-to-all-start = ((bf16[8,32,512]{2,1,0:T(8,128)(2,1)}), bf16[8,32,512]{2,1,0:T(8,128)(2,1)S(1)}, u32[]{:S(2)}, u32[]{:S(2)}) async-start(bf16[8,32,512]{2,1,0:T(8,128)(2,1)} %broadcast_in_dim.4), calls=%async_computation | async-start | bytes 524288 | tf_op jit(solution)/shard_map/all_to_all | solution.py:631
  52.5 21.6 %collective-permute-start.8 = (bf16[96,2,16,128]{3,2,1,0:T(8,128)(2,1)S(1)}, bf16[96,2,16,128]{3,2,1,0:T(8,128)(2,1)S(1)}, u32[]{:S(2)}, u32[]{:S(2)}) collective-permute-start(bf16[96,2,16,128]{3,2,1,0:T(8,128)(2,1)S(1)} %get-tuple-element.36), channel_id=1, source_target_pairs={{0,1},{2,3},{4,5},{6,7},{8,9},{10,11},{12,13},{14,15},{16,17},{18,... | collective-permute-start | bytes 2359304 | tf_op jit(solution)/shard_map/ppermute | solution.py:627
  61.7 1.5 %collective-permute-start.7 = (bf16[8,32,512]{2,1,0:T(8,128)(2,1)S(1)}, bf16[8,32,512]{2,1,0:T(8,128)(2,1)S(1)}, u32[]{:S(2)}, u32[]{:S(2)}) collective-permute-start(bf16[8,32,512]{2,1,0:T(8,128)(2,1)S(1)} %all-to-all-done.mine), channel_id=1, source_target_pairs={{0,1},{1,0},{2,3},{3,2},{4,5},{5,4},{6,7},{7,6},{8,9},{9,8},{10,11... | collective-permute-start | bytes 786440 | tf_op jit(solution)/shard_map/ppermute | solution.py:591
  63.3 3.4 %copy-start.2 = (bf16[512,8192]{1,0:T(8,128)(2,1)S(1)}, bf16[512,8192]{1,0:T(8,128)(2,1)}, u32[]{:S(2)}) copy-start(bf16[512,8192]{1,0:T(8,128)(2,1)} %copy-done.1) | copy-start | bytes 25165828
  69.8 16.9 %copy-start.13 = (f32[8192]{0:T(1024)S(1)}, f32[8192]{0:T(1024)}, u32[]{:S(2)}) copy-start(f32[8192]{0:T(1024)} %gain.1) | copy-start | bytes 98308
  70.5 12.9 %all-to-all-start.1 = ((bf16[8,32,512]{2,1,0:T(8,128)(2,1)}), bf16[8,32,512]{2,1,0:T(8,128)(2,1)S(1)}, u32[]{:S(2)}, u32[]{:S(2)}) async-start(bf16[8,32,512]{2,1,0:T(8,128)(2,1)} %broadcast_in_dim.5), calls=%async_computation.1 | async-start | bytes 524288 | tf_op jit(solution)/shard_map/all_to_all | solution.py:631
  83.4 3.3 %copy-start.4 = (bf16[2048,1024]{1,0:T(8,128)(2,1)S(1)}, bf16[2048,1024]{1,0:T(8,128)(2,1)}, u32[]{:S(2)}) copy-start(bf16[2048,1024]{1,0:T(8,128)(2,1)} %copy-done.3) | copy-start | bytes 12582916
  85.0 1.6 %collective-permute-start.9 = (bf16[8,32,512]{2,1,0:T(8,128)(2,1)S(1)}, bf16[8,32,512]{2,1,0:T(8,128)(2,1)S(1)}, u32[]{:S(2)}, u32[]{:S(2)}) collective-permute-start(bf16[8,32,512]{2,1,0:T(8,128)(2,1)S(1)} %all-to-all-done.1._.mine), channel_id=1, source_target_pairs={{0,1},{1,0},{2,3},{3,2},{4,5},{5,4},{6,7},{7,6},{8,9},{9,8},{10,11... | collective-permute-start | bytes 786440 | tf_op jit(solution)/shard_map/ppermute | solution.py:591
  86.6 5.8 %copy-start = (bf16[8192,1024]{1,0:T(8,128)(2,1)S(1)}, bf16[8192,1024]{1,0:T(8,128)(2,1)}, u32[]{:S(2)}) copy-start(bf16[8192,1024]{1,0:T(8,128)(2,1)} %gate.1) | copy-start | bytes 50331652
  92.4 2.2 %copy-start.6 = (bf16[2048,1024]{1,0:T(8,128)(2,1)S(1)}, bf16[2048,1024]{1,0:T(8,128)(2,1)}, u32[]{:S(2)}) copy-start(bf16[2048,1024]{1,0:T(8,128)(2,1)} %copy-done.5) | copy-start | bytes 12582916
  94.6 2.2 %copy-start.8 = (bf16[2048,1024]{1,0:T(8,128)(2,1)S(1)}, bf16[2048,1024]{1,0:T(8,128)(2,1)}, u32[]{:S(2)}) copy-start(bf16[2048,1024]{1,0:T(8,128)(2,1)} %copy-done.7) | copy-start | bytes 12582916
  96.8 2.2 %copy-start.10 = (bf16[2048,1024]{1,0:T(8,128)(2,1)S(1)}, bf16[2048,1024]{1,0:T(8,128)(2,1)}, u32[]{:S(2)}) copy-start(bf16[2048,1024]{1,0:T(8,128)(2,1)} %copy-done.9) | copy-start | bytes 12582916
  111.9 1.6 %collective-permute-start.10 = (bf16[8,32,512]{2,1,0:T(8,128)(2,1)S(1)}, bf16[8,32,512]{2,1,0:T(8,128)(2,1)S(1)}, u32[]{:S(2)}, u32[]{:S(2)}) collective-permute-start(bf16[8,32,512]{2,1,0:T(8,128)(2,1)S(1)} %get-tuple-element.45), channel_id=1, source_target_pairs={{0,1},{1,0},{2,3},{3,2},{4,5},{5,4},{6,7},{7,6},{8,9},{9,8},{10,11... | collective-permute-start | bytes 786440 | tf_op jit(solution)/shard_map/ppermute | solution.py:591

commit v13 on v11

--- a/solution.py
+++ b/solution.py
@@ -463,7 +463,7 @@
     def _():
         for i, k in late_chunks:
 
-            @pl.loop(0, per_peer)
+            @pl.loop(0, per_peer, unroll=math.gcd(per_peer, 16))
             def _(c):
                 late_copy(i, k, c).start()
 
@@ -514,7 +514,7 @@
     def _():
         for i, k in late_chunks:
 
-            @pl.loop(0, per_peer)
+            @pl.loop(0, per_peer, unroll=math.gcd(per_peer, 16))
             def _(c):
                 late_copy(i, k, c).wait()
 

time: 107 us -> 106 us (level)
  starting transfers between devices: 17.5 us -> 16.4 us
    ppermute x4, starting transfers between devices: 5.63 us -> 4.54 us  [swap(): return lax.ppermute(x, 'pd', [(0, 1), (1, 0)])]
  transfers between devices with their start and end apart: 11 -> 11, of which waited for: 3 -> 3; matrix products, arithmetic and copies ran while one was open for 2% -> 2% of each run, Pallas kernels for 11% -> 12%
where the time goes in v13:
time: 106 us; the launch traced here: 105 us
  blocking collectives  43 us (41%)
  Pallas kernels  37.9 us (36%)
  starting transfers between devices  16.4 us (15%)
  waiting for transfers between devices  3.78 us (4%)
  other arithmetic  1.91 us (2%)
  local copies, waits for them, and re-layouts  1.3 us (1%)
    all_to_all x2, blocking collectives, everywhere(): mine = lax.all_to_all(spread, 'tp', split_axis=0, concat_axis=0)  30.2 us
    pallas_call x1, Pallas kernels, feed_forward(): pl.pallas_call(ffn_kernel, out_shape=[jax.ShapeDtypeStruct(mine.shape, jn...  14 us
    all_to_all x1, blocking collectives, local(): shares = lax.all_to_all(summed, 'tp', split_axis=0, concat_axis=0)  12.7 us
    pallas_call x1, Pallas kernels, prepare(): pl.pallas_call(functools.partial(prepare_kernel, count, parts, groups), o...  9.07 us
    ppermute x5, starting transfers between devices, send(): return lax.ppermute(x, BOTH, route)  8.12 us
    pallas_call x1, Pallas kernels, place_and_attend(): pl.pallas_call(functools.partial(attend_kernel, members, steps, chunks),...  6.19 us
    pallas_call x1, Pallas kernels, pack(): pl.pallas_call(functools.partial(pack_kernel, members), out_shape=[pltpu....  5.45 us
    ppermute x4, starting transfers between devices, swap(): return lax.ppermute(x, 'pd', [(0, 1), (1, 0)])  4.54 us
  transfers between devices with their start and end apart: 11, of which 3 were waited for; matrix products, arithmetic and copies ran while one was open for 2% of the time, Pallas kernels for 12%

profile of v13, /device:TPU:0, one launch (start us, length us, event | category | flops | bytes accessed | tf_op | source)
XLA Modules:
  0.0 105.2 jit_solution(12567326275417350986)
XLA Ops:
  0.6 0.0 copy-start.4
  0.7 0.1 pad_add_fusion.place
  0.7 5.4 %pack_pages.1 = (bf16[64,2,16,128]{3,2,1,0:T(8,128)(2,1)}, bf16[32,2,16,128]{3,2,1,0:T(8,128)(2,1)}, bf16[32,2,16,128]{3,2,1,0:T(8,128)(2,1)}, bf16[32,2,16,128]...) custom-call(s32[2]{0:T(128)S(1)} %pad_add_fusion.place, ...), custom_call_target="tpu_custom_call" | custom-call | tf_op jit(solution)/shard_map/pack_pages/pallas_call | solution.py:119
  6.2 1.3 %collective-permute-start = (bf16[64,2,16,128]{3,2,1,0:T(8,128)(2,1)}, bf16[64,2,16,128]{3,2,1,0:T(8,128)(2,1)S(1)}, u32[]{:S(2)}, u32[]{:S(2)}) collective-permute-start(bf16[64,2,16,128]{3,2,1,0:T(8,128)(2,1)} %get-tuple-element.23.refs_2_), channel_id=1, source_target_pairs={{0,1},{2,3},{4,5},{6,7},{8,9},{10,11},{12,13},{14,15},{16,17},{18,... | collective-permute-start | bytes 1572872 | tf_op jit(solution)/shard_map/ppermute | solution.py:595
  7.5 1.3 %collective-permute-start.2 = (bf16[32,2,16,128]{3,2,1,0:T(8,128)(2,1)}, bf16[32,2,16,128]{3,2,1,0:T(8,128)(2,1)S(1)}, u32[]{:S(2)}, u32[]{:S(2)}) collective-permute-start(bf16[32,2,16,128]{3,2,1,0:T(8,128)(2,1)} %get-tuple-element.29), channel_id=1, source_target_pairs={{0,7},{2,9},{4,11},{6,13},{8,15},{10,1},{12,3},{14,5},{16,23},{18,... | collective-permute-start | bytes 786440 | tf_op jit(solution)/shard_map/ppermute | solution.py:588
  8.8 1.3 %collective-permute-start.3 = (bf16[32,2,16,128]{3,2,1,0:T(8,128)(2,1)}, bf16[32,2,16,128]{3,2,1,0:T(8,128)(2,1)S(1)}, u32[]{:S(2)}, u32[]{:S(2)}) collective-permute-start(bf16[32,2,16,128]{3,2,1,0:T(8,128)(2,1)} %get-tuple-element.30), channel_id=1, source_target_pairs={{0,9},{2,11},{4,13},{6,15},{8,1},{10,3},{12,5},{14,7},{16,25},{18,... | collective-permute-start | bytes 786440 | tf_op jit(solution)/shard_map/ppermute | solution.py:588
  10.1 1.5 %collective-permute-start.4 = (bf16[32,2,16,128]{3,2,1,0:T(8,128)(2,1)}, bf16[32,2,16,128]{3,2,1,0:T(8,128)(2,1)S(1)}, u32[]{:S(2)}, u32[]{:S(2)}) collective-permute-start(bf16[32,2,16,128]{3,2,1,0:T(8,128)(2,1)} %get-tuple-element.31), channel_id=1, source_target_pairs={{0,11},{2,13},{4,15},{6,1},{8,3},{10,5},{12,7},{14,9},{16,27},{18,... | collective-permute-start | bytes 786440 | tf_op jit(solution)/shard_map/ppermute | solution.py:588
  11.7 1.0 fusion
  12.7 1.1 %slice_select_fusion = (bf16[32,2,16,128]{3,2,1,0:T(8,128)(2,1)S(1)}, bf16[32,2,16,128]{3,2,1,0:T(8,128)(2,1)S(1)}) fusion(bf16[32,2,16,128]{3,2,1,0:T(8,128)(2,1)} %get-tuple-element.32, bf16[64,2,16,128]{3,2,1,0:T(8,128)(2,1)S(1)} %collective-permute-done, pred[]{:T(512)S(6)} %eq.4, bf16[32,2,16,128]{3,2,1,0:T(8,128)(2,1)} %get-tuple-element.28), kind=kLoop, calls=%fused_computation.2 | loop fusion | flops 262144 | bytes 1572865 | tf_op jit(solution)/shard_map/jit(_where)/select_n | solution.py:601
  13.8 0.5 collective-permute-start.5
  14.4 3.4 %collective-permute-start.1 = (bf16[32,2,16,128]{3,2,1,0:T(8,128)(2,1)S(1)}, bf16[32,2,16,128]{3,2,1,0:T(8,128)(2,1)S(1)}, u32[]{:S(2)}, u32[]{:S(2)}) collective-permute-start(bf16[32,2,16,128]{3,2,1,0:T(8,128)(2,1)S(1)} %get-tuple-element.45), channel_id=1, source_target_pairs={{0,5},{2,7},{4,9},{6,11},{8,13},{10,15},{12,1},{14,3},{1,2},{3,4},... | collective-permute-start | bytes 786440 | tf_op jit(solution)/shard_map/ppermute | solution.py:588
  17.9 0.1 reshape.9.listed
  18.0 0.0 slice-start
  18.0 9.1 %prepare.1 = (bf16[512,8192]{1,0:T(8,128)(2,1)S(1)}, bf16[2048,1024]{1,0:T(8,128)(2,1)S(1)}, bf16[2048,1024]{1,0:T(8,128)(2,1)S(1)}, bf16[2048,1024]{1,0:T(8,128...) custom-call(s32[2]{0:T(128)S(1)} %pad_add_fusion.place, ...), custom_call_target="tpu_custom_call" | custom-call | bytes 25165824 | tf_op jit(solution)/shard_map/prepare/pallas_call | solution.py:236
  27.1 0.0 copy-start.1
  27.2 6.2 %place_attend.1 = (bf16[312,2,16,128]{3,2,1,0:T(8,128)(2,1)}, f32[128,384]{1,0:T(8,128)S(1)}, f32[128,384]{1,0:T(8,128)S(1)}, bf16[96,2,16,128]{3,2,1,0:T(8,128)(2,1)S(1)}) custom-call(s32[2]{0:T(128)S(1)} %pad_add_fusion.place, s32[8,128]{1,0:T(8,128)S(1)} %get-tuple-element.24.landing, bf16[312,2,16,128]{3,2,1,0:T(8,128)(2,1)} %old_pool.1, ...), custom_call_target="tpu_custom_call" | custom-call | tf_op jit(solution)/shard_map/place_attend/pallas_call | solution.py:369
  33.4 3.8 %collective-permute-start.6 = (f32[128,384]{1,0:T(8,128)S(1)}, f32[128,384]{1,0:T(8,128)S(1)}, u32[]{:S(2)}, u32[]{:S(2)}) collective-permute-start(f32[128,384]{1,0:T(8,128)S(1)} %get-tuple-element.34), channel_id=1, source_target_pairs={{0,1},{1,0},{2,3},{3,2},{4,5},{5,4},{6,7},{7,6},{8,9},{9,8},{10,11... | collective-permute-start | bytes 589832 | tf_op jit(solution)/shard_map/ppermute | solution.py:591
  37.2 1.1 %collective-permute-done.6.other = f32[128,384]{1,0:T(8,128)S(1)} collective-permute-done((f32[128,384]{1,0:T(8,128)S(1)}, f32[128,384]{1,0:T(8,128)S(1)}, u32[]{:S(2)}, u32[]{:S(2)}) %collective-permute-start.6) | collective-permute-done | bytes 196640 | tf_op jit(solution)/shard_map/ppermute | solution.py:591
  38.3 0.1 combine.1
  38.3 0.0 slice-start.3
  38.4 18.3 %all_to_all.15.mine = bf16[8,32,512]{2,1,0:T(8,128)(2,1)S(1)} all-to-all(bf16[8,32,512]{2,1,0:T(8,128)(2,1)S(1)} %broadcast_in_dim.4), channel_id=1, replica_groups=mesh['grp'=2,'tp'=8,'pd'=2] {'tp'}, dimensions={0} | all-to-all | bytes 524288 | tf_op jit(solution)/shard_map/all_to_all | solution.py:631
  56.7 2.4 %collective-permute-start.9 = (bf16[96,2,16,128]{3,2,1,0:T(8,128)(2,1)S(1)}, bf16[96,2,16,128]{3,2,1,0:T(8,128)(2,1)S(1)}, u32[]{:S(2)}, u32[]{:S(2)}) collective-permute-start(bf16[96,2,16,128]{3,2,1,0:T(8,128)(2,1)S(1)} %get-tuple-element.39), channel_id=1, source_target_pairs={{0,1},{2,3},{4,5},{6,7},{8,9},{10,11},{12,13},{14,15},{16,17},{18,... | collective-permute-start | bytes 2359304 | tf_op jit(solution)/shard_map/ppermute | solution.py:627
  59.2 0.0 copy-start.2
  59.2 3.1 %out_projection.1 = bf16[32,512]{1,0:T(8,128)(2,1)S(1)} custom-call(s32[2]{0:T(128)S(1)} %pad_add_fusion.place, bf16[512,8192]{1,0:T(8,128)(2,1)S(1)} %get-tuple-element.25.weight, bf16[32,512]{1,0:T(8,128)(2,1)S(1)} %copy-done.1, bf16[8,32,512]{2,1,0:T(8,128)(2,1)S(1)} %all_to_all.15.mine, bf16[8,32,512]{2,1,0:T(8,128)(2,1)S(1)} %collective-permute-done.7.sibling), custom_call_target="tpu_custom_call" | custom-call | tf_op jit(solution)/shard_map/out_projection/pallas_call | solution.py:434
  62.3 11.9 %all_to_all.16.mine = bf16[8,32,512]{2,1,0:T(8,128)(2,1)S(1)} all-to-all(bf16[8,32,512]{2,1,0:T(8,128)(2,1)S(1)} %broadcast_in_dim.5), channel_id=1, replica_groups=mesh['grp'=2,'tp'=8,'pd'=2] {'tp'}, dimensions={0} | all-to-all | bytes 524288 | tf_op jit(solution)/shard_map/all_to_all | solution.py:631
  74.2 1.5 %collective-permute-done.8.sibling = bf16[8,32,512]{2,1,0:T(8,128)(2,1)S(1)} collective-permute-done((bf16[8,32,512]{2,1,0:T(8,128)(2,1)S(1)}, bf16[8,32,512]{2,1,0:T(8,128)(2,1)S(1)}, u32[]{:S(2)}, u32[]{:S(2)}) %collective-permute-start.8) | collective-permute-done | bytes 262176 | tf_op jit(solution)/shard_map/ppermute | solution.py:591
  75.8 14.0 %feed_forward.1 = (f32[8,32,512]{2,1,0:T(8,128)S(1)}, bf16[8,32,512]{2,1,0:T(8,128)(2,1)S(1)}, bf16[312,2,16,128]{3,2,1,0:T(8,128)(2,1)}) custom-call(s32[2]{0:T(128)S(1)} %pad_add_fusion.place, s32[8,128]{1,0:T(8,128)S(1)} %get-tuple-element.24.landing, bf16[8,32,512]{2,1,0:T(8,128)(2,1)S(1)} %all_to_all.16.mine, ...), custom_call_target="tpu_custom_call", output_to_operand_aliasing={{2}: (12, {})} | custom-call | tf_op jit(solution)/shard_map/feed_forward/pallas_call | solution.py:525
  89.8 0.8 collective-permute-start.10
  90.6 1.2 %collective-permute-done.10 = bf16[8,32,512]{2,1,0:T(8,128)(2,1)S(1)} collective-permute-done((bf16[8,32,512]{2,1,0:T(8,128)(2,1)S(1)}, bf16[8,32,512]{2,1,0:T(8,128)(2,1)S(1)}, u32[]{:S(2)}, u32[]{:S(2)}) %collective-permute-start.10) | collective-permute-done | bytes 262176 | tf_op jit(solution)/shard_map/ppermute | solution.py:591
  91.8 0.1 add_convert_fusion
  91.8 12.7 %all_to_all.17 = bf16[8,32,512]{2,1,0:T(8,128)(2,1)S(1)} all-to-all(bf16[8,32,512]{2,1,0:T(8,128)(2,1)S(1)} %add_convert_fusion), channel_id=1, replica_groups=mesh['grp'=2,'tp'=8,'pd'=2] {'tp'}, dimensions={0} | all-to-all | bytes 524288 | tf_op jit(solution)/shard_map/all_to_all | solution.py:645
  104.6 0.6 add_convert_fusion.1
  (33 shorter events, 0.2 us)
Async XLA Ops:
  0.6 17.2 %copy-start.4 = (s32[2496]{0:T(1024)S(1)}, s32[2496]{0:T(1024)}, u32[]{:S(2)}) copy-start(s32[2496]{0:T(1024)} %pages.1) | copy-start | bytes 29956
  0.6 17.2 %copy-start.3 = (bf16[16,2,2,128]{3,2,1,0:T(2,128)(2,1)S(1)}, bf16[16,2,2,128]{3,2,1,0:T(2,128)(2,1)}, u32[]{:S(2)}) copy-start(bf16[16,2,2,128]{3,2,1,0:T(2,128)(2,1)} %param.17) | copy-start | bytes 49156
  6.2 6.5 %collective-permute-start = (bf16[64,2,16,128]{3,2,1,0:T(8,128)(2,1)}, bf16[64,2,16,128]{3,2,1,0:T(8,128)(2,1)S(1)}, u32[]{:S(2)}, u32[]{:S(2)}) collective-permute-start(bf16[64,2,16,128]{3,2,1,0:T(8,128)(2,1)} %get-tuple-element.23.refs_2_), channel_id=1, source_target_pairs={{0,1},{2,3},{4,5},{6,7},{8,9},{10,11},{12,13},{14,15},{16,17},{18,... | collective-permute-start | bytes 1572872 | tf_op jit(solution)/shard_map/ppermute | solution.py:595
  7.5 19.6 %collective-permute-start.2 = (bf16[32,2,16,128]{3,2,1,0:T(8,128)(2,1)}, bf16[32,2,16,128]{3,2,1,0:T(8,128)(2,1)S(1)}, u32[]{:S(2)}, u32[]{:S(2)}) collective-permute-start(bf16[32,2,16,128]{3,2,1,0:T(8,128)(2,1)} %get-tuple-element.29), channel_id=1, source_target_pairs={{0,7},{2,9},{4,11},{6,13},{8,15},{10,1},{12,3},{14,5},{16,23},{18,... | collective-permute-start | bytes 786440 | tf_op jit(solution)/shard_map/ppermute | solution.py:588
  8.8 18.3 %collective-permute-start.3 = (bf16[32,2,16,128]{3,2,1,0:T(8,128)(2,1)}, bf16[32,2,16,128]{3,2,1,0:T(8,128)(2,1)S(1)}, u32[]{:S(2)}, u32[]{:S(2)}) collective-permute-start(bf16[32,2,16,128]{3,2,1,0:T(8,128)(2,1)} %get-tuple-element.30), channel_id=1, source_target_pairs={{0,9},{2,11},{4,13},{6,15},{8,1},{10,3},{12,5},{14,7},{16,25},{18,... | collective-permute-start | bytes 786440 | tf_op jit(solution)/shard_map/ppermute | solution.py:588
  10.1 17.0 %collective-permute-start.4 = (bf16[32,2,16,128]{3,2,1,0:T(8,128)(2,1)}, bf16[32,2,16,128]{3,2,1,0:T(8,128)(2,1)S(1)}, u32[]{:S(2)}, u32[]{:S(2)}) collective-permute-start(bf16[32,2,16,128]{3,2,1,0:T(8,128)(2,1)} %get-tuple-element.31), channel_id=1, source_target_pairs={{0,11},{2,13},{4,15},{6,1},{8,3},{10,5},{12,7},{14,9},{16,27},{18,... | collective-permute-start | bytes 786440 | tf_op jit(solution)/shard_map/ppermute | solution.py:588
  13.8 13.4 %collective-permute-start.5 = (bf16[32,2,16,128]{3,2,1,0:T(8,128)(2,1)S(1)}, bf16[32,2,16,128]{3,2,1,0:T(8,128)(2,1)S(1)}, u32[]{:S(2)}, u32[]{:S(2)}) collective-permute-start(bf16[32,2,16,128]{3,2,1,0:T(8,128)(2,1)S(1)} %get-tuple-element.44), channel_id=1, source_target_pairs={{0,13},{2,15},{4,1},{6,3},{8,5},{10,7},{12,9},{14,11},{1,14},{3,0}... | collective-permute-start | bytes 786440 | tf_op jit(solution)/shard_map/ppermute | solution.py:588
  14.4 12.8 %collective-permute-start.1 = (bf16[32,2,16,128]{3,2,1,0:T(8,128)(2,1)S(1)}, bf16[32,2,16,128]{3,2,1,0:T(8,128)(2,1)S(1)}, u32[]{:S(2)}, u32[]{:S(2)}) collective-permute-start(bf16[32,2,16,128]{3,2,1,0:T(8,128)(2,1)S(1)} %get-tuple-element.45), channel_id=1, source_target_pairs={{0,5},{2,7},{4,9},{6,11},{8,13},{10,15},{12,1},{14,3},{1,2},{3,4},... | collective-permute-start | bytes 786440 | tf_op jit(solution)/shard_map/ppermute | solution.py:588
  18.0 9.2 %copy-start = (bf16[32,2,16,128]{3,2,1,0:T(8,128)(2,1)S(1)}, bf16[32,2,16,128]{3,2,1,0:T(8,128)(2,1)}, u32[]{:S(2)}) copy-start(bf16[32,2,16,128]{3,2,1,0:T(8,128)(2,1)} %get-tuple-element.27.refs_2_) | copy-start | bytes 786436
  18.0 57.8 %slice-start = ((s8[16777216]{0:T(1024)(128)(4,1)}), s8[4194304]{0:T(1024)(128)(4,1)S(1)}, s32[]{:S(2)}) async-start(s8[16777216]{0:T(1024)(128)(4,1)} %bitcast.8), calls=%async_computation.3 | async-start | bytes 8388608
  18.0 57.7 %slice-start.1 = ((s8[16777216]{0:T(1024)(128)(4,1)}), s8[4194304]{0:T(1024)(128)(4,1)S(1)}, s32[]{:S(2)}) async-start(s8[16777216]{0:T(1024)(128)(4,1)} %bitcast.8), calls=%async_computation.4 | async-start | bytes 8388608
  18.0 57.7 %slice-start.2 = ((s8[16777216]{0:T(1024)(128)(4,1)}), s8[4194304]{0:T(1024)(128)(4,1)S(1)}, s32[]{:S(2)}) async-start(s8[16777216]{0:T(1024)(128)(4,1)} %bitcast.8), calls=%async_computation.5 | async-start | bytes 8388608
  27.1 32.0 %copy-start.1 = (bf16[32,512]{1,0:T(8,128)(2,1)S(1)}, bf16[32,512]{1,0:T(8,128)(2,1)}, u32[]{:S(2)}) copy-start(bf16[32,512]{1,0:T(8,128)(2,1)} %stream.1) | copy-start | bytes 98308
  33.4 4.8 %collective-permute-start.6 = (f32[128,384]{1,0:T(8,128)S(1)}, f32[128,384]{1,0:T(8,128)S(1)}, u32[]{:S(2)}, u32[]{:S(2)}) collective-permute-start(f32[128,384]{1,0:T(8,128)S(1)} %get-tuple-element.34), channel_id=1, source_target_pairs={{0,1},{1,0},{2,3},{3,2},{4,5},{5,4},{6,7},{7,6},{8,9},{9,8},{10,11... | collective-permute-start | bytes 589832 | tf_op jit(solution)/shard_map/ppermute | solution.py:591
  38.3 37.4 %slice-start.3 = ((s8[16777216]{0:T(1024)(128)(4,1)}), s8[4194304]{0:T(1024)(128)(4,1)S(1)}, s32[]{:S(2)}) async-start(s8[16777216]{0:T(1024)(128)(4,1)} %bitcast.8), calls=%async_computation.6 | async-start | bytes 8388608
  56.7 2.5 %collective-permute-start.7 = (bf16[8,32,512]{2,1,0:T(8,128)(2,1)S(1)}, bf16[8,32,512]{2,1,0:T(8,128)(2,1)S(1)}, u32[]{:S(2)}, u32[]{:S(2)}) collective-permute-start(bf16[8,32,512]{2,1,0:T(8,128)(2,1)S(1)} %all_to_all.15.mine), channel_id=1, source_target_pairs={{0,1},{1,0},{2,3},{3,2},{4,5},{5,4},{6,7},{7,6},{8,9},{9,8},{10,11... | collective-permute-start | bytes 786440 | tf_op jit(solution)/shard_map/ppermute | solution.py:591
  56.7 17.6 %collective-permute-start.9 = (bf16[96,2,16,128]{3,2,1,0:T(8,128)(2,1)S(1)}, bf16[96,2,16,128]{3,2,1,0:T(8,128)(2,1)S(1)}, u32[]{:S(2)}, u32[]{:S(2)}) collective-permute-start(bf16[96,2,16,128]{3,2,1,0:T(8,128)(2,1)S(1)} %get-tuple-element.39), channel_id=1, source_target_pairs={{0,1},{2,3},{4,5},{6,7},{8,9},{10,11},{12,13},{14,15},{16,17},{18,... | collective-permute-start | bytes 2359304 | tf_op jit(solution)/shard_map/ppermute | solution.py:627
  59.2 16.6 %copy-start.2 = (f32[8192]{0:T(1024)S(1)}, f32[8192]{0:T(1024)}, u32[]{:S(2)}) copy-start(f32[8192]{0:T(1024)} %gain.1) | copy-start | bytes 98308
  74.2 1.5 %collective-permute-start.8 = (bf16[8,32,512]{2,1,0:T(8,128)(2,1)S(1)}, bf16[8,32,512]{2,1,0:T(8,128)(2,1)S(1)}, u32[]{:S(2)}, u32[]{:S(2)}) collective-permute-start(bf16[8,32,512]{2,1,0:T(8,128)(2,1)S(1)} %all_to_all.16.mine), channel_id=1, source_target_pairs={{0,1},{1,0},{2,3},{3,2},{4,5},{5,4},{6,7},{7,6},{8,9},{9,8},{10,11... | collective-permute-start | bytes 786440 | tf_op jit(solution)/shard_map/ppermute | solution.py:591
  89.8 1.9 %collective-permute-start.10 = (bf16[8,32,512]{2,1,0:T(8,128)(2,1)S(1)}, bf16[8,32,512]{2,1,0:T(8,128)(2,1)S(1)}, u32[]{:S(2)}, u32[]{:S(2)}) collective-permute-start(bf16[8,32,512]{2,1,0:T(8,128)(2,1)S(1)} %get-tuple-element.43), channel_id=1, source_target_pairs={{0,1},{1,0},{2,3},{3,2},{4,5},{5,4},{6,7},{7,6},{8,9},{9,8},{10,11... | collective-permute-start | bytes 786440 | tf_op jit(solution)/shard_map/ppermute | solution.py:591
